TPU v7x, 32 devices: a whole 2x2x4 slice. The times are simulated.
32 devices in a mesh: section: 2 (over x), mp: 16 (over z, y, core).
Axes of the slice: x: 2, y: 2, z: 4, core: 2. Of those that a mesh axis runs over, the one named last changes fastest.
Arguments:
- hidden: bfloat16 [2, 32, 8192], P('section', 'mp'), may hold values from -6 to 6
- attn_gain: float32 [2, 8192], P('section'), may hold values from 0.1 to 1.9
- w_query: bfloat16 [2, 8192, 8192], P('section', None, 'mp'), may hold values from -0.0625 to 0.0625
- w_key: bfloat16 [2, 8192, 1024], P('section', None, 'mp'), may hold values from -0.0625 to 0.0625
- w_value: bfloat16 [2, 8192, 1024], P('section', None, 'mp'), may hold values from -0.0625 to 0.0625
- w_out: bfloat16 [2, 8192, 8192], P('section', 'mp'), may hold values from -0.0625 to 0.0625
- mlp_gain: float32 [2, 8192], P('section'), may hold values from 0.1 to 1.9
- w_gate_up: bfloat16 [2, 8192, 2, 16384], P('section', None, None, 'mp'), may hold values from -0.0625 to 0.0625
- w_down: bfloat16 [2, 16384, 8192], P('section', 'mp'), may hold values from -0.046875 to 0.046875
- key_cache: bfloat16 [2, 2, 32, 512, 1024], P('section', None, 'mp'), may hold values from -620 to 620
- value_cache: bfloat16 [2, 2, 32, 512, 1024], P('section', None, 'mp'), may hold values from -6 to 6
- lengths: int32 [2, 32], P(None, 'mp'), may hold values from 1 to 512, 8192 in all within a row
Outputs:
- out: bfloat16 [2, 32, 8192], P('section', 'mp')
Inputs may be any that keep to these rules, and one draw needn't show every extreme that they name: In each micro-batch the lengths of the 32 batch rows sum to 8192, and one batch row has exactly 512.
All inputs are finite; a program needn't handle non-finite values. No bound on the sum of `lengths` on one device may be relied on, other than what follows from the above.
Results may differ from a plain program's by a relative error of at most 0.039.
Values may be sent and summed in bfloat16 or wider, within the bound.
No kernel may reach another device: no remote copies, remote signals or barrier semaphores. Data moves between devices by JAX's collectives and lax.ppermute only.
A program may use at most 192 MiB of HBM per device.

v0:
```python
import jax
import jax.numpy as jnp
from jax import lax
from jax.sharding import PartitionSpec as P

QUERY_HEADS = 64
KEY_VALUE_HEADS = 8
HEAD_SIZE = 128


epsilon = 1e-05


def passed_along(value, axis, steps):
    count = lax.axis_size(axis)
    pairs = [(source, (source + steps) % count) for source in range(count)]
    return lax.ppermute(value, axis, pairs)


def norm_rows(values, norm_gain):
    wide = values.astype(jnp.float32)
    square_mean = jnp.mean(wide * wide, axis=-1, keepdims=True)
    return (wide * lax.rsqrt(square_mean + epsilon) * norm_gain).astype(jnp.bfloat16)


def rotate(features, positions):
    half_dim = HEAD_SIZE // 2
    frequency = 500000.0 ** (-2.0 * jnp.arange(half_dim, dtype=jnp.float32) / HEAD_SIZE)
    angles = positions.astype(jnp.float32)[:, None] * frequency[None, :]
    cosine = jnp.cos(angles)[:, None, :]
    sine_part = jnp.sin(angles)[:, None, :]
    wide = features.astype(jnp.float32).reshape(features.shape[0], -1, HEAD_SIZE)
    first_half = wide[..., :half_dim]
    second_half = wide[..., half_dim:]
    turned = jnp.concatenate(
        [
            first_half * cosine - second_half * sine_part,
            second_half * cosine + first_half * sine_part,
        ],
        axis=-1,
    )
    return turned.reshape(features.shape).astype(jnp.bfloat16)


def attend(query_rows, fresh_key, fresh_value, cached_key_rows, cached_value_rows, current):
    cached_row_count = query_rows.shape[0]
    heads_per_group = QUERY_HEADS // KEY_VALUE_HEADS
    score_scale = HEAD_SIZE ** (-0.5)
    query_head_rows = query_rows.reshape(
        cached_row_count, KEY_VALUE_HEADS, heads_per_group, HEAD_SIZE
    )
    key_head_rows = cached_key_rows.reshape(cached_row_count, -1, KEY_VALUE_HEADS, HEAD_SIZE)
    value_head_rows = cached_value_rows.reshape(cached_row_count, -1, KEY_VALUE_HEADS, HEAD_SIZE)
    scores = (
        jnp.einsum(
            "rgjd,rlgd->rgjl", query_head_rows, key_head_rows, preferred_element_type=jnp.float32
        )
        * score_scale
    )
    self_score = (
        jnp.einsum(
            "zneh,znh->zne",
            query_head_rows,
            fresh_key.reshape(cached_row_count, KEY_VALUE_HEADS, HEAD_SIZE),
            preferred_element_type=jnp.float32,
        )
        * score_scale
    )
    places = jnp.arange(key_head_rows.shape[1], dtype=jnp.int32)
    live = (places[None, :] < current[:, None])[:, None, None, :]
    scores = jnp.where(live, scores, -1e30)
    highest = jnp.maximum(jnp.max(scores, axis=-1), self_score)
    raised = jnp.exp(scores - highest[..., None])
    own_raised = jnp.exp(self_score - highest)
    denominator = jnp.sum(raised, axis=-1) + own_raised
    weights = (raised / denominator[..., None]).astype(jnp.bfloat16)
    self_weight = (own_raised / denominator).astype(jnp.bfloat16)
    mixed_output = jnp.einsum(
        "rgjl,rlgd->rgjd", weights, value_head_rows, preferred_element_type=jnp.float32
    )
    mixed_output = mixed_output + self_weight.astype(jnp.float32)[..., None] * fresh_value.astype(
        jnp.float32
    ).reshape(cached_row_count, KEY_VALUE_HEADS, 1, HEAD_SIZE)
    return mixed_output.reshape(cached_row_count, QUERY_HEADS * HEAD_SIZE).astype(jnp.bfloat16)


def body(
    hidden,
    attn_gain,
    w_query,
    w_key,
    w_value,
    w_out,
    mlp_gain,
    w_gate_up,
    w_down,
    key_cache,
    value_cache,
    lengths,
):
    rows_dev = hidden.shape[1]
    section_index = lax.axis_index("section")
    model_index = lax.axis_index("mp")
    query_proj = w_query[0]
    key_proj = w_key[0]
    value_proj = w_value[0]
    out_proj = w_out[0]
    gate_up = w_gate_up[0]
    down_proj = w_down[0]
    first_gain = attn_gain[0]
    second_gain = mlp_gain[0]
    key_store = key_cache[0]
    value_store = value_cache[0]
    query_cols = query_proj.shape[1]
    key_cols = key_proj.shape[1]
    whole = lax.all_gather(hidden[0], "mp", axis=0, tiled=True)
    for turn_index in range(2):
        project_normed = norm_rows(whole, first_gain)
        joined = jnp.concatenate(
            [
                jnp.dot(project_normed, query_proj, preferred_element_type=jnp.float32),
                jnp.dot(project_normed, key_proj, preferred_element_type=jnp.float32),
                jnp.dot(project_normed, value_proj, preferred_element_type=jnp.float32),
            ],
            axis=1,
        ).astype(jnp.bfloat16)
        micro_batch = jnp.remainder(section_index + turn_index, 2)
        query_rows = lax.all_to_all(
            joined[:, :query_cols], "mp", split_axis=0, concat_axis=1, tiled=True
        )
        fresh_key = lax.all_to_all(
            joined[:, query_cols : query_cols + key_cols],
            "mp",
            split_axis=0,
            concat_axis=1,
            tiled=True,
        )
        fresh_value = lax.all_to_all(
            joined[:, query_cols + key_cols :], "mp", split_axis=0, concat_axis=1, tiled=True
        )
        current = lax.dynamic_index_in_dim(lengths, micro_batch, 0, keepdims=False)
        cached_key_rows = lax.dynamic_index_in_dim(key_store, micro_batch, 0, keepdims=False)
        cached_value_rows = lax.dynamic_index_in_dim(value_store, micro_batch, 0, keepdims=False)
        mixed_output = attend(
            rotate(query_rows, current),
            rotate(fresh_key, current),
            fresh_value,
            cached_key_rows,
            cached_value_rows,
            current,
        )
        heads_out = lax.all_to_all(mixed_output, "mp", split_axis=1, concat_axis=0, tiled=True)
        attn_part = lax.psum(jnp.dot(heads_out, out_proj, preferred_element_type=jnp.float32), "mp")
        middle = (whole.astype(jnp.float32) + attn_part).astype(jnp.bfloat16)
        gate_and_up = jnp.einsum(
            "rd,dcf->rcf",
            norm_rows(middle, second_gain),
            gate_up,
            preferred_element_type=jnp.float32,
        )
        acts = (jax.nn.silu(gate_and_up[:, 0]) * gate_and_up[:, 1]).astype(jnp.bfloat16)
        mlp_part = lax.psum(jnp.dot(acts, down_proj, preferred_element_type=jnp.float32), "mp")
        whole = (middle.astype(jnp.float32) + mlp_part).astype(jnp.bfloat16)
        if turn_index == 0:
            whole = passed_along(whole, "section", 1)
    stream = lax.dynamic_slice_in_dim(whole, model_index * rows_dev, rows_dev, 0)
    return stream[None]


def solution(mesh):
    placed = (
        P("section", "mp", None),
        P("section", None),
        P("section", None, "mp"),
        P("section", None, "mp"),
        P("section", None, "mp"),
        P("section", "mp", None),
        P("section", None),
        P("section", None, None, "mp"),
        P("section", "mp", None),
        P("section", None, "mp", None, None),
        P("section", None, "mp", None, None),
        P(None, "mp"),
    )
    return jax.shard_map(
        body, mesh=mesh, in_specs=placed, out_specs=P("section", "mp", None), check_vma=False
    )
```

profile of v0, /device:TPU:0, one launch (start us, length us, event | category | flops | bytes accessed | tf_op | source)
XLA Modules:
  0.0 617.5 jit_solution(10743142402774544003)
XLA Ops:
  7.4 26.2 %all-gather = bf16[1,32,8192]{2,0,1:T(2,128)(2,1)S(1)} all-gather(bf16[1,2,8192]{2,0,1:T(2,128)(2,1)S(1)} %copy.35), channel_id=2, replica_groups=mesh['section'=2,'mp'=16] {'mp'}, dimensions={1}, use_global_device_ids=true | all-gather | bytes 557056 | tf_op jit(solution)/shard_map/all_gather | solution.py:116
  37.9 3.4 all-to-all-start.1
  41.4 4.9 fusion.18
  47.3 7.8 %constant_dynamic-slice_fusion.3 = (bf16[1,1,2,512,1024]{4,3,2,1,0:T(8,128)(2,1)}, bf16[1,1,2,512,1024]{4,3,2,1,0:T(8,128)(2,1)}, bf16[1,1,2,512,1024]{4,3,2,1,0:T(8,128)(2,1)}, bf16[1,1,2,512,1024]{4,3,2,1,0:T(8,128)(2,1)}) fusion(bf16[1,2,2,512,1024]{4,3,2,1,0:T(8,128)(2,1)} %param.22, s32[]{:T(128)S(6)} %select_n.34, s32[]{:T(128)S(6)} %select_n.37, ...), kind=kLoop, calls=%fused_computation.120 | loop fusion | bytes 16777224 | tf_op jit(solution)/shard_map/jit(dynamic_index_in_dim)/dynamic_slice | solution.py:143
  55.3 4.0 copy.63
  59.9 3.9 copy.64
  63.9 5.9 all-to-all-start.2
  69.9 6.3 %all-to-all-done.2 = bf16[16,2,64]{2,1,0:T(2,128)(2,1)S(1)} async-done(((bf16[16,2,64]{2,1,0:T(2,128)(2,1)}), bf16[16,2,64]{2,1,0:T(2,128)(2,1)S(1)}, u32[]{:S(2)}, u32[]{:S(2)}) %all-to-all-start.2) | async-done | bytes 4128 | tf_op jit(solution)/shard_map/all_to_all | solution.py:138
  76.2 3.5 all-to-all-start
  80.0 6.3 %all-to-all-done = bf16[16,2,512]{2,1,0:T(2,128)(2,1)S(1)} async-done(((bf16[16,2,512]{2,1,0:T(2,128)(2,1)}), bf16[16,2,512]{2,1,0:T(2,128)(2,1)S(1)}, u32[]{:S(2)}, u32[]{:S(2)}) %all-to-all-start) | async-done | bytes 32800 | tf_op jit(solution)/shard_map/all_to_all | solution.py:128
  89.0 2.3 fusion.24
  91.4 9.2 %all_to_all.110 = bf16[2,16,512]{2,0,1:T(2,128)(2,1)S(1)} all-to-all(bf16[2,16,512]{2,0,1:T(2,128)(2,1)S(1)} %copy.44), channel_id=1, replica_groups=mesh['section'=2,'mp'=16] {'mp'}, dimensions={1} | all-to-all | bytes 65536 | tf_op jit(solution)/shard_map/all_to_all | solution.py:152
  100.7 5.9 fusion.10
  106.8 90.4 %all-reduce.5.cloned.1.call-done = f32[32,8192]{1,0:T(8,128)} async-done(((f32[32,8192]{1,0:T(8,128)}), f32[32,8192]{1,0:T(8,128)}) %all-reduce.5.cloned.1.call-update) | async-done | bytes 1048592 | tf_op jit(solution)/shard_map/psum | solution.py:153
  199.2 20.5 %fusion.2 = f32[32,2,1024]{2,0,1:T(8,128)S(1)} fusion(bf16[8192,2,1024]{2,1,0:T(2,128)(2,1)} %bitcast.127, bf16[32,8192]{1,0:T(8,128)(2,1)S(1)} %get-tuple-element.10, f32[8192]{0:T(1024)S(1)} %bitcast.129, f32[32]{0:T(128)S(1)} %add_rsqrt_fusion.2), kind=kOutput, calls=%fused_computation.2 | convolution fusion | flops 1074790400 | bytes 34373760 | tf_op jit(solution)/shard_map/rd,dcf->rcf/dot_general | solution.py:155
  219.7 9.8 %fusion.6 = f32[32,8192]{1,0:T(8,128)} fusion(bf16[1,1024,8192]{2,1,0:T(8,128)(2,1)} %param.20, f32[32,2,1024]{2,0,1:T(8,128)S(1)} %fusion.2), kind=kOutput, calls=%fused_computation.6 | convolution fusion | flops 537067520 | bytes 18087936 | tf_op jit(solution)/shard_map/dot_general | solution.py:162
  229.5 92.8 %all-reduce.7.cloned.1.call-done = f32[32,8192]{1,0:T(8,128)} async-done(((f32[32,8192]{1,0:T(8,128)}), f32[32,8192]{1,0:T(8,128)}) %all-reduce.7.cloned.1.call-update) | async-done | bytes 1048592 | tf_op jit(solution)/shard_map/psum | solution.py:162
  326.0 3.9 copy.65
  330.0 2.6 copy.66
  332.5 5.4 collective-permute-done
  341.3 3.7 all-to-all-start.6
  345.0 5.3 fusion.21
  353.1 6.0 all-to-all-start.5
  359.2 6.3 %all-to-all-done.5 = bf16[16,2,64]{2,1,0:T(2,128)(2,1)S(1)} async-done(((bf16[16,2,64]{2,1,0:T(2,128)(2,1)}), bf16[16,2,64]{2,1,0:T(2,128)(2,1)S(1)}, u32[]{:S(2)}, u32[]{:S(2)}) %all-to-all-start.5) | async-done | bytes 4128 | tf_op jit(solution)/shard_map/all_to_all | solution.py:131
  365.5 3.5 all-to-all-start.4
  369.3 6.3 %all-to-all-done.4 = bf16[16,2,512]{2,1,0:T(2,128)(2,1)S(1)} async-done(((bf16[16,2,512]{2,1,0:T(2,128)(2,1)}), bf16[16,2,512]{2,1,0:T(2,128)(2,1)S(1)}, u32[]{:S(2)}, u32[]{:S(2)}) %all-to-all-start.4) | async-done | bytes 32800 | tf_op jit(solution)/shard_map/all_to_all | solution.py:128
  379.1 9.2 %all_to_all.111 = bf16[2,16,512]{2,0,1:T(2,128)(2,1)S(1)} all-to-all(bf16[2,16,512]{2,0,1:T(2,128)(2,1)S(1)} %copy.53), channel_id=1, replica_groups=mesh['section'=2,'mp'=16] {'mp'}, dimensions={1} | all-to-all | bytes 65536 | tf_op jit(solution)/shard_map/all_to_all | solution.py:152
  388.3 5.9 fusion.8
  394.3 90.5 %all-reduce.9.cloned.1.call-done = f32[32,8192]{1,0:T(8,128)} async-done(((f32[32,8192]{1,0:T(8,128)}), f32[32,8192]{1,0:T(8,128)}) %all-reduce.9.cloned.1.call-update) | async-done | bytes 1048592 | tf_op jit(solution)/shard_map/psum | solution.py:153
  486.5 20.3 %fusion = f32[32,2,1024]{2,0,1:T(8,128)S(1)} fusion(bf16[8192,2,1024]{2,1,0:T(2,128)(2,1)} %bitcast.128, f32[32,8192]{1,0:T(8,128)S(1)} %get-tuple-element.6, f32[32]{0:T(128)S(1)} %add_rsqrt_fusion, f32[8192]{0:T(1024)S(1)} %bitcast.130), kind=kOutput, calls=%fused_computation | convolution fusion | flops 1074528256 | bytes 34898048 | tf_op jit(solution)/shard_map/rd,dcf->rcf/dot_general | solution.py:155
  506.8 9.8 %fusion.4 = f32[32,8192]{1,0:T(8,128)} fusion(bf16[1,1024,8192]{2,1,0:T(8,128)(2,1)} %param.20, f32[32,2,1024]{2,0,1:T(8,128)S(1)} %fusion), kind=kOutput, calls=%fused_computation.4 | convolution fusion | flops 537067520 | bytes 18087936 | tf_op jit(solution)/shard_map/dot_general | solution.py:162
  516.6 92.7 %all-reduce.11.cloned.1.call-done = f32[32,8192]{1,0:T(8,128)} async-done(((f32[32,8192]{1,0:T(8,128)}), f32[32,8192]{1,0:T(8,128)}) %all-reduce.11.cloned.1.call-update) | async-done | bytes 1048592 | tf_op jit(solution)/shard_map/psum | solution.py:162
  (90 shorter events, 29.3 us)
Async XLA Ops:
  6.5 39.7 %copy-start = (bf16[1,8192,64]{1,2,0:T(8,128)(2,1)S(1)}, bf16[1,8192,64]{1,2,0:T(8,128)(2,1)}, u32[]{:S(2)}) copy-start(bf16[1,8192,64]{1,2,0:T(8,128)(2,1)} %param.16) | copy-start | bytes 3145732
  37.9 25.9 %all-to-all-start.1 = ((bf16[16,2,64]{2,1,0:T(2,128)(2,1)}), bf16[16,2,64]{2,1,0:T(2,128)(2,1)S(1)}, u32[]{:S(2)}, u32[]{:S(2)}) async-start(bf16[16,2,64]{2,1,0:T(2,128)(2,1)} %bitcast.9), calls=%async_computation.1 | async-start | bytes 16384 | tf_op jit(solution)/shard_map/all_to_all | solution.py:131
  41.4 5.9 copy-start.6
  63.9 12.4 %all-to-all-start.2 = ((bf16[16,2,64]{2,1,0:T(2,128)(2,1)}), bf16[16,2,64]{2,1,0:T(2,128)(2,1)S(1)}, u32[]{:S(2)}, u32[]{:S(2)}) async-start(bf16[16,2,64]{2,1,0:T(2,128)(2,1)} %bitcast.16), calls=%async_computation.2 | async-start | bytes 16384 | tf_op jit(solution)/shard_map/all_to_all | solution.py:138
  76.2 10.1 %all-to-all-start = ((bf16[16,2,512]{2,1,0:T(2,128)(2,1)}), bf16[16,2,512]{2,1,0:T(2,128)(2,1)S(1)}, u32[]{:S(2)}, u32[]{:S(2)}) async-start(bf16[16,2,512]{2,1,0:T(2,128)(2,1)} %all_to_all.84), calls=%async_computation | async-start | bytes 65536 | tf_op jit(solution)/shard_map/all_to_all | solution.py:128
  79.7 117.5 %all-reduce.5.cloned.1.call-start = ((), (), s32[]{:S(2)}) async-start(), calls=%async_computation.8 | async-start | bytes 2097152 | tf_op jit(solution)/shard_map/psum | solution.py:153
  100.7 98.6 %copy-start.7 = (f32[1,8192]{1,0:T(1,128)S(1)}, f32[1,8192]{1,0:T(1,128)}, u32[]{:S(2)}) copy-start(f32[1,8192]{1,0:T(1,128)} %param.18) | copy-start | bytes 98308
  106.6 215.7 %all-reduce.7.cloned.1.call-start = ((), (), s32[]{:S(2)}) async-start(), calls=%async_computation.9 | async-start | bytes 2097152 | tf_op jit(solution)/shard_map/psum | solution.py:162
  199.2 20.5 %copy-start.3 = (bf16[32,8192]{1,0:T(8,128)(2,1)}, bf16[32,8192]{1,0:T(8,128)(2,1)S(1)}, u32[]{:S(2)}) copy-start(bf16[32,8192]{1,0:T(8,128)(2,1)S(1)} %get-tuple-element.10) | copy-start | bytes 1572868
  229.5 100.5 %copy-start.1 = (bf16[1,1,2,512,1024]{4,3,2,1,0:T(8,128)(2,1)S(1)}, bf16[1,1,2,512,1024]{4,3,2,1,0:T(8,128)(2,1)}, u32[]{:S(2)}) copy-start(bf16[1,1,2,512,1024]{4,3,2,1,0:T(8,128)(2,1)} %get-tuple-element.16) | copy-start | bytes 6291460
  229.5 109.7 %copy-start.5 = (f32[1,8192]{1,0:T(1,128)S(1)}, f32[1,8192]{1,0:T(1,128)}, u32[]{:S(2)}) copy-start(f32[1,8192]{1,0:T(1,128)} %param.13) | copy-start | bytes 98308
  324.6 13.4 %collective-permute-start = (bf16[32,8192]{1,0:T(8,128)(2,1)}, bf16[32,8192]{1,0:T(8,128)(2,1)}, u32[]{:S(2)}, u32[]{:S(2)}) collective-permute-start(bf16[32,8192]{1,0:T(8,128)(2,1)} %fusion.29), channel_id=1, source_target_pairs={{0,16},{16,0},{1,17},{17,1},{2,18},{18,2},{3,19},{19,3},{4,20},{20... | collective-permute-start | bytes 1572872 | tf_op jit(solution)/shard_map/ppermute | solution.py:17
  341.3 11.8 %all-to-all-start.6 = ((bf16[16,2,64]{2,1,0:T(2,128)(2,1)}), bf16[16,2,64]{2,1,0:T(2,128)(2,1)S(1)}, u32[]{:S(2)}, u32[]{:S(2)}) async-start(bf16[16,2,64]{2,1,0:T(2,128)(2,1)} %bitcast.35), calls=%async_computation.6 | async-start | bytes 16384 | tf_op jit(solution)/shard_map/all_to_all | solution.py:138
  345.0 5.3 copy-start.4
  345.0 33.3 %copy-start.2 = (bf16[1,1,2,512,1024]{3,4,2,1,0:T(8,128)(2,1)S(1)}, bf16[1,1,2,512,1024]{3,4,2,1,0:T(8,128)(2,1)}, u32[]{:S(2)}) copy-start(bf16[1,1,2,512,1024]{3,4,2,1,0:T(8,128)(2,1)} %copy.66) | copy-start | bytes 6291460
  353.1 12.4 %all-to-all-start.5 = ((bf16[16,2,64]{2,1,0:T(2,128)(2,1)}), bf16[16,2,64]{2,1,0:T(2,128)(2,1)S(1)}, u32[]{:S(2)}, u32[]{:S(2)}) async-start(bf16[16,2,64]{2,1,0:T(2,128)(2,1)} %bitcast.29), calls=%async_computation.5 | async-start | bytes 16384 | tf_op jit(solution)/shard_map/all_to_all | solution.py:131
  365.5 10.1 %all-to-all-start.4 = ((bf16[16,2,512]{2,1,0:T(2,128)(2,1)}), bf16[16,2,512]{2,1,0:T(2,128)(2,1)S(1)}, u32[]{:S(2)}, u32[]{:S(2)}) async-start(bf16[16,2,512]{2,1,0:T(2,128)(2,1)} %all_to_all.93), calls=%async_computation.4 | async-start | bytes 65536 | tf_op jit(solution)/shard_map/all_to_all | solution.py:128
  369.0 115.9 %all-reduce.9.cloned.1.call-start = ((), (), s32[]{:S(2)}) async-start(), calls=%async_computation.10 | async-start | bytes 2097152 | tf_op jit(solution)/shard_map/psum | solution.py:153
  394.3 215.0 %all-reduce.11.cloned.1.call-start = ((), (), s32[]{:S(2)}) async-start(), calls=%async_computation.11 | async-start | bytes 2097152 | tf_op jit(solution)/shard_map/psum | solution.py:162
Sparse Core Ops, SparseCore 0:
  106.7 90.4 all-reduce.4
  229.6 92.6 all-reduce.6
  394.4 90.4 all-reduce.8
  516.7 92.5 all-reduce.10
where the time goes:
time: 619 us; the launch traced here: 617 us
  waiting for transfers between devices  397 us (64%)
  matrix products  97.5 us (16%)
  blocking collectives  44.7 us (7%)
  starting transfers between devices  27.8 us (4%)
  local copies, waits for them, and re-layouts  24.9 us (4%)
  between operations  13.5 us (2%)
  other arithmetic  11.9 us (2%)
    psum x2, waiting for transfers between devices, body(): lax.psum(jnp.dot(acts, down_proj, preferred_element_type=jnp.float32), 'mp')  186 us
    psum x2, waiting for transfers between devices, body(): lax.psum(jnp.dot(heads_out, out_proj, preferred_element_type=jnp.float32)...  181 us
    dot_general x2, matrix products, body(): jnp.einsum('rd,dcf->rcf', norm_rows(middle, second_gain), gate_up, prefer...  40.8 us
    all_gather x1, blocking collectives, body(): whole = lax.all_gather(hidden[0], 'mp', axis=0, tiled=True)  26.2 us
    dot_general x2, matrix products, body(): jnp.dot(acts, down_proj, preferred_element_type=jnp.float32)  19.5 us
    all_to_all x2, blocking collectives, body(): lax.all_to_all(mixed_output, 'mp', split_axis=1, concat_axis=0, tiled=True)  18.4 us
    unnamed x21, local copies, waits for them, and re-layouts  15.3 us
    all_to_all x2, waiting for transfers between devices, body(): lax.all_to_all(joined[:, :query_cols], 'mp', split_axis=0, concat_axis=1,...  12.6 us
  transfers between devices with their start and end apart: 11, of which 9 were waited for; matrix products, arithmetic and copies ran while one was open for 6% of the time, Pallas kernels for 0%

commit v1 on v0

v1 whole, which is shorter than its diff:
```python
import functools

import jax
import jax.numpy as jnp
import numpy as np
from jax import lax
from jax.experimental import pallas as pl
from jax.experimental.pallas import tpu as pltpu
from jax.sharding import PartitionSpec as P

QUERY_HEADS = 64
KEY_VALUE_HEADS = 8
HEAD_SIZE = 128

epsilon = 1e-05

VMEM_LIMIT = 58 << 20


def swap(value, mask, axis="mp"):
    count = lax.axis_size(axis)
    return lax.ppermute(value, axis, [(source, source ^ mask) for source in range(count)])


def halving_masks():
    bits = (lax.axis_size("mp") - 1).bit_length()
    return [1, 2] + [1 << b for b in range(bits - 1, 1, -1)]


def relative_ids():
    ids = np.zeros((1,), np.int32)
    for mask in reversed(halving_masks()):
        ids = np.concatenate([ids, ids ^ mask])
    return ids


def finish_halving(held, masks):
    for mask in masks:
        half = held.shape[0] // 2
        got = swap(held[half:].astype(jnp.bfloat16), mask)
        held = held[:half] + got.astype(jnp.float32)
    return held[0]


def scatter_halving(send, keep):
    masks = halving_masks()
    held = keep.astype(jnp.float32) + swap(send, masks[0]).astype(jnp.float32)
    return finish_halving(held, masks[1:])


def scatter_exchange(send, keep):
    count = lax.axis_size("mp")
    half = count // 2
    held = keep.astype(jnp.float32) + swap(send, 1).astype(jnp.float32)
    place = np.argsort(relative_ids()[:half]).astype(np.int32)
    me = lax.axis_index("mp") // 2
    ordered = jnp.take(
        held.astype(jnp.bfloat16), jnp.asarray(place)[jnp.arange(half) ^ me], axis=0
    )
    groups = [list(range(core, count, 2)) for core in range(2)]
    got = lax.all_to_all(
        ordered, "mp", split_axis=0, concat_axis=0, axis_index_groups=groups, tiled=True
    )
    return jnp.sum(got.astype(jnp.float32), axis=0)


def gather_doubling(chunk):
    held = chunk[None]
    for mask in reversed(halving_masks()):
        held = jnp.concatenate([held, swap(held, mask)], axis=0)
    return held


def to_absolute(chunks):
    me = lax.axis_index("mp")
    place = np.argsort(relative_ids()).astype(np.int32)
    return jnp.take(chunks, jnp.asarray(place)[jnp.arange(place.shape[0]) ^ me], axis=0)


def columns_to_chunks(values, count):
    rows, width = values.shape
    return values.reshape(rows, count, width // count).transpose(1, 0, 2)


def vmem():
    return pl.BlockSpec(memory_space=pltpu.VMEM)


def smem():
    return pl.BlockSpec(memory_space=pltpu.SMEM)


def hbm():
    return pl.BlockSpec(memory_space=pl.ANY)


def inverse_rms(x_ref, count, rows):
    width = x_ref.shape[0] * x_ref.shape[2]

    def add(k, total):
        wide = x_ref[k].astype(jnp.float32)
        return total + jnp.sum(wide * wide, axis=-1, keepdims=True)

    total = lax.fori_loop(0, count, add, jnp.zeros((rows, 1), jnp.float32))
    return lax.rsqrt(total / width + epsilon)


def normed_chunk(x_ref, gain_ref, scale, k, place):
    wide = x_ref[k].astype(jnp.float32)
    return (wide * scale * gain_ref[pl.ds(place, 1), :]).astype(jnp.bfloat16)


def project_kernel(ids_ref, x_ref, gain_ref, wq_ref, wk_ref, wv_ref, out_ref,
                   q_buf, kv_buf, q_sum, kv_sum, sems):
    count, rows, chunk = x_ref.shape
    keys = wk_ref.shape[0]
    queries = wq_ref.shape[1]

    def copies(k):
        at = pl.multiple_of(ids_ref[k] * chunk, chunk)
        span = pl.ds(at, chunk)
        return (
            pltpu.make_async_copy(wq_ref.at[span, :], q_buf.at[k], sems.at[0, k]),
            pltpu.make_async_copy(wk_ref.at[:, span], kv_buf.at[k, pl.ds(0, keys)], sems.at[1, k]),
            pltpu.make_async_copy(
                wv_ref.at[:, span], kv_buf.at[k, pl.ds(keys, keys)], sems.at[2, k]
            ),
        )

    @pl.loop(0, count)
    def _(k):
        for copy in copies(k):
            copy.start()

    scale = inverse_rms(x_ref, count, rows)
    q_sum[...] = jnp.zeros_like(q_sum)
    kv_sum[...] = jnp.zeros_like(kv_sum)

    @pl.loop(0, count)
    def _(k):
        normed = normed_chunk(x_ref, gain_ref, scale, k, ids_ref[k])
        for copy in copies(k):
            copy.wait()
        q_sum[...] += jnp.dot(normed, q_buf[k], preferred_element_type=jnp.float32)
        kv_sum[...] += lax.dot_general(
            normed, kv_buf[k], (((1,), (1,)), ((), ())), preferred_element_type=jnp.float32
        )

    out_ref[:, :queries] = q_sum[...].astype(jnp.bfloat16)
    out_ref[:, queries:] = kv_sum[...].astype(jnp.bfloat16)


def project(ids, chunks, gain, wq, wk, wv):
    count, rows, chunk = chunks.shape
    queries, keys = wq.shape[1], wk.shape[0]
    return pl.pallas_call(
        project_kernel,
        out_shape=jax.ShapeDtypeStruct((rows, queries + 2 * keys), jnp.bfloat16),
        in_specs=[smem(), vmem(), vmem(), hbm(), hbm(), hbm()],
        out_specs=vmem(),
        scratch_shapes=[
            pltpu.VMEM((count, chunk, queries), jnp.bfloat16),
            pltpu.VMEM((count, 2 * keys, chunk), jnp.bfloat16),
            pltpu.VMEM((rows, queries), jnp.float32),
            pltpu.VMEM((rows, 2 * keys), jnp.float32),
            pltpu.SemaphoreType.DMA((3, count)),
        ],
        compiler_params=pltpu.CompilerParams(vmem_limit_bytes=VMEM_LIMIT),
    )(ids, chunks, gain.reshape(count, chunk), wq, wk, wv)


def attend_kernel(where_ref, length_ref, q_ref, k_ref, v_ref, cos_ref, sin_ref, keys_ref,
                  values_ref, out_ref, key_buf, value_buf, wide_q, sems):
    rows, heads, size = q_ref.shape
    groups = k_ref.shape[1]
    share = heads // groups
    places = key_buf.shape[1]
    batch = where_ref[0]

    def copies(row):
        return (
            pltpu.make_async_copy(keys_ref.at[batch, row], key_buf.at[row], sems.at[0, row]),
            pltpu.make_async_copy(values_ref.at[batch, row], value_buf.at[row], sems.at[1, row]),
        )

    for row in range(rows):
        for copy in copies(row):
            copy.start()
    wide_q[...] = jnp.zeros_like(wide_q)
    for row in range(rows):
        cosine = cos_ref[pl.ds(row, 1), :]
        sine = sin_ref[pl.ds(row, 1), :]

        def turned(features):
            wide = features.astype(jnp.float32)
            other = jnp.concatenate([wide[:, size // 2 :], wide[:, : size // 2]], axis=1)
            return (wide * cosine + other * sine).astype(jnp.bfloat16)

        query = turned(q_ref[row])
        own_key = turned(k_ref[row]).astype(jnp.float32)
        own_value = v_ref[row].astype(jnp.float32)
        own_parts = []
        for group in range(groups):
            part = query[group * share : (group + 1) * share]
            wide_q[group * share : (group + 1) * share, group * size : (group + 1) * size] = part
            own_parts.append(
                jnp.sum(part.astype(jnp.float32) * own_key[group : group + 1], axis=1, keepdims=True)
            )
        own_score = jnp.concatenate(own_parts, axis=0) * (size ** -0.5)
        key_copy, value_copy = copies(row)
        key_copy.wait()
        scores = lax.dot_general(
            wide_q[...], key_buf[row], (((1,), (1,)), ((), ())), preferred_element_type=jnp.float32
        ) * (size ** -0.5)
        spot = lax.broadcasted_iota(jnp.int32, (heads, places), 1)
        scores = jnp.where(spot < length_ref[batch, row], scores, -1e30)
        highest = jnp.maximum(jnp.max(scores, axis=1, keepdims=True), own_score)
        raised = jnp.exp(scores - highest)
        own_raised = jnp.exp(own_score - highest)
        denominator = jnp.sum(raised, axis=1, keepdims=True) + own_raised
        weights = (raised / denominator).astype(jnp.bfloat16)
        own_weight = (own_raised / denominator).astype(jnp.bfloat16).astype(jnp.float32)
        value_copy.wait()
        mixed = jnp.dot(weights, value_buf[row], preferred_element_type=jnp.float32)
        for group in range(groups):
            span = slice(group * share, (group + 1) * share)
            out_ref[row, span, :] = (
                mixed[span, group * size : (group + 1) * size]
                + own_weight[span] * own_value[group : group + 1]
            ).astype(jnp.bfloat16)


def attend(where, lengths, query, key, value, cosine, sine, key_store, value_store):
    rows, heads, size = query.shape
    places, width = key_store.shape[2:]
    return pl.pallas_call(
        attend_kernel,
        out_shape=jax.ShapeDtypeStruct(query.shape, jnp.bfloat16),
        in_specs=[smem(), smem()] + [vmem()] * 5 + [hbm(), hbm()],
        out_specs=vmem(),
        scratch_shapes=[
            pltpu.VMEM((rows, places, width), jnp.bfloat16),
            pltpu.VMEM((rows, places, width), jnp.bfloat16),
            pltpu.VMEM((heads, width), jnp.bfloat16),
            pltpu.SemaphoreType.DMA((2, rows)),
        ],
        compiler_params=pltpu.CompilerParams(vmem_limit_bytes=VMEM_LIMIT),
    )(where, lengths, query, key, value, cosine, sine, key_store, value_store)


def spread_kernel(ids_ref, x_ref, w_ref, send_ref, keep_ref, w_buf, sems):
    count, _, chunk = w_buf.shape
    half = count // 2

    def copy(k):
        at = pl.multiple_of(ids_ref[k] * chunk, chunk)
        return pltpu.make_async_copy(w_ref.at[:, pl.ds(at, chunk)], w_buf.at[k], sems.at[k])

    @pl.loop(0, count)
    def _(k):
        copy((k + half) % count).start()

    values = x_ref[...]
    for start, target in ((half, send_ref), (0, keep_ref)):

        @pl.loop(0, half)
        def _(k):
            copy(start + k).wait()
            target[k] = jnp.dot(
                values, w_buf[start + k], preferred_element_type=jnp.float32
            ).astype(jnp.bfloat16)


def spread_project(ids, values, weights):
    rows, depth = values.shape
    count = ids.shape[0]
    chunk = weights.shape[1] // count
    shape = jax.ShapeDtypeStruct((count // 2, rows, chunk), jnp.bfloat16)
    return pl.pallas_call(
        spread_kernel,
        out_shape=(shape, shape),
        in_specs=[smem(), vmem(), hbm()],
        out_specs=(vmem(), vmem()),
        scratch_shapes=[
            pltpu.VMEM((count, depth, chunk), jnp.bfloat16),
            pltpu.SemaphoreType.DMA((count,)),
        ],
        compiler_params=pltpu.CompilerParams(vmem_limit_bytes=VMEM_LIMIT),
    )(ids, values, weights)


def mlp_kernel(ids_ref, x_ref, gain_ref, gu_ref, down_ref, send_ref, keep_ref,
               gu_buf, down_buf, wide_x, total, act, gu_sems, down_sems):
    count, rows, chunk = x_ref.shape
    blocks = gu_buf.shape[1]
    half = count // 2

    def gu_copies(k):
        at = pl.multiple_of(ids_ref[k] * chunk, chunk)
        return [
            pltpu.make_async_copy(
                gu_ref.at[pl.ds(at, chunk), :, pl.ds(j * 128, 128)],
                gu_buf.at[k, j],
                gu_sems.at[k, j],
            )
            for j in range(blocks)
        ]

    def down_copy(k):
        at = pl.multiple_of(ids_ref[k] * chunk, chunk)
        return pltpu.make_async_copy(
            down_ref.at[:, pl.ds(at, chunk)], down_buf.at[k], down_sems.at[k]
        )

    @pl.loop(0, count)
    def _(k):
        for copy in gu_copies(k):
            copy.start()

    @pl.loop(0, count)
    def _(k):
        down_copy((k + half) % count).start()

    scale = inverse_rms(x_ref, count, rows)
    total[...] = jnp.zeros_like(total)
    line = lax.broadcasted_iota(jnp.int32, (128, 512), 0)
    column = lax.broadcasted_iota(jnp.int32, (128, 512), 1)
    aim = jnp.where(column < 256, 2 * line, 2 * line + 257)
    widen = jnp.where(column == aim, 1.0, 0.0).astype(jnp.bfloat16)

    @pl.loop(0, count)
    def _(k):
        normed = normed_chunk(x_ref, gain_ref, scale, k, ids_ref[k])
        for b in range(chunk // 128):
            wide = jnp.dot(
                normed[:, b * 128 : (b + 1) * 128], widen, preferred_element_type=jnp.float32
            ).astype(jnp.bfloat16)
            wide_x[:rows, b * 256 : (b + 1) * 256] = wide[:, :256]
            wide_x[rows:, b * 256 : (b + 1) * 256] = wide[:, 256:]
        for copy in gu_copies(k):
            copy.wait()
        for j in range(0, blocks, 2):
            pair = jnp.concatenate(
                [gu_buf.at[k, j + i].reshape(2 * chunk, 128)[...] for i in range(2)], axis=1
            )
            total[:, j * 128 : (j + 2) * 128] += jnp.dot(
                wide_x[...], pair, preferred_element_type=jnp.float32
            )

    gate = total[:rows, :]
    act[...] = (gate / (1.0 + jnp.exp(-gate)) * total[rows:, :]).astype(jnp.bfloat16)

    for start, target in ((half, send_ref), (0, keep_ref)):

        @pl.loop(0, half)
        def _(k):
            down_copy(start + k).wait()
            target[k] = jnp.dot(
                act[...], down_buf[start + k], preferred_element_type=jnp.float32
            ).astype(jnp.bfloat16)


def mlp(ids, chunks, gain, gate_up, down):
    count, rows, chunk = chunks.shape
    units = down.shape[0]
    shape = jax.ShapeDtypeStruct((count // 2, rows, chunk), jnp.bfloat16)
    return pl.pallas_call(
        mlp_kernel,
        out_shape=(shape, shape),
        in_specs=[smem(), vmem(), vmem(), hbm(), hbm()],
        out_specs=(vmem(), vmem()),
        scratch_shapes=[
            pltpu.VMEM((count, units // 128, chunk, 2, 128), jnp.bfloat16),
            pltpu.VMEM((count, units, chunk), jnp.bfloat16),
            pltpu.VMEM((2 * rows, 2 * chunk), jnp.bfloat16),
            pltpu.VMEM((2 * rows, units), jnp.float32),
            pltpu.VMEM((rows, units), jnp.bfloat16),
            pltpu.SemaphoreType.DMA((count, units // 128)),
            pltpu.SemaphoreType.DMA((count,)),
        ],
        compiler_params=pltpu.CompilerParams(vmem_limit_bytes=VMEM_LIMIT),
    )(ids, chunks, gain.reshape(count, chunk), gate_up, down)


def turning(positions):
    half_dim = HEAD_SIZE // 2
    frequency = 500000.0 ** (-2.0 * jnp.arange(half_dim, dtype=jnp.float32) / HEAD_SIZE)
    angles = positions.astype(jnp.float32)[:, None] * frequency[None, :]
    cosine = jnp.cos(angles)
    sine = jnp.sin(angles)
    return jnp.concatenate([cosine, cosine], axis=1), jnp.concatenate([-sine, sine], axis=1)


def body(
    hidden,
    attn_gain,
    w_query,
    w_key,
    w_value,
    w_out,
    mlp_gain,
    w_gate_up,
    w_down,
    key_cache,
    value_cache,
    lengths,
):
    rows_dev = hidden.shape[1]
    count = lax.axis_size("mp")
    rows = rows_dev * count
    section_index = lax.axis_index("section")
    model_index = lax.axis_index("mp")
    query_cols = w_query.shape[2]
    key_cols = w_key.shape[2]
    width = hidden.shape[2]
    ids = jnp.asarray(relative_ids()) ^ model_index
    straight = jnp.arange(count, dtype=jnp.int32)
    wk = w_key[0].T
    wv = w_value[0].T
    start = to_absolute(gather_doubling(hidden[0])).reshape(rows, width)
    chunks = columns_to_chunks(start, count)
    mine = lax.dynamic_index_in_dim(chunks, model_index, 0, keepdims=False)
    order = straight
    for turn_index in range(2):
        batch = jnp.remainder(section_index + turn_index, 2).astype(jnp.int32)
        cosine, sine = turning(lax.dynamic_index_in_dim(lengths, batch, 0, keepdims=False))
        joined = project(order, chunks, attn_gain[0], w_query[0], wk, wv)
        spread = lax.all_to_all(
            joined.reshape(count, rows_dev, -1), "mp", split_axis=0, concat_axis=0
        ).transpose(1, 0, 2)
        query = spread[..., :query_cols].reshape(rows_dev, QUERY_HEADS, HEAD_SIZE)
        key = spread[..., query_cols : query_cols + key_cols].reshape(
            rows_dev, KEY_VALUE_HEADS, HEAD_SIZE
        )
        value = spread[..., query_cols + key_cols :].reshape(rows_dev, KEY_VALUE_HEADS, HEAD_SIZE)
        mixed = attend(
            batch.reshape(1), lengths, query, key, value, cosine, sine, key_cache[0], value_cache[0]
        )
        heads_out = lax.all_to_all(
            mixed.reshape(rows_dev, QUERY_HEADS * HEAD_SIZE),
            "mp",
            split_axis=1,
            concat_axis=0,
            tiled=True,
        )
        attn_part = scatter_halving(*spread_project(ids, heads_out, w_out[0]))
        middle = (mine.astype(jnp.float32) + attn_part).astype(jnp.bfloat16)
        send, keep = mlp(ids, gather_doubling(middle), mlp_gain[0], w_gate_up[0], w_down[0])
        mlp_part = scatter_exchange(send, keep)
        mine = (middle.astype(jnp.float32) + mlp_part).astype(jnp.bfloat16)
        if turn_index == 0:
            mine = swap(mine, 1, "section")
            chunks = gather_doubling(mine)
            order = ids
    parts = lax.all_to_all(
        mine.reshape(count, rows_dev, width // count), "mp", split_axis=0, concat_axis=0
    )
    return parts.transpose(1, 0, 2).reshape(1, rows_dev, width)


def solution(mesh):
    placed = (
        P("section", "mp", None),
        P("section", None),
        P("section", None, "mp"),
        P("section", None, "mp"),
        P("section", None, "mp"),
        P("section", "mp", None),
        P("section", None),
        P("section", None, None, "mp"),
        P("section", "mp", None),
        P("section", None, "mp", None, None),
        P("section", None, "mp", None, None),
        P(None, "mp"),
    )
    return jax.shard_map(
        body, mesh=mesh, in_specs=placed, out_specs=P("section", "mp", None), check_vma=False
    )
```

time: 619 us -> 314 us (0.51)
  waiting for transfers between devices: 397 us -> 106 us
  Pallas kernels: 0 us -> 97.7 us
  matrix products: 97.5 us -> 0 us
  between operations: 13.5 us -> 0.7 us
    psum x4 -> x0, waiting for transfers between devices: 366 us -> none  [the longest x2 186 us: body(): lax.psum(jnp.dot(acts, down_proj, preferred_element_type=jnp.float32), 'mp')]
    pallas_call x0 -> x8, Pallas kernels: none -> 97.7 us  [the longest x2 60.8 us: mlp(): pl.pallas_call(mlp_kernel, out_shape=(shape, shape), in_specs=[smem(), vm...]
    dot_general x18 -> x0, matrix products: 97.5 us -> none  [the longest x2 40.8 us: body(): jnp.einsum('rd,dcf->rcf', norm_rows(middle, second_gain), gate_up, prefer...]
    ppermute x1 -> x27, waiting for transfers between devices: 5.41 us -> 88.6 us  [swap(): lax.ppermute(value, axis, [(source, source ^ mask) for source in range(co...]
    all_gather x1 -> x0, blocking collectives: 26.2 us -> none  [body(): whole = lax.all_gather(hidden[0], 'mp', axis=0, tiled=True)]
    all_to_all x2 -> x4, blocking collectives: 18.4 us -> 43.1 us  [the longest x2 23.8 us: scatter_exchange(): lax.all_to_all(ordered, 'mp', split_axis=0, concat_axis=0, axis_index_gro...]
    ppermute x1 -> x27, starting transfers between devices: 1.47 us -> 16.2 us  [swap(): lax.ppermute(value, axis, [(source, source ^ mask) for source in range(co...]
    all_to_all x6 -> x3, starting transfers between devices: 26 us -> 11.7 us  [the longest x2 8.19 us: body(): lax.all_to_all(joined.reshape(count, rows_dev, -1), 'mp', split_axis=0, c...]
  transfers between devices with their start and end apart: 11 -> 30, of which waited for: 9 -> 29; matrix products, arithmetic and copies ran while one was open for 6% -> 3% of each run, Pallas kernels for 0% -> 0%
where the time goes in v1:
time: 314 us; the launch traced here: 312 us
  waiting for transfers between devices  106 us (34%)
  Pallas kernels  97.7 us (31%)
  blocking collectives  43.1 us (14%)
  starting transfers between devices  27.9 us (9%)
  local copies, waits for them, and re-layouts  22.5 us (7%)
  other arithmetic  13.9 us (4%)
    ppermute x27, waiting for transfers between devices, swap(): lax.ppermute(value, axis, [(source, source ^ mask) for source in range(co...  88.6 us
    pallas_call x2, Pallas kernels, mlp(): pl.pallas_call(mlp_kernel, out_shape=(shape, shape), in_specs=[smem(), vm...  60.8 us
    all_to_all x2, blocking collectives, scatter_exchange(): lax.all_to_all(ordered, 'mp', split_axis=0, concat_axis=0, axis_index_gro...  23.8 us
    ppermute x27, starting transfers between devices, swap(): lax.ppermute(value, axis, [(source, source ^ mask) for source in range(co...  16.2 us
    pallas_call x2, Pallas kernels, project(): pl.pallas_call(project_kernel, out_shape=jax.ShapeDtypeStruct((rows, quer...  15.6 us
    all_to_all x2, waiting for transfers between devices, body(): lax.all_to_all(joined.reshape(count, rows_dev, -1), 'mp', split_axis=0, c...  11.9 us
    pallas_call x2, Pallas kernels, spread_project(): pl.pallas_call(spread_kernel, out_shape=(shape, shape), in_specs=[smem(),...  11.7 us
    all_to_all x1, blocking collectives, body(): lax.all_to_all(mine.reshape(count, rows_dev, width // count), 'mp', split...  10.1 us
  transfers between devices with their start and end apart: 30, of which 29 were waited for; matrix products, arithmetic and copies ran while one was open for 3% of the time, Pallas kernels for 0%

profile of v1, /device:TPU:0, one launch (start us, length us, event | category | flops | bytes accessed | tf_op | source)
XLA Modules:
  0.0 312.3 jit_solution(5797344286216554435)
XLA Ops:
  18.2 3.4 %collective-permute-done.2 = bf16[4,2,8192]{2,1,0:T(2,128)(2,1)S(1)} collective-permute-done((bf16[4,2,8192]{2,1,0:T(2,128)(2,1)S(1)}, bf16[4,2,8192]{2,1,0:T(2,128)(2,1)S(1)}, u32[]{:S(2)}, u32[]{:S(2)}) %collective-permute-start.2) | collective-permute-done | bytes 131104 | tf_op jit(solution)/shard_map/ppermute | solution.py:22
  28.1 7.8 %shard_map.154 = bf16[32,640]{1,0:T(8,128)(2,1)} custom-call(s32[16]{0:T(128)} %iota.21.ids_ref, bf16[16,32,512]{2,1,0:T(8,128)(2,1)} %fusion.20.x_ref, f32[16,512]{1,0:T(8,128)} %reshape_squeeze.8.gain_ref, bf16[8192,512]{1,0:T(8,128)(2,1)} %bitcast.69, bf16[64,8192]{1,0:T(8,128)(2,1)} %bitcast.77, bf16[64,8192]{1,0:T(8,128)(2,1)} %bitcast.79), custom_call_target="tpu_custom_call" | custom-call | tf_op jit(solution)/shard_map/pallas_call | solution.py:156
  37.3 4.5 %all-to-all-start = ((bf16[16,2,640]{2,1,0:T(2,128)(2,1)}), bf16[16,2,640]{2,1,0:T(2,128)(2,1)S(1)}, u32[]{:S(2)}, u32[]{:S(2)}) async-start(bf16[16,2,640]{2,1,0:T(2,128)(2,1)} %reshape.136), calls=%async_computation | async-start | bytes 81920 | tf_op jit(solution)/shard_map/all_to_all | solution.py:428
  42.5 6.0 %all-to-all-done = bf16[16,2,640]{2,1,0:T(2,128)(2,1)S(1)} async-done(((bf16[16,2,640]{2,1,0:T(2,128)(2,1)}), bf16[16,2,640]{2,1,0:T(2,128)(2,1)S(1)}, u32[]{:S(2)}, u32[]{:S(2)}) %all-to-all-start) | async-done | bytes 40992 | tf_op jit(solution)/shard_map/all_to_all | solution.py:428
  50.7 4.8 %shard_map.155 = bf16[2,64,128]{2,1,0:T(8,128)(2,1)} custom-call(s32[1]{0:T(128)} %bitcast.4.where_ref, s32[2,2]{1,0:T(2,128)} %length_ref.3, bf16[2,64,128]{2,1,0:T(8,128)(2,1)} %reshape.137.q_ref, bf16[2,8,128]{2,1,0:T(8,128)(2,1)} %reshape.138.k_ref, bf16[2,8,128]{2,1,0:T(8,128)(2,1)} %reshape.139.v_ref, f32[2,128]{1,0:T(2,128)} %get-tuple-element.43.cos_ref, ...), custom_call_target="tpu_custom_call" | custom-call | tf_op jit(solution)/shard_map/pallas_call | solution.py:236
  56.9 3.5 %all-to-all-start.1 = ((bf16[2,16,512]{2,0,1:T(2,128)(2,1)}), bf16[2,16,512]{2,0,1:T(2,128)(2,1)S(1)}, u32[]{:S(2)}, u32[]{:S(2)}) async-start(bf16[2,16,512]{2,0,1:T(2,128)(2,1)} %copy.32), calls=%async_computation.1 | async-start | bytes 65536 | tf_op jit(solution)/shard_map/all_to_all | solution.py:439
  61.0 6.0 %all-to-all-done.1 = bf16[2,16,512]{2,0,1:T(2,128)(2,1)S(1)} async-done(((bf16[2,16,512]{2,0,1:T(2,128)(2,1)}), bf16[2,16,512]{2,0,1:T(2,128)(2,1)S(1)}, u32[]{:S(2)}, u32[]{:S(2)}) %all-to-all-start.1) | async-done | bytes 32800 | tf_op jit(solution)/shard_map/all_to_all | solution.py:439
  67.6 5.9 %shard_map.156 = (bf16[8,32,512]{2,1,0:T(8,128)(2,1)}, bf16[8,32,512]{2,1,0:T(8,128)(2,1)}) custom-call(s32[16]{0:T(128)} %broadcast_xor_fusion.ids_ref, bf16[32,512]{1,0:T(8,128)(2,1)} %all_to_all.47.x_ref, bf16[512,8192]{1,0:T(8,128)(2,1)} %bitcast.71), custom_call_target="tpu_custom_call" | custom-call | tf_op jit(solution)/shard_map/pallas_call | solution.py:279
  76.8 5.2 %collective-permute-done.5 = bf16[4,32,512]{2,1,0:T(8,128)(2,1)S(1)} collective-permute-done((bf16[4,32,512]{2,1,0:T(8,128)(2,1)S(1)}, bf16[4,32,512]{2,1,0:T(8,128)(2,1)S(1)}, u32[]{:S(2)}, u32[]{:S(2)}) %collective-permute-start.5) | collective-permute-done | bytes 131104 | tf_op jit(solution)/shard_map/ppermute | solution.py:22
  82.5 5.3 %collective-permute-done.6 = bf16[2,32,512]{2,1,0:T(8,128)(2,1)S(1)} collective-permute-done((bf16[2,32,512]{2,1,0:T(8,128)(2,1)S(1)}, bf16[2,32,512]{2,1,0:T(8,128)(2,1)S(1)}, u32[]{:S(2)}, u32[]{:S(2)}) %collective-permute-start.6) | collective-permute-done | bytes 65568 | tf_op jit(solution)/shard_map/ppermute | solution.py:22
  88.2 3.9 %collective-permute-done.7 = bf16[1,32,512]{2,1,0:T(8,128)(2,1)S(1)} collective-permute-done((bf16[1,32,512]{2,1,0:T(8,128)(2,1)S(1)}, bf16[1,32,512]{2,1,0:T(8,128)(2,1)S(1)}, u32[]{:S(2)}, u32[]{:S(2)}) %collective-permute-start.7) | collective-permute-done | bytes 32800 | tf_op jit(solution)/shard_map/ppermute | solution.py:22
  92.2 4.6 %collective-permute-done.8 = bf16[1,32,512]{2,1,0:T(8,128)(2,1)S(1)} collective-permute-done((bf16[1,32,512]{2,1,0:T(8,128)(2,1)S(1)}, bf16[1,32,512]{2,1,0:T(8,128)(2,1)S(1)}, u32[]{:S(2)}, u32[]{:S(2)}) %collective-permute-start.8) | collective-permute-done | bytes 32800 | tf_op jit(solution)/shard_map/ppermute | solution.py:22
  102.7 4.4 %collective-permute-done.10 = bf16[4,32,512]{2,1,0:T(8,128)(2,1)S(1)} collective-permute-done((bf16[4,32,512]{2,1,0:T(8,128)(2,1)S(1)}, bf16[4,32,512]{2,1,0:T(8,128)(2,1)S(1)}, u32[]{:S(2)}, u32[]{:S(2)}) %collective-permute-start.10) | collective-permute-done | bytes 131104 | tf_op jit(solution)/shard_map/ppermute | solution.py:22
  109.5 30.4 %shard_map.157 = (bf16[8,32,512]{2,1,0:T(8,128)(2,1)}, bf16[8,32,512]{2,1,0:T(8,128)(2,1)}) custom-call(s32[16]{0:T(128)} %broadcast_xor_fusion.ids_ref, bf16[16,32,512]{2,1,0:T(8,128)(2,1)} %copy-done.1, f32[16,512]{1,0:T(8,128)} %reshape_squeeze.9.gain_ref, bf16[8192,2,1024]{2,1,0:T(2,128)(2,1)} %bitcast.65, bf16[1024,8192]{1,0:T(8,128)(2,1)} %bitcast.67), custom_call_target="tpu_custom_call" | custom-call | tf_op jit(solution)/shard_map/pallas_call | solution.py:367
  143.4 11.9 %all_to_all.63 = bf16[8,32,512]{2,1,0:T(8,128)(2,1)S(1)} all-to-all(bf16[8,32,512]{2,1,0:T(8,128)(2,1)S(1)} %broadcast_select_fusion.1), channel_id=1, replica_groups={{0,2,4,6,8,10,12,14},{1,3,5,7,9,11,13,15},{16,18,20,22,24,26,28,30},{17..., dimensions={0} | all-to-all | bytes 524288 | tf_op jit(solution)/shard_map/all_to_all | solution.py:61
  164.4 4.8 %collective-permute-done.15 = bf16[2,32,512]{2,1,0:T(8,128)(2,1)S(1)} collective-permute-done((bf16[2,32,512]{2,1,0:T(8,128)(2,1)S(1)}, bf16[2,32,512]{2,1,0:T(8,128)(2,1)S(1)}, u32[]{:S(2)}, u32[]{:S(2)}) %collective-permute-start.15) | collective-permute-done | bytes 65568 | tf_op jit(solution)/shard_map/ppermute | solution.py:22
  170.3 4.0 %collective-permute-done.16 = bf16[4,32,512]{2,1,0:T(8,128)(2,1)S(1)} collective-permute-done((bf16[4,32,512]{2,1,0:T(8,128)(2,1)S(1)}, bf16[4,32,512]{2,1,0:T(8,128)(2,1)S(1)}, u32[]{:S(2)}, u32[]{:S(2)}) %collective-permute-start.16) | collective-permute-done | bytes 131104 | tf_op jit(solution)/shard_map/ppermute | solution.py:22
  176.8 7.8 %shard_map.158 = bf16[32,640]{1,0:T(8,128)(2,1)} custom-call(s32[16]{0:T(128)} %broadcast_xor_fusion.ids_ref, bf16[16,32,512]{2,1,0:T(8,128)(2,1)} %copy-done.3, f32[16,512]{1,0:T(8,128)} %reshape_squeeze.8.gain_ref, bf16[8192,512]{1,0:T(8,128)(2,1)} %bitcast.70, bf16[64,8192]{1,0:T(8,128)(2,1)} %bitcast.78, bf16[64,8192]{1,0:T(8,128)(2,1)} %bitcast.80), custom_call_target="tpu_custom_call" | custom-call | tf_op jit(solution)/shard_map/pallas_call | solution.py:156
  186.0 3.7 %all-to-all-start.3 = ((bf16[16,2,640]{2,1,0:T(2,128)(2,1)}), bf16[16,2,640]{2,1,0:T(2,128)(2,1)S(1)}, u32[]{:S(2)}, u32[]{:S(2)}) async-start(bf16[16,2,640]{2,1,0:T(2,128)(2,1)} %reshape.141), calls=%async_computation.3 | async-start | bytes 81920 | tf_op jit(solution)/shard_map/all_to_all | solution.py:428
  190.3 5.8 %all-to-all-done.3 = bf16[16,2,640]{2,1,0:T(2,128)(2,1)S(1)} async-done(((bf16[16,2,640]{2,1,0:T(2,128)(2,1)}), bf16[16,2,640]{2,1,0:T(2,128)(2,1)S(1)}, u32[]{:S(2)}, u32[]{:S(2)}) %all-to-all-start.3) | async-done | bytes 40992 | tf_op jit(solution)/shard_map/all_to_all | solution.py:428
  198.3 4.8 %shard_map.159 = bf16[2,64,128]{2,1,0:T(8,128)(2,1)} custom-call(s32[1]{0:T(128)} %bitcast.22.where_ref, s32[2,2]{1,0:T(2,128)} %length_ref.3, bf16[2,64,128]{2,1,0:T(8,128)(2,1)} %reshape.142.q_ref, bf16[2,8,128]{2,1,0:T(8,128)(2,1)} %reshape.143.k_ref, bf16[2,8,128]{2,1,0:T(8,128)(2,1)} %reshape.144.v_ref, f32[2,128]{1,0:T(2,128)} %get-tuple-element.45.cos_ref, ...), custom_call_target="tpu_custom_call" | custom-call | tf_op jit(solution)/shard_map/pallas_call | solution.py:236
  203.9 9.2 %all_to_all.64 = bf16[2,16,512]{2,0,1:T(2,128)(2,1)S(1)} all-to-all(bf16[2,16,512]{2,0,1:T(2,128)(2,1)S(1)} %copy.36), channel_id=1, replica_groups=mesh['section'=2,'mp'=16] {'mp'}, dimensions={1} | all-to-all | bytes 65536 | tf_op jit(solution)/shard_map/all_to_all | solution.py:439
  213.8 5.9 %shard_map.160 = (bf16[8,32,512]{2,1,0:T(8,128)(2,1)}, bf16[8,32,512]{2,1,0:T(8,128)(2,1)}) custom-call(s32[16]{0:T(128)} %broadcast_xor_fusion.ids_ref, bf16[32,512]{1,0:T(8,128)(2,1)} %all_to_all.53.x_ref, bf16[512,8192]{1,0:T(8,128)(2,1)} %bitcast.72), custom_call_target="tpu_custom_call" | custom-call | tf_op jit(solution)/shard_map/pallas_call | solution.py:279
  222.9 5.2 %collective-permute-done.19 = bf16[4,32,512]{2,1,0:T(8,128)(2,1)S(1)} collective-permute-done((bf16[4,32,512]{2,1,0:T(8,128)(2,1)S(1)}, bf16[4,32,512]{2,1,0:T(8,128)(2,1)S(1)}, u32[]{:S(2)}, u32[]{:S(2)}) %collective-permute-start.19) | collective-permute-done | bytes 131104 | tf_op jit(solution)/shard_map/ppermute | solution.py:22
  228.6 5.3 %collective-permute-done.20 = bf16[2,32,512]{2,1,0:T(8,128)(2,1)S(1)} collective-permute-done((bf16[2,32,512]{2,1,0:T(8,128)(2,1)S(1)}, bf16[2,32,512]{2,1,0:T(8,128)(2,1)S(1)}, u32[]{:S(2)}, u32[]{:S(2)}) %collective-permute-start.20) | collective-permute-done | bytes 65568 | tf_op jit(solution)/shard_map/ppermute | solution.py:22
  234.0 4.2 %collective-permute-done.21 = bf16[1,32,512]{2,1,0:T(8,128)(2,1)S(1)} collective-permute-done((bf16[1,32,512]{2,1,0:T(8,128)(2,1)S(1)}, bf16[1,32,512]{2,1,0:T(8,128)(2,1)S(1)}, u32[]{:S(2)}, u32[]{:S(2)}) %collective-permute-start.21) | collective-permute-done | bytes 32800 | tf_op jit(solution)/shard_map/ppermute | solution.py:22
  238.3 4.6 %collective-permute-done.22 = bf16[1,32,512]{2,1,0:T(8,128)(2,1)S(1)} collective-permute-done((bf16[1,32,512]{2,1,0:T(8,128)(2,1)S(1)}, bf16[1,32,512]{2,1,0:T(8,128)(2,1)S(1)}, u32[]{:S(2)}, u32[]{:S(2)}) %collective-permute-start.22) | collective-permute-done | bytes 32800 | tf_op jit(solution)/shard_map/ppermute | solution.py:22
  243.0 5.2 %collective-permute-done.23 = bf16[2,32,512]{2,1,0:T(8,128)(2,1)S(1)} collective-permute-done((bf16[2,32,512]{2,1,0:T(8,128)(2,1)S(1)}, bf16[2,32,512]{2,1,0:T(8,128)(2,1)S(1)}, u32[]{:S(2)}, u32[]{:S(2)}) %collective-permute-start.23) | collective-permute-done | bytes 65568 | tf_op jit(solution)/shard_map/ppermute | solution.py:22
  248.8 4.4 %collective-permute-done.24 = bf16[4,32,512]{2,1,0:T(8,128)(2,1)S(1)} collective-permute-done((bf16[4,32,512]{2,1,0:T(8,128)(2,1)S(1)}, bf16[4,32,512]{2,1,0:T(8,128)(2,1)S(1)}, u32[]{:S(2)}, u32[]{:S(2)}) %collective-permute-start.24) | collective-permute-done | bytes 131104 | tf_op jit(solution)/shard_map/ppermute | solution.py:22
  255.6 30.4 %shard_map.161 = (bf16[8,32,512]{2,1,0:T(8,128)(2,1)}, bf16[8,32,512]{2,1,0:T(8,128)(2,1)}) custom-call(s32[16]{0:T(128)} %broadcast_xor_fusion.ids_ref, bf16[16,32,512]{2,1,0:T(8,128)(2,1)} %copy-done.2, f32[16,512]{1,0:T(8,128)} %reshape_squeeze.9.gain_ref, bf16[8192,2,1024]{2,1,0:T(2,128)(2,1)} %bitcast.66, bf16[1024,8192]{1,0:T(8,128)(2,1)} %bitcast.68), custom_call_target="tpu_custom_call" | custom-call | tf_op jit(solution)/shard_map/pallas_call | solution.py:367
  289.6 11.9 %all_to_all.65 = bf16[8,32,512]{2,1,0:T(8,128)(2,1)S(1)} all-to-all(bf16[8,32,512]{2,1,0:T(8,128)(2,1)S(1)} %broadcast_select_fusion), channel_id=1, replica_groups={{0,2,4,6,8,10,12,14},{1,3,5,7,9,11,13,15},{16,18,20,22,24,26,28,30},{17..., dimensions={0} | all-to-all | bytes 524288 | tf_op jit(solution)/shard_map/all_to_all | solution.py:61
  301.6 10.1 %all_to_all.66 = bf16[16,2,512]{2,1,0:T(2,128)(2,1)S(1)} all-to-all(bf16[16,2,512]{2,1,0:T(2,128)(2,1)S(1)} %reshape.145), channel_id=1, replica_groups=mesh['section'=2,'mp'=16] {'mp'}, dimensions={0} | all-to-all | bytes 65536 | tf_op jit(solution)/shard_map/all_to_all | solution.py:455
  (161 shorter events, 76.6 us)
Async XLA Ops:
  0.0 8.9 %collective-permute-start = (bf16[1,2,8192]{2,1,0:T(2,128)(2,1)}, bf16[1,2,8192]{2,1,0:T(2,128)(2,1)S(1)}, u32[]{:S(2)}, u32[]{:S(2)}) collective-permute-start(bf16[1,2,8192]{2,1,0:T(2,128)(2,1)} %param.18), channel_id=1, source_target_pairs={{0,4},{1,5},{2,6},{3,7},{4,0},{5,1},{6,2},{7,3},{8,12},{9,13},{10,... | collective-permute-start | bytes 98312 | tf_op jit(solution)/shard_map/ppermute | solution.py:22
  9.7 5.8 %collective-permute-start.1 = (bf16[2,2,8192]{2,1,0:T(2,128)(2,1)S(1)}, bf16[2,2,8192]{2,1,0:T(2,128)(2,1)S(1)}, u32[]{:S(2)}, u32[]{:S(2)}) collective-permute-start(bf16[2,2,8192]{2,1,0:T(2,128)(2,1)S(1)} %pad_maximum_fusion.8), channel_id=1, source_target_pairs={{0,8},{1,9},{2,10},{3,11},{4,12},{5,13},{6,14},{7,15},{8,0},{9,1},... | collective-permute-start | bytes 196616 | tf_op jit(solution)/shard_map/ppermute | solution.py:22
  16.4 5.1 %collective-permute-start.2 = (bf16[4,2,8192]{2,1,0:T(2,128)(2,1)S(1)}, bf16[4,2,8192]{2,1,0:T(2,128)(2,1)S(1)}, u32[]{:S(2)}, u32[]{:S(2)}) collective-permute-start(bf16[4,2,8192]{2,1,0:T(2,128)(2,1)S(1)} %pad_maximum_fusion.4), channel_id=1, source_target_pairs={{0,2},{1,3},{2,0},{3,1},{4,6},{5,7},{6,4},{7,5},{8,10},{9,11},{10,... | collective-permute-start | bytes 393224 | tf_op jit(solution)/shard_map/ppermute | solution.py:22
  22.7 1.6 collective-permute-start.3
  37.3 11.2 %all-to-all-start = ((bf16[16,2,640]{2,1,0:T(2,128)(2,1)}), bf16[16,2,640]{2,1,0:T(2,128)(2,1)S(1)}, u32[]{:S(2)}, u32[]{:S(2)}) async-start(bf16[16,2,640]{2,1,0:T(2,128)(2,1)} %reshape.136), calls=%async_computation | async-start | bytes 81920 | tf_op jit(solution)/shard_map/all_to_all | solution.py:428
  55.5 41.4 %copy-start.4 = (f32[1,8192]{1,0:T(1,128)S(1)}, f32[1,8192]{1,0:T(1,128)}, u32[]{:S(2)}) copy-start(f32[1,8192]{1,0:T(1,128)} %param.24) | copy-start | bytes 98308
  55.5 42.7 %copy-start = (s32[8]{0:T(128)S(1)}, s32[8]{0:T(128)}, u32[]{:S(2)}) copy-start(s32[8]{0:T(128)} %constant.97.clone) | copy-start | bytes 100
  56.9 10.1 %all-to-all-start.1 = ((bf16[2,16,512]{2,0,1:T(2,128)(2,1)}), bf16[2,16,512]{2,0,1:T(2,128)(2,1)S(1)}, u32[]{:S(2)}, u32[]{:S(2)}) async-start(bf16[2,16,512]{2,0,1:T(2,128)(2,1)} %copy.32), calls=%async_computation.1 | async-start | bytes 65536 | tf_op jit(solution)/shard_map/all_to_all | solution.py:439
  73.5 1.8 collective-permute-start.4
  76.4 5.6 %collective-permute-start.5 = (bf16[4,32,512]{2,1,0:T(8,128)(2,1)S(1)}, bf16[4,32,512]{2,1,0:T(8,128)(2,1)S(1)}, u32[]{:S(2)}, u32[]{:S(2)}) collective-permute-start(bf16[4,32,512]{2,1,0:T(8,128)(2,1)S(1)} %slice.131), channel_id=1, source_target_pairs={{0,2},{1,3},{2,0},{3,1},{4,6},{5,7},{6,4},{7,5},{8,10},{9,11},{10,... | collective-permute-start | bytes 393224 | tf_op jit(solution)/shard_map/ppermute | solution.py:22
  82.0 5.7 %collective-permute-start.6 = (bf16[2,32,512]{2,1,0:T(8,128)(2,1)S(1)}, bf16[2,32,512]{2,1,0:T(8,128)(2,1)S(1)}, u32[]{:S(2)}, u32[]{:S(2)}) collective-permute-start(bf16[2,32,512]{2,1,0:T(8,128)(2,1)S(1)} %slice.133), channel_id=1, source_target_pairs={{0,8},{1,9},{2,10},{3,11},{4,12},{5,13},{6,14},{7,15},{8,0},{9,1},... | collective-permute-start | bytes 196616 | tf_op jit(solution)/shard_map/ppermute | solution.py:22
  87.8 4.3 %collective-permute-start.7 = (bf16[1,32,512]{2,1,0:T(8,128)(2,1)S(1)}, bf16[1,32,512]{2,1,0:T(8,128)(2,1)S(1)}, u32[]{:S(2)}, u32[]{:S(2)}) collective-permute-start(bf16[1,32,512]{2,1,0:T(8,128)(2,1)S(1)} %slice.135), channel_id=1, source_target_pairs={{0,4},{1,5},{2,6},{3,7},{4,0},{5,1},{6,2},{7,3},{8,12},{9,13},{10,... | collective-permute-start | bytes 98312 | tf_op jit(solution)/shard_map/ppermute | solution.py:22
  92.1 4.7 %collective-permute-start.8 = (bf16[1,32,512]{2,1,0:T(8,128)(2,1)S(1)}, bf16[1,32,512]{2,1,0:T(8,128)(2,1)S(1)}, u32[]{:S(2)}, u32[]{:S(2)}) collective-permute-start(bf16[1,32,512]{2,1,0:T(8,128)(2,1)S(1)} %get-tuple-element.25), channel_id=1, source_target_pairs={{0,4},{1,5},{2,6},{3,7},{4,0},{5,1},{6,2},{7,3},{8,12},{9,13},{10,... | collective-permute-start | bytes 98312 | tf_op jit(solution)/shard_map/ppermute | solution.py:22
  96.8 5.2 %collective-permute-start.9 = (bf16[2,32,512]{2,1,0:T(8,128)(2,1)S(1)}, bf16[2,32,512]{2,1,0:T(8,128)(2,1)S(1)}, u32[]{:S(2)}, u32[]{:S(2)}) collective-permute-start(bf16[2,32,512]{2,1,0:T(8,128)(2,1)S(1)} %pad_maximum_fusion.9), channel_id=1, source_target_pairs={{0,8},{1,9},{2,10},{3,11},{4,12},{5,13},{6,14},{7,15},{8,0},{9,1},... | collective-permute-start | bytes 196616 | tf_op jit(solution)/shard_map/ppermute | solution.py:22
  102.0 5.0 %collective-permute-start.10 = (bf16[4,32,512]{2,1,0:T(8,128)(2,1)S(1)}, bf16[4,32,512]{2,1,0:T(8,128)(2,1)S(1)}, u32[]{:S(2)}, u32[]{:S(2)}) collective-permute-start(bf16[4,32,512]{2,1,0:T(8,128)(2,1)S(1)} %pad_maximum_fusion.5), channel_id=1, source_target_pairs={{0,2},{1,3},{2,0},{3,1},{4,6},{5,7},{6,4},{7,5},{8,10},{9,11},{10,... | collective-permute-start | bytes 393224 | tf_op jit(solution)/shard_map/ppermute | solution.py:22
  107.1 1.6 collective-permute-start.11
  139.9 1.8 collective-permute-start.12
  155.4 4.0 %collective-permute-start.13 = (bf16[32,512]{1,0:T(8,128)(2,1)S(1)}, bf16[32,512]{1,0:T(8,128)(2,1)S(1)}, u32[]{:S(2)}, u32[]{:S(2)}) collective-permute-start(bf16[32,512]{1,0:T(8,128)(2,1)S(1)} %add_convert_fusion.3), channel_id=1, source_target_pairs={{0,16},{16,0},{1,17},{17,1},{2,18},{18,2},{3,19},{19,3},{4,20},{20... | collective-permute-start | bytes 98312 | tf_op jit(solution)/shard_map/ppermute | solution.py:22
  159.4 3.9 %collective-permute-start.14 = (bf16[1,32,512]{2,1,0:T(8,128)(2,1)S(1)}, bf16[1,32,512]{2,1,0:T(8,128)(2,1)S(1)}, u32[]{:S(2)}, u32[]{:S(2)}) collective-permute-start(bf16[1,32,512]{2,1,0:T(8,128)(2,1)S(1)} %bitcast.81), channel_id=1, source_target_pairs={{0,4},{1,5},{2,6},{3,7},{4,0},{5,1},{6,2},{7,3},{8,12},{9,13},{10,... | collective-permute-start | bytes 98312 | tf_op jit(solution)/shard_map/ppermute | solution.py:22
  163.3 5.9 %collective-permute-start.15 = (bf16[2,32,512]{2,1,0:T(8,128)(2,1)S(1)}, bf16[2,32,512]{2,1,0:T(8,128)(2,1)S(1)}, u32[]{:S(2)}, u32[]{:S(2)}) collective-permute-start(bf16[2,32,512]{2,1,0:T(8,128)(2,1)S(1)} %pad_maximum_fusion.10), channel_id=1, source_target_pairs={{0,8},{1,9},{2,10},{3,11},{4,12},{5,13},{6,14},{7,15},{8,0},{9,1},... | collective-permute-start | bytes 196616 | tf_op jit(solution)/shard_map/ppermute | solution.py:22
  169.3 5.0 %collective-permute-start.16 = (bf16[4,32,512]{2,1,0:T(8,128)(2,1)S(1)}, bf16[4,32,512]{2,1,0:T(8,128)(2,1)S(1)}, u32[]{:S(2)}, u32[]{:S(2)}) collective-permute-start(bf16[4,32,512]{2,1,0:T(8,128)(2,1)S(1)} %pad_maximum_fusion.6), channel_id=1, source_target_pairs={{0,2},{1,3},{2,0},{3,1},{4,6},{5,7},{6,4},{7,5},{8,10},{9,11},{10,... | collective-permute-start | bytes 393224 | tf_op jit(solution)/shard_map/ppermute | solution.py:22
  174.3 1.6 collective-permute-start.17
  186.0 10.2 %all-to-all-start.3 = ((bf16[16,2,640]{2,1,0:T(2,128)(2,1)}), bf16[16,2,640]{2,1,0:T(2,128)(2,1)S(1)}, u32[]{:S(2)}, u32[]{:S(2)}) async-start(bf16[16,2,640]{2,1,0:T(2,128)(2,1)} %reshape.141), calls=%async_computation.3 | async-start | bytes 81920 | tf_op jit(solution)/shard_map/all_to_all | solution.py:428
  219.6 1.8 collective-permute-start.18
  222.5 5.6 %collective-permute-start.19 = (bf16[4,32,512]{2,1,0:T(8,128)(2,1)S(1)}, bf16[4,32,512]{2,1,0:T(8,128)(2,1)S(1)}, u32[]{:S(2)}, u32[]{:S(2)}) collective-permute-start(bf16[4,32,512]{2,1,0:T(8,128)(2,1)S(1)} %slice.130), channel_id=1, source_target_pairs={{0,2},{1,3},{2,0},{3,1},{4,6},{5,7},{6,4},{7,5},{8,10},{9,11},{10,... | collective-permute-start | bytes 393224 | tf_op jit(solution)/shard_map/ppermute | solution.py:22
  228.2 5.7 %collective-permute-start.20 = (bf16[2,32,512]{2,1,0:T(8,128)(2,1)S(1)}, bf16[2,32,512]{2,1,0:T(8,128)(2,1)S(1)}, u32[]{:S(2)}, u32[]{:S(2)}) collective-permute-start(bf16[2,32,512]{2,1,0:T(8,128)(2,1)S(1)} %slice.132), channel_id=1, source_target_pairs={{0,8},{1,9},{2,10},{3,11},{4,12},{5,13},{6,14},{7,15},{8,0},{9,1},... | collective-permute-start | bytes 196616 | tf_op jit(solution)/shard_map/ppermute | solution.py:22
  233.9 4.3 %collective-permute-start.21 = (bf16[1,32,512]{2,1,0:T(8,128)(2,1)S(1)}, bf16[1,32,512]{2,1,0:T(8,128)(2,1)S(1)}, u32[]{:S(2)}, u32[]{:S(2)}) collective-permute-start(bf16[1,32,512]{2,1,0:T(8,128)(2,1)S(1)} %slice.134), channel_id=1, source_target_pairs={{0,4},{1,5},{2,6},{3,7},{4,0},{5,1},{6,2},{7,3},{8,12},{9,13},{10,... | collective-permute-start | bytes 98312 | tf_op jit(solution)/shard_map/ppermute | solution.py:22
  238.2 4.7 %collective-permute-start.22 = (bf16[1,32,512]{2,1,0:T(8,128)(2,1)S(1)}, bf16[1,32,512]{2,1,0:T(8,128)(2,1)S(1)}, u32[]{:S(2)}, u32[]{:S(2)}) collective-permute-start(bf16[1,32,512]{2,1,0:T(8,128)(2,1)S(1)} %bitcast.85), channel_id=1, source_target_pairs={{0,4},{1,5},{2,6},{3,7},{4,0},{5,1},{6,2},{7,3},{8,12},{9,13},{10,... | collective-permute-start | bytes 98312 | tf_op jit(solution)/shard_map/ppermute | solution.py:22
  242.9 5.2 %collective-permute-start.23 = (bf16[2,32,512]{2,1,0:T(8,128)(2,1)S(1)}, bf16[2,32,512]{2,1,0:T(8,128)(2,1)S(1)}, u32[]{:S(2)}, u32[]{:S(2)}) collective-permute-start(bf16[2,32,512]{2,1,0:T(8,128)(2,1)S(1)} %pad_maximum_fusion.11), channel_id=1, source_target_pairs={{0,8},{1,9},{2,10},{3,11},{4,12},{5,13},{6,14},{7,15},{8,0},{9,1},... | collective-permute-start | bytes 196616 | tf_op jit(solution)/shard_map/ppermute | solution.py:22
  248.2 5.0 %collective-permute-start.24 = (bf16[4,32,512]{2,1,0:T(8,128)(2,1)S(1)}, bf16[4,32,512]{2,1,0:T(8,128)(2,1)S(1)}, u32[]{:S(2)}, u32[]{:S(2)}) collective-permute-start(bf16[4,32,512]{2,1,0:T(8,128)(2,1)S(1)} %pad_maximum_fusion.7), channel_id=1, source_target_pairs={{0,2},{1,3},{2,0},{3,1},{4,6},{5,7},{6,4},{7,5},{8,10},{9,11},{10,... | collective-permute-start | bytes 393224 | tf_op jit(solution)/shard_map/ppermute | solution.py:22
  253.2 1.6 collective-permute-start.25
  286.1 1.8 collective-permute-start.26
  (4 other events, 34.7 us)

commit v2 on v1

v2 whole, which is shorter than its diff:
```python
import functools

import jax
import jax.numpy as jnp
from jax import lax
from jax.experimental import pallas as pl
from jax.experimental.pallas import tpu as pltpu
from jax.sharding import PartitionSpec as P

QUERY_HEADS = 64
KEY_VALUE_HEADS = 8
HEAD_SIZE = 128

epsilon = 1e-05


def swap(value, mask, axis="mp"):
    count = lax.axis_size(axis)
    return lax.ppermute(value, axis, [(source, source ^ mask) for source in range(count)])


def exchange(parts):
    count = lax.axis_size("mp")
    groups = [list(range(core, count, 2)) for core in range(2)]
    return lax.all_to_all(
        parts, "mp", split_axis=0, concat_axis=0, axis_index_groups=groups, tiled=True
    )


def scatter(send, keep):
    held = keep.astype(jnp.float32) + swap(send, 1).astype(jnp.float32)
    return jnp.sum(exchange(held.astype(jnp.bfloat16)).astype(jnp.float32), axis=0)


def gather(part):
    own = exchange(jnp.broadcast_to(part[None], (lax.axis_size("mp") // 2,) + part.shape))
    return own, swap(own, 1)


def columns_to_chunks(values, count):
    rows, width = values.shape
    return values.reshape(rows, count, width // count).transpose(1, 0, 2)


def vmem():
    return pl.BlockSpec(memory_space=pltpu.VMEM)


def smem():
    return pl.BlockSpec(memory_space=pltpu.SMEM)


def resident(weights):
    return pltpu.with_memory_space_constraint(weights, pltpu.VMEM)


def hbm():
    return pl.BlockSpec(memory_space=pl.ANY)


def inverse_rms(x_refs):
    half, rows, chunk = x_refs[0].shape
    total = jnp.zeros((rows, 1), jnp.float32)
    for x_ref in x_refs:

        def add(k, total):
            wide = x_ref[k].astype(jnp.float32)
            return total + jnp.sum(wide * wide, axis=-1, keepdims=True)

        total = lax.fori_loop(0, half, add, total)
    return lax.rsqrt(total / (2 * half * chunk) + epsilon)


def span_of(ids_ref, k, chunk):
    return pl.ds(pl.multiple_of(ids_ref[k] * chunk, chunk), chunk)


def normed_chunk(x_ref, gain_ref, scale, k, span):
    wide = x_ref[k].astype(jnp.float32)
    return (wide * scale * gain_ref[:, span]).astype(jnp.bfloat16)


def project_kernel(ids_ref, own_ref, other_ref, gain_ref, wq_ref, wk_ref, wv_ref, out_ref,
                   q_sum, kv_sum):
    half, rows, chunk = own_ref.shape
    queries = wq_ref.shape[1]
    keys = wk_ref.shape[0]
    count, rows_dev, _ = out_ref.shape
    scale = inverse_rms((own_ref, other_ref))
    q_sum[...] = jnp.zeros_like(q_sum)
    kv_sum[...] = jnp.zeros_like(kv_sum)
    for first, x_ref in ((0, own_ref), (half, other_ref)):

        @pl.loop(0, half)
        def _(k):
            span = span_of(ids_ref, first + k, chunk)
            normed = normed_chunk(x_ref, gain_ref, scale, k, span)
            q_sum[...] += jnp.dot(normed, wq_ref[span, :], preferred_element_type=jnp.float32)
            for at, w_ref in ((0, wk_ref), (keys, wv_ref)):
                kv_sum[:, at : at + keys] += lax.dot_general(
                    normed,
                    w_ref[:, span],
                    (((1,), (1,)), ((), ())),
                    preferred_element_type=jnp.float32,
                )

    for owner in range(count):
        lines = slice(owner * rows_dev, (owner + 1) * rows_dev)
        out_ref[owner, :, :queries] = q_sum[lines, :].astype(jnp.bfloat16)
        out_ref[owner, :, queries:] = kv_sum[lines, :].astype(jnp.bfloat16)


def project(ids, own, other, gain, wq, wk, wv):
    half, rows, _ = own.shape
    queries, keys = wq.shape[1], wk.shape[0]
    size = queries + 2 * keys
    return pl.pallas_call(
        project_kernel,
        out_shape=pltpu.VMEM((2 * half, rows // (2 * half), size), jnp.bfloat16),
        in_specs=[smem()] + [vmem()] * 6,
        out_specs=vmem(),
        scratch_shapes=[
            pltpu.VMEM((rows, queries), jnp.float32),
            pltpu.VMEM((rows, 2 * keys), jnp.float32),
        ],
        compiler_params=pltpu.CompilerParams(vmem_limit_bytes=4 << 20),
        cost_estimate=pl.CostEstimate(
            flops=2 * rows * wq.shape[0] * size,
            bytes_accessed=2 * wq.shape[0] * size,
            transcendentals=0,
        ),
    )(ids, own, other, gain, resident(wq), resident(wk), resident(wv))


def attend_kernel(where_ref, length_ref, q_ref, kv_ref, cos_ref, sin_ref, keys_ref,
                  values_ref, out_ref, key_buf, value_buf, wide_q, sems):
    rows, devices, queries = q_ref.shape
    _, _, groups, size = kv_ref.shape
    slots = queries // size
    heads = devices * slots
    places = key_buf.shape[1]
    batch = where_ref[0]

    def copies(row):
        return (
            pltpu.make_async_copy(keys_ref.at[batch, row], key_buf.at[row], sems.at[0, row]),
            pltpu.make_async_copy(values_ref.at[batch, row], value_buf.at[row], sems.at[1, row]),
        )

    for row in range(rows):
        for which, copy in enumerate(copies(row)):
            copy.start(priority=which)
    line = lax.broadcasted_iota(jnp.int32, (devices, 1), 0)
    group_of = line * groups // devices
    for row in range(rows):
        cosine = cos_ref[pl.ds(row, 1), :]
        sine = sin_ref[pl.ds(row, 1), :]

        def turned(features):
            wide = features.astype(jnp.float32)
            other = jnp.concatenate([wide[:, size // 2 :], wide[:, : size // 2]], axis=1)
            return (wide * cosine + other * sine).astype(jnp.bfloat16).astype(jnp.float32)

        own_key = turned(kv_ref[row, 0])
        own_value = kv_ref[row, 1].astype(jnp.float32)
        key_lines = jnp.zeros((devices, size), jnp.float32)
        value_lines = jnp.zeros((devices, size), jnp.float32)
        for group in range(groups):
            here = group_of == group
            key_lines = jnp.where(here, own_key[group : group + 1], key_lines)
            value_lines = jnp.where(here, own_value[group : group + 1], value_lines)
        own_parts = []
        for slot in range(slots):
            part = turned(q_ref[row, :, slot * size : (slot + 1) * size])
            own_parts.append(jnp.sum(part * key_lines, axis=1, keepdims=True))
            for group in range(groups):
                wide_q[
                    slot * devices : (slot + 1) * devices, group * size : (group + 1) * size
                ] = jnp.where(group_of == group, part, 0.0).astype(jnp.bfloat16)
        own_score = jnp.concatenate(own_parts, axis=0) * (size ** -0.5)
        key_copy, value_copy = copies(row)
        key_copy.wait()
        scores = lax.dot_general(
            wide_q[...], key_buf[row], (((1,), (1,)), ((), ())), preferred_element_type=jnp.float32
        ) * (size ** -0.5)
        spot = lax.broadcasted_iota(jnp.int32, (heads, places), 1)
        scores = jnp.where(spot < length_ref[batch, row], scores, -1e30)
        highest = jnp.maximum(jnp.max(scores, axis=1, keepdims=True), own_score)
        raised = jnp.exp(scores - highest)
        own_raised = jnp.exp(own_score - highest)
        denominator = jnp.sum(raised, axis=1, keepdims=True) + own_raised
        weights = (raised / denominator).astype(jnp.bfloat16)
        own_weight = (own_raised / denominator).astype(jnp.bfloat16).astype(jnp.float32)
        value_copy.wait()
        mixed = jnp.dot(weights, value_buf[row], preferred_element_type=jnp.float32)
        for slot in range(slots):
            lines = slice(slot * devices, (slot + 1) * devices)
            picked = own_weight[lines] * value_lines
            for group in range(groups):
                picked = picked + jnp.where(
                    group_of == group, mixed[lines, group * size : (group + 1) * size], 0.0
                )
            out_ref[row, :, slot * size : (slot + 1) * size] = picked.astype(jnp.bfloat16)


def attend(where, lengths, query, fresh, cosine, sine, key_store, value_store):
    rows, devices, queries = query.shape
    places, width = key_store.shape[2:]
    heads = devices * queries // HEAD_SIZE
    return pl.pallas_call(
        attend_kernel,
        out_shape=pltpu.VMEM(query.shape, jnp.bfloat16),
        in_specs=[smem(), smem()] + [vmem()] * 4 + [hbm(), hbm()],
        out_specs=vmem(),
        scratch_shapes=[
            pltpu.VMEM((rows, places, width), jnp.bfloat16),
            pltpu.VMEM((rows, places, width), jnp.bfloat16),
            pltpu.VMEM((heads, width), jnp.bfloat16),
            pltpu.SemaphoreType.DMA((2, rows)),
        ],
        compiler_params=pltpu.CompilerParams(vmem_limit_bytes=8 << 20),
        cost_estimate=pl.CostEstimate(
            flops=4 * rows * heads * places * width,
            bytes_accessed=4 * rows * places * width,
            transcendentals=rows * heads * places,
        ),
    )(where, lengths, query, fresh, cosine, sine, key_store, value_store)


def spread_kernel(ids_ref, x_ref, w_ref, keep_ref, send_ref, values):
    half, rows, chunk = keep_ref.shape
    count, rows_dev, _ = x_ref.shape
    for owner in range(count):
        values[owner * rows_dev : (owner + 1) * rows_dev, :] = x_ref[owner].astype(jnp.float32)
    ready = values[...].astype(jnp.bfloat16)
    for first, target in ((0, keep_ref), (half, send_ref)):

        @pl.loop(0, half)
        def _(k):
            span = span_of(ids_ref, first + k, chunk)
            target[k] = jnp.dot(
                ready, w_ref[:, span], preferred_element_type=jnp.float32
            ).astype(jnp.bfloat16)


def spread_project(ids, values, weights):
    count, rows_dev, depth = values.shape
    rows = count * rows_dev
    width = weights.shape[1]
    shape = pltpu.VMEM((count // 2, rows, width // count), jnp.bfloat16)
    return pl.pallas_call(
        spread_kernel,
        out_shape=(shape, shape),
        in_specs=[smem(), vmem(), vmem()],
        out_specs=(vmem(), vmem()),
        scratch_shapes=[pltpu.VMEM((rows, depth), jnp.float32)],
        compiler_params=pltpu.CompilerParams(vmem_limit_bytes=4 << 20),
        cost_estimate=pl.CostEstimate(
            flops=2 * rows * depth * width, bytes_accessed=2 * depth * width, transcendentals=0
        ),
    )(ids, values, resident(weights))


def mlp_kernel(by_rows, ids_ref, own_ref, other_ref, gain_ref, gu_ref, down_ref, keep_ref,
               send_ref, gu_buf, wide_x, total, act, gu_sems):
    half, rows, chunk = own_ref.shape
    blocks = gu_buf.shape[1]

    def gu_copies(k):
        span = span_of(ids_ref, k, chunk)
        return [
            pltpu.make_async_copy(
                gu_ref.at[span, :, pl.ds(j * 128, 128)], gu_buf.at[k, j], gu_sems.at[k, j]
            )
            for j in range(blocks)
        ]

    @pl.loop(0, 2 * half)
    def _(k):
        for j, copy in enumerate(gu_copies(k)):
            copy.start(priority=j % 2)

    scale = inverse_rms((own_ref, other_ref))
    total[...] = jnp.zeros_like(total)
    line = lax.broadcasted_iota(jnp.int32, (128, 512), 0)
    column = lax.broadcasted_iota(jnp.int32, (128, 512), 1)
    aim = jnp.where(column < 256, 2 * line, 2 * line + 257)
    widen = jnp.where(column == aim, 1.0, 0.0).astype(jnp.bfloat16)

    for first, x_ref in ((0, own_ref), (half, other_ref)):

        @pl.loop(0, half)
        def _(place):
            k = first + place
            span = span_of(ids_ref, k, chunk)
            normed = normed_chunk(x_ref, gain_ref, scale, place, span)
            for b in range(chunk // 128):
                wide = jnp.dot(
                    normed[:, b * 128 : (b + 1) * 128], widen, preferred_element_type=jnp.float32
                ).astype(jnp.bfloat16)
                wide_x[:rows, b * 256 : (b + 1) * 256] = wide[:, :256]
                wide_x[rows:, b * 256 : (b + 1) * 256] = wide[:, 256:]
            for copy in gu_copies(k):
                copy.wait()
            for j in range(0, blocks, 2):
                pair = jnp.concatenate(
                    [gu_buf.at[k, j + i].reshape(2 * chunk, 128)[...] for i in range(2)], axis=1
                )
                total[:, j * 128 : (j + 2) * 128] += jnp.dot(
                    wide_x[...], pair, preferred_element_type=jnp.float32
                )

    gate = total[:rows, :]
    act[...] = (gate / (1.0 + jnp.exp(-gate)) * total[rows:, :]).astype(jnp.bfloat16)

    def down(span):
        return jnp.dot(act[...], down_ref[:, span], preferred_element_type=jnp.float32)

    if by_rows:
        rows_dev = keep_ref.shape[1]
        first_core = ids_ref[0] == 0

        @pl.loop(0, 2 * half)
        def _(k):
            span = span_of(ids_ref, k, chunk)
            part = down(span)
            for chip in range(half):
                at = 2 * chip * rows_dev
                low = part[at : at + rows_dev]
                high = part[at + rows_dev : at + 2 * rows_dev]
                keep_ref[chip, :, span] = jnp.where(first_core, low, high).astype(jnp.bfloat16)
                send_ref[chip, :, span] = jnp.where(first_core, high, low).astype(jnp.bfloat16)

    else:
        for first, target in ((0, keep_ref), (half, send_ref)):

            @pl.loop(0, half)
            def _(k):
                target[k] = down(span_of(ids_ref, first + k, chunk)).astype(jnp.bfloat16)


def mlp(ids, own, other, gain, gate_up, down, by_rows):
    half, rows, chunk = own.shape
    units, width = down.shape
    part = (half, rows // (2 * half), width) if by_rows else own.shape
    shape = pltpu.VMEM(part, jnp.bfloat16)
    return pl.pallas_call(
        functools.partial(mlp_kernel, by_rows),
        out_shape=(shape, shape),
        in_specs=[smem(), vmem(), vmem(), vmem(), hbm(), vmem()],
        out_specs=(vmem(), vmem()),
        scratch_shapes=[
            pltpu.VMEM((2 * half, units // 128, chunk, 2, 128), jnp.bfloat16),
            pltpu.VMEM((2 * rows, 2 * chunk), jnp.bfloat16),
            pltpu.VMEM((2 * rows, units), jnp.float32),
            pltpu.VMEM((rows, units), jnp.bfloat16),
            pltpu.SemaphoreType.DMA((2 * half, units // 128)),
        ],
        compiler_params=pltpu.CompilerParams(vmem_limit_bytes=37 << 20),
        cost_estimate=pl.CostEstimate(
            flops=6 * rows * units * width, bytes_accessed=6 * units * width, transcendentals=0
        ),
    )(ids, own, other, gain, gate_up, resident(down))


def turning(positions):
    half_dim = HEAD_SIZE // 2
    frequency = 500000.0 ** (-2.0 * jnp.arange(half_dim, dtype=jnp.float32) / HEAD_SIZE)
    angles = positions.astype(jnp.float32)[:, None] * frequency[None, :]
    cosine = jnp.cos(angles)
    sine = jnp.sin(angles)
    return jnp.concatenate([cosine, cosine], axis=1), jnp.concatenate([-sine, sine], axis=1)


def body(
    hidden,
    attn_gain,
    w_query,
    w_key,
    w_value,
    w_out,
    mlp_gain,
    w_gate_up,
    w_down,
    key_cache,
    value_cache,
    lengths,
):
    rows_dev = hidden.shape[1]
    count = lax.axis_size("mp")
    half = count // 2
    rows = rows_dev * count
    section_index = lax.axis_index("section")
    model_index = lax.axis_index("mp")
    core = model_index % 2
    query_cols = w_query.shape[2]
    key_cols = w_key.shape[2]
    width = hidden.shape[2]
    chips = 2 * jnp.arange(half, dtype=jnp.int32)
    ids = jnp.concatenate([chips + core, chips + 1 - core])
    wk = w_key[0].T
    wv = w_value[0].T

    def by_core(own, other):
        pair = jnp.where(core == 0, jnp.stack([own, other], 1), jnp.stack([other, own], 1))
        return pair.reshape((count,) + own.shape[1:])

    start = by_core(*gather(hidden[0])).reshape(rows, width)
    chunks = columns_to_chunks(start, count)
    mine = lax.dynamic_index_in_dim(chunks, model_index, 0, keepdims=False)
    own, other = chunks[:half], chunks[half:]
    order = jnp.arange(count, dtype=jnp.int32)
    for turn_index in range(2):
        batch = jnp.remainder(section_index + turn_index, 2).astype(jnp.int32)
        cosine, sine = turning(lax.dynamic_index_in_dim(lengths, batch, 0, keepdims=False))
        joined = project(order, own, other, attn_gain, w_query[0], wk, wv)
        spread = lax.all_to_all(joined, "mp", split_axis=0, concat_axis=0)
        query = spread[..., :query_cols].transpose(1, 0, 2)
        fresh = (
            spread[..., query_cols:]
            .reshape(count, rows_dev, 2, key_cols)
            .transpose(1, 2, 0, 3)
            .reshape(rows_dev, 2, KEY_VALUE_HEADS, HEAD_SIZE)
        )
        mixed = attend(
            batch.reshape(1), lengths, query, fresh, cosine, sine, key_cache[0], value_cache[0]
        )
        heads_out = lax.all_to_all(mixed.transpose(1, 0, 2), "mp", split_axis=0, concat_axis=0)
        keep, send = spread_project(ids, heads_out, w_out[0])
        middle = (mine.astype(jnp.float32) + scatter(send, keep)).astype(jnp.bfloat16)
        own, other = gather(middle)
        last = turn_index == 1
        keep, send = mlp(ids, own, other, mlp_gain, w_gate_up[0], w_down[0], last)
        mlp_part = scatter(send, keep)
        if last:
            at = model_index * rows_dev
            mine = by_core(
                lax.dynamic_slice_in_dim(own, at, rows_dev, 1),
                lax.dynamic_slice_in_dim(other, at, rows_dev, 1),
            )
            middle = mine.transpose(1, 0, 2).reshape(rows_dev, width)
        mine = (middle.astype(jnp.float32) + mlp_part).astype(jnp.bfloat16)
        if not last:
            mine = swap(mine, 1, "section")
            own, other = gather(mine)
            order = ids
    return mine[None]


def solution(mesh):
    placed = (
        P("section", "mp", None),
        P("section", None),
        P("section", None, "mp"),
        P("section", None, "mp"),
        P("section", None, "mp"),
        P("section", "mp", None),
        P("section", None),
        P("section", None, None, "mp"),
        P("section", "mp", None),
        P("section", None, "mp", None, None),
        P("section", None, "mp", None, None),
        P(None, "mp"),
    )
    return jax.shard_map(
        body, mesh=mesh, in_specs=placed, out_specs=P("section", "mp", None), check_vma=False
    )
```

time: 314 us -> 302 us (0.962)
  waiting for transfers between devices: 106 us -> 59.8 us
  blocking collectives: 43.1 us -> 70.2 us
  local copies, waits for them, and re-layouts: 22.5 us -> 42.8 us
  other arithmetic: 13.9 us -> 4.92 us
    ppermute x27 -> x9, waiting for transfers between devices: 88.6 us -> 14.2 us  [swap(): lax.ppermute(value, axis, [(source, source ^ mask) for source in range(co...]
    unnamed x28 -> x42, local copies, waits for them, and re-layouts: 4.6 us -> 38.4 us
    all_to_all x3 -> x6, waiting for transfers between devices: 17.9 us -> 45.6 us  [the longest x3 25.8 us: exchange(): lax.all_to_all(parts, 'mp', split_axis=0, concat_axis=0, axis_index_group...]
    all_to_all x4 -> x6, blocking collectives: 43.1 us -> 70.2 us  [the longest x5 61 us: exchange(): lax.all_to_all(parts, 'mp', split_axis=0, concat_axis=0, axis_index_group...]
    ppermute x27 -> x9, starting transfers between devices: 16.2 us -> 1.98 us  [swap(): lax.ppermute(value, axis, [(source, source ^ mask) for source in range(co...]
    all_to_all x3 -> x6, starting transfers between devices: 11.7 us -> 24.9 us  [the longest x3 14.3 us: exchange(): lax.all_to_all(parts, 'mp', split_axis=0, concat_axis=0, axis_index_group...]
    reshape x9 -> x6, local copies, waits for them, and re-layouts: 6.84 us -> 0.35 us  [body(): fresh = spread[..., query_cols:].reshape(count, rows_dev, 2, key_cols).tr...]
    gather x6 -> x0, local copies, waits for them, and re-layouts: 5.05 us -> none  [the longest x2 1.97 us: to_absolute(): jnp.take(chunks, jnp.asarray(place)[jnp.arange(place.shape[0]) ^ me], axi...]
  transfers between devices with their start and end apart: 30 -> 15, of which waited for: 29 -> 15; matrix products, arithmetic and copies ran while one was open for 3% -> 1% of each run, Pallas kernels for 0% -> 0%
where the time goes in v2:
time: 302 us; the launch traced here: 300 us
  Pallas kernels  95.5 us (32%)
  blocking collectives  70.2 us (23%)
  waiting for transfers between devices  59.8 us (20%)
  local copies, waits for them, and re-layouts  42.8 us (14%)
  starting transfers between devices  26.9 us (9%)
  other arithmetic  4.92 us (2%)
    pallas_call x2, Pallas kernels, mlp(): pl.pallas_call(functools.partial(mlp_kernel, by_rows), out_shape=(shape,...  66.2 us
    all_to_all x5, blocking collectives, exchange(): lax.all_to_all(parts, 'mp', split_axis=0, concat_axis=0, axis_index_group...  61 us
    unnamed x42, local copies, waits for them, and re-layouts  38.4 us
    all_to_all x3, waiting for transfers between devices, exchange(): lax.all_to_all(parts, 'mp', split_axis=0, concat_axis=0, axis_index_group...  25.8 us
    pallas_call x2, Pallas kernels, project(): pl.pallas_call(project_kernel, out_shape=pltpu.VMEM((2 * half, rows // (2...  15.4 us
    all_to_all x3, starting transfers between devices, exchange(): lax.all_to_all(parts, 'mp', split_axis=0, concat_axis=0, axis_index_group...  14.3 us
    ppermute x9, waiting for transfers between devices, swap(): lax.ppermute(value, axis, [(source, source ^ mask) for source in range(co...  14.2 us
    all_to_all x2, waiting for transfers between devices, body(): spread = lax.all_to_all(joined, 'mp', split_axis=0, concat_axis=0)  13.3 us
  transfers between devices with their start and end apart: 15, of which 15 were waited for; matrix products, arithmetic and copies ran while one was open for 1% of the time, Pallas kernels for 0%

profile of v2, /device:TPU:0, one launch (start us, length us, event | category | flops | bytes accessed | tf_op | source)
XLA Modules:
  0.0 300.4 jit_solution(12752838620789519363)
XLA Ops:
  1.6 7.3 %all-to-all-start = ((bf16[8,2,8192]{2,1,0:T(2,128)(2,1)}), bf16[8,2,8192]{2,1,0:T(2,128)(2,1)S(1)}, u32[]{:S(2)}, u32[]{:S(2)}) async-start(bf16[8,2,8192]{2,1,0:T(2,128)(2,1)} %broadcast_in_dim.11), calls=%async_computation | async-start | bytes 524288 | tf_op jit(solution)/shard_map/all_to_all | solution.py:25
  9.7 8.1 %all-to-all-done = bf16[8,2,8192]{2,1,0:T(2,128)(2,1)S(1)} async-done(((bf16[8,2,8192]{2,1,0:T(2,128)(2,1)}), bf16[8,2,8192]{2,1,0:T(2,128)(2,1)S(1)}, u32[]{:S(2)}, u32[]{:S(2)}) %all-to-all-start) | async-done | bytes 262176 | tf_op jit(solution)/shard_map/all_to_all | solution.py:25
  20.8 3.4 %copy-done.2 = bf16[1,8192,512]{2,1,0:T(8,128)(2,1)S(1)} copy-done((bf16[1,8192,512]{2,1,0:T(8,128)(2,1)S(1)}, bf16[1,8192,512]{2,1,0:T(8,128)(2,1)}, u32[]{:S(2)}) %copy-start.2) | copy-done | bytes 8388632
  27.4 7.7 %shard_map.118 = bf16[16,2,640]{2,1,0:T(2,128)(2,1)} custom-call(s32[16]{0:T(128)S(1)} %iota.17.ids_ref, bf16[8,32,512]{2,1,0:T(8,128)(2,1)S(1)} %get-tuple-element.22.own_ref, bf16[8,32,512]{2,1,0:T(8,128)(2,1)S(1)} %get-tuple-element.21.other_ref, f32[1,8192]{1,0:T(1,128)S(1)} %copy-done.14, bf16[8192,512]{1,0:T(8,128)(2,1)S(1)} %bitcast.66, ...), custom_call_target="tpu_custom_call" | custom-call | flops 335544320 | bytes 10485760 | tf_op jit(solution)/shard_map/pallas_call | solution.py:117
  35.1 3.7 %all-to-all-start.1 = ((bf16[16,2,640]{2,1,0:T(2,128)(2,1)}), bf16[16,2,640]{2,1,0:T(2,128)(2,1)S(1)}, u32[]{:S(2)}, u32[]{:S(2)}) async-start(bf16[16,2,640]{2,1,0:T(2,128)(2,1)} %shard_map.118), calls=%async_computation.1 | async-start | bytes 81920 | tf_op jit(solution)/shard_map/all_to_all | solution.py:417
  38.9 6.7 %all-to-all-done.1 = bf16[16,2,640]{2,1,0:T(2,128)(2,1)S(1)} async-done(((bf16[16,2,640]{2,1,0:T(2,128)(2,1)}), bf16[16,2,640]{2,1,0:T(2,128)(2,1)S(1)}, u32[]{:S(2)}, u32[]{:S(2)}) %all-to-all-start.1) | async-done | bytes 40992 | tf_op jit(solution)/shard_map/all_to_all | solution.py:417
  50.2 3.2 %shard_map.119 = bf16[2,16,512]{2,1,0:T(8,128)(2,1)S(1)} custom-call(s32[1]{0:T(128)} %bitcast.3.where_ref, s32[2,2]{1,0:T(2,128)S(1)} %copy-done.17, bf16[2,16,512]{2,1,0:T(8,128)(2,1)S(1)} %bitcast.78, bf16[2,2,8,128]{3,2,1,0:T(8,128)(2,1)S(1)} %reshape.85.kv_ref, f32[2,128]{1,0:T(2,128)S(1)} %get-tuple-element.36.cos_ref, ...), custom_call_target="tpu_custom_call" | custom-call | flops 268435456 | bytes 4194304 | tf_op jit(solution)/shard_map/pallas_call | solution.py:210
  54.0 3.5 %all-to-all-start.2 = ((bf16[16,2,512]{2,1,0:T(2,128)(2,1)}), bf16[16,2,512]{2,1,0:T(2,128)(2,1)S(1)}, u32[]{:S(2)}, u32[]{:S(2)}) async-start(bf16[16,2,512]{2,1,0:T(2,128)(2,1)} %bitcast.61), calls=%async_computation.2 | async-start | bytes 65536 | tf_op jit(solution)/shard_map/all_to_all | solution.py:428
  57.6 6.5 %all-to-all-done.2.x_ref = bf16[16,2,512]{2,1,0:T(2,128)(2,1)S(1)} async-done(((bf16[16,2,512]{2,1,0:T(2,128)(2,1)}), bf16[16,2,512]{2,1,0:T(2,128)(2,1)S(1)}, u32[]{:S(2)}, u32[]{:S(2)}) %all-to-all-start.2) | async-done | bytes 32800 | tf_op jit(solution)/shard_map/all_to_all | solution.py:428
  64.1 3.4 %copy-done.4 = bf16[1,512,8192]{2,1,0:T(8,128)(2,1)S(1)} copy-done((bf16[1,512,8192]{2,1,0:T(8,128)(2,1)S(1)}, bf16[1,512,8192]{2,1,0:T(8,128)(2,1)}, u32[]{:S(2)}) %copy-start.4) | copy-done | bytes 8388632
  67.5 3.8 %shard_map.120 = (bf16[8,32,512]{2,1,0:T(8,128)(2,1)S(1)}, bf16[8,32,512]{2,1,0:T(8,128)(2,1)S(1)}) custom-call(s32[16]{0:T(128)S(1)} %pad_add_fusion.ids_ref, bf16[16,2,512]{2,1,0:T(2,128)(2,1)S(1)} %all-to-all-done.2.x_ref, bf16[512,8192]{1,0:T(8,128)(2,1)S(1)} %bitcast.68), custom_call_target="tpu_custom_call" | custom-call | flops 268435456 | bytes 8388608 | tf_op jit(solution)/shard_map/pallas_call | solution.py:251
  73.6 3.4 %all-to-all-start.3 = ((bf16[8,32,512]{2,1,0:T(8,128)(2,1)}), bf16[8,32,512]{2,1,0:T(8,128)(2,1)S(1)}, u32[]{:S(2)}, u32[]{:S(2)}) async-start(bf16[8,32,512]{2,1,0:T(8,128)(2,1)} %add_convert_fusion.3), calls=%async_computation.3 | async-start | bytes 524288 | tf_op jit(solution)/shard_map/all_to_all | solution.py:25
  77.0 9.4 %all-to-all-done.3 = bf16[8,32,512]{2,1,0:T(8,128)(2,1)S(1)} async-done(((bf16[8,32,512]{2,1,0:T(8,128)(2,1)}), bf16[8,32,512]{2,1,0:T(8,128)(2,1)S(1)}, u32[]{:S(2)}, u32[]{:S(2)}) %all-to-all-start.3) | async-done | bytes 262176 | tf_op jit(solution)/shard_map/all_to_all | solution.py:25
  86.5 12.4 %all_to_all.60.own_ref = bf16[8,32,512]{2,1,0:T(8,128)(2,1)S(1)} all-to-all(bf16[8,32,512]{2,1,0:T(8,128)(2,1)S(1)} %broadcast_in_dim.12), channel_id=1, replica_groups={{0,2,4,6,8,10,12,14},{1,3,5,7,9,11,13,15},{16,18,20,22,24,26,28,30},{17..., dimensions={0} | all-to-all | bytes 524288 | tf_op jit(solution)/shard_map/all_to_all | solution.py:25
  101.2 5.8 %copy-done = bf16[1,1024,8192]{2,1,0:T(8,128)(2,1)S(1)} copy-done((bf16[1,1024,8192]{2,1,0:T(8,128)(2,1)S(1)}, bf16[1,1024,8192]{2,1,0:T(8,128)(2,1)}, u32[]{:S(2)}) %copy-start) | copy-done | bytes 16777240
  106.9 33.1 %shard_map.121 = (bf16[8,32,512]{2,1,0:T(8,128)(2,1)S(1)}, bf16[8,32,512]{2,1,0:T(8,128)(2,1)S(1)}) custom-call(s32[16]{0:T(128)S(1)} %pad_add_fusion.ids_ref, bf16[8,32,512]{2,1,0:T(8,128)(2,1)S(1)} %all_to_all.60.own_ref, bf16[8,32,512]{2,1,0:T(8,128)(2,1)} %copy-done.19, f32[1,8192]{1,0:T(1,128)S(1)} %copy-done.16, bf16[8192,2,1024]{2,1,0:T(2,128)(2,1)} %bitcast.80, ...), custom_call_target="tpu_custom_call" | custom-call | flops 1610612736 | bytes 50331648 | tf_op jit(solution)/shard_map/pallas_call | solution.py:347
  141.7 12.6 %all_to_all.61 = bf16[8,32,512]{2,1,0:T(8,128)(2,1)S(1)} all-to-all(bf16[8,32,512]{2,1,0:T(8,128)(2,1)S(1)} %add_convert_fusion.2), channel_id=1, replica_groups={{0,2,4,6,8,10,12,14},{1,3,5,7,9,11,13,15},{16,18,20,22,24,26,28,30},{17..., dimensions={0} | all-to-all | bytes 524288 | tf_op jit(solution)/shard_map/all_to_all | solution.py:25
  158.3 11.6 %all_to_all.62.own_ref = bf16[8,32,512]{2,1,0:T(8,128)(2,1)S(1)} all-to-all(bf16[8,32,512]{2,1,0:T(8,128)(2,1)S(1)} %broadcast_in_dim.13), channel_id=1, replica_groups={{0,2,4,6,8,10,12,14},{1,3,5,7,9,11,13,15},{16,18,20,22,24,26,28,30},{17..., dimensions={0} | all-to-all | bytes 524288 | tf_op jit(solution)/shard_map/all_to_all | solution.py:25
  171.5 3.4 %copy-done.3 = bf16[1,8192,512]{2,1,0:T(8,128)(2,1)S(1)} copy-done((bf16[1,8192,512]{2,1,0:T(8,128)(2,1)S(1)}, bf16[1,8192,512]{2,1,0:T(8,128)(2,1)}, u32[]{:S(2)}) %copy-start.3) | copy-done | bytes 8388632
  174.9 7.7 %shard_map.122 = bf16[16,2,640]{2,1,0:T(2,128)(2,1)} custom-call(s32[16]{0:T(128)S(1)} %pad_add_fusion.ids_ref, bf16[8,32,512]{2,1,0:T(8,128)(2,1)S(1)} %all_to_all.62.own_ref, bf16[8,32,512]{2,1,0:T(8,128)(2,1)S(1)} %collective-permute-done.5.other_ref, f32[1,8192]{1,0:T(1,128)S(1)} %copy-done.15, bf16[8192,512]{1,0:T(8,128)(2,1)S(1)} %bitcast.67, ...), custom_call_target="tpu_custom_call" | custom-call | flops 335544320 | bytes 10485760 | tf_op jit(solution)/shard_map/pallas_call | solution.py:117
  182.6 3.5 %all-to-all-start.7 = ((bf16[16,2,640]{2,1,0:T(2,128)(2,1)}), bf16[16,2,640]{2,1,0:T(2,128)(2,1)S(1)}, u32[]{:S(2)}, u32[]{:S(2)}) async-start(bf16[16,2,640]{2,1,0:T(2,128)(2,1)} %shard_map.122), calls=%async_computation.7 | async-start | bytes 81920 | tf_op jit(solution)/shard_map/all_to_all | solution.py:417
  186.2 6.6 %all-to-all-done.7 = bf16[16,2,640]{2,1,0:T(2,128)(2,1)S(1)} async-done(((bf16[16,2,640]{2,1,0:T(2,128)(2,1)}), bf16[16,2,640]{2,1,0:T(2,128)(2,1)S(1)}, u32[]{:S(2)}, u32[]{:S(2)}) %all-to-all-start.7) | async-done | bytes 40992 | tf_op jit(solution)/shard_map/all_to_all | solution.py:417
  197.4 3.2 %shard_map.123 = bf16[2,16,512]{2,1,0:T(8,128)(2,1)S(1)} custom-call(s32[1]{0:T(128)} %bitcast.19.where_ref, s32[2,2]{1,0:T(2,128)S(1)} %copy-done.17, bf16[2,16,512]{2,1,0:T(8,128)(2,1)S(1)} %bitcast.79, bf16[2,2,8,128]{3,2,1,0:T(8,128)(2,1)S(1)} %reshape.88.kv_ref, f32[2,128]{1,0:T(2,128)S(1)} %get-tuple-element.38.cos_ref, ...), custom_call_target="tpu_custom_call" | custom-call | flops 268435456 | bytes 4194304 | tf_op jit(solution)/shard_map/pallas_call | solution.py:210
  200.6 9.2 %all_to_all.63.x_ref = bf16[16,2,512]{2,1,0:T(2,128)(2,1)S(1)} all-to-all(bf16[16,2,512]{2,1,0:T(2,128)(2,1)S(1)} %bitcast.86), channel_id=1, replica_groups=mesh['section'=2,'mp'=16] {'mp'}, dimensions={0} | all-to-all | bytes 65536 | tf_op jit(solution)/shard_map/all_to_all | solution.py:428
  209.8 3.4 %copy-done.5 = bf16[1,512,8192]{2,1,0:T(8,128)(2,1)S(1)} copy-done((bf16[1,512,8192]{2,1,0:T(8,128)(2,1)S(1)}, bf16[1,512,8192]{2,1,0:T(8,128)(2,1)}, u32[]{:S(2)}) %copy-start.5) | copy-done | bytes 8388632
  213.2 3.8 %shard_map.124 = (bf16[8,32,512]{2,1,0:T(8,128)(2,1)S(1)}, bf16[8,32,512]{2,1,0:T(8,128)(2,1)S(1)}) custom-call(s32[16]{0:T(128)S(1)} %pad_add_fusion.ids_ref, bf16[16,2,512]{2,1,0:T(2,128)(2,1)S(1)} %all_to_all.63.x_ref, bf16[512,8192]{1,0:T(8,128)(2,1)S(1)} %bitcast.69), custom_call_target="tpu_custom_call" | custom-call | flops 268435456 | bytes 8388608 | tf_op jit(solution)/shard_map/pallas_call | solution.py:251
  218.6 11.9 %all_to_all.64 = bf16[8,32,512]{2,1,0:T(8,128)(2,1)S(1)} all-to-all(bf16[8,32,512]{2,1,0:T(8,128)(2,1)S(1)} %add_convert_fusion.1), channel_id=1, replica_groups={{0,2,4,6,8,10,12,14},{1,3,5,7,9,11,13,15},{16,18,20,22,24,26,28,30},{17..., dimensions={0} | all-to-all | bytes 524288 | tf_op jit(solution)/shard_map/all_to_all | solution.py:25
  230.6 12.4 %all_to_all.65.own_ref = bf16[8,32,512]{2,1,0:T(8,128)(2,1)S(1)} all-to-all(bf16[8,32,512]{2,1,0:T(8,128)(2,1)S(1)} %broadcast_in_dim.14), channel_id=1, replica_groups={{0,2,4,6,8,10,12,14},{1,3,5,7,9,11,13,15},{16,18,20,22,24,26,28,30},{17..., dimensions={0} | all-to-all | bytes 524288 | tf_op jit(solution)/shard_map/all_to_all | solution.py:25
  245.2 5.8 %copy-done.1 = bf16[1,1024,8192]{2,1,0:T(8,128)(2,1)S(1)} copy-done((bf16[1,1024,8192]{2,1,0:T(8,128)(2,1)S(1)}, bf16[1,1024,8192]{2,1,0:T(8,128)(2,1)}, u32[]{:S(2)}) %copy-start.1) | copy-done | bytes 16777240
  251.0 33.1 %shard_map.125 = (bf16[8,2,8192]{2,1,0:T(2,128)(2,1)S(1)}, bf16[8,2,8192]{2,1,0:T(2,128)(2,1)S(1)}) custom-call(s32[16]{0:T(128)S(1)} %pad_add_fusion.ids_ref, bf16[8,32,512]{2,1,0:T(8,128)(2,1)S(1)} %all_to_all.65.own_ref, bf16[8,32,512]{2,1,0:T(8,128)(2,1)} %copy-done.18, f32[1,8192]{1,0:T(1,128)S(1)} %copy-done.16, bf16[8192,2,1024]{2,1,0:T(2,128)(2,1)} %bitcast.81, ...), custom_call_target="tpu_custom_call" | custom-call | flops 1610612736 | bytes 50331648 | tf_op jit(solution)/shard_map/pallas_call | solution.py:347
  286.7 3.6 %all-to-all-start.11 = ((bf16[8,2,8192]{2,1,0:T(2,128)(2,1)}), bf16[8,2,8192]{2,1,0:T(2,128)(2,1)S(1)}, u32[]{:S(2)}, u32[]{:S(2)}) async-start(bf16[8,2,8192]{2,1,0:T(2,128)(2,1)} %add_convert_fusion), calls=%async_computation.11 | async-start | bytes 524288 | tf_op jit(solution)/shard_map/all_to_all | solution.py:25
  291.3 8.3 %all-to-all-done.11 = bf16[8,2,8192]{2,1,0:T(2,128)(2,1)S(1)} async-done(((bf16[8,2,8192]{2,1,0:T(2,128)(2,1)}), bf16[8,2,8192]{2,1,0:T(2,128)(2,1)S(1)}, u32[]{:S(2)}, u32[]{:S(2)}) %all-to-all-start.11) | async-done | bytes 262176 | tf_op jit(solution)/shard_map/all_to_all | solution.py:25
  (99 shorter events, 38.9 us)
Async XLA Ops:
  0.0 45.8 %copy-start.17 = (s32[2,2]{1,0:T(2,128)S(1)}, s32[2,2]{1,0:T(2,128)}, u32[]{:S(2)}) copy-start(s32[2,2]{1,0:T(2,128)} %length_ref.3) | copy-start | bytes 52
  1.6 16.2 %all-to-all-start = ((bf16[8,2,8192]{2,1,0:T(2,128)(2,1)}), bf16[8,2,8192]{2,1,0:T(2,128)(2,1)S(1)}, u32[]{:S(2)}, u32[]{:S(2)}) async-start(bf16[8,2,8192]{2,1,0:T(2,128)(2,1)} %broadcast_in_dim.11), calls=%async_computation | async-start | bytes 524288 | tf_op jit(solution)/shard_map/all_to_all | solution.py:25
  17.8 1.5 collective-permute-start
  20.8 3.4 %copy-start.2 = (bf16[1,8192,512]{2,1,0:T(8,128)(2,1)S(1)}, bf16[1,8192,512]{2,1,0:T(8,128)(2,1)}, u32[]{:S(2)}) copy-start(bf16[1,8192,512]{2,1,0:T(8,128)(2,1)} %param.14) | copy-start | bytes 25165828
  24.2 1.2 copy-start.10
  25.4 1.2 copy-start.12
  35.1 10.4 %all-to-all-start.1 = ((bf16[16,2,640]{2,1,0:T(2,128)(2,1)}), bf16[16,2,640]{2,1,0:T(2,128)(2,1)S(1)}, u32[]{:S(2)}, u32[]{:S(2)}) async-start(bf16[16,2,640]{2,1,0:T(2,128)(2,1)} %shard_map.118), calls=%async_computation.1 | async-start | bytes 81920 | tf_op jit(solution)/shard_map/all_to_all | solution.py:417
  45.8 2.2 copy-start.6
  48.0 2.2 copy-start.8
  50.2 51.0 %copy-start.16 = (f32[1,8192]{1,0:T(1,128)S(1)}, f32[1,8192]{1,0:T(1,128)}, u32[]{:S(2)}) copy-start(f32[1,8192]{1,0:T(1,128)} %gain_ref.7) | copy-start | bytes 98308
  54.0 10.1 %all-to-all-start.2 = ((bf16[16,2,512]{2,1,0:T(2,128)(2,1)}), bf16[16,2,512]{2,1,0:T(2,128)(2,1)S(1)}, u32[]{:S(2)}, u32[]{:S(2)}) async-start(bf16[16,2,512]{2,1,0:T(2,128)(2,1)} %bitcast.61), calls=%async_computation.2 | async-start | bytes 65536 | tf_op jit(solution)/shard_map/all_to_all | solution.py:428
  64.1 3.4 %copy-start.4 = (bf16[1,512,8192]{2,1,0:T(8,128)(2,1)S(1)}, bf16[1,512,8192]{2,1,0:T(8,128)(2,1)}, u32[]{:S(2)}) copy-start(bf16[1,512,8192]{2,1,0:T(8,128)(2,1)} %param.17) | copy-start | bytes 25165828
  71.2 1.6 collective-permute-start.1
  73.6 12.9 %all-to-all-start.3 = ((bf16[8,32,512]{2,1,0:T(8,128)(2,1)}), bf16[8,32,512]{2,1,0:T(8,128)(2,1)S(1)}, u32[]{:S(2)}, u32[]{:S(2)}) async-start(bf16[8,32,512]{2,1,0:T(8,128)(2,1)} %add_convert_fusion.3), calls=%async_computation.3 | async-start | bytes 524288 | tf_op jit(solution)/shard_map/all_to_all | solution.py:25
  98.9 1.5 collective-permute-start.2
  101.1 5.8 %copy-start = (bf16[1,1024,8192]{2,1,0:T(8,128)(2,1)S(1)}, bf16[1,1024,8192]{2,1,0:T(8,128)(2,1)}, u32[]{:S(2)}) copy-start(bf16[1,1024,8192]{2,1,0:T(8,128)(2,1)} %param.20) | copy-start | bytes 50331652
  106.9 64.6 %copy-start.11 = (bf16[1,8192,64]{1,2,0:T(8,128)(2,1)S(1)}, bf16[1,8192,64]{1,2,0:T(8,128)(2,1)}, u32[]{:S(2)}) copy-start(bf16[1,8192,64]{1,2,0:T(8,128)(2,1)} %param.15) | copy-start | bytes 3145732
  106.9 64.6 %copy-start.13 = (bf16[1,8192,64]{1,2,0:T(8,128)(2,1)S(1)}, bf16[1,8192,64]{1,2,0:T(8,128)(2,1)}, u32[]{:S(2)}) copy-start(bf16[1,8192,64]{1,2,0:T(8,128)(2,1)} %param.16) | copy-start | bytes 3145732
  106.9 64.6 %copy-start.15 = (f32[1,8192]{1,0:T(1,128)S(1)}, f32[1,8192]{1,0:T(1,128)}, u32[]{:S(2)}) copy-start(f32[1,8192]{1,0:T(1,128)} %gain_ref.6) | copy-start | bytes 98308
  140.0 1.6 collective-permute-start.3
  154.3 4.0 %collective-permute-start.4 = (bf16[32,512]{1,0:T(8,128)(2,1)S(1)}, bf16[32,512]{1,0:T(8,128)(2,1)S(1)}, u32[]{:S(2)}, u32[]{:S(2)}) collective-permute-start(bf16[32,512]{1,0:T(8,128)(2,1)S(1)} %add_convert_fusion.5), channel_id=1, source_target_pairs={{0,16},{16,0},{1,17},{17,1},{2,18},{18,2},{3,19},{19,3},{4,20},{20... | collective-permute-start | bytes 98312 | tf_op jit(solution)/shard_map/ppermute | solution.py:19
  169.9 1.5 collective-permute-start.5
  171.5 3.4 %copy-start.3 = (bf16[1,8192,512]{2,1,0:T(8,128)(2,1)S(1)}, bf16[1,8192,512]{2,1,0:T(8,128)(2,1)}, u32[]{:S(2)}) copy-start(bf16[1,8192,512]{2,1,0:T(8,128)(2,1)} %param.14) | copy-start | bytes 25165828
  182.6 10.1 %all-to-all-start.7 = ((bf16[16,2,640]{2,1,0:T(2,128)(2,1)}), bf16[16,2,640]{2,1,0:T(2,128)(2,1)S(1)}, u32[]{:S(2)}, u32[]{:S(2)}) async-start(bf16[16,2,640]{2,1,0:T(2,128)(2,1)} %shard_map.122), calls=%async_computation.7 | async-start | bytes 81920 | tf_op jit(solution)/shard_map/all_to_all | solution.py:417
  193.0 2.2 copy-start.7
  195.2 2.2 copy-start.9
  209.8 3.4 %copy-start.5 = (bf16[1,512,8192]{2,1,0:T(8,128)(2,1)S(1)}, bf16[1,512,8192]{2,1,0:T(8,128)(2,1)}, u32[]{:S(2)}) copy-start(bf16[1,512,8192]{2,1,0:T(8,128)(2,1)} %param.17) | copy-start | bytes 25165828
  216.9 1.6 collective-permute-start.6
  243.0 1.5 collective-permute-start.7
  245.2 5.8 %copy-start.1 = (bf16[1,1024,8192]{2,1,0:T(8,128)(2,1)S(1)}, bf16[1,1024,8192]{2,1,0:T(8,128)(2,1)}, u32[]{:S(2)}) copy-start(bf16[1,1024,8192]{2,1,0:T(8,128)(2,1)} %param.20) | copy-start | bytes 50331652
  284.1 1.6 collective-permute-start.8
  286.7 12.9 %all-to-all-start.11 = ((bf16[8,2,8192]{2,1,0:T(2,128)(2,1)}), bf16[8,2,8192]{2,1,0:T(2,128)(2,1)S(1)}, u32[]{:S(2)}, u32[]{:S(2)}) async-start(bf16[8,2,8192]{2,1,0:T(2,128)(2,1)} %add_convert_fusion), calls=%async_computation.11 | async-start | bytes 524288 | tf_op jit(solution)/shard_map/all_to_all | solution.py:25
  (3 other events, 2.2 us)

commit v3 on v2

--- a/solution.py
+++ b/solution.py
@@ -13,6 +13,8 @@
 
 epsilon = 1e-05
 
+UNROLL = 4
+
 
 def swap(value, mask, axis="mp"):
     count = lax.axis_size(axis)
@@ -27,9 +29,13 @@
     )
 
 
-def scatter(send, keep):
+def merge(send, keep):
     held = keep.astype(jnp.float32) + swap(send, 1).astype(jnp.float32)
-    return jnp.sum(exchange(held.astype(jnp.bfloat16)).astype(jnp.float32), axis=0)
+    return held.astype(jnp.bfloat16)
+
+
+def scatter(held):
+    return jnp.sum(exchange(held).astype(jnp.float32), axis=0)
 
 
 def gather(part):
@@ -50,12 +56,114 @@
     return pl.BlockSpec(memory_space=pltpu.SMEM)
 
 
-def resident(weights):
-    return pltpu.with_memory_space_constraint(weights, pltpu.VMEM)
+def placed_in(values, space):
+    return pltpu.with_memory_space_constraint(values, space)
 
 
 def hbm():
     return pl.BlockSpec(memory_space=pl.ANY)
+
+
+def run_copies(copies):
+    for at, copy in enumerate(copies):
+        copy.start(priority=at % 2)
+    for copy in copies:
+        copy.wait()
+
+
+def fetch_kernel(pieces, token_ref, *refs):
+    arrays = len(pieces)
+    sems = refs[-1]
+    copies = []
+    for array, (count, source, target) in enumerate(zip(pieces, refs, refs[arrays:])):
+        size = source.shape[0] // count
+        for piece in range(count):
+            span = pl.ds(piece * size, size)
+            copies.append(
+                pltpu.make_async_copy(source.at[span], target.at[span], sems.at[array, piece])
+            )
+    run_copies(copies)
+
+
+def fetch(token, *arrays):
+    pieces = [8 if array.shape[0] % 128 == 0 else 1 for array in arrays]
+    return pl.pallas_call(
+        functools.partial(fetch_kernel, pieces),
+        out_shape=[pltpu.VMEM(array.shape, array.dtype) for array in arrays],
+        in_specs=[hbm()] * (1 + len(arrays)),
+        out_specs=[vmem()] * len(arrays),
+        scratch_shapes=[pltpu.SemaphoreType.DMA((len(arrays), 8))],
+        compiler_params=pltpu.CompilerParams(vmem_limit_bytes=1 << 20),
+        cost_estimate=pl.CostEstimate(
+            flops=0, bytes_accessed=sum(2 * array.size for array in arrays), transcendentals=0
+        ),
+    )(token, *[placed_in(array, pltpu.HBM) for array in arrays])
+
+
+def fetch_caches_kernel(token_ref, where_ref, keys_ref, values_ref, key_ref, value_ref, sems):
+    rows, places, _ = key_ref.shape
+    batch = where_ref[0]
+    copies = []
+    for array, (source, target) in enumerate(((keys_ref, key_ref), (values_ref, value_ref))):
+        for row in range(rows):
+            for piece in range(2):
+                span = pl.ds(piece * (places // 2), places // 2)
+                copies.append(
+                    pltpu.make_async_copy(
+                        source.at[batch, row, span],
+                        target.at[row, span],
+                        sems.at[array, row, piece],
+                    )
+                )
+    run_copies(copies)
+
+
+def fetch_caches(token, where, keys, values):
+    shape = pltpu.VMEM(keys.shape[1:], keys.dtype)
+    return pl.pallas_call(
+        fetch_caches_kernel,
+        out_shape=[shape, shape],
+        in_specs=[hbm(), smem(), hbm(), hbm()],
+        out_specs=[vmem(), vmem()],
+        scratch_shapes=[pltpu.SemaphoreType.DMA((2, keys.shape[1], 2))],
+        compiler_params=pltpu.CompilerParams(vmem_limit_bytes=1 << 20),
+        cost_estimate=pl.CostEstimate(
+            flops=0, bytes_accessed=2 * keys.size, transcendentals=0
+        ),
+    )(token, where, placed_in(keys, pltpu.HBM), placed_in(values, pltpu.HBM))
+
+
+def fetch_pairs_kernel(first, token_ref, source, target, sems):
+    blocks, depth = target.shape[:2]
+    size = depth // 4
+    copies = []
+    for block in range(blocks):
+        for piece in range(4):
+            span = pl.ds(piece * size, size)
+            copies.append(
+                pltpu.make_async_copy(
+                    source.at[span, :, pl.ds((first + block) * 128, 128)],
+                    target.at[block, span],
+                    sems.at[block, piece],
+                )
+            )
+    run_copies(copies)
+
+
+def fetch_pairs(token, weights, first, blocks):
+    depth = weights.shape[0]
+    out = pl.pallas_call(
+        functools.partial(fetch_pairs_kernel, first),
+        out_shape=pltpu.VMEM((blocks, depth, 2, 128), weights.dtype),
+        in_specs=[hbm(), hbm()],
+        out_specs=vmem(),
+        scratch_shapes=[pltpu.SemaphoreType.DMA((blocks, 4))],
+        compiler_params=pltpu.CompilerParams(vmem_limit_bytes=1 << 20),
+        cost_estimate=pl.CostEstimate(
+            flops=0, bytes_accessed=4 * blocks * depth * 128, transcendentals=0
+        ),
+    )(token, placed_in(weights, pltpu.HBM))
+    return out.reshape(blocks, 2 * depth, 128)
 
 
 def inverse_rms(x_refs):
@@ -91,18 +199,24 @@
     kv_sum[...] = jnp.zeros_like(kv_sum)
     for first, x_ref in ((0, own_ref), (half, other_ref)):
 
-        @pl.loop(0, half)
-        def _(k):
-            span = span_of(ids_ref, first + k, chunk)
-            normed = normed_chunk(x_ref, gain_ref, scale, k, span)
-            q_sum[...] += jnp.dot(normed, wq_ref[span, :], preferred_element_type=jnp.float32)
-            for at, w_ref in ((0, wk_ref), (keys, wv_ref)):
-                kv_sum[:, at : at + keys] += lax.dot_general(
-                    normed,
-                    w_ref[:, span],
-                    (((1,), (1,)), ((), ())),
-                    preferred_element_type=jnp.float32,
-                )
+        @pl.loop(0, half // UNROLL)
+        def _(group):
+            q_part = 0.0
+            parts = [0.0, 0.0]
+            for step in range(UNROLL):
+                k = group * UNROLL + step
+                span = span_of(ids_ref, first + k, chunk)
+                normed = normed_chunk(x_ref, gain_ref, scale, k, span)
+                q_part += jnp.dot(normed, wq_ref[span, :], preferred_element_type=jnp.float32)
+                for which, w_ref in enumerate((wk_ref, wv_ref)):
+                    parts[which] += lax.dot_general(
+                        normed,
+                        w_ref[:, span],
+                        (((1,), (1,)), ((), ())),
+                        preferred_element_type=jnp.float32,
+                    )
+            q_sum[...] += q_part
+            kv_sum[...] += jnp.concatenate(parts, axis=1)
 
     for owner in range(count):
         lines = slice(owner * rows_dev, (owner + 1) * rows_dev)
@@ -129,11 +243,11 @@
             bytes_accessed=2 * wq.shape[0] * size,
             transcendentals=0,
         ),
-    )(ids, own, other, gain, resident(wq), resident(wk), resident(wv))
-
-
-def attend_kernel(where_ref, length_ref, q_ref, kv_ref, cos_ref, sin_ref, keys_ref,
-                  values_ref, out_ref, key_buf, value_buf, wide_q, sems):
+    )(ids, own, other, gain, *[placed_in(w, pltpu.VMEM) for w in (wq, wk, wv)])
+
+
+def attend_kernel(where_ref, length_ref, q_ref, kv_ref, cos_ref, sin_ref, key_buf,
+                  value_buf, out_ref, wide_q):
     rows, devices, queries = q_ref.shape
     _, _, groups, size = kv_ref.shape
     slots = queries // size
@@ -141,15 +255,6 @@
     places = key_buf.shape[1]
     batch = where_ref[0]
 
-    def copies(row):
-        return (
-            pltpu.make_async_copy(keys_ref.at[batch, row], key_buf.at[row], sems.at[0, row]),
-            pltpu.make_async_copy(values_ref.at[batch, row], value_buf.at[row], sems.at[1, row]),
-        )
-
-    for row in range(rows):
-        for which, copy in enumerate(copies(row)):
-            copy.start(priority=which)
     line = lax.broadcasted_iota(jnp.int32, (devices, 1), 0)
     group_of = line * groups // devices
     for row in range(rows):
@@ -178,8 +283,6 @@
                     slot * devices : (slot + 1) * devices, group * size : (group + 1) * size
                 ] = jnp.where(group_of == group, part, 0.0).astype(jnp.bfloat16)
         own_score = jnp.concatenate(own_parts, axis=0) * (size ** -0.5)
-        key_copy, value_copy = copies(row)
-        key_copy.wait()
         scores = lax.dot_general(
             wide_q[...], key_buf[row], (((1,), (1,)), ((), ())), preferred_element_type=jnp.float32
         ) * (size ** -0.5)
@@ -191,7 +294,6 @@
         denominator = jnp.sum(raised, axis=1, keepdims=True) + own_raised
         weights = (raised / denominator).astype(jnp.bfloat16)
         own_weight = (own_raised / denominator).astype(jnp.bfloat16).astype(jnp.float32)
-        value_copy.wait()
         mixed = jnp.dot(weights, value_buf[row], preferred_element_type=jnp.float32)
         for slot in range(slots):
             lines = slice(slot * devices, (slot + 1) * devices)
@@ -203,28 +305,32 @@
             out_ref[row, :, slot * size : (slot + 1) * size] = picked.astype(jnp.bfloat16)
 
 
-def attend(where, lengths, query, fresh, cosine, sine, key_store, value_store):
+def attend(where, lengths, query, fresh, cosine, sine, keys, values):
     rows, devices, queries = query.shape
-    places, width = key_store.shape[2:]
+    places, width = keys.shape[1:]
     heads = devices * queries // HEAD_SIZE
     return pl.pallas_call(
         attend_kernel,
         out_shape=pltpu.VMEM(query.shape, jnp.bfloat16),
-        in_specs=[smem(), smem()] + [vmem()] * 4 + [hbm(), hbm()],
+        in_specs=[smem(), smem()] + [vmem()] * 6,
         out_specs=vmem(),
-        scratch_shapes=[
-            pltpu.VMEM((rows, places, width), jnp.bfloat16),
-            pltpu.VMEM((rows, places, width), jnp.bfloat16),
-            pltpu.VMEM((heads, width), jnp.bfloat16),
-            pltpu.SemaphoreType.DMA((2, rows)),
-        ],
-        compiler_params=pltpu.CompilerParams(vmem_limit_bytes=8 << 20),
+        scratch_shapes=[pltpu.VMEM((heads, width), jnp.bfloat16)],
+        compiler_params=pltpu.CompilerParams(vmem_limit_bytes=4 << 20),
         cost_estimate=pl.CostEstimate(
             flops=4 * rows * heads * places * width,
             bytes_accessed=4 * rows * places * width,
             transcendentals=rows * heads * places,
         ),
-    )(where, lengths, query, fresh, cosine, sine, key_store, value_store)
+    )(
+        where,
+        lengths,
+        query,
+        fresh,
+        cosine,
+        sine,
+        placed_in(keys, pltpu.VMEM),
+        placed_in(values, pltpu.VMEM),
+    )
 
 
 def spread_kernel(ids_ref, x_ref, w_ref, keep_ref, send_ref, values):
@@ -235,12 +341,14 @@
     ready = values[...].astype(jnp.bfloat16)
     for first, target in ((0, keep_ref), (half, send_ref)):
 
-        @pl.loop(0, half)
-        def _(k):
-            span = span_of(ids_ref, first + k, chunk)
-            target[k] = jnp.dot(
-                ready, w_ref[:, span], preferred_element_type=jnp.float32
-            ).astype(jnp.bfloat16)
+        @pl.loop(0, half // UNROLL)
+        def _(group):
+            for step in range(UNROLL):
+                k = group * UNROLL + step
+                span = span_of(ids_ref, first + k, chunk)
+                target[k] = jnp.dot(
+                    ready, w_ref[:, span], preferred_element_type=jnp.float32
+                ).astype(jnp.bfloat16)
 
 
 def spread_project(ids, values, weights):
@@ -258,57 +366,58 @@
         cost_estimate=pl.CostEstimate(
             flops=2 * rows * depth * width, bytes_accessed=2 * depth * width, transcendentals=0
         ),
-    )(ids, values, resident(weights))
-
-
-def mlp_kernel(by_rows, ids_ref, own_ref, other_ref, gain_ref, gu_ref, down_ref, keep_ref,
-               send_ref, gu_buf, wide_x, total, act, gu_sems):
+    )(ids, values, placed_in(weights, pltpu.VMEM))
+
+
+def mlp_kernel(by_rows, ids_ref, own_ref, other_ref, gain_ref, low_ref, high_ref, down_ref,
+               keep_ref, send_ref, stacked, wide_x, total, act):
     half, rows, chunk = own_ref.shape
-    blocks = gu_buf.shape[1]
-
-    def gu_copies(k):
-        span = span_of(ids_ref, k, chunk)
-        return [
-            pltpu.make_async_copy(
-                gu_ref.at[span, :, pl.ds(j * 128, 128)], gu_buf.at[k, j], gu_sems.at[k, j]
-            )
-            for j in range(blocks)
-        ]
-
-    @pl.loop(0, 2 * half)
-    def _(k):
-        for j, copy in enumerate(gu_copies(k)):
-            copy.start(priority=j % 2)
+    blocks = [ref.at[j] for ref in (low_ref, high_ref) for j in range(ref.shape[0])]
+    per_chunk = chunk // 128
 
     scale = inverse_rms((own_ref, other_ref))
-    total[...] = jnp.zeros_like(total)
+    for first, x_ref in ((0, own_ref), (half, other_ref)):
+
+        @pl.loop(0, half)
+        def _(place):
+            k = first + place
+            normed = normed_chunk(x_ref, gain_ref, scale, place, span_of(ids_ref, k, chunk))
+            for b in range(per_chunk):
+                stacked[k * per_chunk + b] = normed[:, b * 128 : (b + 1) * 128]
+
     line = lax.broadcasted_iota(jnp.int32, (128, 512), 0)
     column = lax.broadcasted_iota(jnp.int32, (128, 512), 1)
     aim = jnp.where(column < 256, 2 * line, 2 * line + 257)
     widen = jnp.where(column == aim, 1.0, 0.0).astype(jnp.bfloat16)
 
-    for first, x_ref in ((0, own_ref), (half, other_ref)):
-
-        @pl.loop(0, half)
-        def _(place):
-            k = first + place
-            span = span_of(ids_ref, k, chunk)
-            normed = normed_chunk(x_ref, gain_ref, scale, place, span)
-            for b in range(chunk // 128):
-                wide = jnp.dot(
-                    normed[:, b * 128 : (b + 1) * 128], widen, preferred_element_type=jnp.float32
-                ).astype(jnp.bfloat16)
-                wide_x[:rows, b * 256 : (b + 1) * 256] = wide[:, :256]
-                wide_x[rows:, b * 256 : (b + 1) * 256] = wide[:, 256:]
-            for copy in gu_copies(k):
-                copy.wait()
-            for j in range(0, blocks, 2):
-                pair = jnp.concatenate(
-                    [gu_buf.at[k, j + i].reshape(2 * chunk, 128)[...] for i in range(2)], axis=1
+    @pl.loop(0, 2 * half * per_chunk // 8)
+    def _(group):
+        span = pl.ds(group * 8, 8)
+        wide = jnp.dot(
+            stacked[span].reshape(8 * rows, 128), widen, preferred_element_type=jnp.float32
+        ).astype(jnp.bfloat16)
+        for b in range(8):
+            lines = slice(b * rows, (b + 1) * rows)
+            wide_x[group, :rows, b * 256 : (b + 1) * 256] = wide[lines, :256]
+            wide_x[group, rows:, b * 256 : (b + 1) * 256] = wide[lines, 256:]
+
+    total[...] = jnp.zeros_like(total)
+    per_group = 8 // per_chunk
+
+    @pl.loop(0, wide_x.shape[0])
+    def _(group):
+        for j in range(0, len(blocks), 2):
+            part = 0.0
+            for step in range(per_group):
+                at = ids_ref[group * per_group + step] * (2 * chunk)
+                span = pl.ds(pl.multiple_of(at, 2 * chunk), 2 * chunk)
+                pair = jnp.concatenate([blocks[j][span, :], blocks[j + 1][span, :]], axis=1)
+                part += jnp.dot(
+                    wide_x[group, :, step * 2 * chunk : (step + 1) * 2 * chunk],
+                    pair,
+                    preferred_element_type=jnp.float32,
                 )
-                total[:, j * 128 : (j + 2) * 128] += jnp.dot(
-                    wide_x[...], pair, preferred_element_type=jnp.float32
-                )
+            total[:, j * 128 : (j + 2) * 128] += part
 
     gate = total[:rows, :]
     act[...] = (gate / (1.0 + jnp.exp(-gate)) * total[rows:, :]).astype(jnp.bfloat16)
@@ -320,26 +429,29 @@
         rows_dev = keep_ref.shape[1]
         first_core = ids_ref[0] == 0
 
-        @pl.loop(0, 2 * half)
-        def _(k):
-            span = span_of(ids_ref, k, chunk)
-            part = down(span)
-            for chip in range(half):
-                at = 2 * chip * rows_dev
-                low = part[at : at + rows_dev]
-                high = part[at + rows_dev : at + 2 * rows_dev]
-                keep_ref[chip, :, span] = jnp.where(first_core, low, high).astype(jnp.bfloat16)
-                send_ref[chip, :, span] = jnp.where(first_core, high, low).astype(jnp.bfloat16)
+        @pl.loop(0, 2 * half // 2)
+        def _(group):
+            for step in range(2):
+                span = span_of(ids_ref, group * 2 + step, chunk)
+                part = down(span)
+                for chip in range(half):
+                    at = 2 * chip * rows_dev
+                    low = part[at : at + rows_dev]
+                    high = part[at + rows_dev : at + 2 * rows_dev]
+                    keep_ref[chip, :, span] = jnp.where(first_core, low, high).astype(jnp.bfloat16)
+                    send_ref[chip, :, span] = jnp.where(first_core, high, low).astype(jnp.bfloat16)
 
     else:
         for first, target in ((0, keep_ref), (half, send_ref)):
 
-            @pl.loop(0, half)
-            def _(k):
-                target[k] = down(span_of(ids_ref, first + k, chunk)).astype(jnp.bfloat16)
-
-
-def mlp(ids, own, other, gain, gate_up, down, by_rows):
+            @pl.loop(0, half // UNROLL)
+            def _(group):
+                for step in range(UNROLL):
+                    k = group * UNROLL + step
+                    target[k] = down(span_of(ids_ref, first + k, chunk)).astype(jnp.bfloat16)
+
+
+def mlp(ids, own, other, gain, low, high, down, by_rows):
     half, rows, chunk = own.shape
     units, width = down.shape
     part = (half, rows // (2 * half), width) if by_rows else own.shape
@@ -347,20 +459,19 @@
     return pl.pallas_call(
         functools.partial(mlp_kernel, by_rows),
         out_shape=(shape, shape),
-        in_specs=[smem(), vmem(), vmem(), vmem(), hbm(), vmem()],
+        in_specs=[smem()] + [vmem()] * 6,
         out_specs=(vmem(), vmem()),
         scratch_shapes=[
-            pltpu.VMEM((2 * half, units // 128, chunk, 2, 128), jnp.bfloat16),
-            pltpu.VMEM((2 * rows, 2 * chunk), jnp.bfloat16),
+            pltpu.VMEM((width // 128, rows, 128), jnp.bfloat16),
+            pltpu.VMEM((width // 1024, 2 * rows, 2048), jnp.bfloat16),
             pltpu.VMEM((2 * rows, units), jnp.float32),
             pltpu.VMEM((rows, units), jnp.bfloat16),
-            pltpu.SemaphoreType.DMA((2 * half, units // 128)),
         ],
-        compiler_params=pltpu.CompilerParams(vmem_limit_bytes=37 << 20),
+        compiler_params=pltpu.CompilerParams(vmem_limit_bytes=(3 << 20) + 10 * rows * width),
         cost_estimate=pl.CostEstimate(
             flops=6 * rows * units * width, bytes_accessed=6 * units * width, transcendentals=0
         ),
-    )(ids, own, other, gain, gate_up, resident(down))
+    )(ids, own, other, gain, *[placed_in(w, pltpu.VMEM) for w in (low, high, down)])
 
 
 def turning(positions):
@@ -405,15 +516,18 @@
         pair = jnp.where(core == 0, jnp.stack([own, other], 1), jnp.stack([other, own], 1))
         return pair.reshape((count,) + own.shape[1:])
 
+    blocks = w_gate_up.shape[3] // 128
+    qkv = fetch(hidden, w_query[0], wk, wv)
     start = by_core(*gather(hidden[0])).reshape(rows, width)
     chunks = columns_to_chunks(start, count)
     mine = lax.dynamic_index_in_dim(chunks, model_index, 0, keepdims=False)
     own, other = chunks[:half], chunks[half:]
     order = jnp.arange(count, dtype=jnp.int32)
     for turn_index in range(2):
-        batch = jnp.remainder(section_index + turn_index, 2).astype(jnp.int32)
-        cosine, sine = turning(lax.dynamic_index_in_dim(lengths, batch, 0, keepdims=False))
-        joined = project(order, own, other, attn_gain, w_query[0], wk, wv)
+        batch = jnp.remainder(section_index + turn_index, 2).astype(jnp.int32).reshape(1)
+        cosine, sine = turning(lax.dynamic_index_in_dim(lengths, batch[0], 0, keepdims=False))
+        joined = project(order, own, other, attn_gain, *qkv)
+        keys, values = fetch_caches(joined, batch, key_cache[0], value_cache[0])
         spread = lax.all_to_all(joined, "mp", split_axis=0, concat_axis=0)
         query = spread[..., :query_cols].transpose(1, 0, 2)
         fresh = (
@@ -422,16 +536,19 @@
             .transpose(1, 2, 0, 3)
             .reshape(rows_dev, 2, KEY_VALUE_HEADS, HEAD_SIZE)
         )
-        mixed = attend(
-            batch.reshape(1), lengths, query, fresh, cosine, sine, key_cache[0], value_cache[0]
-        )
+        mixed = attend(batch, lengths, query, fresh, cosine, sine, keys, values)
+        (out_proj,) = fetch(mixed, w_out[0])
         heads_out = lax.all_to_all(mixed.transpose(1, 0, 2), "mp", split_axis=0, concat_axis=0)
-        keep, send = spread_project(ids, heads_out, w_out[0])
-        middle = (mine.astype(jnp.float32) + scatter(send, keep)).astype(jnp.bfloat16)
+        keep, send = spread_project(ids, heads_out, out_proj)
+        held = merge(send, keep)
+        low = fetch_pairs(held, w_gate_up[0], 0, blocks // 2)
+        middle = (mine.astype(jnp.float32) + scatter(held)).astype(jnp.bfloat16)
+        high = fetch_pairs(middle, w_gate_up[0], blocks // 2, blocks // 2)
+        (down,) = fetch(middle, w_down[0])
         own, other = gather(middle)
         last = turn_index == 1
-        keep, send = mlp(ids, own, other, mlp_gain, w_gate_up[0], w_down[0], last)
-        mlp_part = scatter(send, keep)
+        keep, send = mlp(ids, own, other, mlp_gain, low, high, down, last)
+        mlp_part = scatter(merge(send, keep))
         if last:
             at = model_index * rows_dev
             mine = by_core(
@@ -442,6 +559,7 @@
         mine = (middle.astype(jnp.float32) + mlp_part).astype(jnp.bfloat16)
         if not last:
             mine = swap(mine, 1, "section")
+            qkv = fetch(mine, w_query[0], wk, wv)
             own, other = gather(mine)
             order = ids
     return mine[None]

time: 302 us -> 301 us (level)
  waiting for transfers between devices: 59.8 us -> 32.2 us
  local copies, waits for them, and re-layouts: 42.8 us -> 57 us
  Pallas kernels: 95.5 us -> 106 us
  starting transfers between devices: 26.9 us -> 36 us
  blocking collectives: 70.2 us -> 63.3 us
    pallas_call x0 -> x12, Pallas kernels: none -> 56.2 us  [the longest x6 27.5 us: fetch(): pl.pallas_call(functools.partial(fetch_kernel, pieces), out_shape=[pltpu....]
    pallas_call x2, Pallas kernels: 66.2 us -> 29.6 us  [mlp(): pl.pallas_call(functools.partial(mlp_kernel, by_rows), out_shape=(shape,...]
    unnamed x42 -> x48, local copies, waits for them, and re-layouts: 38.4 us -> 51.1 us
    all_to_all x1 -> x0, blocking collectives: 9.2 us -> none  [body(): lax.all_to_all(mixed.transpose(1, 0, 2), 'mp', split_axis=0, concat_axis=0)]
    all_to_all x3, waiting for transfers between devices: 25.8 us -> 17.5 us  [exchange(): lax.all_to_all(parts, 'mp', split_axis=0, concat_axis=0, axis_index_group...]
    all_to_all x2, waiting for transfers between devices: 13.3 us -> 6.16 us  [body(): spread = lax.all_to_all(joined, 'mp', split_axis=0, concat_axis=0)]
    all_to_all x1 -> x2, waiting for transfers between devices: 6.52 us -> 0.01 us  [body(): lax.all_to_all(mixed.transpose(1, 0, 2), 'mp', split_axis=0, concat_axis=0)]
    ppermute x9, waiting for transfers between devices: 14.2 us -> 8.59 us  [swap(): lax.ppermute(value, axis, [(source, source ^ mask) for source in range(co...]
  transfers between devices with their start and end apart: 15 -> 16, of which waited for: 15 -> 11; matrix products, arithmetic and copies ran while one was open for 1% -> 1% of each run, Pallas kernels for 0% -> 19%
where the time goes in v3:
time: 301 us; the launch traced here: 299 us
  Pallas kernels  106 us (35%)
  blocking collectives  63.3 us (21%)
  local copies, waits for them, and re-layouts  57 us (19%)
  starting transfers between devices  36 us (12%)
  waiting for transfers between devices  32.2 us (11%)
  other arithmetic  4.13 us (1%)
    all_to_all x5, blocking collectives, exchange(): lax.all_to_all(parts, 'mp', split_axis=0, concat_axis=0, axis_index_group...  63.3 us
    unnamed x48, local copies, waits for them, and re-layouts  51.1 us
    pallas_call x2, Pallas kernels, mlp(): pl.pallas_call(functools.partial(mlp_kernel, by_rows), out_shape=(shape,...  29.6 us
    pallas_call x6, Pallas kernels, fetch(): pl.pallas_call(functools.partial(fetch_kernel, pieces), out_shape=[pltpu....  27.5 us
    pallas_call x4, Pallas kernels, fetch_pairs(): pl.pallas_call(functools.partial(fetch_pairs_kernel, first), out_shape=pl...  24.2 us
    all_to_all x3, waiting for transfers between devices, exchange(): lax.all_to_all(parts, 'mp', split_axis=0, concat_axis=0, axis_index_group...  17.5 us
    all_to_all x3, starting transfers between devices, exchange(): lax.all_to_all(parts, 'mp', split_axis=0, concat_axis=0, axis_index_group...  16.7 us
    pallas_call x2, Pallas kernels, project(): pl.pallas_call(project_kernel, out_shape=pltpu.VMEM((2 * half, rows // (2...  10.7 us
  transfers between devices with their start and end apart: 16, of which 11 were waited for; matrix products, arithmetic and copies ran while one was open for 1% of the time, Pallas kernels for 19%

profile of v3, /device:TPU:0, one launch (start us, length us, event | category | flops | bytes accessed | tf_op | source)
XLA Modules:
  0.0 299.3 jit_solution(9404785584134770486)
XLA Ops:
  1.6 7.3 %all-to-all-start = ((bf16[8,2,8192]{2,1,0:T(2,128)(2,1)}), bf16[8,2,8192]{2,1,0:T(2,128)(2,1)S(1)}, u32[]{:S(2)}, u32[]{:S(2)}) async-start(bf16[8,2,8192]{2,1,0:T(2,128)(2,1)} %broadcast_in_dim.11), calls=%async_computation | async-start | bytes 524288 | tf_op jit(solution)/shard_map/all_to_all | solution.py:27
  9.7 4.3 %shard_map.118 = (bf16[8192,512]{1,0:T(8,128)(2,1)S(1)}, bf16[64,8192]{1,0:T(8,128)(2,1)S(1)}, bf16[64,8192]{1,0:T(8,128)(2,1)S(1)}) custom-call(bf16[1,2,8192]{2,1,0:T(2,128)(2,1)S(1)} %copy-done.15, bf16[8192,512]{1,0:T(8,128)(2,1)} %bitcast.79, bf16[64,8192]{1,0:T(8,128)(2,1)} %bitcast.87, bf16[64,8192]{1,0:T(8,128)(2,1)} %bitcast.89), custom_call_target="tpu_custom_call" | custom-call | bytes 10485760 | tf_op jit(solution)/shard_map/pallas_call | solution.py:90
  24.3 5.4 %shard_map.119.token_ref = bf16[16,2,640]{2,1,0:T(2,128)(2,1)} custom-call(s32[16]{0:T(128)S(1)} %iota.17.ids_ref, bf16[8,32,512]{2,1,0:T(8,128)(2,1)S(1)} %get-tuple-element.44.own_ref, bf16[8,32,512]{2,1,0:T(8,128)(2,1)S(1)} %get-tuple-element.43.other_ref, f32[1,8192]{1,0:T(1,128)S(1)} %copy-done.14, bf16[8192,512]{1,0:T(8,128)(2,1)S(1)} %copy-done.9, ...), custom_call_target="tpu_custom_call" | custom-call | flops 335544320 | bytes 10485760 | tf_op jit(solution)/shard_map/pallas_call | solution.py:231
  29.6 5.6 %all-to-all-start.1 = ((bf16[16,2,640]{2,1,0:T(2,128)(2,1)}), bf16[16,2,640]{2,1,0:T(2,128)(2,1)S(1)}, u32[]{:S(2)}, u32[]{:S(2)}) async-start(bf16[16,2,640]{2,1,0:T(2,128)(2,1)} %shard_map.119.token_ref), calls=%async_computation.1 | async-start | bytes 81920 | tf_op jit(solution)/shard_map/all_to_all | solution.py:531
  46.9 3.5 %all-to-all-start.2 = ((bf16[16,2,512]{2,1,0:T(2,128)(2,1)}), bf16[16,2,512]{2,1,0:T(2,128)(2,1)S(1)}, u32[]{:S(2)}, u32[]{:S(2)}) async-start(bf16[16,2,512]{2,1,0:T(2,128)(2,1)} %bitcast.63), calls=%async_computation.2 | async-start | bytes 65536 | tf_op jit(solution)/shard_map/all_to_all | solution.py:541
  50.5 3.5 %shard_map.122.w_ref = bf16[512,8192]{1,0:T(8,128)(2,1)S(1)} custom-call(bf16[2,16,512]{2,1,0:T(8,128)(2,1)S(1)} %shard_map.121.token_ref, bf16[512,8192]{1,0:T(8,128)(2,1)} %bitcast.81), custom_call_target="tpu_custom_call" | custom-call | bytes 8388608 | tf_op jit(solution)/shard_map/pallas_call | solution.py:90
  65.4 5.9 %all-to-all-start.3 = ((bf16[8,32,512]{2,1,0:T(8,128)(2,1)}), bf16[8,32,512]{2,1,0:T(8,128)(2,1)S(1)}, u32[]{:S(2)}, u32[]{:S(2)}) async-start(bf16[8,32,512]{2,1,0:T(8,128)(2,1)} %add_convert_fusion.3.token_ref), calls=%async_computation.3 | async-start | bytes 524288 | tf_op jit(solution)/shard_map/all_to_all | solution.py:27
  71.3 9.2 %all-to-all-done.3 = bf16[8,32,512]{2,1,0:T(8,128)(2,1)S(1)} async-done(((bf16[8,32,512]{2,1,0:T(8,128)(2,1)}), bf16[8,32,512]{2,1,0:T(8,128)(2,1)S(1)}, u32[]{:S(2)}, u32[]{:S(2)}) %all-to-all-start.3) | async-done | bytes 262176 | tf_op jit(solution)/shard_map/all_to_all | solution.py:27
  80.6 12.0 %all_to_all.60.own_ref = bf16[8,32,512]{2,1,0:T(8,128)(2,1)S(1)} all-to-all(bf16[8,32,512]{2,1,0:T(8,128)(2,1)S(1)} %broadcast_in_dim.12), channel_id=1, replica_groups={{0,2,4,6,8,10,12,14},{1,3,5,7,9,11,13,15},{16,18,20,22,24,26,28,30},{17..., dimensions={0} | all-to-all | bytes 524288 | tf_op jit(solution)/shard_map/all_to_all | solution.py:27
  92.6 6.1 %shard_map.124 = bf16[4,8192,2,128]{3,2,1,0:T(2,128)(2,1)S(1)} custom-call(bf16[8,32,512]{2,1,0:T(8,128)(2,1)} %add_convert_fusion.3.token_ref, bf16[8192,2,1024]{2,1,0:T(2,128)(2,1)} %bitcast.73), custom_call_target="tpu_custom_call" | custom-call | bytes 16777216 | tf_op jit(solution)/shard_map/pallas_call | solution.py:155
  98.7 5.7 %copy-done = bf16[4,8192,2,128]{3,2,1,0:T(2,128)(2,1)} copy-done((bf16[4,8192,2,128]{3,2,1,0:T(2,128)(2,1)}, bf16[4,8192,2,128]{3,2,1,0:T(2,128)(2,1)S(1)}, u32[]{:S(2)}) %copy-start) | copy-done | bytes 16777240
  104.5 6.0 %shard_map.125 = bf16[4,8192,2,128]{3,2,1,0:T(2,128)(2,1)S(1)} custom-call(bf16[32,512]{1,0:T(8,128)(2,1)S(1)} %fusion.token_ref, bf16[8192,2,1024]{2,1,0:T(2,128)(2,1)} %bitcast.74), custom_call_target="tpu_custom_call" | custom-call | bytes 16777216 | tf_op jit(solution)/shard_map/pallas_call | solution.py:155
  110.5 6.0 %shard_map.126.down_ref = bf16[1024,8192]{1,0:T(8,128)(2,1)S(1)} custom-call(bf16[32,512]{1,0:T(8,128)(2,1)S(1)} %fusion.token_ref, bf16[1024,8192]{1,0:T(8,128)(2,1)} %bitcast.77), custom_call_target="tpu_custom_call" | custom-call | bytes 16777216 | tf_op jit(solution)/shard_map/pallas_call | solution.py:90
  117.2 5.8 %copy-done.1 = bf16[4,8192,2,128]{3,2,1,0:T(2,128)(2,1)S(1)} copy-done((bf16[4,8192,2,128]{3,2,1,0:T(2,128)(2,1)S(1)}, bf16[4,8192,2,128]{3,2,1,0:T(2,128)(2,1)}, u32[]{:S(2)}) %copy-start.1) | copy-done | bytes 16777240
  123.0 14.5 %shard_map.127 = (bf16[8,32,512]{2,1,0:T(8,128)(2,1)S(1)}, bf16[8,32,512]{2,1,0:T(8,128)(2,1)S(1)}) custom-call(s32[16]{0:T(128)} %copy-done.16, bf16[8,32,512]{2,1,0:T(8,128)(2,1)} %copy-done.20, bf16[8,32,512]{2,1,0:T(8,128)(2,1)} %copy-done.22, f32[1,8192]{1,0:T(1,128)} %gain_ref.7, bf16[4,16384,128]{2,1,0:T(8,128)(2,1)S(1)} %bitcast.66, ...), custom_call_target="tpu_custom_call" | custom-call | flops 1610612736 | bytes 50331648 | tf_op jit(solution)/shard_map/pallas_call | solution.py:459
  139.2 12.8 %all_to_all.61 = bf16[8,32,512]{2,1,0:T(8,128)(2,1)S(1)} all-to-all(bf16[8,32,512]{2,1,0:T(8,128)(2,1)S(1)} %add_convert_fusion.2), channel_id=1, replica_groups={{0,2,4,6,8,10,12,14},{1,3,5,7,9,11,13,15},{16,18,20,22,24,26,28,30},{17..., dimensions={0} | all-to-all | bytes 524288 | tf_op jit(solution)/shard_map/all_to_all | solution.py:27
  156.1 11.6 %all_to_all.62.own_ref = bf16[8,32,512]{2,1,0:T(8,128)(2,1)S(1)} all-to-all(bf16[8,32,512]{2,1,0:T(8,128)(2,1)S(1)} %broadcast_in_dim.13), channel_id=1, replica_groups={{0,2,4,6,8,10,12,14},{1,3,5,7,9,11,13,15},{16,18,20,22,24,26,28,30},{17..., dimensions={0} | all-to-all | bytes 524288 | tf_op jit(solution)/shard_map/all_to_all | solution.py:27
  167.7 4.3 %shard_map.128 = (bf16[8192,512]{1,0:T(8,128)(2,1)S(1)}, bf16[64,8192]{1,0:T(8,128)(2,1)S(1)}, bf16[64,8192]{1,0:T(8,128)(2,1)S(1)}) custom-call(bf16[32,512]{1,0:T(8,128)(2,1)S(1)} %collective-permute-done.4.token_ref, bf16[8192,512]{1,0:T(8,128)(2,1)} %bitcast.80, bf16[64,8192]{1,0:T(8,128)(2,1)} %bitcast.88, bf16[64,8192]{1,0:T(8,128)(2,1)} %bitcast.90), custom_call_target="tpu_custom_call" | custom-call | bytes 10485760 | tf_op jit(solution)/shard_map/pallas_call | solution.py:90
  172.0 5.4 %shard_map.129.token_ref = bf16[16,2,640]{2,1,0:T(2,128)(2,1)} custom-call(s32[16]{0:T(128)S(1)} %copy-done.17, bf16[8,32,512]{2,1,0:T(8,128)(2,1)S(1)} %all_to_all.62.own_ref, bf16[8,32,512]{2,1,0:T(8,128)(2,1)S(1)} %collective-permute-done.5.other_ref, f32[1,8192]{1,0:T(1,128)S(1)} %copy-done.14, bf16[8192,512]{1,0:T(8,128)(2,1)S(1)} %get-tuple-element.32.wq_ref, ...), custom_call_target="tpu_custom_call" | custom-call | flops 335544320 | bytes 10485760 | tf_op jit(solution)/shard_map/pallas_call | solution.py:231
  177.4 3.5 %all-to-all-start.7 = ((bf16[16,2,640]{2,1,0:T(2,128)(2,1)}), bf16[16,2,640]{2,1,0:T(2,128)(2,1)S(1)}, u32[]{:S(2)}, u32[]{:S(2)}) async-start(bf16[16,2,640]{2,1,0:T(2,128)(2,1)} %shard_map.129.token_ref), calls=%async_computation.7 | async-start | bytes 81920 | tf_op jit(solution)/shard_map/all_to_all | solution.py:531
  192.6 3.5 %all-to-all-start.8 = ((bf16[16,2,512]{2,1,0:T(2,128)(2,1)}), bf16[16,2,512]{2,1,0:T(2,128)(2,1)S(1)}, u32[]{:S(2)}, u32[]{:S(2)}) async-start(bf16[16,2,512]{2,1,0:T(2,128)(2,1)} %bitcast.62), calls=%async_computation.8 | async-start | bytes 65536 | tf_op jit(solution)/shard_map/all_to_all | solution.py:541
  196.1 3.5 %shard_map.132.w_ref = bf16[512,8192]{1,0:T(8,128)(2,1)S(1)} custom-call(bf16[2,16,512]{2,1,0:T(8,128)(2,1)S(1)} %shard_map.131.token_ref, bf16[512,8192]{1,0:T(8,128)(2,1)} %bitcast.82), custom_call_target="tpu_custom_call" | custom-call | bytes 8388608 | tf_op jit(solution)/shard_map/pallas_call | solution.py:90
  210.3 14.9 %all_to_all.63 = bf16[8,32,512]{2,1,0:T(8,128)(2,1)S(1)} all-to-all(bf16[8,32,512]{2,1,0:T(8,128)(2,1)S(1)} %add_convert_fusion.1.token_ref), channel_id=1, replica_groups={{0,2,4,6,8,10,12,14},{1,3,5,7,9,11,13,15},{16,18,20,22,24,26,28,30},{17..., dimensions={0} | all-to-all | bytes 524288 | tf_op jit(solution)/shard_map/all_to_all | solution.py:27
  225.3 12.0 %all_to_all.64.own_ref = bf16[8,32,512]{2,1,0:T(8,128)(2,1)S(1)} all-to-all(bf16[8,32,512]{2,1,0:T(8,128)(2,1)S(1)} %broadcast_in_dim.14), channel_id=1, replica_groups={{0,2,4,6,8,10,12,14},{1,3,5,7,9,11,13,15},{16,18,20,22,24,26,28,30},{17..., dimensions={0} | all-to-all | bytes 524288 | tf_op jit(solution)/shard_map/all_to_all | solution.py:27
  237.3 6.1 %shard_map.134 = bf16[4,8192,2,128]{3,2,1,0:T(2,128)(2,1)S(1)} custom-call(bf16[8,32,512]{2,1,0:T(8,128)(2,1)S(1)} %add_convert_fusion.1.token_ref, bf16[8192,2,1024]{2,1,0:T(2,128)(2,1)} %bitcast.75), custom_call_target="tpu_custom_call" | custom-call | bytes 16777216 | tf_op jit(solution)/shard_map/pallas_call | solution.py:155
  243.4 5.7 %copy-done.2 = bf16[4,8192,2,128]{3,2,1,0:T(2,128)(2,1)} copy-done((bf16[4,8192,2,128]{3,2,1,0:T(2,128)(2,1)}, bf16[4,8192,2,128]{3,2,1,0:T(2,128)(2,1)S(1)}, u32[]{:S(2)}) %copy-start.2) | copy-done | bytes 16777240
  249.1 6.0 %shard_map.135 = bf16[4,8192,2,128]{3,2,1,0:T(2,128)(2,1)S(1)} custom-call(bf16[32,512]{1,0:T(8,128)(2,1)S(1)} %add_convert_fusion.4.token_ref, bf16[8192,2,1024]{2,1,0:T(2,128)(2,1)} %bitcast.76), custom_call_target="tpu_custom_call" | custom-call | bytes 16777216 | tf_op jit(solution)/shard_map/pallas_call | solution.py:155
  255.1 6.0 %shard_map.136.down_ref = bf16[1024,8192]{1,0:T(8,128)(2,1)S(1)} custom-call(bf16[32,512]{1,0:T(8,128)(2,1)S(1)} %add_convert_fusion.4.token_ref, bf16[1024,8192]{1,0:T(8,128)(2,1)} %bitcast.78), custom_call_target="tpu_custom_call" | custom-call | bytes 16777216 | tf_op jit(solution)/shard_map/pallas_call | solution.py:90
  261.9 5.8 %copy-done.3 = bf16[4,8192,2,128]{3,2,1,0:T(2,128)(2,1)S(1)} copy-done((bf16[4,8192,2,128]{3,2,1,0:T(2,128)(2,1)S(1)}, bf16[4,8192,2,128]{3,2,1,0:T(2,128)(2,1)}, u32[]{:S(2)}) %copy-start.3) | copy-done | bytes 16777240
  267.6 15.1 %shard_map.137 = (bf16[8,2,8192]{2,1,0:T(2,128)(2,1)S(1)}, bf16[8,2,8192]{2,1,0:T(2,128)(2,1)S(1)}) custom-call(s32[16]{0:T(128)} %copy-done.16, bf16[8,32,512]{2,1,0:T(8,128)(2,1)} %copy-done.19, bf16[8,32,512]{2,1,0:T(8,128)(2,1)} %copy-done.21, f32[1,8192]{1,0:T(1,128)} %gain_ref.7, bf16[4,16384,128]{2,1,0:T(8,128)(2,1)S(1)} %bitcast.67, ...), custom_call_target="tpu_custom_call" | custom-call | flops 1610612736 | bytes 50331648 | tf_op jit(solution)/shard_map/pallas_call | solution.py:459
  285.4 3.6 %all-to-all-start.11 = ((bf16[8,2,8192]{2,1,0:T(2,128)(2,1)}), bf16[8,2,8192]{2,1,0:T(2,128)(2,1)S(1)}, u32[]{:S(2)}, u32[]{:S(2)}) async-start(bf16[8,2,8192]{2,1,0:T(2,128)(2,1)} %add_convert_fusion), calls=%async_computation.11 | async-start | bytes 524288 | tf_op jit(solution)/shard_map/all_to_all | solution.py:27
  290.8 7.7 %all-to-all-done.11 = bf16[8,2,8192]{2,1,0:T(2,128)(2,1)S(1)} async-done(((bf16[8,2,8192]{2,1,0:T(2,128)(2,1)}), bf16[8,2,8192]{2,1,0:T(2,128)(2,1)S(1)}, u32[]{:S(2)}, u32[]{:S(2)}) %all-to-all-start.11) | async-done | bytes 262176 | tf_op jit(solution)/shard_map/all_to_all | solution.py:27
  (117 shorter events, 70.7 us)
Async XLA Ops:
  0.0 17.3 %copy-start.18 = (s32[2,2]{1,0:T(2,128)S(1)}, s32[2,2]{1,0:T(2,128)}, u32[]{:S(2)}) copy-start(s32[2,2]{1,0:T(2,128)} %length_ref.3) | copy-start | bytes 52
  0.0 20.9 %copy-start.14 = (f32[1,8192]{1,0:T(1,128)S(1)}, f32[1,8192]{1,0:T(1,128)}, u32[]{:S(2)}) copy-start(f32[1,8192]{1,0:T(1,128)} %gain_ref.6) | copy-start | bytes 98308
  1.6 16.2 %all-to-all-start = ((bf16[8,2,8192]{2,1,0:T(2,128)(2,1)}), bf16[8,2,8192]{2,1,0:T(2,128)(2,1)S(1)}, u32[]{:S(2)}, u32[]{:S(2)}) async-start(bf16[8,2,8192]{2,1,0:T(2,128)(2,1)} %broadcast_in_dim.11), calls=%async_computation | async-start | bytes 524288 | tf_op jit(solution)/shard_map/all_to_all | solution.py:27
  14.0 3.3 %copy-start.8 = (bf16[8192,512]{1,0:T(8,128)(2,1)}, bf16[8192,512]{1,0:T(8,128)(2,1)S(1)}, u32[]{:S(2)}) copy-start(bf16[8192,512]{1,0:T(8,128)(2,1)S(1)} %get-tuple-element.23.wq_ref) | copy-start | bytes 25165828
  17.8 1.5 collective-permute-start
  20.9 3.4 %copy-start.9 = (bf16[8192,512]{1,0:T(8,128)(2,1)S(1)}, bf16[8192,512]{1,0:T(8,128)(2,1)}, u32[]{:S(2)}) copy-start(bf16[8192,512]{1,0:T(8,128)(2,1)} %copy-done.8) | copy-start | bytes 25165828
  29.6 12.3 %all-to-all-start.1 = ((bf16[16,2,640]{2,1,0:T(2,128)(2,1)}), bf16[16,2,640]{2,1,0:T(2,128)(2,1)S(1)}, u32[]{:S(2)}, u32[]{:S(2)}) async-start(bf16[16,2,640]{2,1,0:T(2,128)(2,1)} %shard_map.119.token_ref), calls=%async_computation.1 | async-start | bytes 81920 | tf_op jit(solution)/shard_map/all_to_all | solution.py:531
  46.9 10.4 %all-to-all-start.2 = ((bf16[16,2,512]{2,1,0:T(2,128)(2,1)}), bf16[16,2,512]{2,1,0:T(2,128)(2,1)S(1)}, u32[]{:S(2)}, u32[]{:S(2)}) async-start(bf16[16,2,512]{2,1,0:T(2,128)(2,1)} %bitcast.63), calls=%async_computation.2 | async-start | bytes 65536 | tf_op jit(solution)/shard_map/all_to_all | solution.py:541
  50.5 6.8 %copy-start.16 = (s32[16]{0:T(128)}, s32[16]{0:T(128)S(1)}, u32[]{:S(2)}) copy-start(s32[16]{0:T(128)S(1)} %pad_add_fusion.ids_ref) | copy-start | bytes 196
  54.0 3.3 %copy-start.4 = (bf16[512,8192]{1,0:T(8,128)(2,1)}, bf16[512,8192]{1,0:T(8,128)(2,1)S(1)}, u32[]{:S(2)}) copy-start(bf16[512,8192]{1,0:T(8,128)(2,1)S(1)} %shard_map.122.w_ref) | copy-start | bytes 25165828
  57.3 3.4 %copy-start.5 = (bf16[512,8192]{1,0:T(8,128)(2,1)S(1)}, bf16[512,8192]{1,0:T(8,128)(2,1)}, u32[]{:S(2)}) copy-start(bf16[512,8192]{1,0:T(8,128)(2,1)} %copy-done.4) | copy-start | bytes 25165828
  63.1 1.6 collective-permute-start.1
  65.4 15.1 %all-to-all-start.3 = ((bf16[8,32,512]{2,1,0:T(8,128)(2,1)}), bf16[8,32,512]{2,1,0:T(8,128)(2,1)S(1)}, u32[]{:S(2)}, u32[]{:S(2)}) async-start(bf16[8,32,512]{2,1,0:T(8,128)(2,1)} %add_convert_fusion.3.token_ref), calls=%async_computation.3 | async-start | bytes 524288 | tf_op jit(solution)/shard_map/all_to_all | solution.py:27
  92.6 6.1 %copy-start.20 = (bf16[8,32,512]{2,1,0:T(8,128)(2,1)}, bf16[8,32,512]{2,1,0:T(8,128)(2,1)S(1)}, u32[]{:S(2)}) copy-start(bf16[8,32,512]{2,1,0:T(8,128)(2,1)S(1)} %all_to_all.60.own_ref) | copy-start | bytes 786436
  92.6 23.9 %collective-permute-start.2 = (bf16[8,32,512]{2,1,0:T(8,128)(2,1)S(1)}, bf16[8,32,512]{2,1,0:T(8,128)(2,1)S(1)}, u32[]{:S(2)}, u32[]{:S(2)}) collective-permute-start(bf16[8,32,512]{2,1,0:T(8,128)(2,1)S(1)} %all_to_all.60.own_ref), channel_id=1, source_target_pairs={{0,1},{1,0},{2,3},{3,2},{4,5},{5,4},{6,7},{7,6},{8,9},{9,8},{10,11... | collective-permute-start | bytes 786440 | tf_op jit(solution)/shard_map/ppermute | solution.py:21
  98.7 5.8 %copy-start = (bf16[4,8192,2,128]{3,2,1,0:T(2,128)(2,1)}, bf16[4,8192,2,128]{3,2,1,0:T(2,128)(2,1)S(1)}, u32[]{:S(2)}) copy-start(bf16[4,8192,2,128]{3,2,1,0:T(2,128)(2,1)S(1)} %shard_map.124) | copy-start | bytes 50331652
  117.2 5.8 %copy-start.1 = (bf16[4,8192,2,128]{3,2,1,0:T(2,128)(2,1)S(1)}, bf16[4,8192,2,128]{3,2,1,0:T(2,128)(2,1)}, u32[]{:S(2)}) copy-start(bf16[4,8192,2,128]{3,2,1,0:T(2,128)(2,1)} %copy-done) | copy-start | bytes 50331652
  137.5 34.5 %copy-start.17 = (s32[16]{0:T(128)S(1)}, s32[16]{0:T(128)}, u32[]{:S(2)}) copy-start(s32[16]{0:T(128)} %copy-done.16) | copy-start | bytes 196
  137.5 1.6 collective-permute-start.3
  152.1 4.0 %collective-permute-start.4 = (bf16[32,512]{1,0:T(8,128)(2,1)S(1)}, bf16[32,512]{1,0:T(8,128)(2,1)S(1)}, u32[]{:S(2)}, u32[]{:S(2)}) collective-permute-start(bf16[32,512]{1,0:T(8,128)(2,1)S(1)} %add_convert_fusion.5), channel_id=1, source_target_pairs={{0,16},{16,0},{1,17},{17,1},{2,18},{18,2},{3,19},{19,3},{4,20},{20... | collective-permute-start | bytes 98312 | tf_op jit(solution)/shard_map/ppermute | solution.py:21
  167.7 4.3 %collective-permute-start.5 = (bf16[8,32,512]{2,1,0:T(8,128)(2,1)S(1)}, bf16[8,32,512]{2,1,0:T(8,128)(2,1)S(1)}, u32[]{:S(2)}, u32[]{:S(2)}) collective-permute-start(bf16[8,32,512]{2,1,0:T(8,128)(2,1)S(1)} %all_to_all.62.own_ref), channel_id=1, source_target_pairs={{0,1},{1,0},{2,3},{3,2},{4,5},{5,4},{6,7},{7,6},{8,9},{9,8},{10,11... | collective-permute-start | bytes 786440 | tf_op jit(solution)/shard_map/ppermute | solution.py:21
  177.4 10.2 %all-to-all-start.7 = ((bf16[16,2,640]{2,1,0:T(2,128)(2,1)}), bf16[16,2,640]{2,1,0:T(2,128)(2,1)S(1)}, u32[]{:S(2)}, u32[]{:S(2)}) async-start(bf16[16,2,640]{2,1,0:T(2,128)(2,1)} %shard_map.129.token_ref), calls=%async_computation.7 | async-start | bytes 81920 | tf_op jit(solution)/shard_map/all_to_all | solution.py:531
  192.6 10.3 %all-to-all-start.8 = ((bf16[16,2,512]{2,1,0:T(2,128)(2,1)}), bf16[16,2,512]{2,1,0:T(2,128)(2,1)S(1)}, u32[]{:S(2)}, u32[]{:S(2)}) async-start(bf16[16,2,512]{2,1,0:T(2,128)(2,1)} %bitcast.62), calls=%async_computation.8 | async-start | bytes 65536 | tf_op jit(solution)/shard_map/all_to_all | solution.py:541
  199.6 3.3 %copy-start.6 = (bf16[512,8192]{1,0:T(8,128)(2,1)}, bf16[512,8192]{1,0:T(8,128)(2,1)S(1)}, u32[]{:S(2)}) copy-start(bf16[512,8192]{1,0:T(8,128)(2,1)S(1)} %shard_map.132.w_ref) | copy-start | bytes 25165828
  202.9 3.4 %copy-start.7 = (bf16[512,8192]{1,0:T(8,128)(2,1)S(1)}, bf16[512,8192]{1,0:T(8,128)(2,1)}, u32[]{:S(2)}) copy-start(bf16[512,8192]{1,0:T(8,128)(2,1)} %copy-done.6) | copy-start | bytes 25165828
  208.7 1.6 collective-permute-start.6
  237.2 6.1 %copy-start.19 = (bf16[8,32,512]{2,1,0:T(8,128)(2,1)}, bf16[8,32,512]{2,1,0:T(8,128)(2,1)S(1)}, u32[]{:S(2)}) copy-start(bf16[8,32,512]{2,1,0:T(8,128)(2,1)S(1)} %all_to_all.64.own_ref) | copy-start | bytes 786436
  237.2 23.9 %collective-permute-start.7 = (bf16[8,32,512]{2,1,0:T(8,128)(2,1)S(1)}, bf16[8,32,512]{2,1,0:T(8,128)(2,1)S(1)}, u32[]{:S(2)}, u32[]{:S(2)}) collective-permute-start(bf16[8,32,512]{2,1,0:T(8,128)(2,1)S(1)} %all_to_all.64.own_ref), channel_id=1, source_target_pairs={{0,1},{1,0},{2,3},{3,2},{4,5},{5,4},{6,7},{7,6},{8,9},{9,8},{10,11... | collective-permute-start | bytes 786440 | tf_op jit(solution)/shard_map/ppermute | solution.py:21
  243.4 5.8 %copy-start.2 = (bf16[4,8192,2,128]{3,2,1,0:T(2,128)(2,1)}, bf16[4,8192,2,128]{3,2,1,0:T(2,128)(2,1)S(1)}, u32[]{:S(2)}) copy-start(bf16[4,8192,2,128]{3,2,1,0:T(2,128)(2,1)S(1)} %shard_map.134) | copy-start | bytes 50331652
  261.9 5.8 %copy-start.3 = (bf16[4,8192,2,128]{3,2,1,0:T(2,128)(2,1)S(1)}, bf16[4,8192,2,128]{3,2,1,0:T(2,128)(2,1)}, u32[]{:S(2)}) copy-start(bf16[4,8192,2,128]{3,2,1,0:T(2,128)(2,1)} %copy-done.2) | copy-start | bytes 50331652
  282.7 1.7 collective-permute-start.8
  285.4 13.1 %all-to-all-start.11 = ((bf16[8,2,8192]{2,1,0:T(2,128)(2,1)}), bf16[8,2,8192]{2,1,0:T(2,128)(2,1)S(1)}, u32[]{:S(2)}, u32[]{:S(2)}) async-start(bf16[8,2,8192]{2,1,0:T(2,128)(2,1)} %add_convert_fusion), calls=%async_computation.11 | async-start | bytes 524288 | tf_op jit(solution)/shard_map/all_to_all | solution.py:27
  (7 other events, 8.1 us)

commit v4 on v3

--- a/solution.py
+++ b/solution.py
@@ -2,6 +2,7 @@
 
 import jax
 import jax.numpy as jnp
+import numpy as np
 from jax import lax
 from jax.experimental import pallas as pl
 from jax.experimental.pallas import tpu as pltpu
@@ -29,23 +30,15 @@
     )
 
 
-def merge(send, keep):
-    held = keep.astype(jnp.float32) + swap(send, 1).astype(jnp.float32)
-    return held.astype(jnp.bfloat16)
-
-
-def scatter(held):
-    return jnp.sum(exchange(held).astype(jnp.float32), axis=0)
-
-
-def gather(part):
-    own = exchange(jnp.broadcast_to(part[None], (lax.axis_size("mp") // 2,) + part.shape))
-    return own, swap(own, 1)
-
-
-def columns_to_chunks(values, count):
-    rows, width = values.shape
-    return values.reshape(rows, count, width // count).transpose(1, 0, 2)
+def chip_masks():
+    return [1 << bit for bit in range(1, (lax.axis_size("mp") - 1).bit_length())]
+
+
+def relative_ids():
+    ids = np.zeros((1,), np.int32)
+    for mask in reversed(chip_masks()):
+        ids = np.concatenate([ids, ids ^ mask])
+    return ids
 
 
 def vmem():
@@ -133,17 +126,17 @@
     )(token, where, placed_in(keys, pltpu.HBM), placed_in(values, pltpu.HBM))
 
 
-def fetch_pairs_kernel(first, token_ref, source, target, sems):
-    blocks, depth = target.shape[:2]
-    size = depth // 4
+def fetch_pairs_kernel(first, token_ref, source, *refs):
+    targets, sems = refs[:-1], refs[-1]
+    size = source.shape[0] // 4
     copies = []
-    for block in range(blocks):
+    for block, target in enumerate(targets):
         for piece in range(4):
             span = pl.ds(piece * size, size)
             copies.append(
                 pltpu.make_async_copy(
                     source.at[span, :, pl.ds((first + block) * 128, 128)],
-                    target.at[block, span],
+                    target.at[span],
                     sems.at[block, piece],
                 )
             )
@@ -152,31 +145,114 @@
 
 def fetch_pairs(token, weights, first, blocks):
     depth = weights.shape[0]
-    out = pl.pallas_call(
+    return pl.pallas_call(
         functools.partial(fetch_pairs_kernel, first),
-        out_shape=pltpu.VMEM((blocks, depth, 2, 128), weights.dtype),
+        out_shape=[pltpu.VMEM((depth, 2, 128), weights.dtype)] * blocks,
         in_specs=[hbm(), hbm()],
-        out_specs=vmem(),
+        out_specs=[vmem()] * blocks,
         scratch_shapes=[pltpu.SemaphoreType.DMA((blocks, 4))],
         compiler_params=pltpu.CompilerParams(vmem_limit_bytes=1 << 20),
         cost_estimate=pl.CostEstimate(
             flops=0, bytes_accessed=4 * blocks * depth * 128, transcendentals=0
         ),
     )(token, placed_in(weights, pltpu.HBM))
-    return out.reshape(blocks, 2 * depth, 128)
+
+
+def step_call(kernel, shapes, operands, held_back):
+    return pl.pallas_call(
+        kernel,
+        out_shape=[pltpu.VMEM(shape, jnp.bfloat16) for shape in shapes],
+        in_specs=[vmem()] * len(operands) + [hbm()] * len(held_back),
+        out_specs=[vmem()] * len(shapes),
+        compiler_params=pltpu.CompilerParams(vmem_limit_bytes=4 << 20),
+        cost_estimate=pl.CostEstimate(
+            flops=2 * operands[0].size, bytes_accessed=6 * operands[0].size, transcendentals=0
+        ),
+    )(*operands, *[placed_in(array, pltpu.VMEM) for array in held_back])
+
+
+def add_kernel(outs, operands, *refs):
+    targets = refs[-outs:]
+    share = targets[0].shape[0]
+    for which, target in enumerate(targets):
+        for place in range(share):
+            total = 0.0
+            for ref in refs[:operands]:
+                total += ref[which * share + place].astype(jnp.float32)
+            target[place] = total.astype(jnp.bfloat16)
+
+
+def add_parts(operands, outs, held_back=()):
+    lead = operands[0].shape[0]
+    shape = (lead // outs,) + operands[0].shape[1:]
+    return step_call(
+        functools.partial(add_kernel, outs, len(operands)), [shape] * outs, operands, held_back
+    )
+
+
+def finish_kernel(own_ref, keep_ref, got_ref, *refs):
+    total = keep_ref[0].astype(jnp.float32) + got_ref[0].astype(jnp.float32)
+    if len(own_ref.shape) == 2:
+        total += own_ref[...].astype(jnp.float32)
+    else:
+        parts = [own_ref[owner].astype(jnp.float32) for owner in range(own_ref.shape[0])]
+        total += jnp.concatenate(parts, axis=0)
+    refs[-1][...] = total.astype(jnp.bfloat16)
+
+
+def join_kernel(low_ref, high_ref, *refs):
+    half = low_ref.shape[0]
+    out_ref = refs[-1]
+    for place in range(half):
+        out_ref[place] = low_ref[place]
+        out_ref[half + place] = high_ref[place]
+
+
+def join(low, high, held_back=()):
+    shape = (2 * low.shape[0],) + low.shape[1:]
+    return step_call(join_kernel, [shape], (low, high), held_back)[0]
+
+
+def run_job(jobs, token):
+    return jobs.pop(0)(token) if jobs else ()
+
+
+def scatter(send, keep):
+    (held,) = add_parts((keep, swap(send, 1)), 1)
+    return jnp.sum(exchange(held).astype(jnp.float32), axis=0)
+
+
+def scatter_halving(send, keep, own, jobs):
+    got = swap(send, 1)
+    held_back = ()
+    for mask in chip_masks():
+        keep, send = add_parts((keep, got), 2, held_back)
+        got = swap(send, mask)
+        held_back = run_job(jobs, send)
+    return step_call(finish_kernel, [keep.shape[1:]], (own, keep, got), held_back)[0]
+
+
+def gather_doubling(part, jobs):
+    held = part[None]
+    for mask in reversed(chip_masks()):
+        got = swap(held, mask)
+        held = join(held, got, run_job(jobs, held))
+    return held, swap(held, 1)
 
 
 def inverse_rms(x_refs):
     half, rows, chunk = x_refs[0].shape
-    total = jnp.zeros((rows, 1), jnp.float32)
+    total = jnp.zeros((rows, chunk), jnp.float32)
     for x_ref in x_refs:
 
-        def add(k, total):
-            wide = x_ref[k].astype(jnp.float32)
-            return total + jnp.sum(wide * wide, axis=-1, keepdims=True)
-
-        total = lax.fori_loop(0, half, add, total)
-    return lax.rsqrt(total / (2 * half * chunk) + epsilon)
+        def add(group, total):
+            for step in range(UNROLL):
+                wide = x_ref[group * UNROLL + step].astype(jnp.float32)
+                total = total + wide * wide
+            return total
+
+        total = lax.fori_loop(0, half // UNROLL, add, total)
+    return lax.rsqrt(jnp.sum(total, axis=-1, keepdims=True) / (2 * half * chunk) + epsilon)
 
 
 def span_of(ids_ref, k, chunk):
@@ -189,12 +265,25 @@
 
 
 def project_kernel(ids_ref, own_ref, other_ref, gain_ref, wq_ref, wk_ref, wv_ref, out_ref,
-                   q_sum, kv_sum):
-    half, rows, chunk = own_ref.shape
+                   mine_ref, q_sum, kv_sum, wide):
     queries = wq_ref.shape[1]
-    keys = wk_ref.shape[0]
     count, rows_dev, _ = out_ref.shape
-    scale = inverse_rms((own_ref, other_ref))
+    half = count // 2
+    by_rows = own_ref.shape[1] == rows_dev
+    chunk = wq_ref.shape[0] // count
+    if by_rows:
+        for first, x_ref in ((0, own_ref), (half, other_ref)):
+            for place in range(half):
+                at = (first + place) * rows_dev
+                wide[at : at + rows_dev, :] = x_ref[place].astype(jnp.float32)
+        total = 0.0
+        for k in range(count):
+            part = wide[:, k * chunk : (k + 1) * chunk]
+            total += part * part
+        mean = jnp.sum(total, axis=-1, keepdims=True) / (count * chunk)
+        scale = lax.rsqrt(mean + epsilon)
+    else:
+        scale = inverse_rms((own_ref, other_ref))
     q_sum[...] = jnp.zeros_like(q_sum)
     kv_sum[...] = jnp.zeros_like(kv_sum)
     for first, x_ref in ((0, own_ref), (half, other_ref)):
@@ -202,81 +291,109 @@
         @pl.loop(0, half // UNROLL)
         def _(group):
             q_part = 0.0
-            parts = [0.0, 0.0]
+            kv_part = 0.0
             for step in range(UNROLL):
                 k = group * UNROLL + step
-                span = span_of(ids_ref, first + k, chunk)
-                normed = normed_chunk(x_ref, gain_ref, scale, k, span)
+                if by_rows:
+                    span = pl.ds(pl.multiple_of((first + k) * chunk, chunk), chunk)
+                    normed = (wide[:, span] * scale * gain_ref[:, span]).astype(jnp.bfloat16)
+                else:
+                    span = span_of(ids_ref, first + k, chunk)
+                    normed = normed_chunk(x_ref, gain_ref, scale, k, span)
                 q_part += jnp.dot(normed, wq_ref[span, :], preferred_element_type=jnp.float32)
-                for which, w_ref in enumerate((wk_ref, wv_ref)):
-                    parts[which] += lax.dot_general(
-                        normed,
-                        w_ref[:, span],
-                        (((1,), (1,)), ((), ())),
-                        preferred_element_type=jnp.float32,
-                    )
+                kv_part += lax.dot_general(
+                    normed,
+                    jnp.concatenate([wk_ref[:, span], wv_ref[:, span]], axis=0),
+                    (((1,), (1,)), ((), ())),
+                    preferred_element_type=jnp.float32,
+                )
             q_sum[...] += q_part
-            kv_sum[...] += jnp.concatenate(parts, axis=1)
-
-    for owner in range(count):
-        lines = slice(owner * rows_dev, (owner + 1) * rows_dev)
+            kv_sum[...] += kv_part
+
+    for place in range(count):
+        owner = ids_ref[place] if by_rows else place
+        lines = slice(place * rows_dev, (place + 1) * rows_dev)
         out_ref[owner, :, :queries] = q_sum[lines, :].astype(jnp.bfloat16)
         out_ref[owner, :, queries:] = kv_sum[lines, :].astype(jnp.bfloat16)
+        if by_rows:
+            span = span_of(ids_ref, 0, chunk)
+            mine_ref[owner] = wide[lines, span].astype(jnp.bfloat16)
 
 
 def project(ids, own, other, gain, wq, wk, wv):
-    half, rows, _ = own.shape
-    queries, keys = wq.shape[1], wk.shape[0]
+    count = ids.shape[0]
+    width, queries = wq.shape
+    keys = wk.shape[0]
     size = queries + 2 * keys
+    rows_dev = 2 * own.size // (count * width)
+    rows = count * rows_dev
+    by_rows = own.shape[1] == rows_dev
     return pl.pallas_call(
         project_kernel,
-        out_shape=pltpu.VMEM((2 * half, rows // (2 * half), size), jnp.bfloat16),
+        out_shape=[
+            pltpu.VMEM((count, rows_dev, size), jnp.bfloat16),
+            pltpu.VMEM((count, rows_dev, width // count), jnp.bfloat16),
+        ],
         in_specs=[smem()] + [vmem()] * 6,
-        out_specs=vmem(),
+        out_specs=[vmem(), vmem()],
         scratch_shapes=[
             pltpu.VMEM((rows, queries), jnp.float32),
             pltpu.VMEM((rows, 2 * keys), jnp.float32),
+            pltpu.VMEM((rows, width if by_rows else 128), jnp.float32),
         ],
-        compiler_params=pltpu.CompilerParams(vmem_limit_bytes=4 << 20),
+        compiler_params=pltpu.CompilerParams(vmem_limit_bytes=(3 << 20) + 4 * rows * width),
         cost_estimate=pl.CostEstimate(
-            flops=2 * rows * wq.shape[0] * size,
-            bytes_accessed=2 * wq.shape[0] * size,
-            transcendentals=0,
+            flops=2 * rows * width * size, bytes_accessed=2 * width * size, transcendentals=0
         ),
     )(ids, own, other, gain, *[placed_in(w, pltpu.VMEM) for w in (wq, wk, wv)])
 
 
-def attend_kernel(where_ref, length_ref, q_ref, kv_ref, cos_ref, sin_ref, key_buf,
-                  value_buf, out_ref, wide_q):
-    rows, devices, queries = q_ref.shape
-    _, _, groups, size = kv_ref.shape
+def attend_kernel(where_ref, length_ref, in_ref, cos_ref, sin_ref, key_buf, value_buf, out_ref,
+                  lined, wide_q):
+    rows, devices, queries = out_ref.shape
+    width = key_buf.shape[2]
+    keys = (in_ref.shape[2] - queries) // 2
+    size = cos_ref.shape[1]
+    groups = width // size
+    pieces = size // keys
     slots = queries // size
     heads = devices * slots
     places = key_buf.shape[1]
     batch = where_ref[0]
 
+    for device in range(devices):
+        wide = in_ref[device].astype(jnp.float32)
+        for row in range(rows):
+            lined[row, device : device + 1, :] = wide[row : row + 1]
     line = lax.broadcasted_iota(jnp.int32, (devices, 1), 0)
     group_of = line * groups // devices
     for row in range(rows):
         cosine = cos_ref[pl.ds(row, 1), :]
         sine = sin_ref[pl.ds(row, 1), :]
 
-        def turned(features):
-            wide = features.astype(jnp.float32)
+        def turned(wide):
             other = jnp.concatenate([wide[:, size // 2 :], wide[:, : size // 2]], axis=1)
             return (wide * cosine + other * sine).astype(jnp.bfloat16).astype(jnp.float32)
 
-        own_key = turned(kv_ref[row, 0])
-        own_value = kv_ref[row, 1].astype(jnp.float32)
         key_lines = jnp.zeros((devices, size), jnp.float32)
         value_lines = jnp.zeros((devices, size), jnp.float32)
         for group in range(groups):
+            own_key, own_value = (
+                jnp.concatenate(
+                    [
+                        lined[row, device : device + 1, at : at + keys]
+                        for device in range(group * pieces, (group + 1) * pieces)
+                    ],
+                    axis=1,
+                )
+                for at in (queries, queries + keys)
+            )
             here = group_of == group
-            key_lines = jnp.where(here, own_key[group : group + 1], key_lines)
-            value_lines = jnp.where(here, own_value[group : group + 1], value_lines)
+            key_lines = jnp.where(here, turned(own_key), key_lines)
+            value_lines = jnp.where(here, own_value, value_lines)
         own_parts = []
         for slot in range(slots):
-            part = turned(q_ref[row, :, slot * size : (slot + 1) * size])
+            part = turned(lined[row, :, slot * size : (slot + 1) * size])
             own_parts.append(jnp.sum(part * key_lines, axis=1, keepdims=True))
             for group in range(groups):
                 wide_q[
@@ -305,16 +422,19 @@
             out_ref[row, :, slot * size : (slot + 1) * size] = picked.astype(jnp.bfloat16)
 
 
-def attend(where, lengths, query, fresh, cosine, sine, keys, values):
-    rows, devices, queries = query.shape
+def attend(where, lengths, spread, cosine, sine, keys, values, queries):
+    devices, rows, length = spread.shape
     places, width = keys.shape[1:]
     heads = devices * queries // HEAD_SIZE
     return pl.pallas_call(
         attend_kernel,
-        out_shape=pltpu.VMEM(query.shape, jnp.bfloat16),
-        in_specs=[smem(), smem()] + [vmem()] * 6,
+        out_shape=pltpu.VMEM((rows, devices, queries), jnp.bfloat16),
+        in_specs=[smem(), smem()] + [vmem()] * 5,
         out_specs=vmem(),
-        scratch_shapes=[pltpu.VMEM((heads, width), jnp.bfloat16)],
+        scratch_shapes=[
+            pltpu.VMEM((rows, devices, length), jnp.float32),
+            pltpu.VMEM((heads, width), jnp.bfloat16),
+        ],
         compiler_params=pltpu.CompilerParams(vmem_limit_bytes=4 << 20),
         cost_estimate=pl.CostEstimate(
             flops=4 * rows * heads * places * width,
@@ -324,8 +444,7 @@
     )(
         where,
         lengths,
-        query,
-        fresh,
+        spread,
         cosine,
         sine,
         placed_in(keys, pltpu.VMEM),
@@ -369,11 +488,24 @@
     )(ids, values, placed_in(weights, pltpu.VMEM))
 
 
-def mlp_kernel(by_rows, ids_ref, own_ref, other_ref, gain_ref, low_ref, high_ref, down_ref,
-               keep_ref, send_ref, stacked, wide_x, total, act):
+def mlp_kernel(by_rows, ids_ref, out_ids_ref, own_ref, other_ref, gain_ref, down_hbm, *refs):
+    pairs, (keep_ref, send_ref, middle_ref), (stacked, wide_x, total, act, down_ref, sems) = (
+        refs[:-9],
+        refs[-9:-6],
+        refs[-6:],
+    )
     half, rows, chunk = own_ref.shape
-    blocks = [ref.at[j] for ref in (low_ref, high_ref) for j in range(ref.shape[0])]
+    blocks = pairs
     per_chunk = chunk // 128
+
+    def down_copy(k):
+        return pltpu.make_async_copy(
+            down_hbm.at[:, span_of(out_ids_ref, k, chunk)], down_ref.at[lax.rem(k, half)], sems.at[k]
+        )
+
+    @pl.loop(0, half)
+    def _(k):
+        down_copy(k).start()
 
     scale = inverse_rms((own_ref, other_ref))
     for first, x_ref in ((0, own_ref), (half, other_ref)):
@@ -384,6 +516,21 @@
             normed = normed_chunk(x_ref, gain_ref, scale, place, span_of(ids_ref, k, chunk))
             for b in range(per_chunk):
                 stacked[k * per_chunk + b] = normed[:, b * 128 : (b + 1) * 128]
+
+    if by_rows:
+        rows_dev = middle_ref.shape[0]
+        line = lax.broadcasted_iota(jnp.int32, (rows, 1), 0)
+        for first, x_ref in ((0, own_ref), (half, other_ref)):
+
+            @pl.loop(0, half)
+            def _(place):
+                wide = x_ref[place].astype(jnp.float32)
+                span = span_of(ids_ref, first + place, chunk)
+                for row in range(rows_dev):
+                    here = line == ids_ref[0] * rows_dev + row
+                    middle_ref[row : row + 1, span] = jnp.sum(
+                        jnp.where(here, wide, 0.0), axis=0, keepdims=True
+                    )
 
     line = lax.broadcasted_iota(jnp.int32, (128, 512), 0)
     column = lax.broadcasted_iota(jnp.int32, (128, 512), 1)
@@ -422,56 +569,66 @@
     gate = total[:rows, :]
     act[...] = (gate / (1.0 + jnp.exp(-gate)) * total[rows:, :]).astype(jnp.bfloat16)
 
-    def down(span):
-        return jnp.dot(act[...], down_ref[:, span], preferred_element_type=jnp.float32)
-
-    if by_rows:
-        rows_dev = keep_ref.shape[1]
-        first_core = ids_ref[0] == 0
-
-        @pl.loop(0, 2 * half // 2)
+    def down(first, k):
+        down_copy(first + k).wait()
+        return jnp.dot(act[...], down_ref[k], preferred_element_type=jnp.float32)
+
+    for first, target in ((0, keep_ref), (half, send_ref)):
+
+        @pl.loop(0, half // UNROLL)
         def _(group):
-            for step in range(2):
-                span = span_of(ids_ref, group * 2 + step, chunk)
-                part = down(span)
+            for step in range(UNROLL):
+                k = group * UNROLL + step
+                part = down(first, k)
+                if not by_rows:
+                    target[k] = part.astype(jnp.bfloat16)
+                    continue
+                span = span_of(out_ids_ref, first + k, chunk)
+                first_core = out_ids_ref[0] == 0
                 for chip in range(half):
                     at = 2 * chip * rows_dev
                     low = part[at : at + rows_dev]
                     high = part[at + rows_dev : at + 2 * rows_dev]
                     keep_ref[chip, :, span] = jnp.where(first_core, low, high).astype(jnp.bfloat16)
                     send_ref[chip, :, span] = jnp.where(first_core, high, low).astype(jnp.bfloat16)
-
-    else:
-        for first, target in ((0, keep_ref), (half, send_ref)):
-
-            @pl.loop(0, half // UNROLL)
-            def _(group):
+            if first == 0:
                 for step in range(UNROLL):
-                    k = group * UNROLL + step
-                    target[k] = down(span_of(ids_ref, first + k, chunk)).astype(jnp.bfloat16)
-
-
-def mlp(ids, own, other, gain, low, high, down, by_rows):
+                    down_copy(half + group * UNROLL + step).start()
+
+
+def mlp(ids, out_ids, own, other, gain, pairs, down, by_rows):
     half, rows, chunk = own.shape
     units, width = down.shape
     part = (half, rows // (2 * half), width) if by_rows else own.shape
     shape = pltpu.VMEM(part, jnp.bfloat16)
     return pl.pallas_call(
         functools.partial(mlp_kernel, by_rows),
-        out_shape=(shape, shape),
-        in_specs=[smem()] + [vmem()] * 6,
-        out_specs=(vmem(), vmem()),
+        out_shape=(shape, shape, pltpu.VMEM((rows // (2 * half), width), jnp.float32)),
+        in_specs=[smem(), smem()] + [vmem()] * 3 + [hbm()] + [vmem()] * len(pairs),
+        out_specs=(vmem(), vmem(), vmem()),
         scratch_shapes=[
             pltpu.VMEM((width // 128, rows, 128), jnp.bfloat16),
             pltpu.VMEM((width // 1024, 2 * rows, 2048), jnp.bfloat16),
             pltpu.VMEM((2 * rows, units), jnp.float32),
             pltpu.VMEM((rows, units), jnp.bfloat16),
+            pltpu.VMEM((half, units, chunk), jnp.bfloat16),
+            pltpu.SemaphoreType.DMA((2 * half,)),
         ],
-        compiler_params=pltpu.CompilerParams(vmem_limit_bytes=(3 << 20) + 10 * rows * width),
+        compiler_params=pltpu.CompilerParams(
+            vmem_limit_bytes=(3 << 19) + 10 * rows * width + (10 * rows + width) * units
+        ),
         cost_estimate=pl.CostEstimate(
             flops=6 * rows * units * width, bytes_accessed=6 * units * width, transcendentals=0
         ),
-    )(ids, own, other, gain, *[placed_in(w, pltpu.VMEM) for w in (low, high, down)])
+    )(
+        ids,
+        out_ids,
+        own,
+        other,
+        gain,
+        placed_in(down, pltpu.HBM),
+        *[placed_in(pair.reshape(2 * width, 128), pltpu.VMEM) for pair in pairs],
+    )
 
 
 def turning(positions):
@@ -500,68 +657,75 @@
     rows_dev = hidden.shape[1]
     count = lax.axis_size("mp")
     half = count // 2
-    rows = rows_dev * count
     section_index = lax.axis_index("section")
     model_index = lax.axis_index("mp")
     core = model_index % 2
-    query_cols = w_query.shape[2]
-    key_cols = w_key.shape[2]
     width = hidden.shape[2]
     chips = 2 * jnp.arange(half, dtype=jnp.int32)
     ids = jnp.concatenate([chips + core, chips + 1 - core])
+    near = jnp.asarray(relative_ids())
+    places = jnp.concatenate([near ^ model_index, near ^ model_index ^ 1])
     wk = w_key[0].T
     wv = w_value[0].T
-
-    def by_core(own, other):
-        pair = jnp.where(core == 0, jnp.stack([own, other], 1), jnp.stack([other, own], 1))
-        return pair.reshape((count,) + own.shape[1:])
-
     blocks = w_gate_up.shape[3] // 128
-    qkv = fetch(hidden, w_query[0], wk, wv)
-    start = by_core(*gather(hidden[0])).reshape(rows, width)
-    chunks = columns_to_chunks(start, count)
-    mine = lax.dynamic_index_in_dim(chunks, model_index, 0, keepdims=False)
-    own, other = chunks[:half], chunks[half:]
-    order = jnp.arange(count, dtype=jnp.int32)
+    share = max(blocks // 4, 1)
+    batches = [
+        jnp.remainder(section_index + turn_index, 2).astype(jnp.int32).reshape(1)
+        for turn_index in range(2)
+    ]
+
+    def attention_jobs(turn_index):
+        got = {}
+
+        def projections(token):
+            got["qkv"] = fetch(token, w_query[0], wk, wv)
+            return got["qkv"]
+
+        def out_projection(token):
+            got["out"] = fetch(token, w_out[0])
+            return got["out"]
+
+        def caches(token):
+            got["caches"] = fetch_caches(token, batches[turn_index], key_cache[0], value_cache[0])
+            return got["caches"]
+
+        return got, [projections, out_projection, caches]
+
+    got, jobs = attention_jobs(0)
+    own, other = gather_doubling(hidden[0], jobs)
+    mine = None
     for turn_index in range(2):
-        batch = jnp.remainder(section_index + turn_index, 2).astype(jnp.int32).reshape(1)
+        last = turn_index == 1
+        batch = batches[turn_index]
         cosine, sine = turning(lax.dynamic_index_in_dim(lengths, batch[0], 0, keepdims=False))
-        joined = project(order, own, other, attn_gain, *qkv)
-        keys, values = fetch_caches(joined, batch, key_cache[0], value_cache[0])
+        joined, by_owner = project(places, own, other, attn_gain, *got["qkv"])
         spread = lax.all_to_all(joined, "mp", split_axis=0, concat_axis=0)
-        query = spread[..., :query_cols].transpose(1, 0, 2)
-        fresh = (
-            spread[..., query_cols:]
-            .reshape(count, rows_dev, 2, key_cols)
-            .transpose(1, 2, 0, 3)
-            .reshape(rows_dev, 2, KEY_VALUE_HEADS, HEAD_SIZE)
+        mixed = attend(
+            batch, lengths, spread, cosine, sine, *got["caches"], w_query.shape[2]
         )
-        mixed = attend(batch, lengths, query, fresh, cosine, sine, keys, values)
-        (out_proj,) = fetch(mixed, w_out[0])
         heads_out = lax.all_to_all(mixed.transpose(1, 0, 2), "mp", split_axis=0, concat_axis=0)
-        keep, send = spread_project(ids, heads_out, out_proj)
-        held = merge(send, keep)
-        low = fetch_pairs(held, w_gate_up[0], 0, blocks // 2)
-        middle = (mine.astype(jnp.float32) + scatter(held)).astype(jnp.bfloat16)
-        high = fetch_pairs(middle, w_gate_up[0], blocks // 2, blocks // 2)
-        (down,) = fetch(middle, w_down[0])
-        own, other = gather(middle)
-        last = turn_index == 1
-        keep, send = mlp(ids, own, other, mlp_gain, low, high, down, last)
-        mlp_part = scatter(merge(send, keep))
+        keep, send = spread_project(places, heads_out, *got["out"])
+        pairs = []
+
+        def pair_job(first):
+            def job(token):
+                pairs.extend(fetch_pairs(token, w_gate_up[0], first, share))
+                return pairs[-share:]
+
+            return job
+
+        jobs = [pair_job(first) for first in range(0, blocks, share)]
+        middle = scatter_halving(send, keep, by_owner if mine is None else mine, jobs)
+        own, other = gather_doubling(middle, jobs)
+        keep, send, own_rows = mlp(places, ids, own, other, mlp_gain, pairs, w_down[0], last)
+        mlp_part = scatter(send, keep)
         if last:
-            at = model_index * rows_dev
-            mine = by_core(
-                lax.dynamic_slice_in_dim(own, at, rows_dev, 1),
-                lax.dynamic_slice_in_dim(other, at, rows_dev, 1),
-            )
-            middle = mine.transpose(1, 0, 2).reshape(rows_dev, width)
+            middle = own_rows
         mine = (middle.astype(jnp.float32) + mlp_part).astype(jnp.bfloat16)
         if not last:
+            got, jobs = attention_jobs(1)
             mine = swap(mine, 1, "section")
-            qkv = fetch(mine, w_query[0], wk, wv)
-            own, other = gather(mine)
-            order = ids
+            own, other = gather_doubling(mine, jobs)
     return mine[None]
 
 

time: 301 us -> 280 us (0.930)
  blocking collectives: 63.3 us -> 43.9 us
  waiting for transfers between devices: 32.2 us -> 49 us
  Pallas kernels: 106 us -> 97.2 us
  starting transfers between devices: 36 us -> 32.8 us
  local copies, waits for them, and re-layouts: 57 us -> 53.9 us
    all_to_all x5 -> x2, blocking collectives: 63.3 us -> 25.4 us  [exchange(): lax.all_to_all(parts, 'mp', split_axis=0, concat_axis=0, axis_index_group...]
    ppermute x9 -> x27, waiting for transfers between devices: 8.59 us -> 35.8 us  [swap(): lax.ppermute(value, axis, [(source, source ^ mask) for source in range(co...]
    all_to_all x5 -> x0, starting transfers between devices: 23.7 us -> none  [the longest x3 16.7 us: exchange(): lax.all_to_all(parts, 'mp', split_axis=0, concat_axis=0, axis_index_group...]
    ppermute x9 -> x27, starting transfers between devices: 3.13 us -> 24.4 us  [swap(): lax.ppermute(value, axis, [(source, source ^ mask) for source in range(co...]
    all_to_all x0 -> x2, blocking collectives: none -> 18.4 us  [body(): lax.all_to_all(mixed.transpose(1, 0, 2), 'mp', split_axis=0, concat_axis=0)]
    all_to_all x5 -> x0, waiting for transfers between devices: 17.5 us -> none  [the longest x3 17.5 us: exchange(): lax.all_to_all(parts, 'mp', split_axis=0, concat_axis=0, axis_index_group...]
    pallas_call x6 -> x4, Pallas kernels: 27.5 us -> 15.5 us  [fetch(): pl.pallas_call(functools.partial(fetch_kernel, pieces), out_shape=[pltpu....]
    all_to_all x2, waiting for transfers between devices: 6.16 us -> 13.2 us  [body(): spread = lax.all_to_all(joined, 'mp', split_axis=0, concat_axis=0)]
  transfers between devices with their start and end apart: 16 -> 29, of which waited for: 11 -> 24; matrix products, arithmetic and copies ran while one was open for 1% -> 0% of each run, Pallas kernels for 19% -> 17%
where the time goes in v4:
time: 280 us; the launch traced here: 279 us
  Pallas kernels  97.2 us (35%)
  local copies, waits for them, and re-layouts  53.9 us (19%)
  waiting for transfers between devices  49 us (18%)
  blocking collectives  43.9 us (16%)
  starting transfers between devices  32.8 us (12%)
    unnamed x68, local copies, waits for them, and re-layouts  53.8 us
    ppermute x27, waiting for transfers between devices, swap(): lax.ppermute(value, axis, [(source, source ^ mask) for source in range(co...  35.8 us
    pallas_call x2, Pallas kernels, mlp(): pl.pallas_call(functools.partial(mlp_kernel, by_rows), out_shape=(shape,...  30.3 us
    pallas_call x8, Pallas kernels, fetch_pairs(): pl.pallas_call(functools.partial(fetch_pairs_kernel, first), out_shape=[p...  28 us
    all_to_all x2, blocking collectives, exchange(): lax.all_to_all(parts, 'mp', split_axis=0, concat_axis=0, axis_index_group...  25.4 us
    ppermute x27, starting transfers between devices, swap(): lax.ppermute(value, axis, [(source, source ^ mask) for source in range(co...  24.4 us
    all_to_all x2, blocking collectives, body(): lax.all_to_all(mixed.transpose(1, 0, 2), 'mp', split_axis=0, concat_axis=0)  18.4 us
    pallas_call x4, Pallas kernels, fetch(): pl.pallas_call(functools.partial(fetch_kernel, pieces), out_shape=[pltpu....  15.5 us
  transfers between devices with their start and end apart: 29, of which 24 were waited for; matrix products, arithmetic and copies ran while one was open for 0% of the time, Pallas kernels for 17%

profile of v4, /device:TPU:0, one launch (start us, length us, event | category | flops | bytes accessed | tf_op | source)
XLA Modules:
  0.0 278.7 jit_solution(17656573879433120402)
XLA Ops:
  0.0 4.0 %collective-permute-start = (bf16[1,2,8192]{2,1,0:T(2,128)(2,1)}, bf16[1,2,8192]{2,1,0:T(2,128)(2,1)S(1)}, u32[]{:S(2)}, u32[]{:S(2)}) collective-permute-start(bf16[1,2,8192]{2,1,0:T(2,128)(2,1)} %low_ref.1), channel_id=1, source_target_pairs={{0,8},{1,9},{2,10},{3,11},{4,12},{5,13},{6,14},{7,15},{8,0},{9,1},... | collective-permute-start | bytes 98312 | tf_op jit(solution)/shard_map/ppermute | solution.py:22
  4.8 4.3 %shard_map.127 = (bf16[8192,512]{1,0:T(8,128)(2,1)S(1)}, bf16[64,8192]{1,0:T(8,128)(2,1)S(1)}, bf16[64,8192]{1,0:T(8,128)(2,1)S(1)}) custom-call(bf16[1,2,8192]{2,1,0:T(2,128)(2,1)S(1)} %copy-done.30, bf16[8192,512]{1,0:T(8,128)(2,1)} %bitcast.80, bf16[64,8192]{1,0:T(8,128)(2,1)} %bitcast.88, bf16[64,8192]{1,0:T(8,128)(2,1)} %bitcast.90), custom_call_target="tpu_custom_call" | custom-call | bytes 10485760 | tf_op jit(solution)/shard_map/pallas_call | solution.py:83
  9.2 3.3 %copy-done.4 = bf16[8192,512]{1,0:T(8,128)(2,1)} copy-done((bf16[8192,512]{1,0:T(8,128)(2,1)}, bf16[8192,512]{1,0:T(8,128)(2,1)S(1)}, u32[]{:S(2)}) %copy-start.4) | copy-done | bytes 8388632
  14.3 3.5 %shard_map.129.refs_0_.w_ref = bf16[512,8192]{1,0:T(8,128)(2,1)S(1)} custom-call(bf16[2,2,8192]{2,1,0:T(2,128)(2,1)S(1)} %shard_map.128.token_ref.low_ref, bf16[512,8192]{1,0:T(8,128)(2,1)} %bitcast.82), custom_call_target="tpu_custom_call" | custom-call | bytes 8388608 | tf_op jit(solution)/shard_map/pallas_call | solution.py:83
  17.9 3.3 %copy-done = bf16[512,8192]{1,0:T(8,128)(2,1)} copy-done((bf16[512,8192]{1,0:T(8,128)(2,1)}, bf16[512,8192]{1,0:T(8,128)(2,1)S(1)}, u32[]{:S(2)}) %copy-start) | copy-done | bytes 8388632
  29.0 3.4 %copy-done.5 = bf16[8192,512]{1,0:T(8,128)(2,1)S(1)} copy-done((bf16[8192,512]{1,0:T(8,128)(2,1)S(1)}, bf16[8192,512]{1,0:T(8,128)(2,1)}, u32[]{:S(2)}) %copy-start.5) | copy-done | bytes 8388632
  32.4 4.2 %shard_map.133 = (bf16[16,2,640]{2,1,0:T(2,128)(2,1)}, bf16[16,2,512]{2,1,0:T(2,128)(2,1)S(1)}) custom-call(s32[16]{0:T(128)S(1)} %pad_add_fusion.ids_ref, bf16[8,2,8192]{2,1,0:T(2,128)(2,1)S(1)} %shard_map.132.own_ref, bf16[8,2,8192]{2,1,0:T(2,128)(2,1)S(1)} %collective-permute-done.3.other_ref, f32[1,8192]{1,0:T(1,128)S(1)} %copy-done.28, ...), custom_call_target="tpu_custom_call" | custom-call | flops 335544320 | bytes 10485760 | tf_op jit(solution)/shard_map/pallas_call | solution.py:331
  36.6 3.5 %all-to-all-start = ((bf16[16,2,640]{2,1,0:T(2,128)(2,1)}), bf16[16,2,640]{2,1,0:T(2,128)(2,1)S(1)}, u32[]{:S(2)}, u32[]{:S(2)}) async-start(bf16[16,2,640]{2,1,0:T(2,128)(2,1)} %get-tuple-element.61), calls=%async_computation | async-start | bytes 81920 | tf_op jit(solution)/shard_map/all_to_all | solution.py:702
  40.2 6.6 %all-to-all-done.in_ref = bf16[16,2,640]{2,1,0:T(2,128)(2,1)S(1)} async-done(((bf16[16,2,640]{2,1,0:T(2,128)(2,1)}), bf16[16,2,640]{2,1,0:T(2,128)(2,1)S(1)}, u32[]{:S(2)}, u32[]{:S(2)}) %all-to-all-start) | async-done | bytes 40992 | tf_op jit(solution)/shard_map/all_to_all | solution.py:702
  51.0 9.2 %all_to_all.30.x_ref = bf16[16,2,512]{2,1,0:T(2,128)(2,1)S(1)} all-to-all(bf16[16,2,512]{2,1,0:T(2,128)(2,1)S(1)} %bitcast.92), channel_id=1, replica_groups=mesh['section'=2,'mp'=16] {'mp'}, dimensions={0} | all-to-all | bytes 65536 | tf_op jit(solution)/shard_map/all_to_all | solution.py:706
  60.2 3.4 %copy-done.1 = bf16[512,8192]{1,0:T(8,128)(2,1)S(1)} copy-done((bf16[512,8192]{1,0:T(8,128)(2,1)S(1)}, bf16[512,8192]{1,0:T(8,128)(2,1)}, u32[]{:S(2)}) %copy-start.1) | copy-done | bytes 8388632
  68.0 3.5 %shard_map.137 = (bf16[8192,2,128]{2,1,0:T(2,128)(2,1)S(1)}, bf16[8192,2,128]{2,1,0:T(2,128)(2,1)S(1)}) custom-call(bf16[4,32,512]{2,1,0:T(8,128)(2,1)S(1)} %get-tuple-element.65.token_ref, bf16[8192,2,1024]{2,1,0:T(2,128)(2,1)} %bitcast.70), custom_call_target="tpu_custom_call" | custom-call | bytes 8388608 | tf_op jit(solution)/shard_map/pallas_call | solution.py:148
  75.5 3.5 %shard_map.139 = (bf16[8192,2,128]{2,1,0:T(2,128)(2,1)S(1)}, bf16[8192,2,128]{2,1,0:T(2,128)(2,1)S(1)}) custom-call(bf16[2,32,512]{2,1,0:T(8,128)(2,1)S(1)} %get-tuple-element.69.token_ref, bf16[8192,2,1024]{2,1,0:T(2,128)(2,1)} %bitcast.71), custom_call_target="tpu_custom_call" | custom-call | bytes 8388608 | tf_op jit(solution)/shard_map/pallas_call | solution.py:148
  83.0 3.5 %shard_map.141 = (bf16[8192,2,128]{2,1,0:T(2,128)(2,1)S(1)}, bf16[8192,2,128]{2,1,0:T(2,128)(2,1)S(1)}) custom-call(bf16[1,32,512]{2,1,0:T(8,128)(2,1)S(1)} %get-tuple-element.73.token_ref, bf16[8192,2,1024]{2,1,0:T(2,128)(2,1)} %bitcast.72), custom_call_target="tpu_custom_call" | custom-call | bytes 8388608 | tf_op jit(solution)/shard_map/pallas_call | solution.py:148
  92.1 3.5 %shard_map.143 = (bf16[8192,2,128]{2,1,0:T(2,128)(2,1)S(1)}, bf16[8192,2,128]{2,1,0:T(2,128)(2,1)S(1)}) custom-call(bf16[1,32,512]{2,1,0:T(8,128)(2,1)S(1)} %bitcast.62, bf16[8192,2,1024]{2,1,0:T(2,128)(2,1)} %bitcast.73), custom_call_target="tpu_custom_call" | custom-call | bytes 8388608 | tf_op jit(solution)/shard_map/pallas_call | solution.py:148
  104.7 3.5 %collective-permute-done.10.high_ref = bf16[4,32,512]{2,1,0:T(8,128)(2,1)S(1)} collective-permute-done((bf16[4,32,512]{2,1,0:T(8,128)(2,1)S(1)}, bf16[4,32,512]{2,1,0:T(8,128)(2,1)S(1)}, u32[]{:S(2)}, u32[]{:S(2)}) %collective-permute-start.10) | collective-permute-done | bytes 131104 | tf_op jit(solution)/shard_map/ppermute | solution.py:22
  127.4 15.1 %shard_map.147 = (bf16[8,32,512]{2,1,0:T(8,128)(2,1)S(1)}, bf16[8,32,512]{2,1,0:T(8,128)(2,1)S(1)}, f32[2,8192]{1,0:T(2,128)}) custom-call(s32[16]{0:T(128)S(1)} %pad_add_fusion.ids_ref, s32[16]{0:T(128)S(1)} %pad_add_fusion.1.out_ids_ref, bf16[8,32,512]{2,1,0:T(8,128)(2,1)S(1)} %shard_map.146.own_ref, ...), custom_call_target="tpu_custom_call" | custom-call | flops 1610612736 | bytes 50331648 | tf_op jit(solution)/shard_map/pallas_call | solution.py:604
  144.2 12.8 %all_to_all.31 = bf16[8,32,512]{2,1,0:T(8,128)(2,1)S(1)} all-to-all(bf16[8,32,512]{2,1,0:T(8,128)(2,1)S(1)} %shard_map.148), channel_id=1, replica_groups={{0,2,4,6,8,10,12,14},{1,3,5,7,9,11,13,15},{16,18,20,22,24,26,28,30},{17..., dimensions={0} | all-to-all | bytes 524288 | tf_op jit(solution)/shard_map/all_to_all | solution.py:28
  162.1 4.3 %shard_map.149 = (bf16[8192,512]{1,0:T(8,128)(2,1)S(1)}, bf16[64,8192]{1,0:T(8,128)(2,1)S(1)}, bf16[64,8192]{1,0:T(8,128)(2,1)S(1)}) custom-call(bf16[1,32,512]{2,1,0:T(8,128)(2,1)S(1)} %bitcast.68, bf16[8192,512]{1,0:T(8,128)(2,1)} %bitcast.81, bf16[64,8192]{1,0:T(8,128)(2,1)} %bitcast.89, bf16[64,8192]{1,0:T(8,128)(2,1)} %bitcast.91), custom_call_target="tpu_custom_call" | custom-call | bytes 10485760 | tf_op jit(solution)/shard_map/pallas_call | solution.py:83
  167.1 3.5 %shard_map.151.refs_0_.w_ref = bf16[512,8192]{1,0:T(8,128)(2,1)S(1)} custom-call(bf16[2,32,512]{2,1,0:T(8,128)(2,1)S(1)} %shard_map.150.token_ref.low_ref, bf16[512,8192]{1,0:T(8,128)(2,1)} %bitcast.83), custom_call_target="tpu_custom_call" | custom-call | bytes 8388608 | tf_op jit(solution)/shard_map/pallas_call | solution.py:83
  180.6 4.0 %shard_map.155 = (bf16[16,2,640]{2,1,0:T(2,128)(2,1)}, bf16[16,2,512]{2,1,0:T(2,128)(2,1)}) custom-call(s32[16]{0:T(128)S(1)} %pad_add_fusion.ids_ref, bf16[8,32,512]{2,1,0:T(8,128)(2,1)S(1)} %shard_map.154.own_ref, bf16[8,32,512]{2,1,0:T(8,128)(2,1)S(1)} %collective-permute-done.17.other_ref, f32[1,8192]{1,0:T(1,128)S(1)} %copy-done.28, ...), custom_call_target="tpu_custom_call" | custom-call | flops 335544320 | bytes 10485760 | tf_op jit(solution)/shard_map/pallas_call | solution.py:331
  184.6 4.9 %all-to-all-start.3 = ((bf16[16,2,640]{2,1,0:T(2,128)(2,1)}), bf16[16,2,640]{2,1,0:T(2,128)(2,1)S(1)}, u32[]{:S(2)}, u32[]{:S(2)}) async-start(bf16[16,2,640]{2,1,0:T(2,128)(2,1)} %get-tuple-element.85), calls=%async_computation.3 | async-start | bytes 81920 | tf_op jit(solution)/shard_map/all_to_all | solution.py:702
  189.6 6.6 %all-to-all-done.3.in_ref = bf16[16,2,640]{2,1,0:T(2,128)(2,1)S(1)} async-done(((bf16[16,2,640]{2,1,0:T(2,128)(2,1)}), bf16[16,2,640]{2,1,0:T(2,128)(2,1)S(1)}, u32[]{:S(2)}, u32[]{:S(2)}) %all-to-all-start.3) | async-done | bytes 40992 | tf_op jit(solution)/shard_map/all_to_all | solution.py:702
  200.3 9.2 %all_to_all.32.x_ref = bf16[16,2,512]{2,1,0:T(2,128)(2,1)S(1)} all-to-all(bf16[16,2,512]{2,1,0:T(2,128)(2,1)S(1)} %bitcast.93), channel_id=1, replica_groups=mesh['section'=2,'mp'=16] {'mp'}, dimensions={0} | all-to-all | bytes 65536 | tf_op jit(solution)/shard_map/all_to_all | solution.py:706
  209.5 3.4 %copy-done.3 = bf16[512,8192]{1,0:T(8,128)(2,1)S(1)} copy-done((bf16[512,8192]{1,0:T(8,128)(2,1)S(1)}, bf16[512,8192]{1,0:T(8,128)(2,1)}, u32[]{:S(2)}) %copy-start.3) | copy-done | bytes 8388632
  217.4 3.5 %shard_map.159 = (bf16[8192,2,128]{2,1,0:T(2,128)(2,1)S(1)}, bf16[8192,2,128]{2,1,0:T(2,128)(2,1)S(1)}) custom-call(bf16[4,32,512]{2,1,0:T(8,128)(2,1)S(1)} %get-tuple-element.89.token_ref, bf16[8192,2,1024]{2,1,0:T(2,128)(2,1)} %bitcast.74), custom_call_target="tpu_custom_call" | custom-call | bytes 8388608 | tf_op jit(solution)/shard_map/pallas_call | solution.py:148
  223.1 3.5 %shard_map.161 = (bf16[8192,2,128]{2,1,0:T(2,128)(2,1)S(1)}, bf16[8192,2,128]{2,1,0:T(2,128)(2,1)S(1)}) custom-call(bf16[2,32,512]{2,1,0:T(8,128)(2,1)S(1)} %get-tuple-element.93.token_ref, bf16[8192,2,1024]{2,1,0:T(2,128)(2,1)} %bitcast.75), custom_call_target="tpu_custom_call" | custom-call | bytes 8388608 | tf_op jit(solution)/shard_map/pallas_call | solution.py:148
  227.5 3.5 %shard_map.163 = (bf16[8192,2,128]{2,1,0:T(2,128)(2,1)S(1)}, bf16[8192,2,128]{2,1,0:T(2,128)(2,1)S(1)}) custom-call(bf16[1,32,512]{2,1,0:T(8,128)(2,1)S(1)} %get-tuple-element.97.token_ref, bf16[8192,2,1024]{2,1,0:T(2,128)(2,1)} %bitcast.76), custom_call_target="tpu_custom_call" | custom-call | bytes 8388608 | tf_op jit(solution)/shard_map/pallas_call | solution.py:148
  233.6 3.5 %shard_map.165 = (bf16[8192,2,128]{2,1,0:T(2,128)(2,1)S(1)}, bf16[8192,2,128]{2,1,0:T(2,128)(2,1)S(1)}) custom-call(bf16[1,32,512]{2,1,0:T(8,128)(2,1)S(1)} %bitcast.65, bf16[8192,2,1024]{2,1,0:T(2,128)(2,1)} %bitcast.77), custom_call_target="tpu_custom_call" | custom-call | bytes 8388608 | tf_op jit(solution)/shard_map/pallas_call | solution.py:148
  241.9 4.6 %collective-permute-done.24.high_ref = bf16[4,32,512]{2,1,0:T(8,128)(2,1)S(1)} collective-permute-done((bf16[4,32,512]{2,1,0:T(8,128)(2,1)S(1)}, bf16[4,32,512]{2,1,0:T(8,128)(2,1)S(1)}, u32[]{:S(2)}, u32[]{:S(2)}) %collective-permute-start.24) | collective-permute-done | bytes 131104 | tf_op jit(solution)/shard_map/ppermute | solution.py:22
  248.1 15.2 %shard_map.169 = (bf16[8,2,8192]{2,1,0:T(2,128)(2,1)S(1)}, bf16[8,2,8192]{2,1,0:T(2,128)(2,1)S(1)}, f32[2,8192]{1,0:T(2,128)S(1)}) custom-call(s32[16]{0:T(128)S(1)} %pad_add_fusion.ids_ref, s32[16]{0:T(128)S(1)} %pad_add_fusion.1.out_ids_ref, bf16[8,32,512]{2,1,0:T(8,128)(2,1)S(1)} %shard_map.168.own_ref, ...), custom_call_target="tpu_custom_call" | custom-call | flops 1610612736 | bytes 50331648 | tf_op jit(solution)/shard_map/pallas_call | solution.py:604
  265.2 12.6 %all_to_all.33 = bf16[8,2,8192]{2,1,0:T(2,128)(2,1)S(1)} all-to-all(bf16[8,2,8192]{2,1,0:T(2,128)(2,1)S(1)} %shard_map.170), channel_id=1, replica_groups={{0,2,4,6,8,10,12,14},{1,3,5,7,9,11,13,15},{16,18,20,22,24,26,28,30},{17..., dimensions={0} | all-to-all | bytes 524288 | tf_op jit(solution)/shard_map/all_to_all | solution.py:28
  (157 shorter events, 101.6 us)
Async XLA Ops:
  0.0 9.1 %collective-permute-start = (bf16[1,2,8192]{2,1,0:T(2,128)(2,1)}, bf16[1,2,8192]{2,1,0:T(2,128)(2,1)S(1)}, u32[]{:S(2)}, u32[]{:S(2)}) collective-permute-start(bf16[1,2,8192]{2,1,0:T(2,128)(2,1)} %low_ref.1), channel_id=1, source_target_pairs={{0,8},{1,9},{2,10},{3,11},{4,12},{5,13},{6,14},{7,15},{8,0},{9,1},... | collective-permute-start | bytes 98312 | tf_op jit(solution)/shard_map/ppermute | solution.py:22
  9.2 5.2 %copy-start.33 = (s32[8]{0:T(128)S(1)}, s32[8]{0:T(128)}, u32[]{:S(2)}) copy-start(s32[8]{0:T(128)} %constant.50.clone) | copy-start | bytes 100
  12.7 5.1 %collective-permute-start.1 = (bf16[2,2,8192]{2,1,0:T(2,128)(2,1)S(1)}, bf16[2,2,8192]{2,1,0:T(2,128)(2,1)S(1)}, u32[]{:S(2)}, u32[]{:S(2)}) collective-permute-start(bf16[2,2,8192]{2,1,0:T(2,128)(2,1)S(1)} %shard_map.128.token_ref.low_ref), channel_id=1, source_target_pairs={{0,4},{1,5},{2,6},{3,7},{4,0},{5,1},{6,2},{7,3},{8,12},{9,13},{10,... | collective-permute-start | bytes 196616 | tf_op jit(solution)/shard_map/ppermute | solution.py:22
  21.2 5.0 %collective-permute-start.2 = (bf16[4,2,8192]{2,1,0:T(2,128)(2,1)S(1)}, bf16[4,2,8192]{2,1,0:T(2,128)(2,1)S(1)}, u32[]{:S(2)}, u32[]{:S(2)}) collective-permute-start(bf16[4,2,8192]{2,1,0:T(2,128)(2,1)S(1)} %shard_map.130.token_ref.low_ref), channel_id=1, source_target_pairs={{0,2},{1,3},{2,0},{3,1},{4,6},{5,7},{6,4},{7,5},{8,10},{9,11},{10,... | collective-permute-start | bytes 393224 | tf_op jit(solution)/shard_map/ppermute | solution.py:22
  27.5 1.5 collective-permute-start.3
  36.6 10.2 %all-to-all-start = ((bf16[16,2,640]{2,1,0:T(2,128)(2,1)}), bf16[16,2,640]{2,1,0:T(2,128)(2,1)S(1)}, u32[]{:S(2)}, u32[]{:S(2)}) async-start(bf16[16,2,640]{2,1,0:T(2,128)(2,1)} %get-tuple-element.61), calls=%async_computation | async-start | bytes 81920 | tf_op jit(solution)/shard_map/all_to_all | solution.py:702
  66.0 1.6 collective-permute-start.4
  67.6 5.6 %collective-permute-start.5 = (bf16[4,32,512]{2,1,0:T(8,128)(2,1)S(1)}, bf16[4,32,512]{2,1,0:T(8,128)(2,1)S(1)}, u32[]{:S(2)}, u32[]{:S(2)}) collective-permute-start(bf16[4,32,512]{2,1,0:T(8,128)(2,1)S(1)} %get-tuple-element.65.token_ref), channel_id=1, source_target_pairs={{0,2},{1,3},{2,0},{3,1},{4,6},{5,7},{6,4},{7,5},{8,10},{9,11},{10,... | collective-permute-start | bytes 393224 | tf_op jit(solution)/shard_map/ppermute | solution.py:22
  74.9 4.3 %collective-permute-start.6 = (bf16[2,32,512]{2,1,0:T(8,128)(2,1)S(1)}, bf16[2,32,512]{2,1,0:T(8,128)(2,1)S(1)}, u32[]{:S(2)}, u32[]{:S(2)}) collective-permute-start(bf16[2,32,512]{2,1,0:T(8,128)(2,1)S(1)} %get-tuple-element.69.token_ref), channel_id=1, source_target_pairs={{0,4},{1,5},{2,6},{3,7},{4,0},{5,1},{6,2},{7,3},{8,12},{9,13},{10,... | collective-permute-start | bytes 196616 | tf_op jit(solution)/shard_map/ppermute | solution.py:22
  82.3 4.8 %collective-permute-start.7 = (bf16[1,32,512]{2,1,0:T(8,128)(2,1)S(1)}, bf16[1,32,512]{2,1,0:T(8,128)(2,1)S(1)}, u32[]{:S(2)}, u32[]{:S(2)}) collective-permute-start(bf16[1,32,512]{2,1,0:T(8,128)(2,1)S(1)} %get-tuple-element.73.token_ref), channel_id=1, source_target_pairs={{0,8},{1,9},{2,10},{3,11},{4,12},{5,13},{6,14},{7,15},{8,0},{9,1},... | collective-permute-start | bytes 98312 | tf_op jit(solution)/shard_map/ppermute | solution.py:22
  89.9 5.8 %collective-permute-start.8 = (bf16[1,32,512]{2,1,0:T(8,128)(2,1)S(1)}, bf16[1,32,512]{2,1,0:T(8,128)(2,1)S(1)}, u32[]{:S(2)}, u32[]{:S(2)}) collective-permute-start(bf16[1,32,512]{2,1,0:T(8,128)(2,1)S(1)} %bitcast.61), channel_id=1, source_target_pairs={{0,8},{1,9},{2,10},{3,11},{4,12},{5,13},{6,14},{7,15},{8,0},{9,1},... | collective-permute-start | bytes 98312 | tf_op jit(solution)/shard_map/ppermute | solution.py:22
  95.7 14.2 %copy-start.29 = (f32[1,8192]{1,0:T(1,128)S(1)}, f32[1,8192]{1,0:T(1,128)}, u32[]{:S(2)}) copy-start(f32[1,8192]{1,0:T(1,128)} %gain_ref.7) | copy-start | bytes 98308
  98.9 4.3 %collective-permute-start.9 = (bf16[2,32,512]{2,1,0:T(8,128)(2,1)S(1)}, bf16[2,32,512]{2,1,0:T(8,128)(2,1)S(1)}, u32[]{:S(2)}, u32[]{:S(2)}) collective-permute-start(bf16[2,32,512]{2,1,0:T(8,128)(2,1)S(1)} %shard_map.144.low_ref), channel_id=1, source_target_pairs={{0,4},{1,5},{2,6},{3,7},{4,0},{5,1},{6,2},{7,3},{8,12},{9,13},{10,... | collective-permute-start | bytes 196616 | tf_op jit(solution)/shard_map/ppermute | solution.py:22
  103.2 5.0 %collective-permute-start.10 = (bf16[4,32,512]{2,1,0:T(8,128)(2,1)S(1)}, bf16[4,32,512]{2,1,0:T(8,128)(2,1)S(1)}, u32[]{:S(2)}, u32[]{:S(2)}) collective-permute-start(bf16[4,32,512]{2,1,0:T(8,128)(2,1)S(1)} %shard_map.145.low_ref), channel_id=1, source_target_pairs={{0,2},{1,3},{2,0},{3,1},{4,6},{5,7},{6,4},{7,5},{8,10},{9,11},{10,... | collective-permute-start | bytes 393224 | tf_op jit(solution)/shard_map/ppermute | solution.py:22
  108.3 1.6 collective-permute-start.11
  142.5 1.6 collective-permute-start.12
  157.1 4.0 %collective-permute-start.13 = (bf16[32,512]{1,0:T(8,128)(2,1)S(1)}, bf16[32,512]{1,0:T(8,128)(2,1)S(1)}, u32[]{:S(2)}, u32[]{:S(2)}) collective-permute-start(bf16[32,512]{1,0:T(8,128)(2,1)S(1)} %add_convert_fusion.1), channel_id=1, source_target_pairs={{0,16},{16,0},{1,17},{17,1},{2,18},{18,2},{3,19},{19,3},{4,20},{20... | collective-permute-start | bytes 98312 | tf_op jit(solution)/shard_map/ppermute | solution.py:22
  161.0 5.3 %collective-permute-start.14 = (bf16[1,32,512]{2,1,0:T(8,128)(2,1)S(1)}, bf16[1,32,512]{2,1,0:T(8,128)(2,1)S(1)}, u32[]{:S(2)}, u32[]{:S(2)}) collective-permute-start(bf16[1,32,512]{2,1,0:T(8,128)(2,1)S(1)} %bitcast.67), channel_id=1, source_target_pairs={{0,8},{1,9},{2,10},{3,11},{4,12},{5,13},{6,14},{7,15},{8,0},{9,1},... | collective-permute-start | bytes 98312 | tf_op jit(solution)/shard_map/ppermute | solution.py:22
  166.4 4.3 %collective-permute-start.15 = (bf16[2,32,512]{2,1,0:T(8,128)(2,1)S(1)}, bf16[2,32,512]{2,1,0:T(8,128)(2,1)S(1)}, u32[]{:S(2)}, u32[]{:S(2)}) collective-permute-start(bf16[2,32,512]{2,1,0:T(8,128)(2,1)S(1)} %shard_map.150.token_ref.low_ref), channel_id=1, source_target_pairs={{0,4},{1,5},{2,6},{3,7},{4,0},{5,1},{6,2},{7,3},{8,12},{9,13},{10,... | collective-permute-start | bytes 196616 | tf_op jit(solution)/shard_map/ppermute | solution.py:22
  174.0 5.0 %collective-permute-start.16 = (bf16[4,32,512]{2,1,0:T(8,128)(2,1)S(1)}, bf16[4,32,512]{2,1,0:T(8,128)(2,1)S(1)}, u32[]{:S(2)}, u32[]{:S(2)}) collective-permute-start(bf16[4,32,512]{2,1,0:T(8,128)(2,1)S(1)} %shard_map.152.token_ref.low_ref), channel_id=1, source_target_pairs={{0,2},{1,3},{2,0},{3,1},{4,6},{5,7},{6,4},{7,5},{8,10},{9,11},{10,... | collective-permute-start | bytes 393224 | tf_op jit(solution)/shard_map/ppermute | solution.py:22
  177.9 6.6 %copy-start.24 = (bf16[2,512,1024]{2,1,0:T(8,128)(2,1)}, bf16[2,512,1024]{2,1,0:T(8,128)(2,1)S(1)}, u32[]{:S(2)}) copy-start(bf16[2,512,1024]{2,1,0:T(8,128)(2,1)S(1)} %get-tuple-element.84.refs_1_.value_buf) | copy-start | bytes 6291460
  179.0 1.6 collective-permute-start.17
  184.6 11.6 %all-to-all-start.3 = ((bf16[16,2,640]{2,1,0:T(2,128)(2,1)}), bf16[16,2,640]{2,1,0:T(2,128)(2,1)S(1)}, u32[]{:S(2)}, u32[]{:S(2)}) async-start(bf16[16,2,640]{2,1,0:T(2,128)(2,1)} %get-tuple-element.85), calls=%async_computation.3 | async-start | bytes 81920 | tf_op jit(solution)/shard_map/all_to_all | solution.py:702
  215.4 1.6 collective-permute-start.18
  217.0 5.6 %collective-permute-start.19 = (bf16[4,32,512]{2,1,0:T(8,128)(2,1)S(1)}, bf16[4,32,512]{2,1,0:T(8,128)(2,1)S(1)}, u32[]{:S(2)}, u32[]{:S(2)}) collective-permute-start(bf16[4,32,512]{2,1,0:T(8,128)(2,1)S(1)} %get-tuple-element.89.token_ref), channel_id=1, source_target_pairs={{0,2},{1,3},{2,0},{3,1},{4,6},{5,7},{6,4},{7,5},{8,10},{9,11},{10,... | collective-permute-start | bytes 393224 | tf_op jit(solution)/shard_map/ppermute | solution.py:22
  222.6 4.3 %collective-permute-start.20 = (bf16[2,32,512]{2,1,0:T(8,128)(2,1)S(1)}, bf16[2,32,512]{2,1,0:T(8,128)(2,1)S(1)}, u32[]{:S(2)}, u32[]{:S(2)}) collective-permute-start(bf16[2,32,512]{2,1,0:T(8,128)(2,1)S(1)} %get-tuple-element.93.token_ref), channel_id=1, source_target_pairs={{0,4},{1,5},{2,6},{3,7},{4,0},{5,1},{6,2},{7,3},{8,12},{9,13},{10,... | collective-permute-start | bytes 196616 | tf_op jit(solution)/shard_map/ppermute | solution.py:22
  227.0 4.9 %collective-permute-start.21 = (bf16[1,32,512]{2,1,0:T(8,128)(2,1)S(1)}, bf16[1,32,512]{2,1,0:T(8,128)(2,1)S(1)}, u32[]{:S(2)}, u32[]{:S(2)}) collective-permute-start(bf16[1,32,512]{2,1,0:T(8,128)(2,1)S(1)} %get-tuple-element.97.token_ref), channel_id=1, source_target_pairs={{0,8},{1,9},{2,10},{3,11},{4,12},{5,13},{6,14},{7,15},{8,0},{9,1},... | collective-permute-start | bytes 98312 | tf_op jit(solution)/shard_map/ppermute | solution.py:22
  231.9 5.2 %collective-permute-start.22 = (bf16[1,32,512]{2,1,0:T(8,128)(2,1)S(1)}, bf16[1,32,512]{2,1,0:T(8,128)(2,1)S(1)}, u32[]{:S(2)}, u32[]{:S(2)}) collective-permute-start(bf16[1,32,512]{2,1,0:T(8,128)(2,1)S(1)} %bitcast.64), channel_id=1, source_target_pairs={{0,8},{1,9},{2,10},{3,11},{4,12},{5,13},{6,14},{7,15},{8,0},{9,1},... | collective-permute-start | bytes 98312 | tf_op jit(solution)/shard_map/ppermute | solution.py:22
  237.1 4.3 %collective-permute-start.23 = (bf16[2,32,512]{2,1,0:T(8,128)(2,1)S(1)}, bf16[2,32,512]{2,1,0:T(8,128)(2,1)S(1)}, u32[]{:S(2)}, u32[]{:S(2)}) collective-permute-start(bf16[2,32,512]{2,1,0:T(8,128)(2,1)S(1)} %shard_map.166.low_ref), channel_id=1, source_target_pairs={{0,4},{1,5},{2,6},{3,7},{4,0},{5,1},{6,2},{7,3},{8,12},{9,13},{10,... | collective-permute-start | bytes 196616 | tf_op jit(solution)/shard_map/ppermute | solution.py:22
  241.5 5.0 %collective-permute-start.24 = (bf16[4,32,512]{2,1,0:T(8,128)(2,1)S(1)}, bf16[4,32,512]{2,1,0:T(8,128)(2,1)S(1)}, u32[]{:S(2)}, u32[]{:S(2)}) collective-permute-start(bf16[4,32,512]{2,1,0:T(8,128)(2,1)S(1)} %shard_map.167.low_ref), channel_id=1, source_target_pairs={{0,2},{1,3},{2,0},{3,1},{4,6},{5,7},{6,4},{7,5},{8,10},{9,11},{10,... | collective-permute-start | bytes 393224 | tf_op jit(solution)/shard_map/ppermute | solution.py:22
  246.5 1.6 collective-permute-start.25
  263.4 1.6 collective-permute-start.26
  (31 other events, 85.6 us)

commit v5 on v4

--- a/solution.py
+++ b/solution.py
@@ -64,9 +64,9 @@
         copy.wait()
 
 
-def fetch_kernel(pieces, token_ref, *refs):
+def fetch_kernel(pieces, tokens, *refs):
     arrays = len(pieces)
-    sems = refs[-1]
+    refs, sems = refs[tokens:-1], refs[-1]
     copies = []
     for array, (count, source, target) in enumerate(zip(pieces, refs, refs[arrays:])):
         size = source.shape[0] // count
@@ -78,19 +78,19 @@
     run_copies(copies)
 
 
-def fetch(token, *arrays):
+def fetch(tokens, *arrays):
     pieces = [8 if array.shape[0] % 128 == 0 else 1 for array in arrays]
     return pl.pallas_call(
-        functools.partial(fetch_kernel, pieces),
+        functools.partial(fetch_kernel, pieces, len(tokens)),
         out_shape=[pltpu.VMEM(array.shape, array.dtype) for array in arrays],
-        in_specs=[hbm()] * (1 + len(arrays)),
+        in_specs=[hbm()] * (len(tokens) + len(arrays)),
         out_specs=[vmem()] * len(arrays),
         scratch_shapes=[pltpu.SemaphoreType.DMA((len(arrays), 8))],
         compiler_params=pltpu.CompilerParams(vmem_limit_bytes=1 << 20),
         cost_estimate=pl.CostEstimate(
             flops=0, bytes_accessed=sum(2 * array.size for array in arrays), transcendentals=0
         ),
-    )(token, *[placed_in(array, pltpu.HBM) for array in arrays])
+    )(*tokens, *[placed_in(array, pltpu.HBM) for array in arrays])
 
 
 def fetch_caches_kernel(token_ref, where_ref, keys_ref, values_ref, key_ref, value_ref, sems):
@@ -222,8 +222,7 @@
     return jnp.sum(exchange(held).astype(jnp.float32), axis=0)
 
 
-def scatter_halving(send, keep, own, jobs):
-    got = swap(send, 1)
+def scatter_halving(keep, got, own, jobs):
     held_back = ()
     for mask in chip_masks():
         keep, send = add_parts((keep, got), 2, held_back)
@@ -232,11 +231,27 @@
     return step_call(finish_kernel, [keep.shape[1:]], (own, keep, got), held_back)[0]
 
 
-def gather_doubling(part, jobs):
+def gather(part):
+    own = exchange(jnp.broadcast_to(part[None], (lax.axis_size("mp") // 2,) + part.shape))
+    return own, swap(own, 1)
+
+
+def hop(part, mask):
+    count = lax.axis_size("mp")
+    pairs = [(source, (source + count) % (2 * count) ^ mask) for source in range(2 * count)]
+    return lax.ppermute(part, ("section", "mp"), pairs)
+
+
+def gather_doubling(part, jobs, hops):
     held = part[None]
-    for mask in reversed(chip_masks()):
-        got = swap(held, mask)
-        held = join(held, got, run_job(jobs, held))
+    for step, mask in enumerate(reversed(chip_masks())):
+        job_token = held
+        if hops and step == 0:
+            got = hop(held, mask)
+            held = hop(held, 0)
+        else:
+            got = swap(held, mask)
+        held = join(held, got, run_job(jobs, job_token))
     return held, swap(held, 1)
 
 
@@ -452,43 +467,44 @@
     )
 
 
-def spread_kernel(ids_ref, x_ref, w_ref, keep_ref, send_ref, values):
-    half, rows, chunk = keep_ref.shape
+def spread_kernel(ids_ref, x_ref, w_ref, out_ref, values):
+    parts, rows, chunk = out_ref.shape
     count, rows_dev, _ = x_ref.shape
     for owner in range(count):
         values[owner * rows_dev : (owner + 1) * rows_dev, :] = x_ref[owner].astype(jnp.float32)
     ready = values[...].astype(jnp.bfloat16)
-    for first, target in ((0, keep_ref), (half, send_ref)):
-
-        @pl.loop(0, half // UNROLL)
-        def _(group):
-            for step in range(UNROLL):
-                k = group * UNROLL + step
-                span = span_of(ids_ref, first + k, chunk)
-                target[k] = jnp.dot(
-                    ready, w_ref[:, span], preferred_element_type=jnp.float32
-                ).astype(jnp.bfloat16)
+
+    @pl.loop(0, parts // UNROLL)
+    def _(group):
+        for step in range(UNROLL):
+            k = group * UNROLL + step
+            span = span_of(ids_ref, k, chunk)
+            out_ref[k] = jnp.dot(
+                ready, w_ref[:, span], preferred_element_type=jnp.float32
+            ).astype(jnp.bfloat16)
 
 
 def spread_project(ids, values, weights):
     count, rows_dev, depth = values.shape
     rows = count * rows_dev
-    width = weights.shape[1]
-    shape = pltpu.VMEM((count // 2, rows, width // count), jnp.bfloat16)
+    chunk = weights.shape[1] // count
+    parts = ids.shape[0]
     return pl.pallas_call(
         spread_kernel,
-        out_shape=(shape, shape),
+        out_shape=pltpu.VMEM((parts, rows, chunk), jnp.bfloat16),
         in_specs=[smem(), vmem(), vmem()],
-        out_specs=(vmem(), vmem()),
+        out_specs=vmem(),
         scratch_shapes=[pltpu.VMEM((rows, depth), jnp.float32)],
         compiler_params=pltpu.CompilerParams(vmem_limit_bytes=4 << 20),
         cost_estimate=pl.CostEstimate(
-            flops=2 * rows * depth * width, bytes_accessed=2 * depth * width, transcendentals=0
+            flops=2 * rows * depth * parts * chunk,
+            bytes_accessed=2 * depth * parts * chunk,
+            transcendentals=0,
         ),
     )(ids, values, placed_in(weights, pltpu.VMEM))
 
 
-def mlp_kernel(by_rows, ids_ref, out_ids_ref, own_ref, other_ref, gain_ref, down_hbm, *refs):
+def mlp_kernel(by_rows, me_ref, ids_ref, own_ref, other_ref, gain_ref, down_hbm, *refs):
     pairs, (keep_ref, send_ref, middle_ref), (stacked, wide_x, total, act, down_ref, sems) = (
         refs[:-9],
         refs[-9:-6],
@@ -500,7 +516,7 @@
 
     def down_copy(k):
         return pltpu.make_async_copy(
-            down_hbm.at[:, span_of(out_ids_ref, k, chunk)], down_ref.at[lax.rem(k, half)], sems.at[k]
+            down_hbm.at[:, span_of(ids_ref, k, chunk)], down_ref.at[lax.rem(k, half)], sems.at[k]
         )
 
     @pl.loop(0, half)
@@ -527,7 +543,7 @@
                 wide = x_ref[place].astype(jnp.float32)
                 span = span_of(ids_ref, first + place, chunk)
                 for row in range(rows_dev):
-                    here = line == ids_ref[0] * rows_dev + row
+                    here = line == me_ref[0] * rows_dev + row
                     middle_ref[row : row + 1, span] = jnp.sum(
                         jnp.where(here, wide, 0.0), axis=0, keepdims=True
                     )
@@ -583,8 +599,8 @@
                 if not by_rows:
                     target[k] = part.astype(jnp.bfloat16)
                     continue
-                span = span_of(out_ids_ref, first + k, chunk)
-                first_core = out_ids_ref[0] == 0
+                span = span_of(ids_ref, first + k, chunk)
+                first_core = ids_ref[0] == 0
                 for chip in range(half):
                     at = 2 * chip * rows_dev
                     low = part[at : at + rows_dev]
@@ -596,7 +612,7 @@
                     down_copy(half + group * UNROLL + step).start()
 
 
-def mlp(ids, out_ids, own, other, gain, pairs, down, by_rows):
+def mlp(me, ids, own, other, gain, pairs, down, by_rows):
     half, rows, chunk = own.shape
     units, width = down.shape
     part = (half, rows // (2 * half), width) if by_rows else own.shape
@@ -621,8 +637,8 @@
             flops=6 * rows * units * width, bytes_accessed=6 * units * width, transcendentals=0
         ),
     )(
+        me,
         ids,
-        out_ids,
         own,
         other,
         gain,
@@ -664,25 +680,34 @@
     chips = 2 * jnp.arange(half, dtype=jnp.int32)
     ids = jnp.concatenate([chips + core, chips + 1 - core])
     near = jnp.asarray(relative_ids())
-    places = jnp.concatenate([near ^ model_index, near ^ model_index ^ 1])
+    near_places, far_places = near ^ model_index, near ^ model_index ^ 1
+    places = jnp.concatenate([near_places, far_places])
     wk = w_key[0].T
     wv = w_value[0].T
     blocks = w_gate_up.shape[3] // 128
-    share = max(blocks // 4, 1)
+    windows = len(chip_masks())
+    bounds = [-(-blocks * step // windows) for step in range(windows + 1)]
     batches = [
         jnp.remainder(section_index + turn_index, 2).astype(jnp.int32).reshape(1)
         for turn_index in range(2)
     ]
 
+    tables = [
+        turning(lax.dynamic_index_in_dim(lengths, batch[0], 0, keepdims=False))
+        for batch in batches
+    ]
+    me = model_index.astype(jnp.int32).reshape(1)
+    early = (ids, places, near_places, far_places, me, *batches, *tables[0], *tables[1])
+
     def attention_jobs(turn_index):
         got = {}
 
         def projections(token):
-            got["qkv"] = fetch(token, w_query[0], wk, wv)
+            got["qkv"] = fetch((token, *early), w_query[0], wk, wv)
             return got["qkv"]
 
         def out_projection(token):
-            got["out"] = fetch(token, w_out[0])
+            got["out"] = fetch((token,), w_out[0])
             return got["out"]
 
         def caches(token):
@@ -692,40 +717,41 @@
         return got, [projections, out_projection, caches]
 
     got, jobs = attention_jobs(0)
-    own, other = gather_doubling(hidden[0], jobs)
+    own, other = gather_doubling(hidden[0], jobs, False)
     mine = None
     for turn_index in range(2):
         last = turn_index == 1
         batch = batches[turn_index]
-        cosine, sine = turning(lax.dynamic_index_in_dim(lengths, batch[0], 0, keepdims=False))
         joined, by_owner = project(places, own, other, attn_gain, *got["qkv"])
         spread = lax.all_to_all(joined, "mp", split_axis=0, concat_axis=0)
         mixed = attend(
-            batch, lengths, spread, cosine, sine, *got["caches"], w_query.shape[2]
+            batch, lengths, spread, *tables[turn_index], *got["caches"], w_query.shape[2]
         )
         heads_out = lax.all_to_all(mixed.transpose(1, 0, 2), "mp", split_axis=0, concat_axis=0)
-        keep, send = spread_project(places, heads_out, *got["out"])
+        got_core = swap(spread_project(far_places, heads_out, *got["out"]), 1)
+        keep = spread_project(near_places, heads_out, *got["out"])
         pairs = []
 
-        def pair_job(first):
+        def pair_job(first, size):
             def job(token):
-                pairs.extend(fetch_pairs(token, w_gate_up[0], first, share))
-                return pairs[-share:]
+                new = fetch_pairs(token, w_gate_up[0], first, size) if size else ()
+                pairs.extend(new)
+                return new
 
             return job
 
-        jobs = [pair_job(first) for first in range(0, blocks, share)]
-        middle = scatter_halving(send, keep, by_owner if mine is None else mine, jobs)
-        own, other = gather_doubling(middle, jobs)
-        keep, send, own_rows = mlp(places, ids, own, other, mlp_gain, pairs, w_down[0], last)
+        jobs = [pair_job(low, high - low) for low, high in zip(bounds, bounds[1:])]
+        middle = scatter_halving(keep, got_core, by_owner if mine is None else mine, jobs)
+        own, other = gather(middle)
+        keep, send, own_rows = mlp(me, ids, own, other, mlp_gain, pairs, w_down[0], last)
         mlp_part = scatter(send, keep)
         if last:
             middle = own_rows
         mine = (middle.astype(jnp.float32) + mlp_part).astype(jnp.bfloat16)
         if not last:
             got, jobs = attention_jobs(1)
-            mine = swap(mine, 1, "section")
-            own, other = gather_doubling(mine, jobs)
+            own, other = gather_doubling(mine, jobs, True)
+            mine = own[0]
     return mine[None]
 
 

time: 280 us -> 221 us (0.79)
  local copies, waits for them, and re-layouts: 53.9 us -> 0.89 us
  blocking collectives: 43.9 us -> 90.3 us
  waiting for transfers between devices: 49 us -> 14 us
  starting transfers between devices: 32.8 us -> 16.2 us
    unnamed x68 -> x10, local copies, waits for them, and re-layouts: 53.8 us -> 0.78 us
    all_to_all x2 -> x4, blocking collectives: 25.4 us -> 51.1 us  [exchange(): lax.all_to_all(parts, 'mp', split_axis=0, concat_axis=0, axis_index_group...]
    ppermute x27 -> x19, waiting for transfers between devices: 35.8 us -> 14 us  [swap(): lax.ppermute(value, axis, [(source, source ^ mask) for source in range(co...]
    all_to_all x0 -> x2, blocking collectives: none -> 20.9 us  [body(): spread = lax.all_to_all(joined, 'mp', split_axis=0, concat_axis=0)]
    all_to_all x2 -> x0, waiting for transfers between devices: 13.2 us -> none  [body(): spread = lax.all_to_all(joined, 'mp', split_axis=0, concat_axis=0)]
    ppermute x27 -> x19, starting transfers between devices: 24.4 us -> 13.6 us  [swap(): lax.ppermute(value, axis, [(source, source ^ mask) for source in range(co...]
    all_to_all x2 -> x0, starting transfers between devices: 8.42 us -> none  [body(): spread = lax.all_to_all(joined, 'mp', split_axis=0, concat_axis=0)]
    pallas_call x8 -> x6, Pallas kernels: 28 us -> 26.2 us  [fetch_pairs(): pl.pallas_call(functools.partial(fetch_pairs_kernel, first), out_shape=[p...]
  transfers between devices with their start and end apart: 29 -> 21, of which waited for: 24 -> 13; matrix products, arithmetic and copies ran while one was open for 0% -> 1% of each run, Pallas kernels for 17% -> 22%
where the time goes in v5:
time: 221 us; the launch traced here: 220 us
  Pallas kernels  95.4 us (43%)
  blocking collectives  90.3 us (41%)
  starting transfers between devices  16.2 us (7%)
  waiting for transfers between devices  14 us (6%)
  other arithmetic  2.78 us (1%)
    all_to_all x4, blocking collectives, exchange(): lax.all_to_all(parts, 'mp', split_axis=0, concat_axis=0, axis_index_group...  51.1 us
    pallas_call x2, Pallas kernels, mlp(): pl.pallas_call(functools.partial(mlp_kernel, by_rows), out_shape=(shape,...  30.2 us
    pallas_call x6, Pallas kernels, fetch_pairs(): pl.pallas_call(functools.partial(fetch_pairs_kernel, first), out_shape=[p...  26.2 us
    all_to_all x2, blocking collectives, body(): spread = lax.all_to_all(joined, 'mp', split_axis=0, concat_axis=0)  20.9 us
    all_to_all x2, blocking collectives, body(): lax.all_to_all(mixed.transpose(1, 0, 2), 'mp', split_axis=0, concat_axis=0)  18.4 us
    pallas_call x4, Pallas kernels, fetch(): pl.pallas_call(functools.partial(fetch_kernel, pieces, len(tokens)), out_...  15.5 us
    ppermute x19, waiting for transfers between devices, swap(): lax.ppermute(value, axis, [(source, source ^ mask) for source in range(co...  14 us
    ppermute x19, starting transfers between devices, swap(): lax.ppermute(value, axis, [(source, source ^ mask) for source in range(co...  13.6 us
  transfers between devices with their start and end apart: 21, of which 13 were waited for; matrix products, arithmetic and copies ran while one was open for 1% of the time, Pallas kernels for 22%

profile of v5, /device:TPU:0, one launch (start us, length us, event | category | flops | bytes accessed | tf_op | source)
XLA Modules:
  0.0 220.0 jit_solution(4765665570030732031)
XLA Ops:
  0.0 4.0 %collective-permute-start = (bf16[1,2,8192]{2,1,0:T(2,128)(2,1)}, bf16[1,2,8192]{2,1,0:T(2,128)(2,1)S(1)}, u32[]{:S(2)}, u32[]{:S(2)}) collective-permute-start(bf16[1,2,8192]{2,1,0:T(2,128)(2,1)} %low_ref.1), channel_id=1, source_target_pairs={{0,8},{1,9},{2,10},{3,11},{4,12},{5,13},{6,14},{7,15},{8,0},{9,1},... | collective-permute-start | bytes 98312 | tf_op jit(solution)/shard_map/ppermute | solution.py:22
  6.7 4.3 %shard_map.127 = (bf16[8192,512]{1,0:T(8,128)(2,1)S(1)}, bf16[64,8192]{1,0:T(8,128)(2,1)S(1)}, bf16[64,8192]{1,0:T(8,128)(2,1)S(1)}) custom-call(bf16[1,2,8192]{2,1,0:T(2,128)(2,1)S(1)} %copy-done.2, s32[16]{0:T(128)S(1)} %pad_add_fusion.refs_1_.ids_ref, s32[16]{0:T(128)S(1)} %pad_add_fusion.1.refs_2_.ids_ref, s32[8]{0:T(128)S(1)} %get-tuple-element.108.refs_3_.ids_ref, ...), custom_call_target="tpu_custom_call" | custom-call | bytes 10485760 | tf_op jit(solution)/shard_map/pallas_call | solution.py:83
  11.0 1.6 collective-permute-start.1
  12.6 3.5 %shard_map.129.refs_0_.w_ref = bf16[512,8192]{1,0:T(8,128)(2,1)S(1)} custom-call(bf16[2,2,8192]{2,1,0:T(2,128)(2,1)S(1)} %shard_map.128.refs_0_.low_ref, bf16[512,8192]{1,0:T(8,128)(2,1)} %bitcast.73), custom_call_target="tpu_custom_call" | custom-call | bytes 8388608 | tf_op jit(solution)/shard_map/pallas_call | solution.py:83
  16.2 1.6 collective-permute-start.2
  17.8 2.2 %shard_map.131 = (bf16[2,512,1024]{2,1,0:T(8,128)(2,1)S(1)}, bf16[2,512,1024]{2,1,0:T(8,128)(2,1)S(1)}) custom-call(bf16[4,2,8192]{2,1,0:T(2,128)(2,1)S(1)} %shard_map.130.token_ref.low_ref, s32[1]{0:T(128)} %bitcast.1.refs_6_.where_ref, bf16[2,2,512,1024]{3,2,1,0:T(8,128)(2,1)} %bitcast.75, bf16[2,2,512,1024]{3,2,1,0:T(8,128)(2,1)} %bitcast.77), custom_call_target="tpu_custom_call" | custom-call | bytes 4194304 | tf_op jit(solution)/shard_map/pallas_call | solution.py:116
  22.8 3.6 %shard_map.133 = (bf16[16,2,640]{2,1,0:T(2,128)(2,1)S(1)}, bf16[16,2,512]{2,1,0:T(2,128)(2,1)S(1)}) custom-call(s32[16]{0:T(128)S(1)} %pad_add_fusion.1.refs_2_.ids_ref, bf16[8,2,8192]{2,1,0:T(2,128)(2,1)S(1)} %shard_map.132.own_ref, bf16[8,2,8192]{2,1,0:T(2,128)(2,1)S(1)} %collective-permute-done.3.other_ref, f32[1,8192]{1,0:T(1,128)S(1)} %copy-done, ...), custom_call_target="tpu_custom_call" | custom-call | flops 335544320 | bytes 10485760 | tf_op jit(solution)/shard_map/pallas_call | solution.py:346
  26.5 9.6 %all_to_all.40.in_ref = bf16[16,2,640]{2,1,0:T(2,128)(2,1)S(1)} all-to-all(bf16[16,2,640]{2,1,0:T(2,128)(2,1)S(1)} %get-tuple-element.57), channel_id=1, replica_groups=mesh['section'=2,'mp'=16] {'mp'}, dimensions={0} | all-to-all | bytes 81920 | tf_op jit(solution)/shard_map/all_to_all | solution.py:726
  36.1 2.5 %shard_map.134 = bf16[2,16,512]{2,1,0:T(8,128)(2,1)S(1)} custom-call(s32[1]{0:T(128)} %bitcast.1.refs_6_.where_ref, s32[2,2]{1,0:T(2,128)S(1)} %copy-done.4, bf16[16,2,640]{2,1,0:T(2,128)(2,1)S(1)} %all_to_all.40.in_ref, f32[2,128]{1,0:T(2,128)S(1)} %get-tuple-element.112.refs_8_.cos_ref, f32[2,128]{1,0:T(2,128)S(1)} %get-tuple-element.113.refs_9_.sin_ref, ...), custom_call_target="tpu_custom_call" | custom-call | flops 268435456 | bytes 4194304 | tf_op jit(solution)/shard_map/pallas_call | solution.py:444
  38.6 9.2 %all_to_all.41.x_ref = bf16[16,2,512]{2,1,0:T(2,128)(2,1)S(1)} all-to-all(bf16[16,2,512]{2,1,0:T(2,128)(2,1)S(1)} %bitcast.83), channel_id=1, replica_groups=mesh['section'=2,'mp'=16] {'mp'}, dimensions={0} | all-to-all | bytes 65536 | tf_op jit(solution)/shard_map/all_to_all | solution.py:730
  51.4 4.8 %shard_map.138 = (bf16[8192,2,128]{2,1,0:T(2,128)(2,1)S(1)}, bf16[8192,2,128]{2,1,0:T(2,128)(2,1)S(1)}, bf16[8192,2,128]{2,1,0:T(2,128)(2,1)S(1)}) custom-call(bf16[4,32,512]{2,1,0:T(8,128)(2,1)S(1)} %get-tuple-element.59.token_ref, bf16[8192,2,1024]{2,1,0:T(2,128)(2,1)} %bitcast.63), custom_call_target="tpu_custom_call" | custom-call | bytes 12582912 | tf_op jit(solution)/shard_map/pallas_call | solution.py:148
  57.3 4.8 %shard_map.140 = (bf16[8192,2,128]{2,1,0:T(2,128)(2,1)S(1)}, bf16[8192,2,128]{2,1,0:T(2,128)(2,1)S(1)}, bf16[8192,2,128]{2,1,0:T(2,128)(2,1)S(1)}) custom-call(bf16[2,32,512]{2,1,0:T(8,128)(2,1)S(1)} %get-tuple-element.64.token_ref, bf16[8192,2,1024]{2,1,0:T(2,128)(2,1)} %bitcast.64), custom_call_target="tpu_custom_call" | custom-call | bytes 12582912 | tf_op jit(solution)/shard_map/pallas_call | solution.py:148
  63.0 3.5 %shard_map.142 = (bf16[8192,2,128]{2,1,0:T(2,128)(2,1)S(1)}, bf16[8192,2,128]{2,1,0:T(2,128)(2,1)S(1)}) custom-call(bf16[1,32,512]{2,1,0:T(8,128)(2,1)S(1)} %get-tuple-element.69.token_ref, bf16[8192,2,1024]{2,1,0:T(2,128)(2,1)} %bitcast.65), custom_call_target="tpu_custom_call" | custom-call | bytes 8388608 | tf_op jit(solution)/shard_map/pallas_call | solution.py:148
  67.1 12.9 %all_to_all.42.own_ref = bf16[8,32,512]{2,1,0:T(8,128)(2,1)S(1)} all-to-all(bf16[8,32,512]{2,1,0:T(8,128)(2,1)S(1)} %broadcast_in_dim.8), channel_id=1, replica_groups={{0,2,4,6,8,10,12,14},{1,3,5,7,9,11,13,15},{16,18,20,22,24,26,28,30},{17..., dimensions={0} | all-to-all | bytes 524288 | tf_op jit(solution)/shard_map/all_to_all | solution.py:28
  80.1 1.5 collective-permute-done.8.other_ref
  81.6 15.0 %shard_map.144 = (bf16[8,32,512]{2,1,0:T(8,128)(2,1)S(1)}, bf16[8,32,512]{2,1,0:T(8,128)(2,1)S(1)}, f32[2,8192]{1,0:T(2,128)}) custom-call(s32[1]{0:T(128)} %bitcast.refs_5_.me_ref, s32[16]{0:T(128)S(1)} %pad_add_fusion.refs_1_.ids_ref, bf16[8,32,512]{2,1,0:T(8,128)(2,1)S(1)} %all_to_all.42.own_ref, ...), custom_call_target="tpu_custom_call" | custom-call | flops 1610612736 | bytes 50331648 | tf_op jit(solution)/shard_map/pallas_call | solution.py:620
  98.3 12.6 %all_to_all.43 = bf16[8,32,512]{2,1,0:T(8,128)(2,1)S(1)} all-to-all(bf16[8,32,512]{2,1,0:T(8,128)(2,1)S(1)} %shard_map.145), channel_id=1, replica_groups={{0,2,4,6,8,10,12,14},{1,3,5,7,9,11,13,15},{16,18,20,22,24,26,28,30},{17..., dimensions={0} | all-to-all | bytes 524288 | tf_op jit(solution)/shard_map/all_to_all | solution.py:28
  111.0 2.0 collective-permute-start.11
  113.6 4.3 %shard_map.146 = (bf16[8192,512]{1,0:T(8,128)(2,1)S(1)}, bf16[64,8192]{1,0:T(8,128)(2,1)S(1)}, bf16[64,8192]{1,0:T(8,128)(2,1)S(1)}) custom-call(bf16[1,32,512]{2,1,0:T(8,128)(2,1)S(1)} %fusion.refs_0_, s32[16]{0:T(128)S(1)} %pad_add_fusion.refs_1_.ids_ref, s32[16]{0:T(128)S(1)} %pad_add_fusion.1.refs_2_.ids_ref, s32[8]{0:T(128)S(1)} %get-tuple-element.108.refs_3_.ids_ref, ...), custom_call_target="tpu_custom_call" | custom-call | bytes 10485760 | tf_op jit(solution)/shard_map/pallas_call | solution.py:83
  118.6 3.5 %shard_map.148.refs_0_.w_ref = bf16[512,8192]{1,0:T(8,128)(2,1)S(1)} custom-call(bf16[2,32,512]{2,1,0:T(8,128)(2,1)S(1)} %shard_map.147.refs_0_.low_ref, bf16[512,8192]{1,0:T(8,128)(2,1)} %bitcast.74), custom_call_target="tpu_custom_call" | custom-call | bytes 8388608 | tf_op jit(solution)/shard_map/pallas_call | solution.py:83
  122.2 1.7 collective-permute-start.13
  123.9 2.2 %shard_map.150 = (bf16[2,512,1024]{2,1,0:T(8,128)(2,1)S(1)}, bf16[2,512,1024]{2,1,0:T(8,128)(2,1)S(1)}) custom-call(bf16[4,32,512]{2,1,0:T(8,128)(2,1)S(1)} %shard_map.149.token_ref.low_ref, s32[1]{0:T(128)} %bitcast.2.refs_7_.where_ref, bf16[2,2,512,1024]{3,2,1,0:T(8,128)(2,1)} %bitcast.76, bf16[2,2,512,1024]{3,2,1,0:T(8,128)(2,1)} %bitcast.78), custom_call_target="tpu_custom_call" | custom-call | bytes 4194304 | tf_op jit(solution)/shard_map/pallas_call | solution.py:116
  128.9 3.8 %shard_map.152 = (bf16[16,2,640]{2,1,0:T(2,128)(2,1)S(1)}, bf16[16,2,512]{2,1,0:T(2,128)(2,1)}) custom-call(s32[16]{0:T(128)S(1)} %pad_add_fusion.1.refs_2_.ids_ref, bf16[8,32,512]{2,1,0:T(8,128)(2,1)S(1)} %shard_map.151.own_ref, bf16[8,32,512]{2,1,0:T(8,128)(2,1)S(1)} %collective-permute-done.14.other_ref, f32[1,8192]{1,0:T(1,128)S(1)} %copy-done, ...), custom_call_target="tpu_custom_call" | custom-call | flops 335544320 | bytes 10485760 | tf_op jit(solution)/shard_map/pallas_call | solution.py:346
  132.7 11.3 %all_to_all.44.in_ref = bf16[16,2,640]{2,1,0:T(2,128)(2,1)S(1)} all-to-all(bf16[16,2,640]{2,1,0:T(2,128)(2,1)S(1)} %get-tuple-element.79), channel_id=1, replica_groups=mesh['section'=2,'mp'=16] {'mp'}, dimensions={0} | all-to-all | bytes 81920 | tf_op jit(solution)/shard_map/all_to_all | solution.py:726
  144.0 2.5 %shard_map.153 = bf16[2,16,512]{2,1,0:T(8,128)(2,1)S(1)} custom-call(s32[1]{0:T(128)} %bitcast.2.refs_7_.where_ref, s32[2,2]{1,0:T(2,128)S(1)} %copy-done.4, bf16[16,2,640]{2,1,0:T(2,128)(2,1)S(1)} %all_to_all.44.in_ref, f32[2,128]{1,0:T(2,128)S(1)} %get-tuple-element.114.refs_10_.cos_ref, f32[2,128]{1,0:T(2,128)S(1)} %get-tuple-element.115.refs_11_.sin_ref, ...), custom_call_target="tpu_custom_call" | custom-call | flops 268435456 | bytes 4194304 | tf_op jit(solution)/shard_map/pallas_call | solution.py:444
  146.5 9.2 %all_to_all.45.x_ref = bf16[16,2,512]{2,1,0:T(2,128)(2,1)S(1)} all-to-all(bf16[16,2,512]{2,1,0:T(2,128)(2,1)S(1)} %bitcast.84), channel_id=1, replica_groups=mesh['section'=2,'mp'=16] {'mp'}, dimensions={0} | all-to-all | bytes 65536 | tf_op jit(solution)/shard_map/all_to_all | solution.py:730
  159.3 4.8 %shard_map.157 = (bf16[8192,2,128]{2,1,0:T(2,128)(2,1)S(1)}, bf16[8192,2,128]{2,1,0:T(2,128)(2,1)S(1)}, bf16[8192,2,128]{2,1,0:T(2,128)(2,1)S(1)}) custom-call(bf16[4,32,512]{2,1,0:T(8,128)(2,1)S(1)} %get-tuple-element.81.token_ref, bf16[8192,2,1024]{2,1,0:T(2,128)(2,1)} %bitcast.66), custom_call_target="tpu_custom_call" | custom-call | bytes 12582912 | tf_op jit(solution)/shard_map/pallas_call | solution.py:148
  165.3 4.8 %shard_map.159 = (bf16[8192,2,128]{2,1,0:T(2,128)(2,1)S(1)}, bf16[8192,2,128]{2,1,0:T(2,128)(2,1)S(1)}, bf16[8192,2,128]{2,1,0:T(2,128)(2,1)S(1)}) custom-call(bf16[2,32,512]{2,1,0:T(8,128)(2,1)S(1)} %get-tuple-element.86.token_ref, bf16[8192,2,1024]{2,1,0:T(2,128)(2,1)} %bitcast.67), custom_call_target="tpu_custom_call" | custom-call | bytes 12582912 | tf_op jit(solution)/shard_map/pallas_call | solution.py:148
  170.9 3.5 %shard_map.161 = (bf16[8192,2,128]{2,1,0:T(2,128)(2,1)S(1)}, bf16[8192,2,128]{2,1,0:T(2,128)(2,1)S(1)}) custom-call(bf16[1,32,512]{2,1,0:T(8,128)(2,1)S(1)} %get-tuple-element.91.token_ref, bf16[8192,2,1024]{2,1,0:T(2,128)(2,1)} %bitcast.68), custom_call_target="tpu_custom_call" | custom-call | bytes 8388608 | tf_op jit(solution)/shard_map/pallas_call | solution.py:148
  175.1 12.9 %all_to_all.46.own_ref = bf16[8,32,512]{2,1,0:T(8,128)(2,1)S(1)} all-to-all(bf16[8,32,512]{2,1,0:T(8,128)(2,1)S(1)} %broadcast_in_dim.10), channel_id=1, replica_groups={{0,2,4,6,8,10,12,14},{1,3,5,7,9,11,13,15},{16,18,20,22,24,26,28,30},{17..., dimensions={0} | all-to-all | bytes 524288 | tf_op jit(solution)/shard_map/all_to_all | solution.py:28
  189.5 15.2 %shard_map.163 = (bf16[8,2,8192]{2,1,0:T(2,128)(2,1)S(1)}, bf16[8,2,8192]{2,1,0:T(2,128)(2,1)S(1)}, f32[2,8192]{1,0:T(2,128)S(1)}) custom-call(s32[1]{0:T(128)} %bitcast.refs_5_.me_ref, s32[16]{0:T(128)S(1)} %pad_add_fusion.refs_1_.ids_ref, bf16[8,32,512]{2,1,0:T(8,128)(2,1)S(1)} %all_to_all.46.own_ref, ...), custom_call_target="tpu_custom_call" | custom-call | flops 1610612736 | bytes 50331648 | tf_op jit(solution)/shard_map/pallas_call | solution.py:620
  206.6 12.6 %all_to_all.47 = bf16[8,2,8192]{2,1,0:T(2,128)(2,1)S(1)} all-to-all(bf16[8,2,8192]{2,1,0:T(2,128)(2,1)S(1)} %shard_map.164), channel_id=1, replica_groups={{0,2,4,6,8,10,12,14},{1,3,5,7,9,11,13,15},{16,18,20,22,24,26,28,30},{17..., dimensions={0} | all-to-all | bytes 524288 | tf_op jit(solution)/shard_map/all_to_all | solution.py:28
  (84 shorter events, 28.0 us)
Async XLA Ops:
  0.0 11.0 %collective-permute-start = (bf16[1,2,8192]{2,1,0:T(2,128)(2,1)}, bf16[1,2,8192]{2,1,0:T(2,128)(2,1)S(1)}, u32[]{:S(2)}, u32[]{:S(2)}) collective-permute-start(bf16[1,2,8192]{2,1,0:T(2,128)(2,1)} %low_ref.1), channel_id=1, source_target_pairs={{0,8},{1,9},{2,10},{3,11},{4,12},{5,13},{6,14},{7,15},{8,0},{9,1},... | collective-permute-start | bytes 98312 | tf_op jit(solution)/shard_map/ppermute | solution.py:22
  5.9 0.8 copy-start.2
  6.7 4.3 %copy-start.3 = (bf16[1,2,8192]{2,1,0:T(2,128)(2,1)S(1)}, bf16[1,2,8192]{2,1,0:T(2,128)(2,1)}, u32[]{:S(2)}) copy-start(bf16[1,2,8192]{2,1,0:T(2,128)(2,1)} %low_ref.1) | copy-start | bytes 98308
  11.0 5.2 %collective-permute-start.1 = (bf16[2,2,8192]{2,1,0:T(2,128)(2,1)S(1)}, bf16[2,2,8192]{2,1,0:T(2,128)(2,1)S(1)}, u32[]{:S(2)}, u32[]{:S(2)}) collective-permute-start(bf16[2,2,8192]{2,1,0:T(2,128)(2,1)S(1)} %shard_map.128.refs_0_.low_ref), channel_id=1, source_target_pairs={{0,4},{1,5},{2,6},{3,7},{4,0},{5,1},{6,2},{7,3},{8,12},{9,13},{10,... | collective-permute-start | bytes 196616 | tf_op jit(solution)/shard_map/ppermute | solution.py:22
  16.2 5.0 %collective-permute-start.2 = (bf16[4,2,8192]{2,1,0:T(2,128)(2,1)S(1)}, bf16[4,2,8192]{2,1,0:T(2,128)(2,1)S(1)}, u32[]{:S(2)}, u32[]{:S(2)}) collective-permute-start(bf16[4,2,8192]{2,1,0:T(2,128)(2,1)S(1)} %shard_map.130.token_ref.low_ref), channel_id=1, source_target_pairs={{0,2},{1,3},{2,0},{3,1},{4,6},{5,7},{6,4},{7,5},{8,10},{9,11},{10,... | collective-permute-start | bytes 393224 | tf_op jit(solution)/shard_map/ppermute | solution.py:22
  20.0 2.9 %copy-start = (f32[1,8192]{1,0:T(1,128)S(1)}, f32[1,8192]{1,0:T(1,128)}, u32[]{:S(2)}) copy-start(f32[1,8192]{1,0:T(1,128)} %gain_ref.6) | copy-start | bytes 98308
  21.2 14.8 %copy-start.4 = (s32[2,2]{1,0:T(2,128)S(1)}, s32[2,2]{1,0:T(2,128)}, u32[]{:S(2)}) copy-start(s32[2,2]{1,0:T(2,128)} %length_ref.3) | copy-start | bytes 52
  21.2 1.6 collective-permute-start.3
  49.3 1.6 collective-permute-start.4
  50.9 6.0 %collective-permute-start.5 = (bf16[4,32,512]{2,1,0:T(8,128)(2,1)S(1)}, bf16[4,32,512]{2,1,0:T(8,128)(2,1)S(1)}, u32[]{:S(2)}, u32[]{:S(2)}) collective-permute-start(bf16[4,32,512]{2,1,0:T(8,128)(2,1)S(1)} %get-tuple-element.59.token_ref), channel_id=1, source_target_pairs={{0,2},{1,3},{2,0},{3,1},{4,6},{5,7},{6,4},{7,5},{8,10},{9,11},{10,... | collective-permute-start | bytes 393224 | tf_op jit(solution)/shard_map/ppermute | solution.py:22
  56.9 5.2 %collective-permute-start.6 = (bf16[2,32,512]{2,1,0:T(8,128)(2,1)S(1)}, bf16[2,32,512]{2,1,0:T(8,128)(2,1)S(1)}, u32[]{:S(2)}, u32[]{:S(2)}) collective-permute-start(bf16[2,32,512]{2,1,0:T(8,128)(2,1)S(1)} %get-tuple-element.64.token_ref), channel_id=1, source_target_pairs={{0,4},{1,5},{2,6},{3,7},{4,0},{5,1},{6,2},{7,3},{8,12},{9,13},{10,... | collective-permute-start | bytes 196616 | tf_op jit(solution)/shard_map/ppermute | solution.py:22
  62.2 4.9 %collective-permute-start.7 = (bf16[1,32,512]{2,1,0:T(8,128)(2,1)S(1)}, bf16[1,32,512]{2,1,0:T(8,128)(2,1)S(1)}, u32[]{:S(2)}, u32[]{:S(2)}) collective-permute-start(bf16[1,32,512]{2,1,0:T(8,128)(2,1)S(1)} %get-tuple-element.69.token_ref), channel_id=1, source_target_pairs={{0,8},{1,9},{2,10},{3,11},{4,12},{5,13},{6,14},{7,15},{8,0},{9,1},... | collective-permute-start | bytes 98312 | tf_op jit(solution)/shard_map/ppermute | solution.py:22
  67.1 14.5 %copy-start.1 = (f32[1,8192]{1,0:T(1,128)S(1)}, f32[1,8192]{1,0:T(1,128)}, u32[]{:S(2)}) copy-start(f32[1,8192]{1,0:T(1,128)} %gain_ref.7) | copy-start | bytes 98308
  80.1 1.5 collective-permute-start.8
  96.7 1.6 collective-permute-start.9
  111.0 6.9 %collective-permute-start.11 = (bf16[1,32,512]{2,1,0:T(8,128)(2,1)S(1)}, bf16[1,32,512]{2,1,0:T(8,128)(2,1)S(1)}, u32[]{:S(2)}, u32[]{:S(2)}) collective-permute-start(bf16[1,32,512]{2,1,0:T(8,128)(2,1)S(1)} %fusion.refs_0_), channel_id=1, source_target_pairs={{0,24},{1,25},{2,26},{3,27},{4,28},{5,29},{6,30},{7,31},{8,16},{9,... | collective-permute-start | bytes 98312 | tf_op jit(solution)/shard_map/ppermute | solution.py:242
  113.0 4.8 %collective-permute-start.10 = (bf16[1,32,512]{2,1,0:T(8,128)(2,1)S(1)}, bf16[1,32,512]{2,1,0:T(8,128)(2,1)S(1)}, u32[]{:S(2)}, u32[]{:S(2)}) collective-permute-start(bf16[1,32,512]{2,1,0:T(8,128)(2,1)S(1)} %fusion.refs_0_), channel_id=1, source_target_pairs={{0,16},{1,17},{2,18},{3,19},{4,20},{5,21},{6,22},{7,23},{8,24},{9,... | collective-permute-start | bytes 98312 | tf_op jit(solution)/shard_map/ppermute | solution.py:242
  117.9 4.3 %collective-permute-start.12 = (bf16[2,32,512]{2,1,0:T(8,128)(2,1)S(1)}, bf16[2,32,512]{2,1,0:T(8,128)(2,1)S(1)}, u32[]{:S(2)}, u32[]{:S(2)}) collective-permute-start(bf16[2,32,512]{2,1,0:T(8,128)(2,1)S(1)} %shard_map.147.refs_0_.low_ref), channel_id=1, source_target_pairs={{0,4},{1,5},{2,6},{3,7},{4,0},{5,1},{6,2},{7,3},{8,12},{9,13},{10,... | collective-permute-start | bytes 196616 | tf_op jit(solution)/shard_map/ppermute | solution.py:22
  122.2 5.0 %collective-permute-start.13 = (bf16[4,32,512]{2,1,0:T(8,128)(2,1)S(1)}, bf16[4,32,512]{2,1,0:T(8,128)(2,1)S(1)}, u32[]{:S(2)}, u32[]{:S(2)}) collective-permute-start(bf16[4,32,512]{2,1,0:T(8,128)(2,1)S(1)} %shard_map.149.token_ref.low_ref), channel_id=1, source_target_pairs={{0,2},{1,3},{2,0},{3,1},{4,6},{5,7},{6,4},{7,5},{8,10},{9,11},{10,... | collective-permute-start | bytes 393224 | tf_op jit(solution)/shard_map/ppermute | solution.py:22
  127.3 1.6 collective-permute-start.14
  157.2 1.6 collective-permute-start.15
  158.9 6.0 %collective-permute-start.16 = (bf16[4,32,512]{2,1,0:T(8,128)(2,1)S(1)}, bf16[4,32,512]{2,1,0:T(8,128)(2,1)S(1)}, u32[]{:S(2)}, u32[]{:S(2)}) collective-permute-start(bf16[4,32,512]{2,1,0:T(8,128)(2,1)S(1)} %get-tuple-element.81.token_ref), channel_id=1, source_target_pairs={{0,2},{1,3},{2,0},{3,1},{4,6},{5,7},{6,4},{7,5},{8,10},{9,11},{10,... | collective-permute-start | bytes 393224 | tf_op jit(solution)/shard_map/ppermute | solution.py:22
  164.8 5.3 %collective-permute-start.17 = (bf16[2,32,512]{2,1,0:T(8,128)(2,1)S(1)}, bf16[2,32,512]{2,1,0:T(8,128)(2,1)S(1)}, u32[]{:S(2)}, u32[]{:S(2)}) collective-permute-start(bf16[2,32,512]{2,1,0:T(8,128)(2,1)S(1)} %get-tuple-element.86.token_ref), channel_id=1, source_target_pairs={{0,4},{1,5},{2,6},{3,7},{4,0},{5,1},{6,2},{7,3},{8,12},{9,13},{10,... | collective-permute-start | bytes 196616 | tf_op jit(solution)/shard_map/ppermute | solution.py:22
  170.1 4.9 %collective-permute-start.18 = (bf16[1,32,512]{2,1,0:T(8,128)(2,1)S(1)}, bf16[1,32,512]{2,1,0:T(8,128)(2,1)S(1)}, u32[]{:S(2)}, u32[]{:S(2)}) collective-permute-start(bf16[1,32,512]{2,1,0:T(8,128)(2,1)S(1)} %get-tuple-element.91.token_ref), channel_id=1, source_target_pairs={{0,8},{1,9},{2,10},{3,11},{4,12},{5,13},{6,14},{7,15},{8,0},{9,1},... | collective-permute-start | bytes 98312 | tf_op jit(solution)/shard_map/ppermute | solution.py:22
  188.0 1.5 collective-permute-start.19
  204.7 1.6 collective-permute-start.20

commit v6 on v5

--- a/solution.py
+++ b/solution.py
@@ -93,7 +93,8 @@
     )(*tokens, *[placed_in(array, pltpu.HBM) for array in arrays])
 
 
-def fetch_caches_kernel(token_ref, where_ref, keys_ref, values_ref, key_ref, value_ref, sems):
+def fetch_caches_kernel(where_ref, keys_ref, values_ref, *refs):
+    key_ref, value_ref, sems = refs[-3:]
     rows, places, _ = key_ref.shape
     batch = where_ref[0]
     copies = []
@@ -111,51 +112,81 @@
     run_copies(copies)
 
 
-def fetch_caches(token, where, keys, values):
+def fetch_caches(tokens, where, keys, values):
     shape = pltpu.VMEM(keys.shape[1:], keys.dtype)
     return pl.pallas_call(
         fetch_caches_kernel,
         out_shape=[shape, shape],
-        in_specs=[hbm(), smem(), hbm(), hbm()],
+        in_specs=[smem(), hbm(), hbm()] + [hbm()] * len(tokens),
         out_specs=[vmem(), vmem()],
         scratch_shapes=[pltpu.SemaphoreType.DMA((2, keys.shape[1], 2))],
         compiler_params=pltpu.CompilerParams(vmem_limit_bytes=1 << 20),
         cost_estimate=pl.CostEstimate(
             flops=0, bytes_accessed=2 * keys.size, transcendentals=0
         ),
-    )(token, where, placed_in(keys, pltpu.HBM), placed_in(values, pltpu.HBM))
-
-
-def fetch_pairs_kernel(first, token_ref, source, *refs):
+    )(where, placed_in(keys, pltpu.HBM), placed_in(values, pltpu.HBM), *tokens)
+
+
+def fetch_chunks_kernel(ids_ref, token_ref, source, target, sems):
+    count, _, chunk = target.shape
+    run_copies(
+        [
+            pltpu.make_async_copy(
+                source.at[:, span_of(ids_ref, k, chunk)], target.at[k], sems.at[k]
+            )
+            for k in range(count)
+        ]
+    )
+
+
+def fetch_chunks(token, ids, weights, chunk):
+    count, depth = ids.shape[0], weights.shape[0]
+    return pl.pallas_call(
+        fetch_chunks_kernel,
+        out_shape=[pltpu.VMEM((count, depth, chunk), weights.dtype)],
+        in_specs=[smem(), hbm(), hbm()],
+        out_specs=[vmem()],
+        scratch_shapes=[pltpu.SemaphoreType.DMA((count,))],
+        compiler_params=pltpu.CompilerParams(vmem_limit_bytes=1 << 20),
+        cost_estimate=pl.CostEstimate(
+            flops=0, bytes_accessed=2 * count * depth * chunk, transcendentals=0
+        ),
+    )(ids, token, placed_in(weights, pltpu.HBM))
+
+
+def fetch_pairs_kernel(items, ids_ref, token_ref, source, *refs):
     targets, sems = refs[:-1], refs[-1]
-    size = source.shape[0] // 4
+    half = sems.shape[1]
+    chunk = targets[0].shape[0] // half
     copies = []
-    for block, target in enumerate(targets):
-        for piece in range(4):
-            span = pl.ds(piece * size, size)
+    for at, ((side, block), target) in enumerate(zip(items, targets)):
+        for k in range(half):
             copies.append(
                 pltpu.make_async_copy(
-                    source.at[span, :, pl.ds((first + block) * 128, 128)],
-                    target.at[span],
-                    sems.at[block, piece],
+                    source.at[
+                        span_of(ids_ref, side * half + k, chunk), :, pl.ds(block * 128, 128)
+                    ],
+                    target.at[pl.ds(k * chunk, chunk)],
+                    sems.at[at, k],
                 )
             )
     run_copies(copies)
 
 
-def fetch_pairs(token, weights, first, blocks):
-    depth = weights.shape[0]
-    return pl.pallas_call(
-        functools.partial(fetch_pairs_kernel, first),
-        out_shape=[pltpu.VMEM((depth, 2, 128), weights.dtype)] * blocks,
-        in_specs=[hbm(), hbm()],
-        out_specs=[vmem()] * blocks,
-        scratch_shapes=[pltpu.SemaphoreType.DMA((blocks, 4))],
+def fetch_pairs(token, ids, weights, items):
+    half = ids.shape[0] // 2
+    size = weights.shape[0] // 2
+    return pl.pallas_call(
+        functools.partial(fetch_pairs_kernel, items),
+        out_shape=[pltpu.VMEM((size, 2, 128), weights.dtype)] * len(items),
+        in_specs=[smem(), hbm(), hbm()],
+        out_specs=[vmem()] * len(items),
+        scratch_shapes=[pltpu.SemaphoreType.DMA((len(items), half))],
         compiler_params=pltpu.CompilerParams(vmem_limit_bytes=1 << 20),
         cost_estimate=pl.CostEstimate(
-            flops=0, bytes_accessed=4 * blocks * depth * 128, transcendentals=0
-        ),
-    )(token, placed_in(weights, pltpu.HBM))
+            flops=0, bytes_accessed=4 * len(items) * size * 128, transcendentals=0
+        ),
+    )(ids, token, placed_in(weights, pltpu.HBM))
 
 
 def step_call(kernel, shapes, operands, held_back):
@@ -190,14 +221,24 @@
     )
 
 
-def finish_kernel(own_ref, keep_ref, got_ref, *refs):
-    total = keep_ref[0].astype(jnp.float32) + got_ref[0].astype(jnp.float32)
+def own_kernel(own_ref, keep_ref, got_ref, *refs):
+    out_ref = refs[-1]
     if len(own_ref.shape) == 2:
-        total += own_ref[...].astype(jnp.float32)
+        own = own_ref[...].astype(jnp.float32)
     else:
         parts = [own_ref[owner].astype(jnp.float32) for owner in range(own_ref.shape[0])]
-        total += jnp.concatenate(parts, axis=0)
-    refs[-1][...] = total.astype(jnp.bfloat16)
+        own = jnp.concatenate(parts, axis=0)
+    for place in range(keep_ref.shape[0]):
+        total = keep_ref[place].astype(jnp.float32) + got_ref[place].astype(jnp.float32)
+        out_ref[place] = (total + own if place == 0 else total).astype(jnp.bfloat16)
+
+
+def cross_kernel(here_ref, there_ref, *refs):
+    out_ref = refs[-1]
+    for place in range(2):
+        out_ref[place] = (
+            here_ref[place].astype(jnp.float32) + there_ref[1 - place].astype(jnp.float32)
+        ).astype(jnp.bfloat16)
 
 
 def join_kernel(low_ref, high_ref, *refs):
@@ -222,37 +263,43 @@
     return jnp.sum(exchange(held).astype(jnp.float32), axis=0)
 
 
-def scatter_halving(keep, got, own, jobs):
+def halve(keep, got, jobs):
     held_back = ()
-    for mask in chip_masks():
+    for mask in chip_masks()[:-1]:
         keep, send = add_parts((keep, got), 2, held_back)
         got = swap(send, mask)
         held_back = run_job(jobs, send)
-    return step_call(finish_kernel, [keep.shape[1:]], (own, keep, got), held_back)[0]
-
-
-def gather(part):
-    own = exchange(jnp.broadcast_to(part[None], (lax.axis_size("mp") // 2,) + part.shape))
-    return own, swap(own, 1)
+    return keep, got, held_back
+
+
+def spread_pair(pair, jobs):
+    held = pair
+    for mask in reversed(chip_masks()[:-1]):
+        got = swap(held, mask)
+        held = join(held, got, run_job(jobs, held))
+    return held, swap(held, 1)
+
+
+def reduce_to_all(keep, got, own, jobs, hops):
+    keep, got, held_back = halve(keep, got, jobs)
+    (held,) = step_call(own_kernel, [keep.shape], (own, keep, got), held_back)
+    far = chip_masks()[-1]
+    here = hop(held, 0) if hops else held
+    there = hop(held, far) if hops else swap(held, far)
+    (pair,) = step_call(cross_kernel, [held.shape], (here, there), run_job(jobs, held))
+    return (pair[0], *spread_pair(pair, jobs))
 
 
 def hop(part, mask):
     count = lax.axis_size("mp")
-    pairs = [(source, (source + count) % (2 * count) ^ mask) for source in range(2 * count)]
+    pairs = [(source, ((source + count) % (2 * count)) ^ mask) for source in range(2 * count)]
     return lax.ppermute(part, ("section", "mp"), pairs)
 
 
-def gather_doubling(part, jobs, hops):
+def gather_doubling(part, jobs):
     held = part[None]
-    for step, mask in enumerate(reversed(chip_masks())):
-        job_token = held
-        if hops and step == 0:
-            got = hop(held, mask)
-            held = hop(held, 0)
-        else:
-            got = swap(held, mask)
-        held = join(held, got, run_job(jobs, job_token))
-    return held, swap(held, 1)
+    got = swap(held, chip_masks()[-1])
+    return spread_pair(join(held, got, run_job(jobs, held)), jobs)
 
 
 def inverse_rms(x_refs):
@@ -504,67 +551,36 @@
     )(ids, values, placed_in(weights, pltpu.VMEM))
 
 
-def mlp_kernel(by_rows, me_ref, ids_ref, own_ref, other_ref, gain_ref, down_hbm, *refs):
-    pairs, (keep_ref, send_ref, middle_ref), (stacked, wide_x, total, act, down_ref, sems) = (
-        refs[:-9],
-        refs[-9:-6],
-        refs[-6:],
-    )
-    half, rows, chunk = own_ref.shape
-    blocks = pairs
+def gate_up(ids_ref, first, x_ref, gain_ref, blocks, stacked, wide_x, total_ref):
+    half, rows, chunk = x_ref.shape
     per_chunk = chunk // 128
 
-    def down_copy(k):
-        return pltpu.make_async_copy(
-            down_hbm.at[:, span_of(ids_ref, k, chunk)], down_ref.at[lax.rem(k, half)], sems.at[k]
-        )
-
-    @pl.loop(0, half)
-    def _(k):
-        down_copy(k).start()
-
-    scale = inverse_rms((own_ref, other_ref))
-    for first, x_ref in ((0, own_ref), (half, other_ref)):
-
-        @pl.loop(0, half)
-        def _(place):
-            k = first + place
-            normed = normed_chunk(x_ref, gain_ref, scale, place, span_of(ids_ref, k, chunk))
+    @pl.loop(0, half // UNROLL)
+    def _(group):
+        for step in range(UNROLL):
+            place = group * UNROLL + step
+            span = span_of(ids_ref, first + place, chunk)
+            scaled = (x_ref[place].astype(jnp.float32) * gain_ref[:, span]).astype(jnp.bfloat16)
             for b in range(per_chunk):
-                stacked[k * per_chunk + b] = normed[:, b * 128 : (b + 1) * 128]
-
-    if by_rows:
-        rows_dev = middle_ref.shape[0]
-        line = lax.broadcasted_iota(jnp.int32, (rows, 1), 0)
-        for first, x_ref in ((0, own_ref), (half, other_ref)):
-
-            @pl.loop(0, half)
-            def _(place):
-                wide = x_ref[place].astype(jnp.float32)
-                span = span_of(ids_ref, first + place, chunk)
-                for row in range(rows_dev):
-                    here = line == me_ref[0] * rows_dev + row
-                    middle_ref[row : row + 1, span] = jnp.sum(
-                        jnp.where(here, wide, 0.0), axis=0, keepdims=True
-                    )
+                stacked[place * per_chunk + b] = scaled[:, b * 128 : (b + 1) * 128]
 
     line = lax.broadcasted_iota(jnp.int32, (128, 512), 0)
     column = lax.broadcasted_iota(jnp.int32, (128, 512), 1)
     aim = jnp.where(column < 256, 2 * line, 2 * line + 257)
     widen = jnp.where(column == aim, 1.0, 0.0).astype(jnp.bfloat16)
 
-    @pl.loop(0, 2 * half * per_chunk // 8)
+    @pl.loop(0, wide_x.shape[0])
     def _(group):
-        span = pl.ds(group * 8, 8)
         wide = jnp.dot(
-            stacked[span].reshape(8 * rows, 128), widen, preferred_element_type=jnp.float32
+            stacked[pl.ds(group * 8, 8)].reshape(8 * rows, 128),
+            widen,
+            preferred_element_type=jnp.float32,
         ).astype(jnp.bfloat16)
         for b in range(8):
             lines = slice(b * rows, (b + 1) * rows)
             wide_x[group, :rows, b * 256 : (b + 1) * 256] = wide[lines, :256]
             wide_x[group, rows:, b * 256 : (b + 1) * 256] = wide[lines, 256:]
 
-    total[...] = jnp.zeros_like(total)
     per_group = 8 // per_chunk
 
     @pl.loop(0, wide_x.shape[0])
@@ -572,7 +588,7 @@
         for j in range(0, len(blocks), 2):
             part = 0.0
             for step in range(per_group):
-                at = ids_ref[group * per_group + step] * (2 * chunk)
+                at = (group * per_group + step) * (2 * chunk)
                 span = pl.ds(pl.multiple_of(at, 2 * chunk), 2 * chunk)
                 pair = jnp.concatenate([blocks[j][span, :], blocks[j + 1][span, :]], axis=1)
                 part += jnp.dot(
@@ -580,71 +596,152 @@
                     pair,
                     preferred_element_type=jnp.float32,
                 )
-            total[:, j * 128 : (j + 2) * 128] += part
-
-    gate = total[:rows, :]
-    act[...] = (gate / (1.0 + jnp.exp(-gate)) * total[rows:, :]).astype(jnp.bfloat16)
-
-    def down(first, k):
-        down_copy(first + k).wait()
-        return jnp.dot(act[...], down_ref[k], preferred_element_type=jnp.float32)
-
-    for first, target in ((0, keep_ref), (half, send_ref)):
+            total_ref[:, j * 128 : (j + 2) * 128] += part
+
+
+def own_half_kernel(ids_ref, own_ref, gain_ref, *refs):
+    blocks, (total_ref, stacked, wide_x) = refs[:-3], refs[-3:]
+    total_ref[...] = jnp.zeros_like(total_ref)
+    gate_up(ids_ref, 0, own_ref, gain_ref, blocks, stacked, wide_x, total_ref)
+
+
+def own_half(ids, own, gain, pairs):
+    half, rows, chunk = own.shape
+    units = 128 * len(pairs)
+    width = 2 * half * chunk
+    return pl.pallas_call(
+        own_half_kernel,
+        out_shape=pltpu.VMEM((2 * rows, units), jnp.float32),
+        in_specs=[smem(), vmem(), vmem()] + [vmem()] * len(pairs),
+        out_specs=vmem(),
+        scratch_shapes=[
+            pltpu.VMEM((width // 256, rows, 128), jnp.bfloat16),
+            pltpu.VMEM((width // 2048, 2 * rows, 2048), jnp.bfloat16),
+        ],
+        compiler_params=pltpu.CompilerParams(vmem_limit_bytes=(2 << 20) + 5 * rows * width),
+        cost_estimate=pl.CostEstimate(
+            flops=2 * rows * units * width, bytes_accessed=2 * units * width, transcendentals=0
+        ),
+    )(ids, own, gain, *pairs)
+
+
+def other_half_kernel(last, me_ref, ids_ref, own_ref, other_ref, gain_ref, own_total, near_ref,
+                      down_hbm, *refs):
+    blocks, outs, (stacked, wide_x, total, act, far_ref, sems) = refs[:-9], refs[-9:-6], refs[-6:]
+    half, rows, chunk = own_ref.shape
+
+    def far_copy(k):
+        return pltpu.make_async_copy(
+            down_hbm.at[:, span_of(ids_ref, half + k, chunk)], far_ref.at[k], sems.at[k]
+        )
+
+    @pl.loop(0, half)
+    def _(k):
+        far_copy(k).start()
+
+    total[...] = own_total[...]
+    gate_up(ids_ref, half, other_ref, gain_ref, blocks, stacked, wide_x, total)
+    scale = inverse_rms((own_ref, other_ref))
+    gate = total[:rows, :] * scale
+    act[...] = (gate / (1.0 + jnp.exp(-gate)) * (total[rows:, :] * scale)).astype(jnp.bfloat16)
+
+    def down(weights):
+        return jnp.dot(act[...], weights, preferred_element_type=jnp.float32)
+
+    if not last:
+        send_ref, act_ref, _ = outs
+        act_ref[...] = act[...]
 
         @pl.loop(0, half // UNROLL)
         def _(group):
             for step in range(UNROLL):
                 k = group * UNROLL + step
-                part = down(first, k)
-                if not by_rows:
-                    target[k] = part.astype(jnp.bfloat16)
-                    continue
+                far_copy(k).wait()
+                send_ref[k] = down(far_ref[k]).astype(jnp.bfloat16)
+
+        return
+
+    send_ref, keep_ref, middle_ref = outs
+    rows_dev = middle_ref.shape[0]
+    line = lax.broadcasted_iota(jnp.int32, (rows, 1), 0)
+    first_core = lax.rem(me_ref[0], 2) == 0
+    for first, x_ref in ((0, own_ref), (half, other_ref)):
+
+        @pl.loop(0, half // UNROLL)
+        def _(group):
+            for step in range(UNROLL):
+                k = group * UNROLL + step
                 span = span_of(ids_ref, first + k, chunk)
-                first_core = ids_ref[0] == 0
+                wide = x_ref[k].astype(jnp.float32)
+                for row in range(rows_dev):
+                    here = line == me_ref[0] * rows_dev + row
+                    middle_ref[row : row + 1, span] = jnp.sum(
+                        jnp.where(here, wide, 0.0), axis=0, keepdims=True
+                    )
+                if first:
+                    far_copy(k).wait()
+                part = down(far_ref[k] if first else near_ref[k])
                 for chip in range(half):
                     at = 2 * chip * rows_dev
                     low = part[at : at + rows_dev]
                     high = part[at + rows_dev : at + 2 * rows_dev]
                     keep_ref[chip, :, span] = jnp.where(first_core, low, high).astype(jnp.bfloat16)
                     send_ref[chip, :, span] = jnp.where(first_core, high, low).astype(jnp.bfloat16)
-            if first == 0:
-                for step in range(UNROLL):
-                    down_copy(half + group * UNROLL + step).start()
-
-
-def mlp(me, ids, own, other, gain, pairs, down, by_rows):
+
+
+def other_half(last, me, ids, own, other, gain, own_total, near, down, pairs):
     half, rows, chunk = own.shape
     units, width = down.shape
-    part = (half, rows // (2 * half), width) if by_rows else own.shape
-    shape = pltpu.VMEM(part, jnp.bfloat16)
-    return pl.pallas_call(
-        functools.partial(mlp_kernel, by_rows),
-        out_shape=(shape, shape, pltpu.VMEM((rows // (2 * half), width), jnp.float32)),
-        in_specs=[smem(), smem()] + [vmem()] * 3 + [hbm()] + [vmem()] * len(pairs),
-        out_specs=(vmem(), vmem(), vmem()),
+    rows_dev = rows // (2 * half)
+    if last:
+        shapes = [((half, rows_dev, width), jnp.bfloat16)] * 2 + [((rows_dev, width), jnp.float32)]
+    else:
+        shapes = [(own.shape, jnp.bfloat16), ((rows, units), jnp.bfloat16), ((8, 128), jnp.float32)]
+    return pl.pallas_call(
+        functools.partial(other_half_kernel, last),
+        out_shape=[pltpu.VMEM(shape, kind) for shape, kind in shapes],
+        in_specs=[smem(), smem()] + [vmem()] * 5 + [hbm()] + [vmem()] * len(pairs),
+        out_specs=[vmem()] * 3,
         scratch_shapes=[
-            pltpu.VMEM((width // 128, rows, 128), jnp.bfloat16),
-            pltpu.VMEM((width // 1024, 2 * rows, 2048), jnp.bfloat16),
+            pltpu.VMEM((width // 256, rows, 128), jnp.bfloat16),
+            pltpu.VMEM((width // 2048, 2 * rows, 2048), jnp.bfloat16),
             pltpu.VMEM((2 * rows, units), jnp.float32),
             pltpu.VMEM((rows, units), jnp.bfloat16),
             pltpu.VMEM((half, units, chunk), jnp.bfloat16),
-            pltpu.SemaphoreType.DMA((2 * half,)),
+            pltpu.SemaphoreType.DMA((half,)),
         ],
         compiler_params=pltpu.CompilerParams(
-            vmem_limit_bytes=(3 << 19) + 10 * rows * width + (10 * rows + width) * units
-        ),
-        cost_estimate=pl.CostEstimate(
-            flops=6 * rows * units * width, bytes_accessed=6 * units * width, transcendentals=0
-        ),
-    )(
-        me,
-        ids,
-        own,
-        other,
-        gain,
-        placed_in(down, pltpu.HBM),
-        *[placed_in(pair.reshape(2 * width, 128), pltpu.VMEM) for pair in pairs],
-    )
+            vmem_limit_bytes=(2 << 20) + 5 * rows * width + (10 * rows + width) * units
+        ),
+        cost_estimate=pl.CostEstimate(
+            flops=4 * rows * units * width, bytes_accessed=3 * units * width, transcendentals=0
+        ),
+    )(me, ids, own, other, gain, own_total, near, placed_in(down, pltpu.HBM), *pairs)
+
+
+def keep_kernel(act_ref, near_ref, out_ref):
+    @pl.loop(0, out_ref.shape[0] // UNROLL)
+    def _(group):
+        for step in range(UNROLL):
+            k = group * UNROLL + step
+            out_ref[k] = jnp.dot(
+                act_ref[...], near_ref[k], preferred_element_type=jnp.float32
+            ).astype(jnp.bfloat16)
+
+
+def keep_half(act, near):
+    rows = act.shape[0]
+    half, _, chunk = near.shape
+    return pl.pallas_call(
+        keep_kernel,
+        out_shape=pltpu.VMEM((half, rows, chunk), jnp.bfloat16),
+        in_specs=[vmem(), vmem()],
+        out_specs=vmem(),
+        compiler_params=pltpu.CompilerParams(vmem_limit_bytes=4 << 20),
+        cost_estimate=pl.CostEstimate(
+            flops=2 * rows * near.size, bytes_accessed=2 * near.size, transcendentals=0
+        ),
+    )(act, near)
 
 
 def turning(positions):
@@ -672,13 +769,9 @@
 ):
     rows_dev = hidden.shape[1]
     count = lax.axis_size("mp")
-    half = count // 2
     section_index = lax.axis_index("section")
     model_index = lax.axis_index("mp")
-    core = model_index % 2
     width = hidden.shape[2]
-    chips = 2 * jnp.arange(half, dtype=jnp.int32)
-    ids = jnp.concatenate([chips + core, chips + 1 - core])
     near = jnp.asarray(relative_ids())
     near_places, far_places = near ^ model_index, near ^ model_index ^ 1
     places = jnp.concatenate([near_places, far_places])
@@ -686,7 +779,7 @@
     wv = w_value[0].T
     blocks = w_gate_up.shape[3] // 128
     windows = len(chip_masks())
-    bounds = [-(-blocks * step // windows) for step in range(windows + 1)]
+    bounds = [(4 * blocks * step + windows) // (2 * windows) for step in range(windows + 1)]
     batches = [
         jnp.remainder(section_index + turn_index, 2).astype(jnp.int32).reshape(1)
         for turn_index in range(2)
@@ -697,13 +790,13 @@
         for batch in batches
     ]
     me = model_index.astype(jnp.int32).reshape(1)
-    early = (ids, places, near_places, far_places, me, *batches, *tables[0], *tables[1])
+    early = (places, near_places, far_places, me, *batches, *tables[0], *tables[1])
 
     def attention_jobs(turn_index):
         got = {}
 
         def projections(token):
-            got["qkv"] = fetch((token, *early), w_query[0], wk, wv)
+            got["qkv"] = fetch((token,), w_query[0], wk, wv)
             return got["qkv"]
 
         def out_projection(token):
@@ -711,14 +804,14 @@
             return got["out"]
 
         def caches(token):
-            got["caches"] = fetch_caches(token, batches[turn_index], key_cache[0], value_cache[0])
+            tokens = (token,) if turn_index else (token, *early)
+            got["caches"] = fetch_caches(tokens, batches[turn_index], key_cache[0], value_cache[0])
             return got["caches"]
 
-        return got, [projections, out_projection, caches]
+        return got, [caches, projections, out_projection]
 
     got, jobs = attention_jobs(0)
-    own, other = gather_doubling(hidden[0], jobs, False)
-    mine = None
+    own, other = gather_doubling(hidden[0], jobs)
     for turn_index in range(2):
         last = turn_index == 1
         batch = batches[turn_index]
@@ -730,28 +823,47 @@
         heads_out = lax.all_to_all(mixed.transpose(1, 0, 2), "mp", split_axis=0, concat_axis=0)
         got_core = swap(spread_project(far_places, heads_out, *got["out"]), 1)
         keep = spread_project(near_places, heads_out, *got["out"])
-        pairs = []
-
-        def pair_job(first, size):
+        pairs = {}
+
+        def pair_job(new):
             def job(token):
-                new = fetch_pairs(token, w_gate_up[0], first, size) if size else ()
-                pairs.extend(new)
-                return new
+                if not new:
+                    return ()
+                arrays = fetch_pairs(token, places, w_gate_up[0], new)
+                pairs.update(zip(new, arrays))
+                return arrays
 
             return job
 
-        jobs = [pair_job(low, high - low) for low, high in zip(bounds, bounds[1:])]
-        middle = scatter_halving(keep, got_core, by_owner if mine is None else mine, jobs)
-        own, other = gather(middle)
-        keep, send, own_rows = mlp(me, ids, own, other, mlp_gain, pairs, w_down[0], last)
-        mlp_part = scatter(send, keep)
+        items = [(side, block) for side in range(2) for block in range(blocks)]
+        jobs = [pair_job(items[low:high]) for low, high in zip(bounds, bounds[1:])]
+        near_down = []
+
+        def down_job(token):
+            near_down.extend(fetch_chunks(token, near_places, w_down[0], width // count))
+            return near_down
+
+        jobs.append(down_job)
+        addend = by_owner if turn_index == 0 else mine
+        middle, own, other = reduce_to_all(keep, got_core, addend, jobs, False)
+        near_pairs, far_pairs = (
+            [
+                placed_in(pairs[side, block].reshape(width, 128), pltpu.VMEM)
+                for block in range(blocks)
+            ]
+            for side in range(2)
+        )
+        own_total = own_half(places, own, mlp_gain, near_pairs)
+        send, act, own_rows = other_half(
+            last, me, places, own, other, mlp_gain, own_total, near_down[0], w_down[0], far_pairs
+        )
         if last:
-            middle = own_rows
-        mine = (middle.astype(jnp.float32) + mlp_part).astype(jnp.bfloat16)
-        if not last:
+            mine = (own_rows + scatter(send, act)).astype(jnp.bfloat16)
+        else:
             got, jobs = attention_jobs(1)
-            own, other = gather_doubling(mine, jobs, True)
-            mine = own[0]
+            got_core = swap(send, 1)
+            keep = keep_half(act, near_down[0])
+            mine, own, other = reduce_to_all(keep, got_core, middle, jobs, True)
     return mine[None]
 
 

time: 221 us -> 211 us (0.955)
  blocking collectives: 90.3 us -> 52.1 us
  Pallas kernels: 95.4 us -> 107 us
  starting transfers between devices: 16.2 us -> 26.5 us
  waiting for transfers between devices: 14 us -> 21.3 us
    all_to_all x4 -> x1, blocking collectives: 51.1 us -> 13.6 us  [exchange(): lax.all_to_all(parts, 'mp', split_axis=0, concat_axis=0, axis_index_group...]
    pallas_call x10 -> x15, Pallas kernels: 60.8 us -> 72.4 us  [the longest x6 30.8 us: fetch_pairs(): pl.pallas_call(functools.partial(fetch_pairs_kernel, items), out_shape=[p...]
    ppermute x19 -> x25, starting transfers between devices: 13.6 us -> 23.1 us  [swap(): lax.ppermute(value, axis, [(source, source ^ mask) for source in range(co...]
    ppermute x19 -> x25, waiting for transfers between devices: 14 us -> 21 us  [swap(): lax.ppermute(value, axis, [(source, source ^ mask) for source in range(co...]
  transfers between devices with their start and end apart: 21 -> 27, of which waited for: 13 -> 11; matrix products, arithmetic and copies ran while one was open for 1% -> 1% of each run, Pallas kernels for 22% -> 35%
where the time goes in v6:
time: 211 us
  Pallas kernels  107 us (51%)
  blocking collectives  52.1 us (25%)
  starting transfers between devices  26.5 us (13%)
  waiting for transfers between devices  21.3 us (10%)
  other arithmetic  2.65 us (1%)
    pallas_call x6, Pallas kernels, fetch_pairs(): pl.pallas_call(functools.partial(fetch_pairs_kernel, items), out_shape=[p...  30.8 us
    ppermute x25, starting transfers between devices, swap(): lax.ppermute(value, axis, [(source, source ^ mask) for source in range(co...  23.1 us
    ppermute x25, waiting for transfers between devices, swap(): lax.ppermute(value, axis, [(source, source ^ mask) for source in range(co...  21 us
    all_to_all x2, blocking collectives, body(): spread = lax.all_to_all(joined, 'mp', split_axis=0, concat_axis=0)  20.2 us
    all_to_all x2, blocking collectives, body(): lax.all_to_all(mixed.transpose(1, 0, 2), 'mp', split_axis=0, concat_axis=0)  18.4 us
    pallas_call x2, Pallas kernels, other_half(): pl.pallas_call(functools.partial(other_half_kernel, last), out_shape=[plt...  17.3 us
    pallas_call x4, Pallas kernels, fetch(): pl.pallas_call(functools.partial(fetch_kernel, pieces, len(tokens)), out_...  15.5 us
    all_to_all x1, blocking collectives, exchange(): lax.all_to_all(parts, 'mp', split_axis=0, concat_axis=0, axis_index_group...  13.6 us
  transfers between devices with their start and end apart: 27, of which 11 were waited for; matrix products, arithmetic and copies ran while one was open for 1% of the time, Pallas kernels for 35%

profile of v6, /device:TPU:0, one launch (start us, length us, event | category | flops | bytes accessed | tf_op | source)
XLA Modules:
  0.0 211.1 jit_solution(2807095139526071137)
XLA Ops:
  0.0 4.0 %collective-permute-start = (bf16[1,2,8192]{2,1,0:T(2,128)(2,1)}, bf16[1,2,8192]{2,1,0:T(2,128)(2,1)S(1)}, u32[]{:S(2)}, u32[]{:S(2)}) collective-permute-start(bf16[1,2,8192]{2,1,0:T(2,128)(2,1)} %low_ref.1), channel_id=1, source_target_pairs={{0,8},{1,9},{2,10},{3,11},{4,12},{5,13},{6,14},{7,15},{8,0},{9,1},... | collective-permute-start | bytes 98312 | tf_op jit(solution)/shard_map/ppermute | solution.py:22
  6.6 2.2 %shard_map.127 = (bf16[2,512,1024]{2,1,0:T(8,128)(2,1)S(1)}, bf16[2,512,1024]{2,1,0:T(8,128)(2,1)S(1)}) custom-call(s32[1]{0:T(128)} %bitcast.1.where_ref.refs_5_, bf16[2,2,512,1024]{3,2,1,0:T(8,128)(2,1)} %bitcast.109, bf16[2,2,512,1024]{3,2,1,0:T(8,128)(2,1)} %bitcast.111, bf16[1,2,8192]{2,1,0:T(2,128)(2,1)S(1)} %copy-done.1, ...), custom_call_target="tpu_custom_call" | custom-call | bytes 4194304 | tf_op jit(solution)/shard_map/pallas_call | solution.py:117
  10.5 4.3 %shard_map.129 = (bf16[8192,512]{1,0:T(8,128)(2,1)S(1)}, bf16[64,8192]{1,0:T(8,128)(2,1)S(1)}, bf16[64,8192]{1,0:T(8,128)(2,1)S(1)}) custom-call(bf16[2,2,8192]{2,1,0:T(2,128)(2,1)S(1)} %shard_map.128.refs_0_.low_ref, bf16[8192,512]{1,0:T(8,128)(2,1)} %bitcast.105, bf16[64,8192]{1,0:T(8,128)(2,1)} %bitcast.113, bf16[64,8192]{1,0:T(8,128)(2,1)} %bitcast.115), custom_call_target="tpu_custom_call" | custom-call | bytes 10485760 | tf_op jit(solution)/shard_map/pallas_call | solution.py:83
  16.4 3.5 %shard_map.131.refs_0_.w_ref = bf16[512,8192]{1,0:T(8,128)(2,1)S(1)} custom-call(bf16[4,2,8192]{2,1,0:T(2,128)(2,1)S(1)} %shard_map.130.refs_0_.low_ref, bf16[512,8192]{1,0:T(8,128)(2,1)} %bitcast.107), custom_call_target="tpu_custom_call" | custom-call | bytes 8388608 | tf_op jit(solution)/shard_map/pallas_call | solution.py:83
  21.6 3.6 %shard_map.133 = (bf16[16,2,640]{2,1,0:T(2,128)(2,1)S(1)}, bf16[16,2,512]{2,1,0:T(2,128)(2,1)S(1)}) custom-call(s32[16]{0:T(128)S(1)} %pad_add_fusion.refs_1_.ids_ref, bf16[8,2,8192]{2,1,0:T(2,128)(2,1)S(1)} %shard_map.132.own_ref, bf16[8,2,8192]{2,1,0:T(2,128)(2,1)S(1)} %collective-permute-done.3.other_ref, f32[1,8192]{1,0:T(1,128)S(1)} %copy-done.3, ...), custom_call_target="tpu_custom_call" | custom-call | flops 335544320 | bytes 10485760 | tf_op jit(solution)/shard_map/pallas_call | solution.py:393
  25.2 9.3 %all_to_all.25.in_ref = bf16[16,2,640]{2,1,0:T(2,128)(2,1)S(1)} all-to-all(bf16[16,2,640]{2,1,0:T(2,128)(2,1)S(1)} %get-tuple-element.73), channel_id=1, replica_groups=mesh['section'=2,'mp'=16] {'mp'}, dimensions={0} | all-to-all | bytes 81920 | tf_op jit(solution)/shard_map/all_to_all | solution.py:819
  34.5 2.5 %shard_map.134 = bf16[2,16,512]{2,1,0:T(8,128)(2,1)S(1)} custom-call(s32[1]{0:T(128)} %bitcast.1.where_ref.refs_5_, s32[2,2]{1,0:T(2,128)S(1)} %copy-done.4, bf16[16,2,640]{2,1,0:T(2,128)(2,1)S(1)} %all_to_all.25.in_ref, f32[2,128]{1,0:T(2,128)S(1)} %get-tuple-element.142.refs_7_.cos_ref, f32[2,128]{1,0:T(2,128)S(1)} %get-tuple-element.143.refs_8_.sin_ref, ...), custom_call_target="tpu_custom_call" | custom-call | flops 268435456 | bytes 4194304 | tf_op jit(solution)/shard_map/pallas_call | solution.py:491
  37.1 9.2 %all_to_all.26.x_ref = bf16[16,2,512]{2,1,0:T(2,128)(2,1)S(1)} all-to-all(bf16[16,2,512]{2,1,0:T(2,128)(2,1)S(1)} %bitcast.117), channel_id=1, replica_groups=mesh['section'=2,'mp'=16] {'mp'}, dimensions={0} | all-to-all | bytes 65536 | tf_op jit(solution)/shard_map/all_to_all | solution.py:823
  49.9 4.9 %shard_map.138 = (bf16[4096,2,128]{2,1,0:T(2,128)(2,1)S(1)}, bf16[4096,2,128]{2,1,0:T(2,128)(2,1)S(1)}, bf16[4096,2,128]{2,1,0:T(2,128)(2,1)S(1)}, bf16[4096,2,1...) custom-call(s32[16]{0:T(128)S(1)} %pad_add_fusion.refs_1_.ids_ref, bf16[4,32,512]{2,1,0:T(8,128)(2,1)S(1)} %get-tuple-element.75.token_ref, ...), custom_call_target="tpu_custom_call" | custom-call | bytes 10485760 | tf_op jit(solution)/shard_map/pallas_call | solution.py:179
  55.8 5.6 %shard_map.140 = (bf16[4096,2,128]{2,1,0:T(2,128)(2,1)S(1)}, bf16[4096,2,128]{2,1,0:T(2,128)(2,1)S(1)}, bf16[4096,2,128]{2,1,0:T(2,128)(2,1)S(1)}, bf16[4096,2,1...) custom-call(s32[16]{0:T(128)S(1)} %pad_add_fusion.refs_1_.ids_ref, ...), custom_call_target="tpu_custom_call" | custom-call | bytes 12582912 | tf_op jit(solution)/shard_map/pallas_call | solution.py:179
  62.2 4.9 %shard_map.142 = (bf16[4096,2,128]{2,1,0:T(2,128)(2,1)S(1)}, bf16[4096,2,128]{2,1,0:T(2,128)(2,1)S(1)}, bf16[4096,2,128]{2,1,0:T(2,128)(2,1)S(1)}, bf16[4096,2,1...) custom-call(s32[16]{0:T(128)S(1)} %pad_add_fusion.refs_1_.ids_ref, bf16[2,32,512]{2,1,0:T(8,128)(2,1)S(1)} %shard_map.141.token_ref.here_ref, ...), custom_call_target="tpu_custom_call" | custom-call | bytes 10485760 | tf_op jit(solution)/shard_map/pallas_call | solution.py:179
  68.6 4.2 %shard_map.144.refs_0_.near_ref = bf16[8,1024,512]{2,1,0:T(8,128)(2,1)S(1)} custom-call(s32[8]{0:T(128)S(1)} %get-tuple-element.140.refs_2_.ids_ref, bf16[2,32,512]{2,1,0:T(8,128)(2,1)S(1)} %shard_map.143.token_ref.low_ref, bf16[1024,8192]{1,0:T(8,128)(2,1)} %bitcast.101), custom_call_target="tpu_custom_call" | custom-call | bytes 8388608 | tf_op jit(solution)/shard_map/pallas_call | solution.py:144
  74.0 3.8 %collective-permute-done.9.high_ref = bf16[4,32,512]{2,1,0:T(8,128)(2,1)S(1)} collective-permute-done((bf16[4,32,512]{2,1,0:T(8,128)(2,1)S(1)}, bf16[4,32,512]{2,1,0:T(8,128)(2,1)S(1)}, u32[]{:S(2)}, u32[]{:S(2)}) %collective-permute-start.9) | collective-permute-done | bytes 131104 | tf_op jit(solution)/shard_map/ppermute | solution.py:22
  78.0 4.9 %shard_map.147.own_total = f32[64,1024]{1,0:T(8,128)S(1)} custom-call(s32[16]{0:T(128)S(1)} %pad_add_fusion.refs_1_.ids_ref, bf16[8,32,512]{2,1,0:T(8,128)(2,1)S(1)} %shard_map.146.own_ref, f32[1,8192]{1,0:T(1,128)S(1)} %copy-done, bf16[8192,128]{1,0:T(8,128)(2,1)S(1)} %bitcast.74, bf16[8192,128]{1,0:T(8,128)(2,1)S(1)} %bitcast.75, ...), custom_call_target="tpu_custom_call" | custom-call | flops 536870912 | bytes 16777216 | tf_op jit(solution)/shard_map/pallas_call | solution.py:612
  82.9 7.9 %shard_map.148 = (bf16[8,32,512]{2,1,0:T(8,128)(2,1)S(1)}, bf16[32,1024]{1,0:T(8,128)(2,1)S(1)}, f32[8,128]{1,0:T(8,128)}) custom-call(s32[1]{0:T(128)} %bitcast.refs_4_.me_ref, s32[16]{0:T(128)S(1)} %pad_add_fusion.refs_1_.ids_ref, bf16[8,32,512]{2,1,0:T(8,128)(2,1)S(1)} %shard_map.146.own_ref, bf16[8,32,512]{2,1,0:T(8,128)(2,1)S(1)} %collective-permute-done.10.other_ref, ...), custom_call_target="tpu_custom_call" | custom-call | flops 1073741824 | bytes 25165824 | tf_op jit(solution)/shard_map/pallas_call | solution.py:700
  99.6 4.3 %shard_map.153 = (bf16[8192,512]{1,0:T(8,128)(2,1)S(1)}, bf16[64,8192]{1,0:T(8,128)(2,1)S(1)}, bf16[64,8192]{1,0:T(8,128)(2,1)S(1)}) custom-call(bf16[2,32,512]{2,1,0:T(8,128)(2,1)S(1)} %get-tuple-element.101.refs_0_, bf16[8192,512]{1,0:T(8,128)(2,1)} %bitcast.106, bf16[64,8192]{1,0:T(8,128)(2,1)} %bitcast.114, bf16[64,8192]{1,0:T(8,128)(2,1)} %bitcast.116), custom_call_target="tpu_custom_call" | custom-call | bytes 10485760 | tf_op jit(solution)/shard_map/pallas_call | solution.py:83
  104.0 2.9 %collective-permute-start.15 = (bf16[2,32,512]{2,1,0:T(8,128)(2,1)S(1)}, bf16[2,32,512]{2,1,0:T(8,128)(2,1)S(1)}, u32[]{:S(2)}, u32[]{:S(2)}) collective-permute-start(bf16[2,32,512]{2,1,0:T(8,128)(2,1)S(1)} %shard_map.154.refs_0_), channel_id=1, source_target_pairs={{0,24},{1,25},{2,26},{3,27},{4,28},{5,29},{6,30},{7,31},{8,16},{9,... | collective-permute-start | bytes 196616 | tf_op jit(solution)/shard_map/ppermute | solution.py:296
  107.4 3.5 %shard_map.155.refs_0_.w_ref = bf16[512,8192]{1,0:T(8,128)(2,1)S(1)} custom-call(bf16[2,32,512]{2,1,0:T(8,128)(2,1)S(1)} %shard_map.154.refs_0_, bf16[512,8192]{1,0:T(8,128)(2,1)} %bitcast.108), custom_call_target="tpu_custom_call" | custom-call | bytes 8388608 | tf_op jit(solution)/shard_map/pallas_call | solution.py:83
  112.9 2.7 %collective-permute-done.16.high_ref = bf16[2,32,512]{2,1,0:T(8,128)(2,1)S(1)} collective-permute-done((bf16[2,32,512]{2,1,0:T(8,128)(2,1)S(1)}, bf16[2,32,512]{2,1,0:T(8,128)(2,1)S(1)}, u32[]{:S(2)}, u32[]{:S(2)}) %collective-permute-start.16) | collective-permute-done | bytes 65568 | tf_op jit(solution)/shard_map/ppermute | solution.py:22
  117.4 3.2 %collective-permute-done.17.high_ref = bf16[4,32,512]{2,1,0:T(8,128)(2,1)S(1)} collective-permute-done((bf16[4,32,512]{2,1,0:T(8,128)(2,1)S(1)}, bf16[4,32,512]{2,1,0:T(8,128)(2,1)S(1)}, u32[]{:S(2)}, u32[]{:S(2)}) %collective-permute-start.17) | collective-permute-done | bytes 131104 | tf_op jit(solution)/shard_map/ppermute | solution.py:22
  122.2 3.8 %shard_map.159 = (bf16[16,2,640]{2,1,0:T(2,128)(2,1)S(1)}, bf16[16,2,512]{2,1,0:T(2,128)(2,1)}) custom-call(s32[16]{0:T(128)S(1)} %pad_add_fusion.refs_1_.ids_ref, bf16[8,32,512]{2,1,0:T(8,128)(2,1)S(1)} %shard_map.158.own_ref, bf16[8,32,512]{2,1,0:T(8,128)(2,1)S(1)} %collective-permute-done.18.other_ref, f32[1,8192]{1,0:T(1,128)S(1)} %copy-done.3, ...), custom_call_target="tpu_custom_call" | custom-call | flops 335544320 | bytes 10485760 | tf_op jit(solution)/shard_map/pallas_call | solution.py:393
  126.0 10.9 %all_to_all.27.in_ref = bf16[16,2,640]{2,1,0:T(2,128)(2,1)S(1)} all-to-all(bf16[16,2,640]{2,1,0:T(2,128)(2,1)S(1)} %get-tuple-element.105), channel_id=1, replica_groups=mesh['section'=2,'mp'=16] {'mp'}, dimensions={0} | all-to-all | bytes 81920 | tf_op jit(solution)/shard_map/all_to_all | solution.py:819
  136.9 2.5 %shard_map.160 = bf16[2,16,512]{2,1,0:T(8,128)(2,1)S(1)} custom-call(s32[1]{0:T(128)} %bitcast.4.refs_6_.where_ref, s32[2,2]{1,0:T(2,128)S(1)} %copy-done.4, bf16[16,2,640]{2,1,0:T(2,128)(2,1)S(1)} %all_to_all.27.in_ref, f32[2,128]{1,0:T(2,128)S(1)} %get-tuple-element.144.refs_9_.cos_ref, f32[2,128]{1,0:T(2,128)S(1)} %get-tuple-element.145.refs_10_.sin_ref, ...), custom_call_target="tpu_custom_call" | custom-call | flops 268435456 | bytes 4194304 | tf_op jit(solution)/shard_map/pallas_call | solution.py:491
  139.4 9.2 %all_to_all.28.x_ref = bf16[16,2,512]{2,1,0:T(2,128)(2,1)S(1)} all-to-all(bf16[16,2,512]{2,1,0:T(2,128)(2,1)S(1)} %bitcast.118), channel_id=1, replica_groups=mesh['section'=2,'mp'=16] {'mp'}, dimensions={0} | all-to-all | bytes 65536 | tf_op jit(solution)/shard_map/all_to_all | solution.py:823
  152.2 4.9 %shard_map.164 = (bf16[4096,2,128]{2,1,0:T(2,128)(2,1)S(1)}, bf16[4096,2,128]{2,1,0:T(2,128)(2,1)S(1)}, bf16[4096,2,128]{2,1,0:T(2,128)(2,1)S(1)}, bf16[4096,2,1...) custom-call(s32[16]{0:T(128)S(1)} %pad_add_fusion.refs_1_.ids_ref, bf16[4,32,512]{2,1,0:T(8,128)(2,1)S(1)} %get-tuple-element.107.token_ref, ...), custom_call_target="tpu_custom_call" | custom-call | bytes 10485760 | tf_op jit(solution)/shard_map/pallas_call | solution.py:179
  158.2 5.6 %shard_map.166 = (bf16[4096,2,128]{2,1,0:T(2,128)(2,1)S(1)}, bf16[4096,2,128]{2,1,0:T(2,128)(2,1)S(1)}, bf16[4096,2,128]{2,1,0:T(2,128)(2,1)S(1)}, bf16[4096,2,1...) custom-call(s32[16]{0:T(128)S(1)} %pad_add_fusion.refs_1_.ids_ref, ...), custom_call_target="tpu_custom_call" | custom-call | bytes 12582912 | tf_op jit(solution)/shard_map/pallas_call | solution.py:179
  164.6 4.9 %shard_map.168 = (bf16[4096,2,128]{2,1,0:T(2,128)(2,1)S(1)}, bf16[4096,2,128]{2,1,0:T(2,128)(2,1)S(1)}, bf16[4096,2,128]{2,1,0:T(2,128)(2,1)S(1)}, bf16[4096,2,1...) custom-call(s32[16]{0:T(128)S(1)} %pad_add_fusion.refs_1_.ids_ref, bf16[2,32,512]{2,1,0:T(8,128)(2,1)S(1)} %shard_map.167.token_ref.here_ref, ...), custom_call_target="tpu_custom_call" | custom-call | bytes 10485760 | tf_op jit(solution)/shard_map/pallas_call | solution.py:179
  171.0 4.2 %shard_map.170.refs_0_.near_ref = bf16[8,1024,512]{2,1,0:T(8,128)(2,1)S(1)} custom-call(s32[8]{0:T(128)S(1)} %get-tuple-element.140.refs_2_.ids_ref, bf16[2,32,512]{2,1,0:T(8,128)(2,1)S(1)} %shard_map.169.token_ref.low_ref, bf16[1024,8192]{1,0:T(8,128)(2,1)} %bitcast.103), custom_call_target="tpu_custom_call" | custom-call | bytes 8388608 | tf_op jit(solution)/shard_map/pallas_call | solution.py:144
  176.4 3.8 %collective-permute-done.24.high_ref = bf16[4,32,512]{2,1,0:T(8,128)(2,1)S(1)} collective-permute-done((bf16[4,32,512]{2,1,0:T(8,128)(2,1)S(1)}, bf16[4,32,512]{2,1,0:T(8,128)(2,1)S(1)}, u32[]{:S(2)}, u32[]{:S(2)}) %collective-permute-start.24) | collective-permute-done | bytes 131104 | tf_op jit(solution)/shard_map/ppermute | solution.py:22
  180.3 4.9 %shard_map.173.own_total = f32[64,1024]{1,0:T(8,128)S(1)} custom-call(s32[16]{0:T(128)S(1)} %pad_add_fusion.refs_1_.ids_ref, bf16[8,32,512]{2,1,0:T(8,128)(2,1)S(1)} %shard_map.172.own_ref, f32[1,8192]{1,0:T(1,128)S(1)} %copy-done, bf16[8192,128]{1,0:T(8,128)(2,1)S(1)} %bitcast.69, bf16[8192,128]{1,0:T(8,128)(2,1)S(1)} %bitcast.70, ...), custom_call_target="tpu_custom_call" | custom-call | flops 536870912 | bytes 16777216 | tf_op jit(solution)/shard_map/pallas_call | solution.py:612
  185.2 9.4 %shard_map.174 = (bf16[8,2,8192]{2,1,0:T(2,128)(2,1)S(1)}, bf16[8,2,8192]{2,1,0:T(2,128)(2,1)S(1)}, f32[2,8192]{1,0:T(2,128)S(1)}) custom-call(s32[1]{0:T(128)} %bitcast.refs_4_.me_ref, s32[16]{0:T(128)S(1)} %pad_add_fusion.refs_1_.ids_ref, bf16[8,32,512]{2,1,0:T(8,128)(2,1)S(1)} %shard_map.172.own_ref, ...), custom_call_target="tpu_custom_call" | custom-call | flops 1073741824 | bytes 25165824 | tf_op jit(solution)/shard_map/pallas_call | solution.py:700
  196.6 13.6 %all_to_all.29 = bf16[8,2,8192]{2,1,0:T(2,128)(2,1)S(1)} all-to-all(bf16[8,2,8192]{2,1,0:T(2,128)(2,1)S(1)} %shard_map.175), channel_id=1, replica_groups={{0,2,4,6,8,10,12,14},{1,3,5,7,9,11,13,15},{16,18,20,22,24,26,28,30},{17..., dimensions={0} | all-to-all | bytes 524288 | tf_op jit(solution)/shard_map/all_to_all | solution.py:28
  (99 shorter events, 41.5 us)
Async XLA Ops:
  0.0 8.8 %collective-permute-start = (bf16[1,2,8192]{2,1,0:T(2,128)(2,1)}, bf16[1,2,8192]{2,1,0:T(2,128)(2,1)S(1)}, u32[]{:S(2)}, u32[]{:S(2)}) collective-permute-start(bf16[1,2,8192]{2,1,0:T(2,128)(2,1)} %low_ref.1), channel_id=1, source_target_pairs={{0,8},{1,9},{2,10},{3,11},{4,12},{5,13},{6,14},{7,15},{8,0},{9,1},... | collective-permute-start | bytes 98312 | tf_op jit(solution)/shard_map/ppermute | solution.py:22
  5.8 0.8 copy-start.1
  6.6 2.2 %copy-start.2 = (bf16[1,2,8192]{2,1,0:T(2,128)(2,1)S(1)}, bf16[1,2,8192]{2,1,0:T(2,128)(2,1)}, u32[]{:S(2)}) copy-start(bf16[1,2,8192]{2,1,0:T(2,128)(2,1)} %low_ref.1) | copy-start | bytes 98308
  8.8 5.9 %collective-permute-start.1 = (bf16[2,2,8192]{2,1,0:T(2,128)(2,1)S(1)}, bf16[2,2,8192]{2,1,0:T(2,128)(2,1)S(1)}, u32[]{:S(2)}, u32[]{:S(2)}) collective-permute-start(bf16[2,2,8192]{2,1,0:T(2,128)(2,1)S(1)} %shard_map.128.refs_0_.low_ref), channel_id=1, source_target_pairs={{0,4},{1,5},{2,6},{3,7},{4,0},{5,1},{6,2},{7,3},{8,12},{9,13},{10,... | collective-permute-start | bytes 196616 | tf_op jit(solution)/shard_map/ppermute | solution.py:22
  14.8 5.1 %collective-permute-start.2 = (bf16[4,2,8192]{2,1,0:T(2,128)(2,1)S(1)}, bf16[4,2,8192]{2,1,0:T(2,128)(2,1)S(1)}, u32[]{:S(2)}, u32[]{:S(2)}) collective-permute-start(bf16[4,2,8192]{2,1,0:T(2,128)(2,1)S(1)} %shard_map.130.refs_0_.low_ref), channel_id=1, source_target_pairs={{0,2},{1,3},{2,0},{3,1},{4,6},{5,7},{6,4},{7,5},{8,10},{9,11},{10,... | collective-permute-start | bytes 393224 | tf_op jit(solution)/shard_map/ppermute | solution.py:22
  19.9 1.7 copy-start.3
  19.9 14.6 %copy-start.4 = (s32[2,2]{1,0:T(2,128)S(1)}, s32[2,2]{1,0:T(2,128)}, u32[]{:S(2)}) copy-start(s32[2,2]{1,0:T(2,128)} %length_ref.3) | copy-start | bytes 52
  20.0 1.6 collective-permute-start.3
  47.8 1.6 collective-permute-start.4
  49.4 6.0 %collective-permute-start.5 = (bf16[4,32,512]{2,1,0:T(8,128)(2,1)S(1)}, bf16[4,32,512]{2,1,0:T(8,128)(2,1)S(1)}, u32[]{:S(2)}, u32[]{:S(2)}) collective-permute-start(bf16[4,32,512]{2,1,0:T(8,128)(2,1)S(1)} %get-tuple-element.75.token_ref), channel_id=1, source_target_pairs={{0,2},{1,3},{2,0},{3,1},{4,6},{5,7},{6,4},{7,5},{8,10},{9,11},{10,... | collective-permute-start | bytes 393224 | tf_op jit(solution)/shard_map/ppermute | solution.py:22
  55.4 6.0 %collective-permute-start.6 = (bf16[2,32,512]{2,1,0:T(8,128)(2,1)S(1)}, bf16[2,32,512]{2,1,0:T(8,128)(2,1)S(1)}, u32[]{:S(2)}, u32[]{:S(2)}) collective-permute-start(bf16[2,32,512]{2,1,0:T(8,128)(2,1)S(1)} %get-tuple-element.82.token_ref), channel_id=1, source_target_pairs={{0,4},{1,5},{2,6},{3,7},{4,0},{5,1},{6,2},{7,3},{8,12},{9,13},{10,... | collective-permute-start | bytes 196616 | tf_op jit(solution)/shard_map/ppermute | solution.py:22
  61.4 5.7 %collective-permute-start.7 = (bf16[2,32,512]{2,1,0:T(8,128)(2,1)S(1)}, bf16[2,32,512]{2,1,0:T(8,128)(2,1)S(1)}, u32[]{:S(2)}, u32[]{:S(2)}) collective-permute-start(bf16[2,32,512]{2,1,0:T(8,128)(2,1)S(1)} %shard_map.141.token_ref.here_ref), channel_id=1, source_target_pairs={{0,8},{1,9},{2,10},{3,11},{4,12},{5,13},{6,14},{7,15},{8,0},{9,1},... | collective-permute-start | bytes 196616 | tf_op jit(solution)/shard_map/ppermute | solution.py:22
  67.2 5.6 %collective-permute-start.8 = (bf16[2,32,512]{2,1,0:T(8,128)(2,1)S(1)}, bf16[2,32,512]{2,1,0:T(8,128)(2,1)S(1)}, u32[]{:S(2)}, u32[]{:S(2)}) collective-permute-start(bf16[2,32,512]{2,1,0:T(8,128)(2,1)S(1)} %shard_map.143.token_ref.low_ref), channel_id=1, source_target_pairs={{0,4},{1,5},{2,6},{3,7},{4,0},{5,1},{6,2},{7,3},{8,12},{9,13},{10,... | collective-permute-start | bytes 196616 | tf_op jit(solution)/shard_map/ppermute | solution.py:22
  72.8 5.2 %copy-start = (f32[1,8192]{1,0:T(1,128)S(1)}, f32[1,8192]{1,0:T(1,128)}, u32[]{:S(2)}) copy-start(f32[1,8192]{1,0:T(1,128)} %gain_ref.11) | copy-start | bytes 98308
  72.8 5.0 %collective-permute-start.9 = (bf16[4,32,512]{2,1,0:T(8,128)(2,1)S(1)}, bf16[4,32,512]{2,1,0:T(8,128)(2,1)S(1)}, u32[]{:S(2)}, u32[]{:S(2)}) collective-permute-start(bf16[4,32,512]{2,1,0:T(8,128)(2,1)S(1)} %shard_map.145.low_ref), channel_id=1, source_target_pairs={{0,2},{1,3},{2,0},{3,1},{4,6},{5,7},{6,4},{7,5},{8,10},{9,11},{10,... | collective-permute-start | bytes 393224 | tf_op jit(solution)/shard_map/ppermute | solution.py:22
  77.9 5.0 %collective-permute-start.10 = (bf16[8,32,512]{2,1,0:T(8,128)(2,1)S(1)}, bf16[8,32,512]{2,1,0:T(8,128)(2,1)S(1)}, u32[]{:S(2)}, u32[]{:S(2)}) collective-permute-start(bf16[8,32,512]{2,1,0:T(8,128)(2,1)S(1)} %shard_map.146.own_ref), channel_id=1, source_target_pairs={{0,1},{1,0},{2,3},{3,2},{4,5},{5,4},{6,7},{7,6},{8,9},{9,8},{10,11... | collective-permute-start | bytes 786440 | tf_op jit(solution)/shard_map/ppermute | solution.py:22
  90.8 2.2 %collective-permute-start.11 = (bf16[8,32,512]{2,1,0:T(8,128)(2,1)S(1)}, bf16[8,32,512]{2,1,0:T(8,128)(2,1)S(1)}, u32[]{:S(2)}, u32[]{:S(2)}) collective-permute-start(bf16[8,32,512]{2,1,0:T(8,128)(2,1)S(1)} %get-tuple-element.95), channel_id=1, source_target_pairs={{0,1},{1,0},{2,3},{3,2},{4,5},{5,4},{6,7},{7,6},{8,9},{9,8},{10,11... | collective-permute-start | bytes 786440 | tf_op jit(solution)/shard_map/ppermute | solution.py:22
  93.1 5.5 %collective-permute-start.12 = (bf16[4,32,512]{2,1,0:T(8,128)(2,1)S(1)}, bf16[4,32,512]{2,1,0:T(8,128)(2,1)S(1)}, u32[]{:S(2)}, u32[]{:S(2)}) collective-permute-start(bf16[4,32,512]{2,1,0:T(8,128)(2,1)S(1)} %get-tuple-element.97.refs_0_), channel_id=1, source_target_pairs={{0,2},{1,3},{2,0},{3,1},{4,6},{5,7},{6,4},{7,5},{8,10},{9,11},{10,... | collective-permute-start | bytes 393224 | tf_op jit(solution)/shard_map/ppermute | solution.py:22
  98.6 5.3 %collective-permute-start.13 = (bf16[2,32,512]{2,1,0:T(8,128)(2,1)S(1)}, bf16[2,32,512]{2,1,0:T(8,128)(2,1)S(1)}, u32[]{:S(2)}, u32[]{:S(2)}) collective-permute-start(bf16[2,32,512]{2,1,0:T(8,128)(2,1)S(1)} %get-tuple-element.101.refs_0_), channel_id=1, source_target_pairs={{0,4},{1,5},{2,6},{3,7},{4,0},{5,1},{6,2},{7,3},{8,12},{9,13},{10,... | collective-permute-start | bytes 196616 | tf_op jit(solution)/shard_map/ppermute | solution.py:22
  104.0 6.9 %collective-permute-start.15 = (bf16[2,32,512]{2,1,0:T(8,128)(2,1)S(1)}, bf16[2,32,512]{2,1,0:T(8,128)(2,1)S(1)}, u32[]{:S(2)}, u32[]{:S(2)}) collective-permute-start(bf16[2,32,512]{2,1,0:T(8,128)(2,1)S(1)} %shard_map.154.refs_0_), channel_id=1, source_target_pairs={{0,24},{1,25},{2,26},{3,27},{4,28},{5,29},{6,30},{7,31},{8,16},{9,... | collective-permute-start | bytes 196616 | tf_op jit(solution)/shard_map/ppermute | solution.py:296
  106.9 4.4 %collective-permute-start.14 = (bf16[2,32,512]{2,1,0:T(8,128)(2,1)S(1)}, bf16[2,32,512]{2,1,0:T(8,128)(2,1)S(1)}, u32[]{:S(2)}, u32[]{:S(2)}) collective-permute-start(bf16[2,32,512]{2,1,0:T(8,128)(2,1)S(1)} %shard_map.154.refs_0_), channel_id=1, source_target_pairs={{0,16},{1,17},{2,18},{3,19},{4,20},{5,21},{6,22},{7,23},{8,24},{9,... | collective-permute-start | bytes 196616 | tf_op jit(solution)/shard_map/ppermute | solution.py:296
  111.2 4.3 %collective-permute-start.16 = (bf16[2,32,512]{2,1,0:T(8,128)(2,1)S(1)}, bf16[2,32,512]{2,1,0:T(8,128)(2,1)S(1)}, u32[]{:S(2)}, u32[]{:S(2)}) collective-permute-start(bf16[2,32,512]{2,1,0:T(8,128)(2,1)S(1)} %shard_map.156.low_ref), channel_id=1, source_target_pairs={{0,4},{1,5},{2,6},{3,7},{4,0},{5,1},{6,2},{7,3},{8,12},{9,13},{10,... | collective-permute-start | bytes 196616 | tf_op jit(solution)/shard_map/ppermute | solution.py:22
  115.6 5.0 %collective-permute-start.17 = (bf16[4,32,512]{2,1,0:T(8,128)(2,1)S(1)}, bf16[4,32,512]{2,1,0:T(8,128)(2,1)S(1)}, u32[]{:S(2)}, u32[]{:S(2)}) collective-permute-start(bf16[4,32,512]{2,1,0:T(8,128)(2,1)S(1)} %shard_map.157.low_ref), channel_id=1, source_target_pairs={{0,2},{1,3},{2,0},{3,1},{4,6},{5,7},{6,4},{7,5},{8,10},{9,11},{10,... | collective-permute-start | bytes 393224 | tf_op jit(solution)/shard_map/ppermute | solution.py:22
  120.6 1.6 collective-permute-start.18
  150.1 1.6 collective-permute-start.19
  151.7 6.0 %collective-permute-start.20 = (bf16[4,32,512]{2,1,0:T(8,128)(2,1)S(1)}, bf16[4,32,512]{2,1,0:T(8,128)(2,1)S(1)}, u32[]{:S(2)}, u32[]{:S(2)}) collective-permute-start(bf16[4,32,512]{2,1,0:T(8,128)(2,1)S(1)} %get-tuple-element.107.token_ref), channel_id=1, source_target_pairs={{0,2},{1,3},{2,0},{3,1},{4,6},{5,7},{6,4},{7,5},{8,10},{9,11},{10,... | collective-permute-start | bytes 393224 | tf_op jit(solution)/shard_map/ppermute | solution.py:22
  157.7 6.0 %collective-permute-start.21 = (bf16[2,32,512]{2,1,0:T(8,128)(2,1)S(1)}, bf16[2,32,512]{2,1,0:T(8,128)(2,1)S(1)}, u32[]{:S(2)}, u32[]{:S(2)}) collective-permute-start(bf16[2,32,512]{2,1,0:T(8,128)(2,1)S(1)} %get-tuple-element.114.token_ref), channel_id=1, source_target_pairs={{0,4},{1,5},{2,6},{3,7},{4,0},{5,1},{6,2},{7,3},{8,12},{9,13},{10,... | collective-permute-start | bytes 196616 | tf_op jit(solution)/shard_map/ppermute | solution.py:22
  163.8 5.7 %collective-permute-start.22 = (bf16[2,32,512]{2,1,0:T(8,128)(2,1)S(1)}, bf16[2,32,512]{2,1,0:T(8,128)(2,1)S(1)}, u32[]{:S(2)}, u32[]{:S(2)}) collective-permute-start(bf16[2,32,512]{2,1,0:T(8,128)(2,1)S(1)} %shard_map.167.token_ref.here_ref), channel_id=1, source_target_pairs={{0,8},{1,9},{2,10},{3,11},{4,12},{5,13},{6,14},{7,15},{8,0},{9,1},... | collective-permute-start | bytes 196616 | tf_op jit(solution)/shard_map/ppermute | solution.py:22
  169.5 5.6 %collective-permute-start.23 = (bf16[2,32,512]{2,1,0:T(8,128)(2,1)S(1)}, bf16[2,32,512]{2,1,0:T(8,128)(2,1)S(1)}, u32[]{:S(2)}, u32[]{:S(2)}) collective-permute-start(bf16[2,32,512]{2,1,0:T(8,128)(2,1)S(1)} %shard_map.169.token_ref.low_ref), channel_id=1, source_target_pairs={{0,4},{1,5},{2,6},{3,7},{4,0},{5,1},{6,2},{7,3},{8,12},{9,13},{10,... | collective-permute-start | bytes 196616 | tf_op jit(solution)/shard_map/ppermute | solution.py:22
  175.2 5.0 %collective-permute-start.24 = (bf16[4,32,512]{2,1,0:T(8,128)(2,1)S(1)}, bf16[4,32,512]{2,1,0:T(8,128)(2,1)S(1)}, u32[]{:S(2)}, u32[]{:S(2)}) collective-permute-start(bf16[4,32,512]{2,1,0:T(8,128)(2,1)S(1)} %shard_map.171.low_ref), channel_id=1, source_target_pairs={{0,2},{1,3},{2,0},{3,1},{4,6},{5,7},{6,4},{7,5},{8,10},{9,11},{10,... | collective-permute-start | bytes 393224 | tf_op jit(solution)/shard_map/ppermute | solution.py:22
  180.2 5.0 %collective-permute-start.25 = (bf16[8,32,512]{2,1,0:T(8,128)(2,1)S(1)}, bf16[8,32,512]{2,1,0:T(8,128)(2,1)S(1)}, u32[]{:S(2)}, u32[]{:S(2)}) collective-permute-start(bf16[8,32,512]{2,1,0:T(8,128)(2,1)S(1)} %shard_map.172.own_ref), channel_id=1, source_target_pairs={{0,1},{1,0},{2,3},{3,2},{4,5},{5,4},{6,7},{7,6},{8,9},{9,8},{10,11... | collective-permute-start | bytes 786440 | tf_op jit(solution)/shard_map/ppermute | solution.py:22
  194.7 1.7 collective-permute-start.26

commit v7 on v6

--- a/solution.py
+++ b/solution.py
@@ -127,33 +127,6 @@
     )(where, placed_in(keys, pltpu.HBM), placed_in(values, pltpu.HBM), *tokens)
 
 
-def fetch_chunks_kernel(ids_ref, token_ref, source, target, sems):
-    count, _, chunk = target.shape
-    run_copies(
-        [
-            pltpu.make_async_copy(
-                source.at[:, span_of(ids_ref, k, chunk)], target.at[k], sems.at[k]
-            )
-            for k in range(count)
-        ]
-    )
-
-
-def fetch_chunks(token, ids, weights, chunk):
-    count, depth = ids.shape[0], weights.shape[0]
-    return pl.pallas_call(
-        fetch_chunks_kernel,
-        out_shape=[pltpu.VMEM((count, depth, chunk), weights.dtype)],
-        in_specs=[smem(), hbm(), hbm()],
-        out_specs=[vmem()],
-        scratch_shapes=[pltpu.SemaphoreType.DMA((count,))],
-        compiler_params=pltpu.CompilerParams(vmem_limit_bytes=1 << 20),
-        cost_estimate=pl.CostEstimate(
-            flops=0, bytes_accessed=2 * count * depth * chunk, transcendentals=0
-        ),
-    )(ids, token, placed_in(weights, pltpu.HBM))
-
-
 def fetch_pairs_kernel(items, ids_ref, token_ref, source, *refs):
     targets, sems = refs[:-1], refs[-1]
     half = sems.shape[1]
@@ -189,6 +162,10 @@
     )(ids, token, placed_in(weights, pltpu.HBM))
 
 
+def in_vmem(arrays):
+    return [placed_in(x, pltpu.VMEM) if x.size > 1 << 14 else x for x in arrays]
+
+
 def step_call(kernel, shapes, operands, held_back):
     return pl.pallas_call(
         kernel,
@@ -197,9 +174,9 @@
         out_specs=[vmem()] * len(shapes),
         compiler_params=pltpu.CompilerParams(vmem_limit_bytes=4 << 20),
         cost_estimate=pl.CostEstimate(
-            flops=2 * operands[0].size, bytes_accessed=6 * operands[0].size, transcendentals=0
-        ),
-    )(*operands, *[placed_in(array, pltpu.VMEM) for array in held_back])
+            flops=2 * operands[-1].size, bytes_accessed=6 * operands[-1].size, transcendentals=0
+        ),
+    )(*operands, *in_vmem(held_back))
 
 
 def add_kernel(outs, operands, *refs):
@@ -221,23 +198,19 @@
     )
 
 
-def own_kernel(own_ref, keep_ref, got_ref, *refs):
-    out_ref = refs[-1]
-    if len(own_ref.shape) == 2:
-        own = own_ref[...].astype(jnp.float32)
-    else:
-        parts = [own_ref[owner].astype(jnp.float32) for owner in range(own_ref.shape[0])]
-        own = jnp.concatenate(parts, axis=0)
-    for place in range(keep_ref.shape[0]):
-        total = keep_ref[place].astype(jnp.float32) + got_ref[place].astype(jnp.float32)
-        out_ref[place] = (total + own if place == 0 else total).astype(jnp.bfloat16)
-
-
-def cross_kernel(here_ref, there_ref, *refs):
+def cross_kernel(addend_ref, here_ref, there_ref, *refs):
     out_ref = refs[-1]
     for place in range(2):
+        if len(addend_ref.shape) == 3:
+            addend = addend_ref[place].astype(jnp.float32)
+        else:
+            owners = range(addend_ref.shape[1])
+            parts = [addend_ref[place, owner].astype(jnp.float32) for owner in owners]
+            addend = jnp.concatenate(parts, axis=0)
         out_ref[place] = (
-            here_ref[place].astype(jnp.float32) + there_ref[1 - place].astype(jnp.float32)
+            addend
+            + here_ref[place].astype(jnp.float32)
+            + there_ref[1 - place].astype(jnp.float32)
         ).astype(jnp.bfloat16)
 
 
@@ -272,38 +245,52 @@
     return keep, got, held_back
 
 
-def spread_pair(pair, jobs):
-    held = pair
-    for mask in reversed(chip_masks()[:-1]):
-        got = swap(held, mask)
-        held = join(held, got, run_job(jobs, held))
-    return held, swap(held, 1)
-
-
-def reduce_to_all(keep, got, own, jobs, hops):
-    keep, got, held_back = halve(keep, got, jobs)
-    (held,) = step_call(own_kernel, [keep.shape], (own, keep, got), held_back)
-    far = chip_masks()[-1]
-    here = hop(held, 0) if hops else held
-    there = hop(held, far) if hops else swap(held, far)
-    (pair,) = step_call(cross_kernel, [held.shape], (here, there), run_job(jobs, held))
-    return (pair[0], *spread_pair(pair, jobs))
-
-
 def hop(part, mask):
     count = lax.axis_size("mp")
     pairs = [(source, ((source + count) % (2 * count)) ^ mask) for source in range(2 * count)]
     return lax.ppermute(part, ("section", "mp"), pairs)
 
 
+def reduce_to_pair(keep, got, addend, jobs, hops):
+    keep, got, held_back = halve(keep, got, jobs)
+    (held,) = add_parts((keep, got), 1, held_back)
+    far = chip_masks()[-1]
+    here = hop(held, 0) if hops else held
+    there = hop(held, far) if hops else swap(held, far)
+    if hops:
+        addend = hop(addend, 0)
+    return step_call(cross_kernel, [held.shape], (addend, here, there), run_job(jobs, held))[0]
+
+
+def spread_pair(pair, jobs):
+    held = pair
+    for mask in reversed(chip_masks()[1:-1]):
+        got = swap(held, mask)
+        held = join(held, got, run_job(jobs, held))
+    got = swap(held, chip_masks()[0])
+    return held, swap(held, 1), got
+
+
+def all_quarters(quarters):
+    return *quarters, swap(quarters[2], 1)
+
+
+def pass_kernel(in_ref, *refs):
+    refs[-1][...] = in_ref[...]
+
+
 def gather_doubling(part, jobs):
     held = part[None]
     got = swap(held, chip_masks()[-1])
     return spread_pair(join(held, got, run_job(jobs, held)), jobs)
 
 
+def quarter_starts(count):
+    return 0, count // 2, count // 4, count // 2 + count // 4
+
+
 def inverse_rms(x_refs):
-    half, rows, chunk = x_refs[0].shape
+    parts, rows, chunk = x_refs[0].shape
     total = jnp.zeros((rows, chunk), jnp.float32)
     for x_ref in x_refs:
 
@@ -313,8 +300,9 @@
                 total = total + wide * wide
             return total
 
-        total = lax.fori_loop(0, half // UNROLL, add, total)
-    return lax.rsqrt(jnp.sum(total, axis=-1, keepdims=True) / (2 * half * chunk) + epsilon)
+        total = lax.fori_loop(0, parts // UNROLL, add, total)
+    mean = jnp.sum(total, axis=-1, keepdims=True) / (4 * parts * chunk)
+    return lax.rsqrt(mean + epsilon)
 
 
 def span_of(ids_ref, k, chunk):
@@ -326,16 +314,18 @@
     return (wide * scale * gain_ref[:, span]).astype(jnp.bfloat16)
 
 
-def project_kernel(ids_ref, own_ref, other_ref, gain_ref, wq_ref, wk_ref, wv_ref, out_ref,
-                   mine_ref, q_sum, kv_sum, wide):
+def project_kernel(ids_ref, *refs):
+    x_refs, (gain_ref, wq_ref, wk_ref, wv_ref) = refs[:4], refs[4:8]
+    out_ref, mine_ref, q_sum, kv_sum, wide = refs[-5:]
     queries = wq_ref.shape[1]
     count, rows_dev, _ = out_ref.shape
-    half = count // 2
-    by_rows = own_ref.shape[1] == rows_dev
+    quarter = count // 4
+    by_rows = x_refs[0].shape[1] == rows_dev
     chunk = wq_ref.shape[0] // count
+    starts = quarter_starts(count)
     if by_rows:
-        for first, x_ref in ((0, own_ref), (half, other_ref)):
-            for place in range(half):
+        for first, x_ref in zip(starts, x_refs):
+            for place in range(quarter):
                 at = (first + place) * rows_dev
                 wide[at : at + rows_dev, :] = x_ref[place].astype(jnp.float32)
         total = 0.0
@@ -345,12 +335,12 @@
         mean = jnp.sum(total, axis=-1, keepdims=True) / (count * chunk)
         scale = lax.rsqrt(mean + epsilon)
     else:
-        scale = inverse_rms((own_ref, other_ref))
+        scale = inverse_rms(x_refs)
     q_sum[...] = jnp.zeros_like(q_sum)
     kv_sum[...] = jnp.zeros_like(kv_sum)
-    for first, x_ref in ((0, own_ref), (half, other_ref)):
-
-        @pl.loop(0, half // UNROLL)
+    for first, x_ref in zip(starts, x_refs):
+
+        @pl.loop(0, quarter // UNROLL)
         def _(group):
             q_part = 0.0
             kv_part = 0.0
@@ -378,25 +368,26 @@
         out_ref[owner, :, :queries] = q_sum[lines, :].astype(jnp.bfloat16)
         out_ref[owner, :, queries:] = kv_sum[lines, :].astype(jnp.bfloat16)
         if by_rows:
-            span = span_of(ids_ref, 0, chunk)
-            mine_ref[owner] = wide[lines, span].astype(jnp.bfloat16)
-
-
-def project(ids, own, other, gain, wq, wk, wv):
+            for which in range(2):
+                span = span_of(ids_ref, which, chunk)
+                mine_ref[which, owner] = wide[lines, span].astype(jnp.bfloat16)
+
+
+def project(ids, quarters, gain, wq, wk, wv, held_back):
     count = ids.shape[0]
     width, queries = wq.shape
     keys = wk.shape[0]
     size = queries + 2 * keys
-    rows_dev = 2 * own.size // (count * width)
+    rows_dev = 4 * quarters[0].size // (count * width)
     rows = count * rows_dev
-    by_rows = own.shape[1] == rows_dev
+    by_rows = quarters[0].shape[1] == rows_dev
     return pl.pallas_call(
         project_kernel,
         out_shape=[
             pltpu.VMEM((count, rows_dev, size), jnp.bfloat16),
-            pltpu.VMEM((count, rows_dev, width // count), jnp.bfloat16),
+            pltpu.VMEM((2, count, rows_dev, width // count), jnp.bfloat16),
         ],
-        in_specs=[smem()] + [vmem()] * 6,
+        in_specs=[smem()] + [vmem()] * 8 + [hbm()] * len(held_back),
         out_specs=[vmem(), vmem()],
         scratch_shapes=[
             pltpu.VMEM((rows, queries), jnp.float32),
@@ -407,7 +398,7 @@
         cost_estimate=pl.CostEstimate(
             flops=2 * rows * width * size, bytes_accessed=2 * width * size, transcendentals=0
         ),
-    )(ids, own, other, gain, *[placed_in(w, pltpu.VMEM) for w in (wq, wk, wv)])
+    )(ids, *quarters, gain, *in_vmem((wq, wk, wv, *held_back)))
 
 
 def attend_kernel(where_ref, length_ref, in_ref, cos_ref, sin_ref, key_buf, value_buf, out_ref,
@@ -552,10 +543,11 @@
 
 
 def gate_up(ids_ref, first, x_ref, gain_ref, blocks, stacked, wide_x, total_ref):
-    half, rows, chunk = x_ref.shape
+    parts, rows, chunk = x_ref.shape
     per_chunk = chunk // 128
-
-    @pl.loop(0, half // UNROLL)
+    base = first % (2 * parts)
+
+    @pl.loop(0, parts // UNROLL)
     def _(group):
         for step in range(UNROLL):
             place = group * UNROLL + step
@@ -568,11 +560,10 @@
     column = lax.broadcasted_iota(jnp.int32, (128, 512), 1)
     aim = jnp.where(column < 256, 2 * line, 2 * line + 257)
     widen = jnp.where(column == aim, 1.0, 0.0).astype(jnp.bfloat16)
-
-    @pl.loop(0, wide_x.shape[0])
-    def _(group):
+    groups = parts * per_chunk // 8
+    for group in range(groups):
         wide = jnp.dot(
-            stacked[pl.ds(group * 8, 8)].reshape(8 * rows, 128),
+            stacked[group * 8 : (group + 1) * 8].reshape(8 * rows, 128),
             widen,
             preferred_element_type=jnp.float32,
         ).astype(jnp.bfloat16)
@@ -583,12 +574,12 @@
 
     per_group = 8 // per_chunk
 
-    @pl.loop(0, wide_x.shape[0])
+    @pl.loop(0, groups)
     def _(group):
         for j in range(0, len(blocks), 2):
             part = 0.0
             for step in range(per_group):
-                at = (group * per_group + step) * (2 * chunk)
+                at = (base + group * per_group + step) * (2 * chunk)
                 span = pl.ds(pl.multiple_of(at, 2 * chunk), 2 * chunk)
                 pair = jnp.concatenate([blocks[j][span, :], blocks[j + 1][span, :]], axis=1)
                 part += jnp.dot(
@@ -599,55 +590,77 @@
             total_ref[:, j * 128 : (j + 2) * 128] += part
 
 
-def own_half_kernel(ids_ref, own_ref, gain_ref, *refs):
-    blocks, (total_ref, stacked, wide_x) = refs[:-3], refs[-3:]
-    total_ref[...] = jnp.zeros_like(total_ref)
-    gate_up(ids_ref, 0, own_ref, gain_ref, blocks, stacked, wide_x, total_ref)
-
-
-def own_half(ids, own, gain, pairs):
-    half, rows, chunk = own.shape
-    units = 128 * len(pairs)
-    width = 2 * half * chunk
+def down_copies(ids_ref, first, source, target, sems):
+    count, _, chunk = target.shape
+
+    def copy(k):
+        return pltpu.make_async_copy(
+            source.at[:, span_of(ids_ref, first + k, chunk)], target.at[k], sems.at[k]
+        )
+
+    return [copy(k) for k in range(count)]
+
+
+def quarter_kernel(first, fetch_first, ids_ref, x_ref, gain_ref, before_ref, down_hbm, *refs):
+    blocks, (total_ref, down_ref, stacked, wide_x, sems) = refs[:-5], refs[-5:]
+    copies = []
+    if fetch_first is not None:
+        copies = down_copies(ids_ref, fetch_first, down_hbm, down_ref, sems)
+    for copy in copies:
+        copy.start()
+    if first:
+        total_ref[...] = before_ref[...]
+    else:
+        total_ref[...] = jnp.zeros_like(total_ref)
+    gate_up(ids_ref, first, x_ref, gain_ref, blocks, stacked, wide_x, total_ref)
+    for copy in copies:
+        copy.wait()
+
+
+def quarter(first, fetch_first, ids, x, gain, before, down, pairs):
+    parts, rows, chunk = x.shape
+    units, width = down.shape
+    got = (parts, units, chunk) if fetch_first is not None else (1, 8, 128)
     return pl.pallas_call(
-        own_half_kernel,
-        out_shape=pltpu.VMEM((2 * rows, units), jnp.float32),
-        in_specs=[smem(), vmem(), vmem()] + [vmem()] * len(pairs),
-        out_specs=vmem(),
+        functools.partial(quarter_kernel, first, fetch_first),
+        out_shape=[
+            pltpu.VMEM((2 * rows, units), jnp.float32),
+            pltpu.VMEM(got, jnp.bfloat16),
+        ],
+        in_specs=[smem()] + [vmem()] * 3 + [hbm()] + [vmem()] * len(pairs),
+        out_specs=[vmem(), vmem()],
         scratch_shapes=[
-            pltpu.VMEM((width // 256, rows, 128), jnp.bfloat16),
-            pltpu.VMEM((width // 2048, 2 * rows, 2048), jnp.bfloat16),
+            pltpu.VMEM((width // 512, rows, 128), jnp.bfloat16),
+            pltpu.VMEM((width // 4096, 2 * rows, 2048), jnp.bfloat16),
+            pltpu.SemaphoreType.DMA((parts,)),
         ],
-        compiler_params=pltpu.CompilerParams(vmem_limit_bytes=(2 << 20) + 5 * rows * width),
+        compiler_params=pltpu.CompilerParams(vmem_limit_bytes=(2 << 20) + 5 * rows * width // 2),
         cost_estimate=pl.CostEstimate(
-            flops=2 * rows * units * width, bytes_accessed=2 * units * width, transcendentals=0
-        ),
-    )(ids, own, gain, *pairs)
-
-
-def other_half_kernel(last, me_ref, ids_ref, own_ref, other_ref, gain_ref, own_total, near_ref,
-                      down_hbm, *refs):
-    blocks, outs, (stacked, wide_x, total, act, far_ref, sems) = refs[:-9], refs[-9:-6], refs[-6:]
-    half, rows, chunk = own_ref.shape
-
-    def far_copy(k):
-        return pltpu.make_async_copy(
-            down_hbm.at[:, span_of(ids_ref, half + k, chunk)], far_ref.at[k], sems.at[k]
-        )
-
-    @pl.loop(0, half)
-    def _(k):
-        far_copy(k).start()
-
-    total[...] = own_total[...]
-    gate_up(ids_ref, half, other_ref, gain_ref, blocks, stacked, wide_x, total)
-    scale = inverse_rms((own_ref, other_ref))
+            flops=rows * units * width, bytes_accessed=units * width, transcendentals=0
+        ),
+    )(ids, x, gain, before, placed_in(down, pltpu.HBM), *pairs)
+
+
+def finish_kernel(last, me_ref, ids_ref, *refs):
+    x_refs, (gain_ref, before_ref, low_ref, high_ref, down_hbm) = refs[:4], refs[4:9]
+    blocks, outs, (stacked, wide_x, total, act, far_ref, sems) = refs[9:-9], refs[-9:-6], refs[-6:]
+    parts, rows, chunk = x_refs[0].shape
+    half = 2 * parts
+    copies = down_copies(ids_ref, half, down_hbm, far_ref, sems)
+    for copy in copies:
+        copy.start()
+    total[...] = before_ref[...]
+    starts = quarter_starts(2 * half)
+    gate_up(ids_ref, starts[3], x_refs[3], gain_ref, blocks, stacked, wide_x, total)
+    scale = inverse_rms(x_refs)
     gate = total[:rows, :] * scale
     act[...] = (gate / (1.0 + jnp.exp(-gate)) * (total[rows:, :] * scale)).astype(jnp.bfloat16)
 
     def down(weights):
         return jnp.dot(act[...], weights, preferred_element_type=jnp.float32)
 
+    for copy in copies:
+        copy.wait()
     if not last:
         send_ref, act_ref, _ = outs
         act_ref[...] = act[...]
@@ -656,7 +669,6 @@
         def _(group):
             for step in range(UNROLL):
                 k = group * UNROLL + step
-                far_copy(k).wait()
                 send_ref[k] = down(far_ref[k]).astype(jnp.bfloat16)
 
         return
@@ -665,9 +677,9 @@
     rows_dev = middle_ref.shape[0]
     line = lax.broadcasted_iota(jnp.int32, (rows, 1), 0)
     first_core = lax.rem(me_ref[0], 2) == 0
-    for first, x_ref in ((0, own_ref), (half, other_ref)):
-
-        @pl.loop(0, half // UNROLL)
+    for which, (first, x_ref) in enumerate(zip(starts, x_refs)):
+
+        @pl.loop(0, parts // UNROLL)
         def _(group):
             for step in range(UNROLL):
                 k = group * UNROLL + step
@@ -678,9 +690,10 @@
                     middle_ref[row : row + 1, span] = jnp.sum(
                         jnp.where(here, wide, 0.0), axis=0, keepdims=True
                     )
-                if first:
-                    far_copy(k).wait()
-                part = down(far_ref[k] if first else near_ref[k])
+                if which % 2:
+                    part = down(far_ref[first - half + k])
+                else:
+                    part = down((high_ref if which else low_ref)[k])
                 for chip in range(half):
                     at = 2 * chip * rows_dev
                     low = part[at : at + rows_dev]
@@ -689,59 +702,76 @@
                     send_ref[chip, :, span] = jnp.where(first_core, high, low).astype(jnp.bfloat16)
 
 
-def other_half(last, me, ids, own, other, gain, own_total, near, down, pairs):
-    half, rows, chunk = own.shape
+def finish(last, me, ids, quarters, gain, before, low, high, down, pairs):
+    parts, rows, chunk = quarters[0].shape
+    half = 2 * parts
     units, width = down.shape
     rows_dev = rows // (2 * half)
     if last:
         shapes = [((half, rows_dev, width), jnp.bfloat16)] * 2 + [((rows_dev, width), jnp.float32)]
     else:
-        shapes = [(own.shape, jnp.bfloat16), ((rows, units), jnp.bfloat16), ((8, 128), jnp.float32)]
+        shapes = [
+            ((half, rows, chunk), jnp.bfloat16),
+            ((rows, units), jnp.bfloat16),
+            ((8, 128), jnp.float32),
+        ]
     return pl.pallas_call(
-        functools.partial(other_half_kernel, last),
+        functools.partial(finish_kernel, last),
         out_shape=[pltpu.VMEM(shape, kind) for shape, kind in shapes],
-        in_specs=[smem(), smem()] + [vmem()] * 5 + [hbm()] + [vmem()] * len(pairs),
+        in_specs=[smem(), smem()] + [vmem()] * 8 + [hbm()] + [vmem()] * len(pairs),
         out_specs=[vmem()] * 3,
         scratch_shapes=[
-            pltpu.VMEM((width // 256, rows, 128), jnp.bfloat16),
-            pltpu.VMEM((width // 2048, 2 * rows, 2048), jnp.bfloat16),
+            pltpu.VMEM((width // 512, rows, 128), jnp.bfloat16),
+            pltpu.VMEM((width // 4096, 2 * rows, 2048), jnp.bfloat16),
             pltpu.VMEM((2 * rows, units), jnp.float32),
             pltpu.VMEM((rows, units), jnp.bfloat16),
             pltpu.VMEM((half, units, chunk), jnp.bfloat16),
             pltpu.SemaphoreType.DMA((half,)),
         ],
         compiler_params=pltpu.CompilerParams(
-            vmem_limit_bytes=(2 << 20) + 5 * rows * width + (10 * rows + width) * units
+            vmem_limit_bytes=(2 << 20) + 5 * rows * width // 2 + (10 * rows + width) * units
         ),
         cost_estimate=pl.CostEstimate(
-            flops=4 * rows * units * width, bytes_accessed=3 * units * width, transcendentals=0
-        ),
-    )(me, ids, own, other, gain, own_total, near, placed_in(down, pltpu.HBM), *pairs)
-
-
-def keep_kernel(act_ref, near_ref, out_ref):
-    @pl.loop(0, out_ref.shape[0] // UNROLL)
-    def _(group):
-        for step in range(UNROLL):
-            k = group * UNROLL + step
-            out_ref[k] = jnp.dot(
-                act_ref[...], near_ref[k], preferred_element_type=jnp.float32
-            ).astype(jnp.bfloat16)
-
-
-def keep_half(act, near):
+            flops=3 * rows * units * width, bytes_accessed=2 * units * width, transcendentals=0
+        ),
+    )(
+        me,
+        ids,
+        *quarters,
+        gain,
+        before,
+        *in_vmem((low, high)),
+        placed_in(down, pltpu.HBM),
+        *pairs,
+    )
+
+
+def keep_kernel(act_ref, low_ref, high_ref, out_ref):
+    parts = low_ref.shape[0]
+    for first, near_ref in ((0, low_ref), (parts, high_ref)):
+
+        @pl.loop(0, parts // UNROLL)
+        def _(group):
+            for step in range(UNROLL):
+                k = group * UNROLL + step
+                out_ref[first + k] = jnp.dot(
+                    act_ref[...], near_ref[k], preferred_element_type=jnp.float32
+                ).astype(jnp.bfloat16)
+
+
+def keep_half(act, low, high):
     rows = act.shape[0]
-    half, _, chunk = near.shape
+    parts, _, chunk = low.shape
     return pl.pallas_call(
         keep_kernel,
-        out_shape=pltpu.VMEM((half, rows, chunk), jnp.bfloat16),
-        in_specs=[vmem(), vmem()],
+        out_shape=pltpu.VMEM((2 * parts, rows, chunk), jnp.bfloat16),
+        in_specs=[vmem(), vmem(), vmem()],
         out_specs=vmem(),
         compiler_params=pltpu.CompilerParams(vmem_limit_bytes=4 << 20),
         cost_estimate=pl.CostEstimate(
-            flops=2 * rows * near.size, bytes_accessed=2 * near.size, transcendentals=0
-        ),
-    )(act, near)
+            flops=4 * rows * low.size, bytes_accessed=4 * low.size, transcendentals=0
+        ),
+    )(act, *in_vmem((low, high)))
 
 
 def turning(positions):
@@ -778,7 +808,7 @@
     wk = w_key[0].T
     wv = w_value[0].T
     blocks = w_gate_up.shape[3] // 128
-    windows = len(chip_masks())
+    windows = 2 * len(chip_masks()) - 2
     bounds = [(4 * blocks * step + windows) // (2 * windows) for step in range(windows + 1)]
     batches = [
         jnp.remainder(section_index + turn_index, 2).astype(jnp.int32).reshape(1)
@@ -804,18 +834,24 @@
             return got["out"]
 
         def caches(token):
-            tokens = (token,) if turn_index else (token, *early)
-            got["caches"] = fetch_caches(tokens, batches[turn_index], key_cache[0], value_cache[0])
+            got["caches"] = fetch_caches((token,), batches[turn_index], key_cache[0], value_cache[0])
             return got["caches"]
 
-        return got, [caches, projections, out_projection]
-
-    got, jobs = attention_jobs(0)
-    own, other = gather_doubling(hidden[0], jobs)
+        if turn_index == 0:
+            return got, [lambda token: early, projections], [out_projection, caches]
+        return got, [projections, caches, out_projection], []
+
+    got, jobs, rest = attention_jobs(0)
+    quarters = gather_doubling(hidden[0], jobs)
+    for job in rest:
+        job(quarters[0])
     for turn_index in range(2):
         last = turn_index == 1
         batch = batches[turn_index]
-        joined, by_owner = project(places, own, other, attn_gain, *got["qkv"])
+        held_back = (*got["out"], *got["caches"])
+        joined, by_owner = project(places, all_quarters(quarters), attn_gain, *got["qkv"], held_back)
+        if turn_index == 0:
+            addend = by_owner
         spread = lax.all_to_all(joined, "mp", split_axis=0, concat_axis=0)
         mixed = attend(
             batch, lengths, spread, *tables[turn_index], *got["caches"], w_query.shape[2]
@@ -837,33 +873,39 @@
 
         items = [(side, block) for side in range(2) for block in range(blocks)]
         jobs = [pair_job(items[low:high]) for low, high in zip(bounds, bounds[1:])]
-        near_down = []
-
-        def down_job(token):
-            near_down.extend(fetch_chunks(token, near_places, w_down[0], width // count))
-            return near_down
-
-        jobs.append(down_job)
-        addend = by_owner if turn_index == 0 else mine
-        middle, own, other = reduce_to_all(keep, got_core, addend, jobs, False)
-        near_pairs, far_pairs = (
+        middle = reduce_to_pair(keep, got_core, addend, jobs, False)
+        quarters = spread_pair(middle, jobs)
+        sides = [
             [
                 placed_in(pairs[side, block].reshape(width, 128), pltpu.VMEM)
                 for block in range(blocks)
             ]
             for side in range(2)
-        )
-        own_total = own_half(places, own, mlp_gain, near_pairs)
-        send, act, own_rows = other_half(
-            last, me, places, own, other, mlp_gain, own_total, near_down[0], w_down[0], far_pairs
+        ]
+        total = jnp.zeros((8, 128), jnp.float32)
+        down = []
+        for which, first in enumerate(quarter_starts(count)[:3]):
+            if which == 2:
+                far_parts = quarters[2]
+                (far_parts,) = step_call(pass_kernel, [far_parts.shape], (far_parts,), (total,))
+                quarters = all_quarters((*quarters[:2], far_parts))
+            fetch_first = (0, count // 4, None)[which]
+            total, got_down = quarter(
+                first, fetch_first, places, quarters[which], mlp_gain, total, w_down[0],
+                sides[which % 2],
+            )
+            down.append(got_down)
+        send, act, own_rows = finish(
+            last, me, places, quarters, mlp_gain, total, *down[:2], w_down[0], sides[1]
         )
         if last:
             mine = (own_rows + scatter(send, act)).astype(jnp.bfloat16)
         else:
-            got, jobs = attention_jobs(1)
+            got, jobs, _ = attention_jobs(1)
             got_core = swap(send, 1)
-            keep = keep_half(act, near_down[0])
-            mine, own, other = reduce_to_all(keep, got_core, middle, jobs, True)
+            keep = keep_half(act, *down[:2])
+            addend = reduce_to_pair(keep, got_core, middle, jobs, True)
+            quarters = spread_pair(addend, jobs)
     return mine[None]
 
 

time: 211 us -> 205 us (0.972)
  Pallas kernels: 107 us -> 103 us
  waiting for transfers between devices: 21.3 us -> 18.7 us
  blocking collectives: 52.1 us -> 54.3 us
    pallas_call x7 -> x9, Pallas kernels: 37.1 us -> 31.3 us  [the longest x6 16.7 us: quarter(): pl.pallas_call(functools.partial(quarter_kernel, first, fetch_first), out...]
    ppermute x25 -> x29, waiting for transfers between devices: 21 us -> 17.9 us  [swap(): lax.ppermute(value, axis, [(source, source ^ mask) for source in range(co...]
    pallas_call x6 -> x8, Pallas kernels: 30.8 us -> 33.7 us  [fetch_pairs(): pl.pallas_call(functools.partial(fetch_pairs_kernel, items), out_shape=[p...]
    ppermute x25 -> x29, starting transfers between devices: 23.1 us -> 20.5 us  [swap(): lax.ppermute(value, axis, [(source, source ^ mask) for source in range(co...]
  transfers between devices with their start and end apart: 27 -> 32, of which waited for: 11 -> 11; matrix products, arithmetic and copies ran while one was open for 1% -> 1% of each run, Pallas kernels for 35% -> 37%
where the time goes in v7:
time: 205 us
  Pallas kernels  103 us (50%)
  blocking collectives  54.3 us (26%)
  starting transfers between devices  24.7 us (12%)
  waiting for transfers between devices  18.7 us (9%)
  other arithmetic  2.65 us (1%)
    pallas_call x8, Pallas kernels, fetch_pairs(): pl.pallas_call(functools.partial(fetch_pairs_kernel, items), out_shape=[p...  33.7 us
    all_to_all x2, blocking collectives, body(): spread = lax.all_to_all(joined, 'mp', split_axis=0, concat_axis=0)  22.2 us
    ppermute x29, starting transfers between devices, swap(): lax.ppermute(value, axis, [(source, source ^ mask) for source in range(co...  20.5 us
    all_to_all x2, blocking collectives, body(): lax.all_to_all(mixed.transpose(1, 0, 2), 'mp', split_axis=0, concat_axis=0)  18.4 us
    ppermute x29, waiting for transfers between devices, swap(): lax.ppermute(value, axis, [(source, source ^ mask) for source in range(co...  17.9 us
    pallas_call x6, Pallas kernels, quarter(): pl.pallas_call(functools.partial(quarter_kernel, first, fetch_first), out...  16.7 us
    pallas_call x4, Pallas kernels, fetch(): pl.pallas_call(functools.partial(fetch_kernel, pieces, len(tokens)), out_...  15.5 us
    all_to_all x1, blocking collectives, exchange(): lax.all_to_all(parts, 'mp', split_axis=0, concat_axis=0, axis_index_group...  13.6 us
  transfers between devices with their start and end apart: 32, of which 11 were waited for; matrix products, arithmetic and copies ran while one was open for 1% of the time, Pallas kernels for 37%

profile of v7, /device:TPU:0, one launch (start us, length us, event | category | flops | bytes accessed | tf_op | source)
XLA Modules:
  0.0 204.9 jit_solution(13391416690230901996)
XLA Ops:
  0.0 4.0 %collective-permute-start = (bf16[1,2,8192]{2,1,0:T(2,128)(2,1)}, bf16[1,2,8192]{2,1,0:T(2,128)(2,1)S(1)}, u32[]{:S(2)}, u32[]{:S(2)}) collective-permute-start(bf16[1,2,8192]{2,1,0:T(2,128)(2,1)} %low_ref.1), channel_id=1, source_target_pairs={{0,8},{1,9},{2,10},{3,11},{4,12},{5,13},{6,14},{7,15},{8,0},{9,1},... | collective-permute-start | bytes 98312 | tf_op jit(solution)/shard_map/ppermute | solution.py:22
  8.8 4.3 %shard_map.128 = (bf16[8192,512]{1,0:T(8,128)(2,1)S(1)}, bf16[64,8192]{1,0:T(8,128)(2,1)S(1)}, bf16[64,8192]{1,0:T(8,128)(2,1)S(1)}) custom-call(bf16[2,2,8192]{2,1,0:T(2,128)(2,1)S(1)} %shard_map.127.refs_0_.low_ref, bf16[8192,512]{1,0:T(8,128)(2,1)} %bitcast.139, bf16[64,8192]{1,0:T(8,128)(2,1)} %bitcast.147, bf16[64,8192]{1,0:T(8,128)(2,1)} %bitcast.149), custom_call_target="tpu_custom_call" | custom-call | bytes 10485760 | tf_op jit(solution)/shard_map/pallas_call | solution.py:83
  14.7 3.4 %collective-permute-done.3.refs_2_ = bf16[4,2,8192]{2,1,0:T(2,128)(2,1)S(1)} collective-permute-done((bf16[4,2,8192]{2,1,0:T(2,128)(2,1)S(1)}, bf16[4,2,8192]{2,1,0:T(2,128)(2,1)S(1)}, u32[]{:S(2)}, u32[]{:S(2)}) %collective-permute-start.3) | collective-permute-done | bytes 131104 | tf_op jit(solution)/shard_map/ppermute | solution.py:22
  18.2 3.5 %shard_map.130.refs_8_.w_ref = bf16[512,8192]{1,0:T(8,128)(2,1)S(1)} custom-call(bf16[4,2,8192]{2,1,0:T(2,128)(2,1)S(1)} %shard_map.129.refs_0_, bf16[512,8192]{1,0:T(8,128)(2,1)} %bitcast.141), custom_call_target="tpu_custom_call" | custom-call | bytes 8388608 | tf_op jit(solution)/shard_map/pallas_call | solution.py:83
  24.0 3.0 %shard_map.132 = (bf16[16,2,640]{2,1,0:T(2,128)(2,1)S(1)}, bf16[2,16,2,512]{3,2,1,0:T(2,128)(2,1)S(1)}) custom-call(s32[16]{0:T(128)S(1)} %pad_add_fusion.refs_0_.ids_ref, bf16[4,2,8192]{2,1,0:T(2,128)(2,1)S(1)} %shard_map.129.refs_0_, bf16[4,2,8192]{2,1,0:T(2,128)(2,1)S(1)} %collective-permute-done.2.refs_1_, ...), custom_call_target="tpu_custom_call" | custom-call | flops 335544320 | bytes 10485760 | tf_op jit(solution)/shard_map/pallas_call | solution.py:384
  27.0 11.8 %all_to_all.25.in_ref = bf16[16,2,640]{2,1,0:T(2,128)(2,1)S(1)} all-to-all(bf16[16,2,640]{2,1,0:T(2,128)(2,1)S(1)} %get-tuple-element.83), channel_id=1, replica_groups=mesh['section'=2,'mp'=16] {'mp'}, dimensions={0} | all-to-all | bytes 81920 | tf_op jit(solution)/shard_map/all_to_all | solution.py:855
  41.3 9.2 %all_to_all.26.x_ref = bf16[16,2,512]{2,1,0:T(2,128)(2,1)S(1)} all-to-all(bf16[16,2,512]{2,1,0:T(2,128)(2,1)S(1)} %bitcast.151), channel_id=1, replica_groups=mesh['section'=2,'mp'=16] {'mp'}, dimensions={0} | all-to-all | bytes 65536 | tf_op jit(solution)/shard_map/all_to_all | solution.py:859
  54.1 4.2 %shard_map.137 = (bf16[4096,2,128]{2,1,0:T(2,128)(2,1)S(1)}, bf16[4096,2,128]{2,1,0:T(2,128)(2,1)S(1)}, bf16[4096,2,128]{2,1,0:T(2,128)(2,1)S(1)}, bf16[4096,2,128]{2,1,0:T(2,128)(2,1)S(1)}) custom-call(s32[16]{0:T(128)S(1)} %pad_add_fusion.refs_0_.ids_ref, bf16[4,32,512]{2,1,0:T(8,128)(2,1)S(1)} %get-tuple-element.85.token_ref, bf16[8192,2,1024]{2,1,0:T(2,128)(2,1)} %bitcast.123), custom_call_target="tpu_custom_call" | custom-call | bytes 8388608 | tf_op jit(solution)/shard_map/pallas_call | solution.py:152
  60.0 4.2 %shard_map.139 = (bf16[4096,2,128]{2,1,0:T(2,128)(2,1)S(1)}, bf16[4096,2,128]{2,1,0:T(2,128)(2,1)S(1)}, bf16[4096,2,128]{2,1,0:T(2,128)(2,1)S(1)}, bf16[4096,2,128]{2,1,0:T(2,128)(2,1)S(1)}) custom-call(s32[16]{0:T(128)S(1)} %pad_add_fusion.refs_0_.ids_ref, bf16[2,32,512]{2,1,0:T(8,128)(2,1)S(1)} %get-tuple-element.91.token_ref, bf16[8192,2,1024]{2,1,0:T(2,128)(2,1)} %bitcast.124), custom_call_target="tpu_custom_call" | custom-call | bytes 8388608 | tf_op jit(solution)/shard_map/pallas_call | solution.py:152
  65.0 4.2 %shard_map.141 = (bf16[4096,2,128]{2,1,0:T(2,128)(2,1)S(1)}, bf16[4096,2,128]{2,1,0:T(2,128)(2,1)S(1)}, bf16[4096,2,128]{2,1,0:T(2,128)(2,1)S(1)}, bf16[4096,2,128]{2,1,0:T(2,128)(2,1)S(1)}) custom-call(s32[16]{0:T(128)S(1)} %pad_add_fusion.refs_0_.ids_ref, bf16[2,32,512]{2,1,0:T(8,128)(2,1)S(1)} %shard_map.140.token_ref.here_ref, ...), custom_call_target="tpu_custom_call" | custom-call | bytes 8388608 | tf_op jit(solution)/shard_map/pallas_call | solution.py:152
  71.3 4.2 %shard_map.143 = (bf16[4096,2,128]{2,1,0:T(2,128)(2,1)S(1)}, bf16[4096,2,128]{2,1,0:T(2,128)(2,1)S(1)}, bf16[4096,2,128]{2,1,0:T(2,128)(2,1)S(1)}, bf16[4096,2,128]{2,1,0:T(2,128)(2,1)S(1)}) custom-call(s32[16]{0:T(128)S(1)} %pad_add_fusion.refs_0_.ids_ref, bf16[2,32,512]{2,1,0:T(8,128)(2,1)S(1)} %shard_map.142.token_ref.low_ref, ...), custom_call_target="tpu_custom_call" | custom-call | bytes 8388608 | tf_op jit(solution)/shard_map/pallas_call | solution.py:152
  76.3 2.8 %shard_map.145 = (f32[64,1024]{1,0:T(8,128)S(1)}, bf16[4,1024,512]{2,1,0:T(8,128)(2,1)S(1)}) custom-call(s32[16]{0:T(128)S(1)} %pad_add_fusion.refs_0_.ids_ref, bf16[4,32,512]{2,1,0:T(8,128)(2,1)S(1)} %shard_map.144.x_ref.refs_0_, f32[1,8192]{1,0:T(1,128)S(1)} %copy-done, f32[8,128]{1,0:T(8,128)S(1)} %broadcast_5_before_ref.2.before_ref, ...), custom_call_target="tpu_custom_call" | custom-call | flops 268435456 | bytes 8388608 | tf_op jit(solution)/shard_map/pallas_call | solution.py:624
  79.2 2.9 %shard_map.146 = (f32[64,1024]{1,0:T(8,128)S(1)}, bf16[4,1024,512]{2,1,0:T(8,128)(2,1)S(1)}) custom-call(s32[16]{0:T(128)S(1)} %pad_add_fusion.refs_0_.ids_ref, bf16[4,32,512]{2,1,0:T(8,128)(2,1)S(1)} %collective-permute-done.11.x_ref.refs_1_, f32[1,8192]{1,0:T(1,128)S(1)} %copy-done, f32[64,1024]{1,0:T(8,128)S(1)} %get-tuple-element.104.before_ref, ...), custom_call_target="tpu_custom_call" | custom-call | flops 268435456 | bytes 8388608 | tf_op jit(solution)/shard_map/pallas_call | solution.py:624
  82.1 2.7 %shard_map.148 = (f32[64,1024]{1,0:T(8,128)S(1)}, bf16[1,8,128]{2,1,0:T(8,128)(2,1)}) custom-call(s32[16]{0:T(128)S(1)} %pad_add_fusion.refs_0_.ids_ref, bf16[4,32,512]{2,1,0:T(8,128)(2,1)S(1)} %shard_map.147.x_ref.refs_2_, f32[1,8192]{1,0:T(1,128)S(1)} %copy-done, f32[64,1024]{1,0:T(8,128)S(1)} %get-tuple-element.105.refs_0_.before_ref, ...), custom_call_target="tpu_custom_call" | custom-call | flops 268435456 | bytes 8388608 | tf_op jit(solution)/shard_map/pallas_call | solution.py:624
  84.8 5.9 %shard_map.149 = (bf16[8,32,512]{2,1,0:T(8,128)(2,1)S(1)}, bf16[32,1024]{1,0:T(8,128)(2,1)S(1)}, f32[8,128]{1,0:T(8,128)}) custom-call(s32[1]{0:T(128)} %bitcast.refs_3_.me_ref, s32[16]{0:T(128)S(1)} %pad_add_fusion.refs_0_.ids_ref, bf16[4,32,512]{2,1,0:T(8,128)(2,1)S(1)} %shard_map.144.x_ref.refs_0_, ...), custom_call_target="tpu_custom_call" | custom-call | flops 805306368 | bytes 16777216 | tf_op jit(solution)/shard_map/pallas_call | solution.py:718
  94.4 4.3 %shard_map.152 = (bf16[8192,512]{1,0:T(8,128)(2,1)S(1)}, bf16[64,8192]{1,0:T(8,128)(2,1)S(1)}, bf16[64,8192]{1,0:T(8,128)(2,1)S(1)}) custom-call(bf16[4,32,512]{2,1,0:T(8,128)(2,1)S(1)} %get-tuple-element.112.refs_0_, bf16[8192,512]{1,0:T(8,128)(2,1)} %bitcast.140, bf16[64,8192]{1,0:T(8,128)(2,1)} %bitcast.148, bf16[64,8192]{1,0:T(8,128)(2,1)} %bitcast.150), custom_call_target="tpu_custom_call" | custom-call | bytes 10485760 | tf_op jit(solution)/shard_map/pallas_call | solution.py:83
  106.6 3.5 %shard_map.156.refs_0_.refs_8_.w_ref = bf16[512,8192]{1,0:T(8,128)(2,1)S(1)} custom-call(bf16[2,32,512]{2,1,0:T(8,128)(2,1)S(1)} %shard_map.155.refs_0_, bf16[512,8192]{1,0:T(8,128)(2,1)} %bitcast.142), custom_call_target="tpu_custom_call" | custom-call | bytes 8388608 | tf_op jit(solution)/shard_map/pallas_call | solution.py:83
  111.8 3.5 %collective-permute-done.19.high_ref = bf16[2,32,512]{2,1,0:T(8,128)(2,1)S(1)} collective-permute-done((bf16[2,32,512]{2,1,0:T(8,128)(2,1)S(1)}, bf16[2,32,512]{2,1,0:T(8,128)(2,1)S(1)}, u32[]{:S(2)}, u32[]{:S(2)}) %collective-permute-start.19) | collective-permute-done | bytes 65568 | tf_op jit(solution)/shard_map/ppermute | solution.py:22
  116.1 4.2 %collective-permute-done.21.refs_2_ = bf16[4,32,512]{2,1,0:T(8,128)(2,1)S(1)} collective-permute-done((bf16[4,32,512]{2,1,0:T(8,128)(2,1)S(1)}, bf16[4,32,512]{2,1,0:T(8,128)(2,1)S(1)}, u32[]{:S(2)}, u32[]{:S(2)}) %collective-permute-start.21) | collective-permute-done | bytes 131104 | tf_op jit(solution)/shard_map/ppermute | solution.py:22
  121.7 3.2 %shard_map.159 = (bf16[16,2,640]{2,1,0:T(2,128)(2,1)S(1)}, bf16[2,16,2,512]{3,2,1,0:T(2,128)(2,1)}) custom-call(s32[16]{0:T(128)S(1)} %pad_add_fusion.refs_0_.ids_ref, bf16[4,32,512]{2,1,0:T(8,128)(2,1)S(1)} %shard_map.158.refs_0_, bf16[4,32,512]{2,1,0:T(8,128)(2,1)S(1)} %collective-permute-done.20.refs_1_, ...), custom_call_target="tpu_custom_call" | custom-call | flops 335544320 | bytes 10485760 | tf_op jit(solution)/shard_map/pallas_call | solution.py:384
  124.9 10.5 %all_to_all.27.in_ref = bf16[16,2,640]{2,1,0:T(2,128)(2,1)S(1)} all-to-all(bf16[16,2,640]{2,1,0:T(2,128)(2,1)S(1)} %get-tuple-element.120), channel_id=1, replica_groups=mesh['section'=2,'mp'=16] {'mp'}, dimensions={0} | all-to-all | bytes 81920 | tf_op jit(solution)/shard_map/all_to_all | solution.py:855
  135.3 2.5 %shard_map.160 = bf16[2,16,512]{2,1,0:T(8,128)(2,1)S(1)} custom-call(s32[1]{0:T(128)} %bitcast.2.refs_5_.where_ref, s32[2,2]{1,0:T(2,128)S(1)} %copy-done.3, bf16[16,2,640]{2,1,0:T(2,128)(2,1)S(1)} %all_to_all.27.in_ref, f32[2,128]{1,0:T(2,128)S(1)} %get-tuple-element.164.refs_8_.cos_ref, f32[2,128]{1,0:T(2,128)S(1)} %get-tuple-element.165.refs_9_.sin_ref, ...), custom_call_target="tpu_custom_call" | custom-call | flops 268435456 | bytes 4194304 | tf_op jit(solution)/shard_map/pallas_call | solution.py:482
  137.9 9.2 %all_to_all.28.x_ref = bf16[16,2,512]{2,1,0:T(2,128)(2,1)S(1)} all-to-all(bf16[16,2,512]{2,1,0:T(2,128)(2,1)S(1)} %bitcast.152), channel_id=1, replica_groups=mesh['section'=2,'mp'=16] {'mp'}, dimensions={0} | all-to-all | bytes 65536 | tf_op jit(solution)/shard_map/all_to_all | solution.py:859
  150.7 4.2 %shard_map.164 = (bf16[4096,2,128]{2,1,0:T(2,128)(2,1)S(1)}, bf16[4096,2,128]{2,1,0:T(2,128)(2,1)S(1)}, bf16[4096,2,128]{2,1,0:T(2,128)(2,1)S(1)}, bf16[4096,2,128]{2,1,0:T(2,128)(2,1)S(1)}) custom-call(s32[16]{0:T(128)S(1)} %pad_add_fusion.refs_0_.ids_ref, bf16[4,32,512]{2,1,0:T(8,128)(2,1)S(1)} %get-tuple-element.122.token_ref, ...), custom_call_target="tpu_custom_call" | custom-call | bytes 8388608 | tf_op jit(solution)/shard_map/pallas_call | solution.py:152
  156.6 4.2 %shard_map.166 = (bf16[4096,2,128]{2,1,0:T(2,128)(2,1)S(1)}, bf16[4096,2,128]{2,1,0:T(2,128)(2,1)S(1)}, bf16[4096,2,128]{2,1,0:T(2,128)(2,1)S(1)}, bf16[4096,2,128]{2,1,0:T(2,128)(2,1)S(1)}) custom-call(s32[16]{0:T(128)S(1)} %pad_add_fusion.refs_0_.ids_ref, bf16[2,32,512]{2,1,0:T(8,128)(2,1)S(1)} %get-tuple-element.128.token_ref, ...), custom_call_target="tpu_custom_call" | custom-call | bytes 8388608 | tf_op jit(solution)/shard_map/pallas_call | solution.py:152
  161.6 4.2 %shard_map.168 = (bf16[4096,2,128]{2,1,0:T(2,128)(2,1)S(1)}, bf16[4096,2,128]{2,1,0:T(2,128)(2,1)S(1)}, bf16[4096,2,128]{2,1,0:T(2,128)(2,1)S(1)}, bf16[4096,2,128]{2,1,0:T(2,128)(2,1)S(1)}) custom-call(s32[16]{0:T(128)S(1)} %pad_add_fusion.refs_0_.ids_ref, bf16[2,32,512]{2,1,0:T(8,128)(2,1)S(1)} %shard_map.167.token_ref.here_ref, ...), custom_call_target="tpu_custom_call" | custom-call | bytes 8388608 | tf_op jit(solution)/shard_map/pallas_call | solution.py:152
  167.9 4.2 %shard_map.170 = (bf16[4096,2,128]{2,1,0:T(2,128)(2,1)S(1)}, bf16[4096,2,128]{2,1,0:T(2,128)(2,1)S(1)}, bf16[4096,2,128]{2,1,0:T(2,128)(2,1)S(1)}, bf16[4096,2,128]{2,1,0:T(2,128)(2,1)S(1)}) custom-call(s32[16]{0:T(128)S(1)} %pad_add_fusion.refs_0_.ids_ref, bf16[2,32,512]{2,1,0:T(8,128)(2,1)S(1)} %shard_map.169.token_ref.low_ref, ...), custom_call_target="tpu_custom_call" | custom-call | bytes 8388608 | tf_op jit(solution)/shard_map/pallas_call | solution.py:152
  172.6 2.8 %shard_map.172 = (f32[64,1024]{1,0:T(8,128)S(1)}, bf16[4,1024,512]{2,1,0:T(8,128)(2,1)S(1)}) custom-call(s32[16]{0:T(128)S(1)} %pad_add_fusion.refs_0_.ids_ref, bf16[4,32,512]{2,1,0:T(8,128)(2,1)S(1)} %shard_map.171.x_ref.refs_0_, f32[1,8192]{1,0:T(1,128)S(1)} %copy-done, f32[8,128]{1,0:T(8,128)S(1)} %broadcast_5_before_ref.2.before_ref, ...), custom_call_target="tpu_custom_call" | custom-call | flops 268435456 | bytes 8388608 | tf_op jit(solution)/shard_map/pallas_call | solution.py:624
  175.5 2.9 %shard_map.173 = (f32[64,1024]{1,0:T(8,128)S(1)}, bf16[4,1024,512]{2,1,0:T(8,128)(2,1)S(1)}) custom-call(s32[16]{0:T(128)S(1)} %pad_add_fusion.refs_0_.ids_ref, bf16[4,32,512]{2,1,0:T(8,128)(2,1)S(1)} %collective-permute-done.28.x_ref.refs_1_, f32[1,8192]{1,0:T(1,128)S(1)} %copy-done, f32[64,1024]{1,0:T(8,128)S(1)} %get-tuple-element.141.before_ref, ...), custom_call_target="tpu_custom_call" | custom-call | flops 268435456 | bytes 8388608 | tf_op jit(solution)/shard_map/pallas_call | solution.py:624
  178.6 2.6 %shard_map.175 = (f32[64,1024]{1,0:T(8,128)S(1)}, bf16[1,8,128]{2,1,0:T(8,128)(2,1)}) custom-call(s32[16]{0:T(128)S(1)} %pad_add_fusion.refs_0_.ids_ref, bf16[4,32,512]{2,1,0:T(8,128)(2,1)S(1)} %shard_map.174.x_ref.refs_2_, f32[1,8192]{1,0:T(1,128)S(1)} %copy-done, f32[64,1024]{1,0:T(8,128)S(1)} %get-tuple-element.142.refs_0_.before_ref, ...), custom_call_target="tpu_custom_call" | custom-call | flops 268435456 | bytes 8388608 | tf_op jit(solution)/shard_map/pallas_call | solution.py:624
  181.3 7.2 %shard_map.176 = (bf16[8,2,8192]{2,1,0:T(2,128)(2,1)S(1)}, bf16[8,2,8192]{2,1,0:T(2,128)(2,1)S(1)}, f32[2,8192]{1,0:T(2,128)S(1)}) custom-call(s32[1]{0:T(128)} %bitcast.refs_3_.me_ref, s32[16]{0:T(128)S(1)} %pad_add_fusion.refs_0_.ids_ref, bf16[4,32,512]{2,1,0:T(8,128)(2,1)S(1)} %shard_map.171.x_ref.refs_0_, ...), custom_call_target="tpu_custom_call" | custom-call | flops 805306368 | bytes 16777216 | tf_op jit(solution)/shard_map/pallas_call | solution.py:718
  190.4 13.6 %all_to_all.29 = bf16[8,2,8192]{2,1,0:T(2,128)(2,1)S(1)} all-to-all(bf16[8,2,8192]{2,1,0:T(2,128)(2,1)S(1)} %shard_map.177), channel_id=1, replica_groups={{0,2,4,6,8,10,12,14},{1,3,5,7,9,11,13,15},{16,18,20,22,24,26,28,30},{17..., dimensions={0} | all-to-all | bytes 524288 | tf_op jit(solution)/shard_map/all_to_all | solution.py:28
  (108 shorter events, 47.2 us)
Async XLA Ops:
  0.0 6.5 %collective-permute-start = (bf16[1,2,8192]{2,1,0:T(2,128)(2,1)}, bf16[1,2,8192]{2,1,0:T(2,128)(2,1)S(1)}, u32[]{:S(2)}, u32[]{:S(2)}) collective-permute-start(bf16[1,2,8192]{2,1,0:T(2,128)(2,1)} %low_ref.1), channel_id=1, source_target_pairs={{0,8},{1,9},{2,10},{3,11},{4,12},{5,13},{6,14},{7,15},{8,0},{9,1},... | collective-permute-start | bytes 98312 | tf_op jit(solution)/shard_map/ppermute | solution.py:22
  7.3 5.8 %collective-permute-start.1 = (bf16[2,2,8192]{2,1,0:T(2,128)(2,1)S(1)}, bf16[2,2,8192]{2,1,0:T(2,128)(2,1)S(1)}, u32[]{:S(2)}, u32[]{:S(2)}) collective-permute-start(bf16[2,2,8192]{2,1,0:T(2,128)(2,1)S(1)} %shard_map.127.refs_0_.low_ref), channel_id=1, source_target_pairs={{0,4},{1,5},{2,6},{3,7},{4,0},{5,1},{6,2},{7,3},{8,12},{9,13},{10,... | collective-permute-start | bytes 196616 | tf_op jit(solution)/shard_map/ppermute | solution.py:22
  13.1 5.0 %collective-permute-start.3 = (bf16[4,2,8192]{2,1,0:T(2,128)(2,1)S(1)}, bf16[4,2,8192]{2,1,0:T(2,128)(2,1)S(1)}, u32[]{:S(2)}, u32[]{:S(2)}) collective-permute-start(bf16[4,2,8192]{2,1,0:T(2,128)(2,1)S(1)} %shard_map.129.refs_0_), channel_id=1, source_target_pairs={{0,2},{1,3},{2,0},{3,1},{4,6},{5,7},{6,4},{7,5},{8,10},{9,11},{10,... | collective-permute-start | bytes 393224 | tf_op jit(solution)/shard_map/ppermute | solution.py:22
  14.7 9.2 %collective-permute-start.2 = (bf16[4,2,8192]{2,1,0:T(2,128)(2,1)S(1)}, bf16[4,2,8192]{2,1,0:T(2,128)(2,1)S(1)}, u32[]{:S(2)}, u32[]{:S(2)}) collective-permute-start(bf16[4,2,8192]{2,1,0:T(2,128)(2,1)S(1)} %shard_map.129.refs_0_), channel_id=1, source_target_pairs={{0,1},{1,0},{2,3},{3,2},{4,5},{5,4},{6,7},{7,6},{8,9},{9,8},{10,11... | collective-permute-start | bytes 393224 | tf_op jit(solution)/shard_map/ppermute | solution.py:22
  18.2 5.8 %collective-permute-start.4 = (bf16[4,2,8192]{2,1,0:T(2,128)(2,1)S(1)}, bf16[4,2,8192]{2,1,0:T(2,128)(2,1)S(1)}, u32[]{:S(2)}, u32[]{:S(2)}) collective-permute-start(bf16[4,2,8192]{2,1,0:T(2,128)(2,1)S(1)} %collective-permute-done.3.refs_2_), channel_id=1, source_target_pairs={{0,1},{1,0},{2,3},{3,2},{4,5},{5,4},{6,7},{7,6},{8,9},{9,8},{10,11... | collective-permute-start | bytes 393224 | tf_op jit(solution)/shard_map/ppermute | solution.py:22
  52.0 1.6 collective-permute-start.5
  53.6 6.0 %collective-permute-start.6 = (bf16[4,32,512]{2,1,0:T(8,128)(2,1)S(1)}, bf16[4,32,512]{2,1,0:T(8,128)(2,1)S(1)}, u32[]{:S(2)}, u32[]{:S(2)}) collective-permute-start(bf16[4,32,512]{2,1,0:T(8,128)(2,1)S(1)} %get-tuple-element.85.token_ref), channel_id=1, source_target_pairs={{0,2},{1,3},{2,0},{3,1},{4,6},{5,7},{6,4},{7,5},{8,10},{9,11},{10,... | collective-permute-start | bytes 393224 | tf_op jit(solution)/shard_map/ppermute | solution.py:22
  59.6 4.6 %collective-permute-start.7 = (bf16[2,32,512]{2,1,0:T(8,128)(2,1)S(1)}, bf16[2,32,512]{2,1,0:T(8,128)(2,1)S(1)}, u32[]{:S(2)}, u32[]{:S(2)}) collective-permute-start(bf16[2,32,512]{2,1,0:T(8,128)(2,1)S(1)} %get-tuple-element.91.token_ref), channel_id=1, source_target_pairs={{0,4},{1,5},{2,6},{3,7},{4,0},{5,1},{6,2},{7,3},{8,12},{9,13},{10,... | collective-permute-start | bytes 196616 | tf_op jit(solution)/shard_map/ppermute | solution.py:22
  64.3 5.5 %collective-permute-start.8 = (bf16[2,32,512]{2,1,0:T(8,128)(2,1)S(1)}, bf16[2,32,512]{2,1,0:T(8,128)(2,1)S(1)}, u32[]{:S(2)}, u32[]{:S(2)}) collective-permute-start(bf16[2,32,512]{2,1,0:T(8,128)(2,1)S(1)} %shard_map.140.token_ref.here_ref), channel_id=1, source_target_pairs={{0,8},{1,9},{2,10},{3,11},{4,12},{5,13},{6,14},{7,15},{8,0},{9,1},... | collective-permute-start | bytes 196616 | tf_op jit(solution)/shard_map/ppermute | solution.py:22
  69.9 5.7 %collective-permute-start.10 = (bf16[2,32,512]{2,1,0:T(8,128)(2,1)S(1)}, bf16[2,32,512]{2,1,0:T(8,128)(2,1)S(1)}, u32[]{:S(2)}, u32[]{:S(2)}) collective-permute-start(bf16[2,32,512]{2,1,0:T(8,128)(2,1)S(1)} %shard_map.142.token_ref.low_ref), channel_id=1, source_target_pairs={{0,4},{1,5},{2,6},{3,7},{4,0},{5,1},{6,2},{7,3},{8,12},{9,13},{10,... | collective-permute-start | bytes 196616 | tf_op jit(solution)/shard_map/ppermute | solution.py:22
  75.6 3.6 %collective-permute-start.11 = (bf16[4,32,512]{2,1,0:T(8,128)(2,1)S(1)}, bf16[4,32,512]{2,1,0:T(8,128)(2,1)S(1)}, u32[]{:S(2)}, u32[]{:S(2)}) collective-permute-start(bf16[4,32,512]{2,1,0:T(8,128)(2,1)S(1)} %shard_map.144.x_ref.refs_0_), channel_id=1, source_target_pairs={{0,1},{1,0},{2,3},{3,2},{4,5},{5,4},{6,7},{7,6},{8,9},{9,8},{10,11... | collective-permute-start | bytes 393224 | tf_op jit(solution)/shard_map/ppermute | solution.py:22
  75.7 6.4 %collective-permute-start.12 = (bf16[4,32,512]{2,1,0:T(8,128)(2,1)S(1)}, bf16[4,32,512]{2,1,0:T(8,128)(2,1)S(1)}, u32[]{:S(2)}, u32[]{:S(2)}) collective-permute-start(bf16[4,32,512]{2,1,0:T(8,128)(2,1)S(1)} %shard_map.144.x_ref.refs_0_), channel_id=1, source_target_pairs={{0,2},{1,3},{2,0},{3,1},{4,6},{5,7},{6,4},{7,5},{8,10},{9,11},{10,... | collective-permute-start | bytes 393224 | tf_op jit(solution)/shard_map/ppermute | solution.py:22
  82.1 2.7 %collective-permute-start.13 = (bf16[4,32,512]{2,1,0:T(8,128)(2,1)S(1)}, bf16[4,32,512]{2,1,0:T(8,128)(2,1)S(1)}, u32[]{:S(2)}, u32[]{:S(2)}) collective-permute-start(bf16[4,32,512]{2,1,0:T(8,128)(2,1)S(1)} %shard_map.147.x_ref.refs_2_), channel_id=1, source_target_pairs={{0,1},{1,0},{2,3},{3,2},{4,5},{5,4},{6,7},{7,6},{8,9},{9,8},{10,11... | collective-permute-start | bytes 393224 | tf_op jit(solution)/shard_map/ppermute | solution.py:22
  90.7 2.1 %collective-permute-start.14 = (bf16[8,32,512]{2,1,0:T(8,128)(2,1)S(1)}, bf16[8,32,512]{2,1,0:T(8,128)(2,1)S(1)}, u32[]{:S(2)}, u32[]{:S(2)}) collective-permute-start(bf16[8,32,512]{2,1,0:T(8,128)(2,1)S(1)} %get-tuple-element.110), channel_id=1, source_target_pairs={{0,1},{1,0},{2,3},{3,2},{4,5},{5,4},{6,7},{7,6},{8,9},{9,8},{10,11... | collective-permute-start | bytes 786440 | tf_op jit(solution)/shard_map/ppermute | solution.py:22
  92.9 5.8 %collective-permute-start.15 = (bf16[4,32,512]{2,1,0:T(8,128)(2,1)S(1)}, bf16[4,32,512]{2,1,0:T(8,128)(2,1)S(1)}, u32[]{:S(2)}, u32[]{:S(2)}) collective-permute-start(bf16[4,32,512]{2,1,0:T(8,128)(2,1)S(1)} %get-tuple-element.112.refs_0_), channel_id=1, source_target_pairs={{0,2},{1,3},{2,0},{3,1},{4,6},{5,7},{6,4},{7,5},{8,10},{9,11},{10,... | collective-permute-start | bytes 393224 | tf_op jit(solution)/shard_map/ppermute | solution.py:22
  98.8 5.2 %collective-permute-start.16 = (bf16[2,32,512]{2,1,0:T(8,128)(2,1)S(1)}, bf16[2,32,512]{2,1,0:T(8,128)(2,1)S(1)}, u32[]{:S(2)}, u32[]{:S(2)}) collective-permute-start(bf16[2,32,512]{2,1,0:T(8,128)(2,1)S(1)} %get-tuple-element.117.refs_0_), channel_id=1, source_target_pairs={{0,4},{1,5},{2,6},{3,7},{4,0},{5,1},{6,2},{7,3},{8,12},{9,13},{10,... | collective-permute-start | bytes 196616 | tf_op jit(solution)/shard_map/ppermute | solution.py:22
  100.2 9.9 %collective-permute-start.9 = (bf16[2,32,512]{2,1,0:T(8,128)(2,1)S(1)}, bf16[2,32,512]{2,1,0:T(8,128)(2,1)S(1)}, u32[]{:S(2)}, u32[]{:S(2)}) collective-permute-start(bf16[2,32,512]{2,1,0:T(8,128)(2,1)S(1)} %shard_map.142.token_ref.low_ref), channel_id=1, source_target_pairs={{0,16},{1,17},{2,18},{3,19},{4,20},{5,21},{6,22},{7,23},{8,24},{9,... | collective-permute-start | bytes 196616 | tf_op jit(solution)/shard_map/ppermute | solution.py:251
  104.0 6.9 %collective-permute-start.18 = (bf16[2,32,512]{2,1,0:T(8,128)(2,1)S(1)}, bf16[2,32,512]{2,1,0:T(8,128)(2,1)S(1)}, u32[]{:S(2)}, u32[]{:S(2)}) collective-permute-start(bf16[2,32,512]{2,1,0:T(8,128)(2,1)S(1)} %shard_map.155.refs_0_), channel_id=1, source_target_pairs={{0,24},{1,25},{2,26},{3,27},{4,28},{5,29},{6,30},{7,31},{8,16},{9,... | collective-permute-start | bytes 196616 | tf_op jit(solution)/shard_map/ppermute | solution.py:251
  106.1 4.8 %collective-permute-start.17 = (bf16[2,32,512]{2,1,0:T(8,128)(2,1)S(1)}, bf16[2,32,512]{2,1,0:T(8,128)(2,1)S(1)}, u32[]{:S(2)}, u32[]{:S(2)}) collective-permute-start(bf16[2,32,512]{2,1,0:T(8,128)(2,1)S(1)} %shard_map.155.refs_0_), channel_id=1, source_target_pairs={{0,16},{1,17},{2,18},{3,19},{4,20},{5,21},{6,22},{7,23},{8,24},{9,... | collective-permute-start | bytes 196616 | tf_op jit(solution)/shard_map/ppermute | solution.py:251
  110.9 4.3 %collective-permute-start.19 = (bf16[2,32,512]{2,1,0:T(8,128)(2,1)S(1)}, bf16[2,32,512]{2,1,0:T(8,128)(2,1)S(1)}, u32[]{:S(2)}, u32[]{:S(2)}) collective-permute-start(bf16[2,32,512]{2,1,0:T(8,128)(2,1)S(1)} %shard_map.157.low_ref.addend_ref), channel_id=1, source_target_pairs={{0,4},{1,5},{2,6},{3,7},{4,0},{5,1},{6,2},{7,3},{8,12},{9,13},{10,... | collective-permute-start | bytes 196616 | tf_op jit(solution)/shard_map/ppermute | solution.py:22
  115.3 5.0 %collective-permute-start.21 = (bf16[4,32,512]{2,1,0:T(8,128)(2,1)S(1)}, bf16[4,32,512]{2,1,0:T(8,128)(2,1)S(1)}, u32[]{:S(2)}, u32[]{:S(2)}) collective-permute-start(bf16[4,32,512]{2,1,0:T(8,128)(2,1)S(1)} %shard_map.158.refs_0_), channel_id=1, source_target_pairs={{0,2},{1,3},{2,0},{3,1},{4,6},{5,7},{6,4},{7,5},{8,10},{9,11},{10,... | collective-permute-start | bytes 393224 | tf_op jit(solution)/shard_map/ppermute | solution.py:22
  116.1 4.2 %collective-permute-start.20 = (bf16[4,32,512]{2,1,0:T(8,128)(2,1)S(1)}, bf16[4,32,512]{2,1,0:T(8,128)(2,1)S(1)}, u32[]{:S(2)}, u32[]{:S(2)}) collective-permute-start(bf16[4,32,512]{2,1,0:T(8,128)(2,1)S(1)} %shard_map.158.refs_0_), channel_id=1, source_target_pairs={{0,1},{1,0},{2,3},{3,2},{4,5},{5,4},{6,7},{7,6},{8,9},{9,8},{10,11... | collective-permute-start | bytes 393224 | tf_op jit(solution)/shard_map/ppermute | solution.py:22
  120.3 1.3 collective-permute-start.22
  148.6 1.6 collective-permute-start.23
  150.2 6.0 %collective-permute-start.24 = (bf16[4,32,512]{2,1,0:T(8,128)(2,1)S(1)}, bf16[4,32,512]{2,1,0:T(8,128)(2,1)S(1)}, u32[]{:S(2)}, u32[]{:S(2)}) collective-permute-start(bf16[4,32,512]{2,1,0:T(8,128)(2,1)S(1)} %get-tuple-element.122.token_ref), channel_id=1, source_target_pairs={{0,2},{1,3},{2,0},{3,1},{4,6},{5,7},{6,4},{7,5},{8,10},{9,11},{10,... | collective-permute-start | bytes 393224 | tf_op jit(solution)/shard_map/ppermute | solution.py:22
  156.2 4.7 %collective-permute-start.25 = (bf16[2,32,512]{2,1,0:T(8,128)(2,1)S(1)}, bf16[2,32,512]{2,1,0:T(8,128)(2,1)S(1)}, u32[]{:S(2)}, u32[]{:S(2)}) collective-permute-start(bf16[2,32,512]{2,1,0:T(8,128)(2,1)S(1)} %get-tuple-element.128.token_ref), channel_id=1, source_target_pairs={{0,4},{1,5},{2,6},{3,7},{4,0},{5,1},{6,2},{7,3},{8,12},{9,13},{10,... | collective-permute-start | bytes 196616 | tf_op jit(solution)/shard_map/ppermute | solution.py:22
  160.9 5.5 %collective-permute-start.26 = (bf16[2,32,512]{2,1,0:T(8,128)(2,1)S(1)}, bf16[2,32,512]{2,1,0:T(8,128)(2,1)S(1)}, u32[]{:S(2)}, u32[]{:S(2)}) collective-permute-start(bf16[2,32,512]{2,1,0:T(8,128)(2,1)S(1)} %shard_map.167.token_ref.here_ref), channel_id=1, source_target_pairs={{0,8},{1,9},{2,10},{3,11},{4,12},{5,13},{6,14},{7,15},{8,0},{9,1},... | collective-permute-start | bytes 196616 | tf_op jit(solution)/shard_map/ppermute | solution.py:22
  166.4 5.7 %collective-permute-start.27 = (bf16[2,32,512]{2,1,0:T(8,128)(2,1)S(1)}, bf16[2,32,512]{2,1,0:T(8,128)(2,1)S(1)}, u32[]{:S(2)}, u32[]{:S(2)}) collective-permute-start(bf16[2,32,512]{2,1,0:T(8,128)(2,1)S(1)} %shard_map.169.token_ref.low_ref), channel_id=1, source_target_pairs={{0,4},{1,5},{2,6},{3,7},{4,0},{5,1},{6,2},{7,3},{8,12},{9,13},{10,... | collective-permute-start | bytes 196616 | tf_op jit(solution)/shard_map/ppermute | solution.py:22
  172.1 3.4 %collective-permute-start.28 = (bf16[4,32,512]{2,1,0:T(8,128)(2,1)S(1)}, bf16[4,32,512]{2,1,0:T(8,128)(2,1)S(1)}, u32[]{:S(2)}, u32[]{:S(2)}) collective-permute-start(bf16[4,32,512]{2,1,0:T(8,128)(2,1)S(1)} %shard_map.171.x_ref.refs_0_), channel_id=1, source_target_pairs={{0,1},{1,0},{2,3},{3,2},{4,5},{5,4},{6,7},{7,6},{8,9},{9,8},{10,11... | collective-permute-start | bytes 393224 | tf_op jit(solution)/shard_map/ppermute | solution.py:22
  172.2 6.2 %collective-permute-start.29 = (bf16[4,32,512]{2,1,0:T(8,128)(2,1)S(1)}, bf16[4,32,512]{2,1,0:T(8,128)(2,1)S(1)}, u32[]{:S(2)}, u32[]{:S(2)}) collective-permute-start(bf16[4,32,512]{2,1,0:T(8,128)(2,1)S(1)} %shard_map.171.x_ref.refs_0_), channel_id=1, source_target_pairs={{0,2},{1,3},{2,0},{3,1},{4,6},{5,7},{6,4},{7,5},{8,10},{9,11},{10,... | collective-permute-start | bytes 393224 | tf_op jit(solution)/shard_map/ppermute | solution.py:22
  178.4 2.9 %collective-permute-start.30 = (bf16[4,32,512]{2,1,0:T(8,128)(2,1)S(1)}, bf16[4,32,512]{2,1,0:T(8,128)(2,1)S(1)}, u32[]{:S(2)}, u32[]{:S(2)}) collective-permute-start(bf16[4,32,512]{2,1,0:T(8,128)(2,1)S(1)} %shard_map.174.x_ref.refs_2_), channel_id=1, source_target_pairs={{0,1},{1,0},{2,3},{3,2},{4,5},{5,4},{6,7},{7,6},{8,9},{9,8},{10,11... | collective-permute-start | bytes 393224 | tf_op jit(solution)/shard_map/ppermute | solution.py:22
  188.5 1.6 collective-permute-start.31
  (4 other events, 18.6 us)

commit v8 on v7

--- a/solution.py
+++ b/solution.py
@@ -202,7 +202,7 @@
     out_ref = refs[-1]
     for place in range(2):
         if len(addend_ref.shape) == 3:
-            addend = addend_ref[place].astype(jnp.float32)
+            addend = addend_ref[addend_ref.shape[0] - 2 + place].astype(jnp.float32)
         else:
             owners = range(addend_ref.shape[1])
             parts = [addend_ref[place, owner].astype(jnp.float32) for owner in owners]
@@ -255,10 +255,12 @@
     keep, got, held_back = halve(keep, got, jobs)
     (held,) = add_parts((keep, got), 1, held_back)
     far = chip_masks()[-1]
-    here = hop(held, 0) if hops else held
-    there = hop(held, far) if hops else swap(held, far)
     if hops:
-        addend = hop(addend, 0)
+        here = hop(join(held, addend), 0)
+        return step_call(
+            cross_kernel, [held.shape], (here, here, hop(held, far)), run_job(jobs, held)
+        )[0]
+    here, there = held, swap(held, far)
     return step_call(cross_kernel, [held.shape], (addend, here, there), run_job(jobs, held))[0]
 
 
@@ -271,10 +273,6 @@
     return held, swap(held, 1), got
 
 
-def all_quarters(quarters):
-    return *quarters, swap(quarters[2], 1)
-
-
 def pass_kernel(in_ref, *refs):
     refs[-1][...] = in_ref[...]
 
@@ -282,7 +280,8 @@
 def gather_doubling(part, jobs):
     held = part[None]
     got = swap(held, chip_masks()[-1])
-    return spread_pair(join(held, got, run_job(jobs, held)), jobs)
+    (near,) = step_call(pass_kernel, [held.shape], (held,), run_job(jobs, held))
+    return spread_pair(join(near, got), jobs)
 
 
 def quarter_starts(count):
@@ -309,14 +308,74 @@
     return pl.ds(pl.multiple_of(ids_ref[k] * chunk, chunk), chunk)
 
 
-def normed_chunk(x_ref, gain_ref, scale, k, span):
-    wide = x_ref[k].astype(jnp.float32)
-    return (wide * scale * gain_ref[:, span]).astype(jnp.bfloat16)
+def project_into(read, spans, groups, gain_ref, wq_ref, wk_ref, wv_ref, q_sum, kv_sum):
+    @pl.loop(0, groups)
+    def _(group):
+        q_part = 0.0
+        kv_part = 0.0
+        for step in range(UNROLL):
+            k = group * UNROLL + step
+            span = spans(k)
+            scaled = (read(k) * gain_ref[:, span]).astype(jnp.bfloat16)
+            q_part += jnp.dot(scaled, wq_ref[span, :], preferred_element_type=jnp.float32)
+            kv_part += lax.dot_general(
+                scaled,
+                jnp.concatenate([wk_ref[:, span], wv_ref[:, span]], axis=0),
+                (((1,), (1,)), ((), ())),
+                preferred_element_type=jnp.float32,
+            )
+        q_sum[...] += q_part
+        kv_sum[...] += kv_part
+
+
+def project_quarters(ids_ref, starts, x_refs, *rest):
+    parts, _, chunk = x_refs[0].shape
+    for first, x_ref in zip(starts, x_refs):
+        project_into(
+            lambda k: x_ref[k].astype(jnp.float32),
+            lambda k: span_of(ids_ref, first + k, chunk),
+            parts // UNROLL,
+            *rest,
+        )
+
+
+def project_near_kernel(ids_ref, near_ref, other_ref, gain_ref, wq_ref, wk_ref, wv_ref, q_sum,
+                        kv_sum):
+    q_sum[...] = jnp.zeros_like(q_sum)
+    kv_sum[...] = jnp.zeros_like(kv_sum)
+    starts = quarter_starts(4 * near_ref.shape[0])[:2]
+    project_quarters(
+        ids_ref, starts, (near_ref, other_ref), gain_ref, wq_ref, wk_ref, wv_ref, q_sum, kv_sum
+    )
+
+
+def project_cost(rows, width, size):
+    return pl.CostEstimate(
+        flops=2 * rows * width * size, bytes_accessed=2 * width * size, transcendentals=0
+    )
+
+
+def project_near(ids, near, other, gain, wq, wk, wv):
+    rows = near.shape[1]
+    width, queries = wq.shape
+    keys = wk.shape[0]
+    return pl.pallas_call(
+        project_near_kernel,
+        out_shape=[
+            pltpu.VMEM((rows, queries), jnp.float32),
+            pltpu.VMEM((rows, 2 * keys), jnp.float32),
+        ],
+        in_specs=[smem()] + [vmem()] * 6,
+        out_specs=[vmem(), vmem()],
+        compiler_params=pltpu.CompilerParams(vmem_limit_bytes=3 << 20),
+        cost_estimate=project_cost(rows, width // 2, queries + 2 * keys),
+    )(ids, near, other, gain, *in_vmem((wq, wk, wv)))
 
 
 def project_kernel(ids_ref, *refs):
-    x_refs, (gain_ref, wq_ref, wk_ref, wv_ref) = refs[:4], refs[4:8]
+    x_refs, (gain_ref, wq_ref, wk_ref, wv_ref, q_before, kv_before) = refs[:4], refs[4:10]
     out_ref, mine_ref, q_sum, kv_sum, wide = refs[-5:]
+    weights = (wq_ref, wk_ref, wv_ref)
     queries = wq_ref.shape[1]
     count, rows_dev, _ = out_ref.shape
     quarter = count // 4
@@ -324,6 +383,8 @@
     chunk = wq_ref.shape[0] // count
     starts = quarter_starts(count)
     if by_rows:
+        q_sum[...] = jnp.zeros_like(q_sum)
+        kv_sum[...] = jnp.zeros_like(kv_sum)
         for first, x_ref in zip(starts, x_refs):
             for place in range(quarter):
                 at = (first + place) * rows_dev
@@ -334,34 +395,27 @@
             total += part * part
         mean = jnp.sum(total, axis=-1, keepdims=True) / (count * chunk)
         scale = lax.rsqrt(mean + epsilon)
+
+        def straight(k):
+            return pl.ds(pl.multiple_of(k * chunk, chunk), chunk)
+
+        project_into(
+            lambda k: wide[:, straight(k)],
+            straight,
+            count // UNROLL,
+            gain_ref,
+            *weights,
+            q_sum,
+            kv_sum,
+        )
     else:
+        q_sum[...] = q_before[...]
+        kv_sum[...] = kv_before[...]
         scale = inverse_rms(x_refs)
-    q_sum[...] = jnp.zeros_like(q_sum)
-    kv_sum[...] = jnp.zeros_like(kv_sum)
-    for first, x_ref in zip(starts, x_refs):
-
-        @pl.loop(0, quarter // UNROLL)
-        def _(group):
-            q_part = 0.0
-            kv_part = 0.0
-            for step in range(UNROLL):
-                k = group * UNROLL + step
-                if by_rows:
-                    span = pl.ds(pl.multiple_of((first + k) * chunk, chunk), chunk)
-                    normed = (wide[:, span] * scale * gain_ref[:, span]).astype(jnp.bfloat16)
-                else:
-                    span = span_of(ids_ref, first + k, chunk)
-                    normed = normed_chunk(x_ref, gain_ref, scale, k, span)
-                q_part += jnp.dot(normed, wq_ref[span, :], preferred_element_type=jnp.float32)
-                kv_part += lax.dot_general(
-                    normed,
-                    jnp.concatenate([wk_ref[:, span], wv_ref[:, span]], axis=0),
-                    (((1,), (1,)), ((), ())),
-                    preferred_element_type=jnp.float32,
-                )
-            q_sum[...] += q_part
-            kv_sum[...] += kv_part
-
+        project_quarters(ids_ref, starts[2:], x_refs[2:], gain_ref, *weights, q_sum, kv_sum)
+
+    q_sum[...] *= scale
+    kv_sum[...] *= scale
     for place in range(count):
         owner = ids_ref[place] if by_rows else place
         lines = slice(place * rows_dev, (place + 1) * rows_dev)
@@ -373,7 +427,7 @@
                 mine_ref[which, owner] = wide[lines, span].astype(jnp.bfloat16)
 
 
-def project(ids, quarters, gain, wq, wk, wv, held_back):
+def project(ids, quarters, gain, wq, wk, wv, before, held_back):
     count = ids.shape[0]
     width, queries = wq.shape
     keys = wk.shape[0]
@@ -387,7 +441,7 @@
             pltpu.VMEM((count, rows_dev, size), jnp.bfloat16),
             pltpu.VMEM((2, count, rows_dev, width // count), jnp.bfloat16),
         ],
-        in_specs=[smem()] + [vmem()] * 8 + [hbm()] * len(held_back),
+        in_specs=[smem()] + [vmem()] * 10 + [hbm()] * len(held_back),
         out_specs=[vmem(), vmem()],
         scratch_shapes=[
             pltpu.VMEM((rows, queries), jnp.float32),
@@ -395,10 +449,8 @@
             pltpu.VMEM((rows, width if by_rows else 128), jnp.float32),
         ],
         compiler_params=pltpu.CompilerParams(vmem_limit_bytes=(3 << 20) + 4 * rows * width),
-        cost_estimate=pl.CostEstimate(
-            flops=2 * rows * width * size, bytes_accessed=2 * width * size, transcendentals=0
-        ),
-    )(ids, *quarters, gain, *in_vmem((wq, wk, wv, *held_back)))
+        cost_estimate=project_cost(rows, width, size),
+    )(ids, *quarters, gain, *in_vmem((wq, wk, wv)), *before, *in_vmem(held_back))
 
 
 def attend_kernel(where_ref, length_ref, in_ref, cos_ref, sin_ref, key_buf, value_buf, out_ref,
@@ -808,8 +860,9 @@
     wk = w_key[0].T
     wv = w_value[0].T
     blocks = w_gate_up.shape[3] // 128
-    windows = 2 * len(chip_masks()) - 2
-    bounds = [(4 * blocks * step + windows) // (2 * windows) for step in range(windows + 1)]
+    levels = len(chip_masks())
+    loads = np.array([5] + [3] * (levels - 2) + [5] + [3] * (levels - 2))
+    bounds = [0, *np.rint(2 * blocks * np.cumsum(loads) / np.sum(loads)).astype(int).tolist()]
     batches = [
         jnp.remainder(section_index + turn_index, 2).astype(jnp.int32).reshape(1)
         for turn_index in range(2)
@@ -841,15 +894,25 @@
             return got, [lambda token: early, projections], [out_projection, caches]
         return got, [projections, caches, out_projection], []
 
+    def passed(quarters, held_back):
+        far_parts = quarters[2]
+        (far_parts,) = step_call(pass_kernel, [far_parts.shape], (far_parts,), held_back)
+        return *quarters[:2], far_parts, swap(far_parts, 1)
+
     got, jobs, rest = attention_jobs(0)
     quarters = gather_doubling(hidden[0], jobs)
-    for job in rest:
-        job(quarters[0])
+    waited = [array for job in rest for array in job(quarters[0])]
+    before = [jnp.zeros((8, 128), jnp.float32)] * 2
     for turn_index in range(2):
         last = turn_index == 1
         batch = batches[turn_index]
         held_back = (*got["out"], *got["caches"])
-        joined, by_owner = project(places, all_quarters(quarters), attn_gain, *got["qkv"], held_back)
+        if last:
+            before = waited = project_near(places, *quarters[:2], attn_gain, *got["qkv"])
+        quarters = passed(quarters, waited)
+        joined, by_owner = project(
+            places, quarters, attn_gain, *got["qkv"], before, held_back
+        )
         if turn_index == 0:
             addend = by_owner
         spread = lax.all_to_all(joined, "mp", split_axis=0, concat_axis=0)
@@ -886,9 +949,7 @@
         down = []
         for which, first in enumerate(quarter_starts(count)[:3]):
             if which == 2:
-                far_parts = quarters[2]
-                (far_parts,) = step_call(pass_kernel, [far_parts.shape], (far_parts,), (total,))
-                quarters = all_quarters((*quarters[:2], far_parts))
+                quarters = passed(quarters, (total,))
             fetch_first = (0, count // 4, None)[which]
             total, got_down = quarter(
                 first, fetch_first, places, quarters[which], mlp_gain, total, w_down[0],

time: 205 us -> 201 us (0.980)
  waiting for transfers between devices: 18.7 us -> 13.6 us
    ppermute x29, waiting for transfers between devices: 17.9 us -> 13.2 us  [swap(): lax.ppermute(value, axis, [(source, source ^ mask) for source in range(co...]
    ppermute x3 -> x2, starting transfers between devices: 4.14 us -> 3.7 us  [hop(): return lax.ppermute(part, ('section', 'mp'), pairs)]
  transfers between devices with their start and end apart: 32 -> 31, of which waited for: 11 -> 13; matrix products, arithmetic and copies ran while one was open for 1% -> 1% of each run, Pallas kernels for 37% -> 38%
where the time goes in v8:
time: 201 us
  Pallas kernels  104 us (52%)
  blocking collectives  52.8 us (26%)
  starting transfers between devices  26 us (13%)
  waiting for transfers between devices  13.6 us (7%)
  other arithmetic  2.65 us (1%)
    pallas_call x8, Pallas kernels, fetch_pairs(): pl.pallas_call(functools.partial(fetch_pairs_kernel, items), out_shape=[p...  33.7 us
    ppermute x29, starting transfers between devices, swap(): lax.ppermute(value, axis, [(source, source ^ mask) for source in range(co...  22.3 us
    all_to_all x2, blocking collectives, body(): spread = lax.all_to_all(joined, 'mp', split_axis=0, concat_axis=0)  21.1 us
    all_to_all x2, blocking collectives, body(): lax.all_to_all(mixed.transpose(1, 0, 2), 'mp', split_axis=0, concat_axis=0)  18.4 us
    pallas_call x6, Pallas kernels, quarter(): pl.pallas_call(functools.partial(quarter_kernel, first, fetch_first), out...  16.7 us
    pallas_call x4, Pallas kernels, fetch(): pl.pallas_call(functools.partial(fetch_kernel, pieces, len(tokens)), out_...  15.5 us
    all_to_all x1, blocking collectives, exchange(): lax.all_to_all(parts, 'mp', split_axis=0, concat_axis=0, axis_index_group...  13.3 us
    ppermute x29, waiting for transfers between devices, swap(): lax.ppermute(value, axis, [(source, source ^ mask) for source in range(co...  13.2 us
  transfers between devices with their start and end apart: 31, of which 13 were waited for; matrix products, arithmetic and copies ran while one was open for 1% of the time, Pallas kernels for 38%

profile of v8, /device:TPU:0, one launch (start us, length us, event | category | flops | bytes accessed | tf_op | source)
XLA Modules:
  0.0 200.6 jit_solution(12366488052456604801)
XLA Ops:
  0.0 4.0 %collective-permute-start = (bf16[1,2,8192]{2,1,0:T(2,128)(2,1)}, bf16[1,2,8192]{2,1,0:T(2,128)(2,1)S(1)}, u32[]{:S(2)}, u32[]{:S(2)}) collective-permute-start(bf16[1,2,8192]{2,1,0:T(2,128)(2,1)} %in_ref.1), channel_id=1, source_target_pairs={{0,8},{1,9},{2,10},{3,11},{4,12},{5,13},{6,14},{7,15},{8,0},{9,1},... | collective-permute-start | bytes 98312 | tf_op jit(solution)/shard_map/ppermute | solution.py:22
  8.2 4.3 %shard_map.129 = (bf16[8192,512]{1,0:T(8,128)(2,1)S(1)}, bf16[64,8192]{1,0:T(8,128)(2,1)S(1)}, bf16[64,8192]{1,0:T(8,128)(2,1)S(1)}) custom-call(bf16[2,2,8192]{2,1,0:T(2,128)(2,1)S(1)} %shard_map.128.refs_0_.low_ref, bf16[8192,512]{1,0:T(8,128)(2,1)} %bitcast.139, bf16[64,8192]{1,0:T(8,128)(2,1)} %bitcast.147, bf16[64,8192]{1,0:T(8,128)(2,1)} %bitcast.149), custom_call_target="tpu_custom_call" | custom-call | bytes 10485760 | tf_op jit(solution)/shard_map/pallas_call | solution.py:83
  14.1 3.5 %shard_map.131.refs_0_.refs_10_.w_ref = bf16[512,8192]{1,0:T(8,128)(2,1)S(1)} custom-call(bf16[4,2,8192]{2,1,0:T(2,128)(2,1)S(1)} %shard_map.130.refs_0_, bf16[512,8192]{1,0:T(8,128)(2,1)} %bitcast.141), custom_call_target="tpu_custom_call" | custom-call | bytes 8388608 | tf_op jit(solution)/shard_map/pallas_call | solution.py:83
  17.6 2.2 %shard_map.132 = (bf16[2,512,1024]{2,1,0:T(8,128)(2,1)S(1)}, bf16[2,512,1024]{2,1,0:T(8,128)(2,1)S(1)}) custom-call(s32[1]{0:T(128)} %bitcast.1.refs_4_.where_ref, bf16[2,2,512,1024]{3,2,1,0:T(8,128)(2,1)} %bitcast.143, bf16[2,2,512,1024]{3,2,1,0:T(8,128)(2,1)} %bitcast.145, bf16[4,2,8192]{2,1,0:T(2,128)(2,1)S(1)} %shard_map.130.refs_0_), custom_call_target="tpu_custom_call" | custom-call | bytes 4194304 | tf_op jit(solution)/shard_map/pallas_call | solution.py:117
  21.5 3.6 %shard_map.134 = (bf16[16,2,640]{2,1,0:T(2,128)(2,1)S(1)}, bf16[2,16,2,512]{3,2,1,0:T(2,128)(2,1)S(1)}) custom-call(s32[16]{0:T(128)S(1)} %pad_add_fusion.refs_0_.ids_ref, bf16[4,2,8192]{2,1,0:T(2,128)(2,1)S(1)} %shard_map.130.refs_0_, bf16[4,2,8192]{2,1,0:T(2,128)(2,1)S(1)} %collective-permute-done.2.refs_1_, bf16[4,2,8192]{2,1,0:T(2,128)(2,1)S(1)} %shard_map.133.refs_2_, ...), custom_call_target="tpu_custom_call" | custom-call | flops 335544320 | bytes 10485760 | tf_op jit(solution)/shard_map/pallas_call | solution.py:438
  25.1 10.5 %all_to_all.25.in_ref = bf16[16,2,640]{2,1,0:T(2,128)(2,1)S(1)} all-to-all(bf16[16,2,640]{2,1,0:T(2,128)(2,1)S(1)} %get-tuple-element.85), channel_id=1, replica_groups=mesh['section'=2,'mp'=16] {'mp'}, dimensions={0} | all-to-all | bytes 81920 | tf_op jit(solution)/shard_map/all_to_all | solution.py:918
  35.7 2.5 %shard_map.135 = bf16[2,16,512]{2,1,0:T(8,128)(2,1)S(1)} custom-call(s32[1]{0:T(128)} %bitcast.1.refs_4_.where_ref, s32[2,2]{1,0:T(2,128)S(1)} %copy-done.3, bf16[16,2,640]{2,1,0:T(2,128)(2,1)S(1)} %all_to_all.25.in_ref, f32[2,128]{1,0:T(2,128)S(1)} %get-tuple-element.166.refs_6_.cos_ref, f32[2,128]{1,0:T(2,128)S(1)} %get-tuple-element.167.refs_7_.sin_ref, ...), custom_call_target="tpu_custom_call" | custom-call | flops 268435456 | bytes 4194304 | tf_op jit(solution)/shard_map/pallas_call | solution.py:534
  38.2 9.2 %all_to_all.26.x_ref = bf16[16,2,512]{2,1,0:T(2,128)(2,1)S(1)} all-to-all(bf16[16,2,512]{2,1,0:T(2,128)(2,1)S(1)} %bitcast.151), channel_id=1, replica_groups=mesh['section'=2,'mp'=16] {'mp'}, dimensions={0} | all-to-all | bytes 65536 | tf_op jit(solution)/shard_map/all_to_all | solution.py:922
  51.1 4.9 %shard_map.139 = (bf16[4096,2,128]{2,1,0:T(2,128)(2,1)S(1)}, bf16[4096,2,128]{2,1,0:T(2,128)(2,1)S(1)}, bf16[4096,2,128]{2,1,0:T(2,128)(2,1)S(1)}, bf16[4096,2,1...) custom-call(s32[16]{0:T(128)S(1)} %pad_add_fusion.refs_0_.ids_ref, bf16[4,32,512]{2,1,0:T(8,128)(2,1)S(1)} %get-tuple-element.87.token_ref, ...), custom_call_target="tpu_custom_call" | custom-call | bytes 10485760 | tf_op jit(solution)/shard_map/pallas_call | solution.py:152
  57.0 3.5 %shard_map.141 = (bf16[4096,2,128]{2,1,0:T(2,128)(2,1)S(1)}, bf16[4096,2,128]{2,1,0:T(2,128)(2,1)S(1)}, bf16[4096,2,128]{2,1,0:T(2,128)(2,1)S(1)}) custom-call(s32[16]{0:T(128)S(1)} %pad_add_fusion.refs_0_.ids_ref, bf16[2,32,512]{2,1,0:T(8,128)(2,1)S(1)} %get-tuple-element.94.token_ref, bf16[8192,2,1024]{2,1,0:T(2,128)(2,1)} %bitcast.124), custom_call_target="tpu_custom_call" | custom-call | bytes 6291456 | tf_op jit(solution)/shard_map/pallas_call | solution.py:152
  61.4 4.9 %shard_map.143 = (bf16[4096,2,128]{2,1,0:T(2,128)(2,1)S(1)}, bf16[4096,2,128]{2,1,0:T(2,128)(2,1)S(1)}, bf16[4096,2,128]{2,1,0:T(2,128)(2,1)S(1)}, bf16[4096,2,1...) custom-call(s32[16]{0:T(128)S(1)} %pad_add_fusion.refs_0_.ids_ref, bf16[2,32,512]{2,1,0:T(8,128)(2,1)S(1)} %shard_map.142.token_ref.here_ref, ...), custom_call_target="tpu_custom_call" | custom-call | bytes 10485760 | tf_op jit(solution)/shard_map/pallas_call | solution.py:152
  67.7 3.5 %shard_map.145 = (bf16[4096,2,128]{2,1,0:T(2,128)(2,1)S(1)}, bf16[4096,2,128]{2,1,0:T(2,128)(2,1)S(1)}, bf16[4096,2,128]{2,1,0:T(2,128)(2,1)S(1)}) custom-call(s32[16]{0:T(128)S(1)} %pad_add_fusion.refs_0_.ids_ref, bf16[2,32,512]{2,1,0:T(8,128)(2,1)S(1)} %shard_map.144.token_ref.low_ref.high_ref, bf16[8192,2,1024]{2,1,0:T(2,128)(2,1)} %bitcast.126), custom_call_target="tpu_custom_call" | custom-call | bytes 6291456 | tf_op jit(solution)/shard_map/pallas_call | solution.py:152
  72.8 2.8 %shard_map.147 = (f32[64,1024]{1,0:T(8,128)S(1)}, bf16[4,1024,512]{2,1,0:T(8,128)(2,1)S(1)}) custom-call(s32[16]{0:T(128)S(1)} %pad_add_fusion.refs_0_.ids_ref, bf16[4,32,512]{2,1,0:T(8,128)(2,1)S(1)} %shard_map.146.x_ref.refs_0_, f32[1,8192]{1,0:T(1,128)S(1)} %copy-done, f32[8,128]{1,0:T(8,128)S(1)} %broadcast_5_refs_8__refs_9__before_ref.2.refs_8_.refs_9_.before_ref, ...), custom_call_target="tpu_custom_call" | custom-call | flops 268435456 | bytes 8388608 | tf_op jit(solution)/shard_map/pallas_call | solution.py:676
  75.7 2.9 %shard_map.148 = (f32[64,1024]{1,0:T(8,128)S(1)}, bf16[4,1024,512]{2,1,0:T(8,128)(2,1)S(1)}) custom-call(s32[16]{0:T(128)S(1)} %pad_add_fusion.refs_0_.ids_ref, bf16[4,32,512]{2,1,0:T(8,128)(2,1)S(1)} %collective-permute-done.10.x_ref.refs_1_, f32[1,8192]{1,0:T(1,128)S(1)} %copy-done, f32[64,1024]{1,0:T(8,128)S(1)} %get-tuple-element.106.before_ref, ...), custom_call_target="tpu_custom_call" | custom-call | flops 268435456 | bytes 8388608 | tf_op jit(solution)/shard_map/pallas_call | solution.py:676
  78.8 2.6 %shard_map.150 = (f32[64,1024]{1,0:T(8,128)S(1)}, bf16[1,8,128]{2,1,0:T(8,128)(2,1)}) custom-call(s32[16]{0:T(128)S(1)} %pad_add_fusion.refs_0_.ids_ref, bf16[4,32,512]{2,1,0:T(8,128)(2,1)S(1)} %shard_map.149.x_ref.refs_2_, f32[1,8192]{1,0:T(1,128)S(1)} %copy-done, f32[64,1024]{1,0:T(8,128)S(1)} %get-tuple-element.107.refs_0_.before_ref, ...), custom_call_target="tpu_custom_call" | custom-call | flops 268435456 | bytes 8388608 | tf_op jit(solution)/shard_map/pallas_call | solution.py:676
  81.5 5.9 %shard_map.151 = (bf16[8,32,512]{2,1,0:T(8,128)(2,1)S(1)}, bf16[32,1024]{1,0:T(8,128)(2,1)S(1)}, f32[8,128]{1,0:T(8,128)}) custom-call(s32[1]{0:T(128)} %bitcast.refs_3_.me_ref, s32[16]{0:T(128)S(1)} %pad_add_fusion.refs_0_.ids_ref, bf16[4,32,512]{2,1,0:T(8,128)(2,1)S(1)} %shard_map.146.x_ref.refs_0_, ...), custom_call_target="tpu_custom_call" | custom-call | flops 805306368 | bytes 16777216 | tf_op jit(solution)/shard_map/pallas_call | solution.py:770
  90.1 4.3 %shard_map.154 = (bf16[8192,512]{1,0:T(8,128)(2,1)S(1)}, bf16[64,8192]{1,0:T(8,128)(2,1)S(1)}, bf16[64,8192]{1,0:T(8,128)(2,1)S(1)}) custom-call(bf16[4,32,512]{2,1,0:T(8,128)(2,1)S(1)} %get-tuple-element.114.refs_0_, bf16[8192,512]{1,0:T(8,128)(2,1)} %bitcast.140, bf16[64,8192]{1,0:T(8,128)(2,1)} %bitcast.148, bf16[64,8192]{1,0:T(8,128)(2,1)} %bitcast.150), custom_call_target="tpu_custom_call" | custom-call | bytes 10485760 | tf_op jit(solution)/shard_map/pallas_call | solution.py:83
  103.1 3.5 %shard_map.159.refs_0_.refs_10_.w_ref = bf16[512,8192]{1,0:T(8,128)(2,1)S(1)} custom-call(bf16[2,32,512]{2,1,0:T(8,128)(2,1)S(1)} %shard_map.157.low_ref.refs_0_, bf16[512,8192]{1,0:T(8,128)(2,1)} %bitcast.142), custom_call_target="tpu_custom_call" | custom-call | bytes 8388608 | tf_op jit(solution)/shard_map/pallas_call | solution.py:83
  108.5 3.0 %collective-permute-done.18.high_ref = bf16[2,32,512]{2,1,0:T(8,128)(2,1)S(1)} collective-permute-done((bf16[2,32,512]{2,1,0:T(8,128)(2,1)S(1)}, bf16[2,32,512]{2,1,0:T(8,128)(2,1)S(1)}, u32[]{:S(2)}, u32[]{:S(2)}) %collective-permute-start.18) | collective-permute-done | bytes 65568 | tf_op jit(solution)/shard_map/ppermute | solution.py:22
  114.5 2.9 %collective-permute-done.20.in_ref = bf16[4,32,512]{2,1,0:T(8,128)(2,1)S(1)} collective-permute-done((bf16[4,32,512]{2,1,0:T(8,128)(2,1)S(1)}, bf16[4,32,512]{2,1,0:T(8,128)(2,1)S(1)}, u32[]{:S(2)}, u32[]{:S(2)}) %collective-permute-start.20) | collective-permute-done | bytes 131104 | tf_op jit(solution)/shard_map/ppermute | solution.py:22
  121.0 10.6 %all_to_all.27.in_ref = bf16[16,2,640]{2,1,0:T(2,128)(2,1)S(1)} all-to-all(bf16[16,2,640]{2,1,0:T(2,128)(2,1)S(1)} %get-tuple-element.124), channel_id=1, replica_groups=mesh['section'=2,'mp'=16] {'mp'}, dimensions={0} | all-to-all | bytes 81920 | tf_op jit(solution)/shard_map/all_to_all | solution.py:918
  131.6 2.5 %shard_map.165 = bf16[2,16,512]{2,1,0:T(8,128)(2,1)S(1)} custom-call(s32[1]{0:T(128)} %bitcast.2.refs_5_.where_ref, s32[2,2]{1,0:T(2,128)S(1)} %copy-done.3, bf16[16,2,640]{2,1,0:T(2,128)(2,1)S(1)} %all_to_all.27.in_ref, f32[2,128]{1,0:T(2,128)S(1)} %get-tuple-element.168.refs_8_.cos_ref, f32[2,128]{1,0:T(2,128)S(1)} %get-tuple-element.169.refs_9_.sin_ref, ...), custom_call_target="tpu_custom_call" | custom-call | flops 268435456 | bytes 4194304 | tf_op jit(solution)/shard_map/pallas_call | solution.py:534
  134.1 9.2 %all_to_all.28.x_ref = bf16[16,2,512]{2,1,0:T(2,128)(2,1)S(1)} all-to-all(bf16[16,2,512]{2,1,0:T(2,128)(2,1)S(1)} %bitcast.152), channel_id=1, replica_groups=mesh['section'=2,'mp'=16] {'mp'}, dimensions={0} | all-to-all | bytes 65536 | tf_op jit(solution)/shard_map/all_to_all | solution.py:922
  146.9 4.9 %shard_map.169 = (bf16[4096,2,128]{2,1,0:T(2,128)(2,1)S(1)}, bf16[4096,2,128]{2,1,0:T(2,128)(2,1)S(1)}, bf16[4096,2,128]{2,1,0:T(2,128)(2,1)S(1)}, bf16[4096,2,1...) custom-call(s32[16]{0:T(128)S(1)} %pad_add_fusion.refs_0_.ids_ref, bf16[4,32,512]{2,1,0:T(8,128)(2,1)S(1)} %get-tuple-element.126.token_ref, ...), custom_call_target="tpu_custom_call" | custom-call | bytes 10485760 | tf_op jit(solution)/shard_map/pallas_call | solution.py:152
  152.8 3.5 %shard_map.171 = (bf16[4096,2,128]{2,1,0:T(2,128)(2,1)S(1)}, bf16[4096,2,128]{2,1,0:T(2,128)(2,1)S(1)}, bf16[4096,2,128]{2,1,0:T(2,128)(2,1)S(1)}) custom-call(s32[16]{0:T(128)S(1)} %pad_add_fusion.refs_0_.ids_ref, bf16[2,32,512]{2,1,0:T(8,128)(2,1)S(1)} %get-tuple-element.133.token_ref, bf16[8192,2,1024]{2,1,0:T(2,128)(2,1)} %bitcast.128), custom_call_target="tpu_custom_call" | custom-call | bytes 6291456 | tf_op jit(solution)/shard_map/pallas_call | solution.py:152
  157.3 4.9 %shard_map.173 = (bf16[4096,2,128]{2,1,0:T(2,128)(2,1)S(1)}, bf16[4096,2,128]{2,1,0:T(2,128)(2,1)S(1)}, bf16[4096,2,128]{2,1,0:T(2,128)(2,1)S(1)}, bf16[4096,2,1...) custom-call(s32[16]{0:T(128)S(1)} %pad_add_fusion.refs_0_.ids_ref, bf16[2,32,512]{2,1,0:T(8,128)(2,1)S(1)} %shard_map.172.token_ref.here_ref, ...), custom_call_target="tpu_custom_call" | custom-call | bytes 10485760 | tf_op jit(solution)/shard_map/pallas_call | solution.py:152
  163.6 3.5 %shard_map.175 = (bf16[4096,2,128]{2,1,0:T(2,128)(2,1)S(1)}, bf16[4096,2,128]{2,1,0:T(2,128)(2,1)S(1)}, bf16[4096,2,128]{2,1,0:T(2,128)(2,1)S(1)}) custom-call(s32[16]{0:T(128)S(1)} %pad_add_fusion.refs_0_.ids_ref, bf16[2,32,512]{2,1,0:T(8,128)(2,1)S(1)} %shard_map.174.token_ref.low_ref, bf16[8192,2,1024]{2,1,0:T(2,128)(2,1)} %bitcast.130), custom_call_target="tpu_custom_call" | custom-call | bytes 6291456 | tf_op jit(solution)/shard_map/pallas_call | solution.py:152
  168.7 2.8 %shard_map.177 = (f32[64,1024]{1,0:T(8,128)S(1)}, bf16[4,1024,512]{2,1,0:T(8,128)(2,1)S(1)}) custom-call(s32[16]{0:T(128)S(1)} %pad_add_fusion.refs_0_.ids_ref, bf16[4,32,512]{2,1,0:T(8,128)(2,1)S(1)} %shard_map.176.x_ref.refs_0_, f32[1,8192]{1,0:T(1,128)S(1)} %copy-done, f32[8,128]{1,0:T(8,128)S(1)} %broadcast_5_refs_8__refs_9__before_ref.2.refs_8_.refs_9_.before_ref, ...), custom_call_target="tpu_custom_call" | custom-call | flops 268435456 | bytes 8388608 | tf_op jit(solution)/shard_map/pallas_call | solution.py:676
  171.6 2.9 %shard_map.178 = (f32[64,1024]{1,0:T(8,128)S(1)}, bf16[4,1024,512]{2,1,0:T(8,128)(2,1)S(1)}) custom-call(s32[16]{0:T(128)S(1)} %pad_add_fusion.refs_0_.ids_ref, bf16[4,32,512]{2,1,0:T(8,128)(2,1)S(1)} %collective-permute-done.27.x_ref.refs_1_, f32[1,8192]{1,0:T(1,128)S(1)} %copy-done, f32[64,1024]{1,0:T(8,128)S(1)} %get-tuple-element.145.before_ref, ...), custom_call_target="tpu_custom_call" | custom-call | flops 268435456 | bytes 8388608 | tf_op jit(solution)/shard_map/pallas_call | solution.py:676
  174.7 2.6 %shard_map.180 = (f32[64,1024]{1,0:T(8,128)S(1)}, bf16[1,8,128]{2,1,0:T(8,128)(2,1)}) custom-call(s32[16]{0:T(128)S(1)} %pad_add_fusion.refs_0_.ids_ref, bf16[4,32,512]{2,1,0:T(8,128)(2,1)S(1)} %shard_map.179.x_ref.refs_2_, f32[1,8192]{1,0:T(1,128)S(1)} %copy-done, f32[64,1024]{1,0:T(8,128)S(1)} %get-tuple-element.146.refs_0_.before_ref, ...), custom_call_target="tpu_custom_call" | custom-call | flops 268435456 | bytes 8388608 | tf_op jit(solution)/shard_map/pallas_call | solution.py:676
  177.4 7.2 %shard_map.181 = (bf16[8,2,8192]{2,1,0:T(2,128)(2,1)S(1)}, bf16[8,2,8192]{2,1,0:T(2,128)(2,1)S(1)}, f32[2,8192]{1,0:T(2,128)S(1)}) custom-call(s32[1]{0:T(128)} %bitcast.refs_3_.me_ref, s32[16]{0:T(128)S(1)} %pad_add_fusion.refs_0_.ids_ref, bf16[4,32,512]{2,1,0:T(8,128)(2,1)S(1)} %shard_map.176.x_ref.refs_0_, ...), custom_call_target="tpu_custom_call" | custom-call | flops 805306368 | bytes 16777216 | tf_op jit(solution)/shard_map/pallas_call | solution.py:770
  186.5 13.3 %all_to_all.29 = bf16[8,2,8192]{2,1,0:T(2,128)(2,1)S(1)} all-to-all(bf16[8,2,8192]{2,1,0:T(2,128)(2,1)S(1)} %shard_map.182), channel_id=1, replica_groups={{0,2,4,6,8,10,12,14},{1,3,5,7,9,11,13,15},{16,18,20,22,24,26,28,30},{17..., dimensions={0} | all-to-all | bytes 524288 | tf_op jit(solution)/shard_map/all_to_all | solution.py:28
  (111 shorter events, 47.4 us)
Async XLA Ops:
  0.0 6.6 %collective-permute-start = (bf16[1,2,8192]{2,1,0:T(2,128)(2,1)}, bf16[1,2,8192]{2,1,0:T(2,128)(2,1)S(1)}, u32[]{:S(2)}, u32[]{:S(2)}) collective-permute-start(bf16[1,2,8192]{2,1,0:T(2,128)(2,1)} %in_ref.1), channel_id=1, source_target_pairs={{0,8},{1,9},{2,10},{3,11},{4,12},{5,13},{6,14},{7,15},{8,0},{9,1},... | collective-permute-start | bytes 98312 | tf_op jit(solution)/shard_map/ppermute | solution.py:22
  6.6 5.9 %collective-permute-start.1 = (bf16[2,2,8192]{2,1,0:T(2,128)(2,1)S(1)}, bf16[2,2,8192]{2,1,0:T(2,128)(2,1)S(1)}, u32[]{:S(2)}, u32[]{:S(2)}) collective-permute-start(bf16[2,2,8192]{2,1,0:T(2,128)(2,1)S(1)} %shard_map.128.refs_0_.low_ref), channel_id=1, source_target_pairs={{0,4},{1,5},{2,6},{3,7},{4,0},{5,1},{6,2},{7,3},{8,12},{9,13},{10,... | collective-permute-start | bytes 196616 | tf_op jit(solution)/shard_map/ppermute | solution.py:22
  12.6 7.3 %collective-permute-start.3 = (bf16[4,2,8192]{2,1,0:T(2,128)(2,1)S(1)}, bf16[4,2,8192]{2,1,0:T(2,128)(2,1)S(1)}, u32[]{:S(2)}, u32[]{:S(2)}) collective-permute-start(bf16[4,2,8192]{2,1,0:T(2,128)(2,1)S(1)} %shard_map.130.refs_0_), channel_id=1, source_target_pairs={{0,2},{1,3},{2,0},{3,1},{4,6},{5,7},{6,4},{7,5},{8,10},{9,11},{10,... | collective-permute-start | bytes 393224 | tf_op jit(solution)/shard_map/ppermute | solution.py:22
  14.1 6.4 %collective-permute-start.2 = (bf16[4,2,8192]{2,1,0:T(2,128)(2,1)S(1)}, bf16[4,2,8192]{2,1,0:T(2,128)(2,1)S(1)}, u32[]{:S(2)}, u32[]{:S(2)}) collective-permute-start(bf16[4,2,8192]{2,1,0:T(2,128)(2,1)S(1)} %shard_map.130.refs_0_), channel_id=1, source_target_pairs={{0,1},{1,0},{2,3},{3,2},{4,5},{5,4},{6,7},{7,6},{8,9},{9,8},{10,11... | collective-permute-start | bytes 393224 | tf_op jit(solution)/shard_map/ppermute | solution.py:22
  19.9 1.6 collective-permute-start.4
  21.5 14.2 %copy-start.3 = (s32[2,2]{1,0:T(2,128)S(1)}, s32[2,2]{1,0:T(2,128)}, u32[]{:S(2)}) copy-start(s32[2,2]{1,0:T(2,128)} %length_ref.3) | copy-start | bytes 52
  48.9 1.6 collective-permute-start.5
  50.5 6.0 %collective-permute-start.6 = (bf16[4,32,512]{2,1,0:T(8,128)(2,1)S(1)}, bf16[4,32,512]{2,1,0:T(8,128)(2,1)S(1)}, u32[]{:S(2)}, u32[]{:S(2)}) collective-permute-start(bf16[4,32,512]{2,1,0:T(8,128)(2,1)S(1)} %get-tuple-element.87.token_ref), channel_id=1, source_target_pairs={{0,2},{1,3},{2,0},{3,1},{4,6},{5,7},{6,4},{7,5},{8,10},{9,11},{10,... | collective-permute-start | bytes 393224 | tf_op jit(solution)/shard_map/ppermute | solution.py:22
  56.5 4.3 %collective-permute-start.7 = (bf16[2,32,512]{2,1,0:T(8,128)(2,1)S(1)}, bf16[2,32,512]{2,1,0:T(8,128)(2,1)S(1)}, u32[]{:S(2)}, u32[]{:S(2)}) collective-permute-start(bf16[2,32,512]{2,1,0:T(8,128)(2,1)S(1)} %get-tuple-element.94.token_ref), channel_id=1, source_target_pairs={{0,4},{1,5},{2,6},{3,7},{4,0},{5,1},{6,2},{7,3},{8,12},{9,13},{10,... | collective-permute-start | bytes 196616 | tf_op jit(solution)/shard_map/ppermute | solution.py:22
  60.9 5.4 %collective-permute-start.8 = (bf16[2,32,512]{2,1,0:T(8,128)(2,1)S(1)}, bf16[2,32,512]{2,1,0:T(8,128)(2,1)S(1)}, u32[]{:S(2)}, u32[]{:S(2)}) collective-permute-start(bf16[2,32,512]{2,1,0:T(8,128)(2,1)S(1)} %shard_map.142.token_ref.here_ref), channel_id=1, source_target_pairs={{0,8},{1,9},{2,10},{3,11},{4,12},{5,13},{6,14},{7,15},{8,0},{9,1},... | collective-permute-start | bytes 196616 | tf_op jit(solution)/shard_map/ppermute | solution.py:22
  66.4 4.9 %collective-permute-start.9 = (bf16[2,32,512]{2,1,0:T(8,128)(2,1)S(1)}, bf16[2,32,512]{2,1,0:T(8,128)(2,1)S(1)}, u32[]{:S(2)}, u32[]{:S(2)}) collective-permute-start(bf16[2,32,512]{2,1,0:T(8,128)(2,1)S(1)} %shard_map.144.token_ref.low_ref.high_ref), channel_id=1, source_target_pairs={{0,4},{1,5},{2,6},{3,7},{4,0},{5,1},{6,2},{7,3},{8,12},{9,13},{10,... | collective-permute-start | bytes 196616 | tf_op jit(solution)/shard_map/ppermute | solution.py:22
  71.3 4.4 %collective-permute-start.10 = (bf16[4,32,512]{2,1,0:T(8,128)(2,1)S(1)}, bf16[4,32,512]{2,1,0:T(8,128)(2,1)S(1)}, u32[]{:S(2)}, u32[]{:S(2)}) collective-permute-start(bf16[4,32,512]{2,1,0:T(8,128)(2,1)S(1)} %shard_map.146.x_ref.refs_0_), channel_id=1, source_target_pairs={{0,1},{1,0},{2,3},{3,2},{4,5},{5,4},{6,7},{7,6},{8,9},{9,8},{10,11... | collective-permute-start | bytes 393224 | tf_op jit(solution)/shard_map/ppermute | solution.py:22
  71.4 7.2 %collective-permute-start.11 = (bf16[4,32,512]{2,1,0:T(8,128)(2,1)S(1)}, bf16[4,32,512]{2,1,0:T(8,128)(2,1)S(1)}, u32[]{:S(2)}, u32[]{:S(2)}) collective-permute-start(bf16[4,32,512]{2,1,0:T(8,128)(2,1)S(1)} %shard_map.146.x_ref.refs_0_), channel_id=1, source_target_pairs={{0,2},{1,3},{2,0},{3,1},{4,6},{5,7},{6,4},{7,5},{8,10},{9,11},{10,... | collective-permute-start | bytes 393224 | tf_op jit(solution)/shard_map/ppermute | solution.py:22
  78.6 2.9 %collective-permute-start.12 = (bf16[4,32,512]{2,1,0:T(8,128)(2,1)S(1)}, bf16[4,32,512]{2,1,0:T(8,128)(2,1)S(1)}, u32[]{:S(2)}, u32[]{:S(2)}) collective-permute-start(bf16[4,32,512]{2,1,0:T(8,128)(2,1)S(1)} %shard_map.149.x_ref.refs_2_), channel_id=1, source_target_pairs={{0,1},{1,0},{2,3},{3,2},{4,5},{5,4},{6,7},{7,6},{8,9},{9,8},{10,11... | collective-permute-start | bytes 393224 | tf_op jit(solution)/shard_map/ppermute | solution.py:22
  87.4 2.0 collective-permute-start.13
  89.4 5.6 %collective-permute-start.14 = (bf16[4,32,512]{2,1,0:T(8,128)(2,1)S(1)}, bf16[4,32,512]{2,1,0:T(8,128)(2,1)S(1)}, u32[]{:S(2)}, u32[]{:S(2)}) collective-permute-start(bf16[4,32,512]{2,1,0:T(8,128)(2,1)S(1)} %get-tuple-element.114.refs_0_), channel_id=1, source_target_pairs={{0,2},{1,3},{2,0},{3,1},{4,6},{5,7},{6,4},{7,5},{8,10},{9,11},{10,... | collective-permute-start | bytes 393224 | tf_op jit(solution)/shard_map/ppermute | solution.py:22
  95.1 4.3 %collective-permute-start.15 = (bf16[2,32,512]{2,1,0:T(8,128)(2,1)S(1)}, bf16[2,32,512]{2,1,0:T(8,128)(2,1)S(1)}, u32[]{:S(2)}, u32[]{:S(2)}) collective-permute-start(bf16[2,32,512]{2,1,0:T(8,128)(2,1)S(1)} %get-tuple-element.119.refs_0_), channel_id=1, source_target_pairs={{0,4},{1,5},{2,6},{3,7},{4,0},{5,1},{6,2},{7,3},{8,12},{9,13},{10,... | collective-permute-start | bytes 196616 | tf_op jit(solution)/shard_map/ppermute | solution.py:22
  99.4 7.6 %collective-permute-start.16 = (bf16[4,32,512]{2,1,0:T(8,128)(2,1)S(1)}, bf16[4,32,512]{2,1,0:T(8,128)(2,1)S(1)}, u32[]{:S(2)}, u32[]{:S(2)}) collective-permute-start(bf16[4,32,512]{2,1,0:T(8,128)(2,1)S(1)} %shard_map.158), channel_id=1, source_target_pairs={{0,16},{1,17},{2,18},{3,19},{4,20},{5,21},{6,22},{7,23},{8,24},{9,... | collective-permute-start | bytes 393224 | tf_op jit(solution)/shard_map/ppermute | solution.py:251
  101.0 6.1 %collective-permute-start.17 = (bf16[2,32,512]{2,1,0:T(8,128)(2,1)S(1)}, bf16[2,32,512]{2,1,0:T(8,128)(2,1)S(1)}, u32[]{:S(2)}, u32[]{:S(2)}) collective-permute-start(bf16[2,32,512]{2,1,0:T(8,128)(2,1)S(1)} %shard_map.157.low_ref.refs_0_), channel_id=1, source_target_pairs={{0,24},{1,25},{2,26},{3,27},{4,28},{5,29},{6,30},{7,31},{8,16},{9,... | collective-permute-start | bytes 196616 | tf_op jit(solution)/shard_map/ppermute | solution.py:251
  107.1 4.3 %collective-permute-start.18 = (bf16[2,32,512]{2,1,0:T(8,128)(2,1)S(1)}, bf16[2,32,512]{2,1,0:T(8,128)(2,1)S(1)}, u32[]{:S(2)}, u32[]{:S(2)}) collective-permute-start(bf16[2,32,512]{2,1,0:T(8,128)(2,1)S(1)} %shard_map.160.low_ref.addend_ref), channel_id=1, source_target_pairs={{0,4},{1,5},{2,6},{3,7},{4,0},{5,1},{6,2},{7,3},{8,12},{9,13},{10,... | collective-permute-start | bytes 196616 | tf_op jit(solution)/shard_map/ppermute | solution.py:22
  111.4 1.4 collective-permute-start.19
  111.5 5.9 %collective-permute-start.20 = (bf16[4,32,512]{2,1,0:T(8,128)(2,1)S(1)}, bf16[4,32,512]{2,1,0:T(8,128)(2,1)S(1)}, u32[]{:S(2)}, u32[]{:S(2)}) collective-permute-start(bf16[4,32,512]{2,1,0:T(8,128)(2,1)S(1)} %shard_map.161.near_ref.refs_0_), channel_id=1, source_target_pairs={{0,2},{1,3},{2,0},{3,1},{4,6},{5,7},{6,4},{7,5},{8,10},{9,11},{10,... | collective-permute-start | bytes 393224 | tf_op jit(solution)/shard_map/ppermute | solution.py:22
  117.4 1.4 collective-permute-start.21
  144.8 1.6 collective-permute-start.22
  146.4 6.0 %collective-permute-start.23 = (bf16[4,32,512]{2,1,0:T(8,128)(2,1)S(1)}, bf16[4,32,512]{2,1,0:T(8,128)(2,1)S(1)}, u32[]{:S(2)}, u32[]{:S(2)}) collective-permute-start(bf16[4,32,512]{2,1,0:T(8,128)(2,1)S(1)} %get-tuple-element.126.token_ref), channel_id=1, source_target_pairs={{0,2},{1,3},{2,0},{3,1},{4,6},{5,7},{6,4},{7,5},{8,10},{9,11},{10,... | collective-permute-start | bytes 393224 | tf_op jit(solution)/shard_map/ppermute | solution.py:22
  152.4 4.3 %collective-permute-start.24 = (bf16[2,32,512]{2,1,0:T(8,128)(2,1)S(1)}, bf16[2,32,512]{2,1,0:T(8,128)(2,1)S(1)}, u32[]{:S(2)}, u32[]{:S(2)}) collective-permute-start(bf16[2,32,512]{2,1,0:T(8,128)(2,1)S(1)} %get-tuple-element.133.token_ref), channel_id=1, source_target_pairs={{0,4},{1,5},{2,6},{3,7},{4,0},{5,1},{6,2},{7,3},{8,12},{9,13},{10,... | collective-permute-start | bytes 196616 | tf_op jit(solution)/shard_map/ppermute | solution.py:22
  156.8 5.4 %collective-permute-start.25 = (bf16[2,32,512]{2,1,0:T(8,128)(2,1)S(1)}, bf16[2,32,512]{2,1,0:T(8,128)(2,1)S(1)}, u32[]{:S(2)}, u32[]{:S(2)}) collective-permute-start(bf16[2,32,512]{2,1,0:T(8,128)(2,1)S(1)} %shard_map.172.token_ref.here_ref), channel_id=1, source_target_pairs={{0,8},{1,9},{2,10},{3,11},{4,12},{5,13},{6,14},{7,15},{8,0},{9,1},... | collective-permute-start | bytes 196616 | tf_op jit(solution)/shard_map/ppermute | solution.py:22
  162.2 4.9 %collective-permute-start.26 = (bf16[2,32,512]{2,1,0:T(8,128)(2,1)S(1)}, bf16[2,32,512]{2,1,0:T(8,128)(2,1)S(1)}, u32[]{:S(2)}, u32[]{:S(2)}) collective-permute-start(bf16[2,32,512]{2,1,0:T(8,128)(2,1)S(1)} %shard_map.174.token_ref.low_ref), channel_id=1, source_target_pairs={{0,4},{1,5},{2,6},{3,7},{4,0},{5,1},{6,2},{7,3},{8,12},{9,13},{10,... | collective-permute-start | bytes 196616 | tf_op jit(solution)/shard_map/ppermute | solution.py:22
  167.1 4.4 %collective-permute-start.27 = (bf16[4,32,512]{2,1,0:T(8,128)(2,1)S(1)}, bf16[4,32,512]{2,1,0:T(8,128)(2,1)S(1)}, u32[]{:S(2)}, u32[]{:S(2)}) collective-permute-start(bf16[4,32,512]{2,1,0:T(8,128)(2,1)S(1)} %shard_map.176.x_ref.refs_0_), channel_id=1, source_target_pairs={{0,1},{1,0},{2,3},{3,2},{4,5},{5,4},{6,7},{7,6},{8,9},{9,8},{10,11... | collective-permute-start | bytes 393224 | tf_op jit(solution)/shard_map/ppermute | solution.py:22
  167.2 7.2 %collective-permute-start.28 = (bf16[4,32,512]{2,1,0:T(8,128)(2,1)S(1)}, bf16[4,32,512]{2,1,0:T(8,128)(2,1)S(1)}, u32[]{:S(2)}, u32[]{:S(2)}) collective-permute-start(bf16[4,32,512]{2,1,0:T(8,128)(2,1)S(1)} %shard_map.176.x_ref.refs_0_), channel_id=1, source_target_pairs={{0,2},{1,3},{2,0},{3,1},{4,6},{5,7},{6,4},{7,5},{8,10},{9,11},{10,... | collective-permute-start | bytes 393224 | tf_op jit(solution)/shard_map/ppermute | solution.py:22
  174.5 2.9 %collective-permute-start.29 = (bf16[4,32,512]{2,1,0:T(8,128)(2,1)S(1)}, bf16[4,32,512]{2,1,0:T(8,128)(2,1)S(1)}, u32[]{:S(2)}, u32[]{:S(2)}) collective-permute-start(bf16[4,32,512]{2,1,0:T(8,128)(2,1)S(1)} %shard_map.179.x_ref.refs_2_), channel_id=1, source_target_pairs={{0,1},{1,0},{2,3},{3,2},{4,5},{5,4},{6,7},{7,6},{8,9},{9,8},{10,11... | collective-permute-start | bytes 393224 | tf_op jit(solution)/shard_map/ppermute | solution.py:22
  184.6 1.6 collective-permute-start.30
  (3 other events, 3.9 us)
